TPU v7x, 32 devices: a whole 2x2x4 slice. The times are simulated.
32 devices in a mesh: groups: 2 (over y), wide: 4 (over z), planes: 2 (over x), rep: 2 (over core).
Axes of the slice: x: 2, y: 2, z: 4, core: 2. Of those that a mesh axis runs over, the one named last changes fastest.
Arguments:
- movie_frames: bfloat16 [4, 128, 256, 128], P('planes', ('groups', 'wide'), 'rep'), parts along dimension 1, may hold values from -6 to 6
- pixel_mask: int32 [256, 128], P('rep'), may hold values 0 or 1
- tile_owner: int32 [256, 1], P('rep'), may hold values from 0 to 3; in each aligned block of 128 rows (0 to 127, 128 to 255, ...) at most 48 rows name the same one
- support: int32 [256, 128], P('rep'), may hold values from 0 to 511
- templates: bfloat16 [512, 4, 128], P(None, 'planes'), may hold values from -0.25 to 0.25
- row_taps: float32 [25], replicated, may hold values from -1.25 to 1.25
- col_taps: float32 [25], replicated, may hold values from -1.25 to 1.25
- lag_gains: float32 [4, 3, 65], P('wide'), may hold values from -0.4375 to 0.4375
- dilations: int32 [4, 3], P('wide'), may hold values from 1 to 8
Outputs:
- traces: bfloat16 [128, 128, 256], P('planes', ('groups', 'wide'), 'rep'), parts along dimension 1
- back_projected: bfloat16 [4, 128, 256, 128], P('planes', ('groups', 'wide'), 'rep'), parts along dimension 1
There are 2 independent parts, one for each index of `groups`. A program takes and returns all parts, laid end to end along the dimension named above; an argument that names none is the same for every part. Nothing has to cross between parts.
Inputs may be any that keep to these rules, and one draw needn't show every extreme that they name: Strip h belongs to region class tile_owner[h,0]; the 128 rows of one device name each class at most 48 times.
All inputs are finite; a program needn't handle non-finite values. No bound on the sum of `pixel_mask` on one device may be relied on, other than what follows from the above.
Results may differ from a plain program's by a relative error of at most 0.015.
Values may be sent and summed in bfloat16 or wider, within the bound.
No kernel may reach another device: no remote copies, remote signals or barrier semaphores. Data moves between devices by JAX's collectives and lax.ppermute only.
A program may use at most 64 MiB of HBM per device.

v0:
```python
import jax
import jax.numpy as jnp
from jax import lax
from jax.sharding import PartitionSpec as P


def extended(cells, sides, width):
    for axis, dim in sides:
        count = lax.axis_size(axis)
        ends = count - 1
        head = lax.slice_in_dim(cells, 0, width, axis=dim)
        tail = lax.slice_in_dim(cells, cells.shape[dim] - width, cells.shape[dim], axis=dim)
        cells = jnp.concatenate(
            [
                lax.ppermute(tail, axis, [(i, (i + 1) % count) for i in range(ends)]),
                cells,
                lax.ppermute(head, axis, [((i + 1) % count, i) for i in range(ends)]),
            ],
            axis=dim,
        )
    return cells


def band_matrix(tap_values, rows_in, rows_out, sign, offset):
    inner_idx = jnp.arange(rows_in, dtype=jnp.int32)[:, None]
    outer_idx = jnp.arange(rows_out, dtype=jnp.int32)[None, :]
    where_tap = sign * (inner_idx - outer_idx) + offset
    tap_index = jnp.arange(tap_values.shape[0], dtype=jnp.int32)
    picked_taps = where_tap[:, :, None] == tap_index[None, None, :]
    weights = jnp.where(picked_taps, tap_values[None, None, :], jnp.zeros((), tap_values.dtype))
    return jnp.sum(weights, axis=2).astype(jnp.bfloat16)


def lag_matrix(cluster_gains, cluster_lags, frame_count):
    tap_count = cluster_gains.shape[1]
    half_taps = (tap_count - 1) // 2
    lag_values = jnp.arange(2 * frame_count - 1, dtype=jnp.int32) - (frame_count - 1)
    tap_offsets = jnp.arange(tap_count, dtype=jnp.int32) - half_taps
    lag_hits = lag_values[None, :, None] == cluster_lags[:, None, None] * tap_offsets[None, None, :]
    spread = jnp.where(lag_hits, cluster_gains[:, None, :], jnp.zeros((), cluster_gains.dtype))
    kernel = jnp.sum(spread, axis=(0, 2))
    flipped = jnp.concatenate([kernel[::-1], jnp.zeros((1,), kernel.dtype)])
    tiled = jnp.broadcast_to(flipped, (frame_count, 2 * frame_count)).reshape(-1)
    tiled = tiled[: frame_count * (2 * frame_count - 1)].reshape(frame_count, 2 * frame_count - 1)
    return tiled[:, frame_count - 1 :].astype(jnp.bfloat16)


def slot_table(owners, cluster_count, capacity):
    row_count = owners.shape[0]
    owner_marks = (owners[:, None] == jnp.arange(cluster_count, dtype=jnp.int32)[None, :]).astype(
        jnp.int32
    )
    before = jnp.cumsum(owner_marks, axis=0) - owner_marks
    slot_ranks = jnp.sum(before * owner_marks, axis=1)
    slot_of = owners * capacity + slot_ranks
    places = jnp.arange(cluster_count * capacity, dtype=jnp.int32)
    chosen = (slot_of[None, :] == places[:, None]).astype(jnp.int32)
    sources = jnp.sum(chosen * jnp.arange(row_count, dtype=jnp.int32)[None, :], axis=1)
    return (slot_of, sources)


def on_device(
    movie_frames,
    pixel_mask,
    tile_owner,
    support,
    templates,
    row_taps,
    col_taps,
    lag_gains,
    dilations,
):
    planes_here, frames_here, rows_here, col_count = movie_frames.shape
    wide_count = lax.axis_size("wide")
    capacity = max(2, 3 * rows_here // (2 * wide_count))
    rim_width = (row_taps.shape[0] - 1) // 2
    mask_value = pixel_mask.astype(jnp.float32)
    col_fwd = band_matrix(col_taps, col_count, col_count, 1, rim_width)
    smooth = jnp.dot(movie_frames, col_fwd, preferred_element_type=jnp.float32).astype(jnp.bfloat16)
    padded = extended(smooth, (("rep", 2),), rim_width)
    row_fwd = band_matrix(row_taps, rows_here + 2 * rim_width, rows_here, 1, 0)
    along = jnp.einsum("pfew,eh->pfhw", padded, row_fwd, preferred_element_type=jnp.float32)
    filtered = (along * mask_value[None, None]).astype(jnp.bfloat16)
    owners = tile_owner[:, 0]
    slot_of, sources = slot_table(owners, wide_count, capacity)
    packed = jnp.take(filtered, sources, axis=2)
    wide_here = lax.axis_index("wide")
    my_sources = lax.dynamic_slice_in_dim(sources, wide_here * capacity, capacity, 0)
    lag_table = lag_matrix(lag_gains[0], dilations[0], frames_here * wide_count)
    columns = lax.all_to_all(packed, "wide", split_axis=2, concat_axis=1, tiled=True)
    mixed_part = jnp.einsum("pscw,st->ptcw", columns, lag_table, preferred_element_type=jnp.float32)
    columns, mixed_cols = (columns, mixed_part.astype(jnp.bfloat16))
    shapes = jnp.take(templates, jnp.take(support, my_sources, axis=0), axis=0)
    partial_scores = jnp.einsum(
        "cjpw,ptcw->cjt", shapes, mixed_cols, preferred_element_type=jnp.float32
    )
    plane_count = lax.axis_size("planes")
    share_rows = shapes.shape[1] // plane_count
    plane_here = lax.axis_index("planes")
    scores = lax.psum(partial_scores.astype(jnp.bfloat16), "planes").astype(jnp.float32)
    traces = jnp.maximum(scores, 0.0).astype(jnp.bfloat16)
    trace_share = lax.dynamic_slice_in_dim(traces, plane_here * share_rows, share_rows, 1)
    model_part = jnp.einsum("cjpw,cjt->ptcw", shapes, traces, preferred_element_type=jnp.float32)
    slot_masks = jnp.take(mask_value, my_sources, axis=0)
    resid_cols = (columns.astype(jnp.float32) - slot_masks[None, None] * model_part).astype(
        jnp.bfloat16
    )
    resid_back = lax.all_to_all(resid_cols, "wide", split_axis=1, concat_axis=2, tiled=True)
    residual = jnp.take(resid_back, slot_of, axis=2)
    share_back = lax.all_to_all(trace_share, "wide", split_axis=2, concat_axis=0, tiled=True)
    tile_share = jnp.take(share_back, slot_of, axis=0)
    padded_back = extended(residual, (("rep", 2),), rim_width)
    row_adj = band_matrix(row_taps, rows_here + 2 * rim_width, rows_here, -1, 2 * rim_width)
    back_rows = jnp.einsum(
        "pfew,eh->pfhw", padded_back, row_adj, preferred_element_type=jnp.float32
    ).astype(jnp.bfloat16)
    col_adj = band_matrix(col_taps, col_count, col_count, -1, rim_width)
    back_projected = jnp.dot(back_rows, col_adj, preferred_element_type=jnp.float32).astype(
        jnp.bfloat16
    )
    trace_out = jnp.transpose(tile_share, (1, 2, 0))
    return (trace_out, back_projected)


def solution(mesh):
    return jax.shard_map(
        on_device,
        mesh=mesh,
        in_specs=(
            P("planes", ("groups", "wide"), "rep", None),
            P("rep", None),
            P("rep", None),
            P("rep", None),
            P(None, "planes", None),
            P(),
            P(),
            P("wide", None, None),
            P("wide", None),
        ),
        out_specs=(
            P("planes", ("groups", "wide"), "rep"),
            P("planes", ("groups", "wide"), "rep", None),
        ),
        check_vma=False,
    )
```

profile of v0, /device:TPU:1, one launch (start us, length us, event | category | flops | bytes accessed | tf_op | source)
XLA Modules:
  0.0 193.1 jit_solution(7658494077274293809)
XLA Ops:
  7.2 1.1 select_reduce_fusion.2
  8.4 0.4 fusion.9
  8.9 1.3 collective-permute-start
  10.2 3.0 %collective-permute-start.1 = (bf16[2,16,12,128]{3,2,1,0:T(8,128)(2,1)S(1)}, bf16[2,16,12,128]{3,2,1,0:T(8,128)(2,1)S(1)}, u32[]{:S(2)}, u32[]{:S(2)}) collective-permute-start(bf16[2,16,12,128]{3,2,1,0:T(8,128)(2,1)S(1)} %get-tuple-element.21), channel_id=1, source_target_pairs={{1,0},{3,2},{5,4},{7,6},{9,8},{11,10},{13,12},{15,14},{17,16},{19,... | collective-permute-start | bytes 294920 | tf_op jit(solution)/shard_map/ppermute | solution.py:17
  13.3 0.1 fusion.29
  13.4 0.2 reduce_window_sum.11
  13.5 0.2 select_reduce_fusion.6
  13.7 0.1 select_reduce_fusion.5
  13.9 0.4 select_reduce_fusion
  14.4 0.7 fusion.8
  15.1 0.7 copy.43
  15.8 2.1 %gather_fusion.2 = bf16[192,2,16,128]{3,2,1,0:T(8,128)(2,1)} fusion(bf16[2,16,128,128]{3,1,2,0:T(8,128)(2,1)S(1)} %copy.43, s32[1024]{0:T(1024)S(1)} %pad_clamp_fusion.1), kind=kCustom, calls=%fused_computation.2 | custom fusion | bytes 3146496 | tf_op jit(solution)/shard_map/jit(_take)/gather | solution.py:86
  17.8 2.8 %select_bitcast_fusion = bf16[2,16,192,128]{3,1,0,2:T(8,128)(2,1)} fusion(bf16[192,2,16,128]{3,2,1,0:T(8,128)(2,1)} %gather_fusion.2, pred[192]{0:T(512)(128)(4,1)S(1)} %compare_and_fusion.1), kind=kLoop, calls=%fused_computation.23 | loop fusion | flops 786432 | bytes 3145920 | tf_op jit(solution)/shard_map/jit(_take)/select_n | solution.py:86
  20.7 5.6 %all-to-all-start = ((bf16[2,16,192,128]{3,1,0,2:T(8,128)(2,1)}), bf16[2,16,192,128]{3,1,0,2:T(8,128)(2,1)S(1)}, u32[]{:S(2)}, u32[]{:S(2)}) async-start(bf16[2,16,192,128]{3,1,0,2:T(8,128)(2,1)} %select_bitcast_fusion), calls=%async_computation | async-start | bytes 3145728 | tf_op jit(solution)/shard_map/all_to_all | solution.py:90
  26.3 0.1 select_reduce_fusion.4
  26.5 0.1 rev.3
  26.7 0.2 reshape.203
  26.8 0.1 compare_and_fusion.2
  26.9 0.6 gather_fusion
  27.6 40.1 %gather_fusion.1 = bf16[6144,2,128]{2,1,0:T(2,128)(2,1)} fusion(bf16[512,2,128]{2,1,0:T(2,128)(2,1)S(1)} %copy-done.1, s32[6144]{0:T(1024)S(1)} %fusion.41), kind=kCustom, calls=%fused_computation.1 | custom fusion | bytes 6316032 | tf_op jit(solution)/shard_map/jit(_take)/gather | solution.py:93
  67.7 0.1 compare_and_fusion
  67.8 1.6 copy.44
  69.4 5.0 %bitcast_convert_fusion = bf16[48,128,64]{1,2,0:T(8,128)(2,1)} fusion(bf16[2,64,48,128]{3,1,0,2:T(8,128)(2,1)} %bitcast.111, bf16[48,128,2,128]{3,2,1,0:T(2,128)(2,1)} %bitcast.107, pred[48,128]{1,0:T(8,128)(4,1)S(1)} %compare_and_fusion, bf16[64,127]{1,0:T(8,128)(2,1)S(1)} %reshape.203), kind=kOutput, calls=%fused_computation.21 | convolution fusion | flops 304742400 | bytes 5527424 | tf_op jit(solution)/shard_map/cjpw,ptcw->cjt/dot_general | solution.py:94
  74.5 0.6 gather_fusion.4
  75.0 35.2 %all-reduce.2.cloned.1.call-done = bf16[48,128,64]{1,2,0:T(8,128)(2,1)} async-done(((bf16[48,128,64]{1,2,0:T(8,128)(2,1)}), bf16[48,128,64]{1,2,0:T(8,128)(2,1)}) %all-reduce.2.cloned.1.call-update) | async-done | bytes 786448 | tf_op jit(solution)/shard_map/psum | solution.py:100
  110.2 1.3 maximum_convert_fusion
  111.5 0.3 constant_dynamic-slice_fusion
  111.9 0.5 copy.74
  112.4 1.3 reshape.262
  113.7 4.3 %all-to-all-start.1 = ((bf16[4,2,24576]{2,1,0:T(2,128)(2,1)}), bf16[4,2,24576]{2,1,0:T(2,128)(2,1)S(1)}, u32[]{:S(2)}, u32[]{:S(2)}) async-start(bf16[4,2,24576]{2,1,0:T(2,128)(2,1)} %reshape.262), calls=%async_computation.1 | async-start | bytes 786432 | tf_op jit(solution)/shard_map/all_to_all | solution.py:110
  118.1 3.5 %fusion = bf16[2,64,48,128]{3,1,0,2:T(8,128)(2,1)S(1)} fusion(bf16[2,64,48,128]{3,1,0,2:T(8,128)(2,1)S(1)} %bitcast.112, f32[48,128]{1,0:T(8,128)S(1)} %broadcast_select_fusion, bf16[48,128,2,128]{3,2,1,0:T(2,128)(2,1)} %bitcast.108, pred[48,128]{1,0:T(8,128)(4,1)S(1)} %compare_and_fusion, bf16[48,128,64]{1,2,0:T(8,128)(2,1)} %all-reduce.2.cloned.1.call-done), kind=kOutput, calls=%fused_computation.7 | convolution fusion | flops 207224832 | bytes 7108608 | tf_op jit(solution)/shard_map/cjpw,cjt->ptcw/dot_general | solution.py:103
  121.5 2.8 %copy.47 = bf16[2,64,48,128]{3,0,2,1:T(2,128)(2,1)} copy(bf16[2,64,48,128]{3,1,0,2:T(8,128)(2,1)S(1)} %fusion) | data formatting | bytes 3145728 | tf_op jit(solution)/shard_map/convert_element_type | solution.py:105
  124.3 4.6 %all-to-all-done.1 = bf16[4,2,24576]{2,1,0:T(2,128)(2,1)S(1)} async-done(((bf16[4,2,24576]{2,1,0:T(2,128)(2,1)}), bf16[4,2,24576]{2,1,0:T(2,128)(2,1)S(1)}, u32[]{:S(2)}, u32[]{:S(2)}) %all-to-all-start.1) | async-done | bytes 393248 | tf_op jit(solution)/shard_map/all_to_all | solution.py:110
  128.9 4.5 %all-to-all-start.2 = ((bf16[2,64,48,128]{3,0,2,1:T(2,128)(2,1)}), bf16[2,64,48,128]{3,0,2,1:T(2,128)(2,1)}, u32[]{:S(2)}, u32[]{:S(2)}) async-start(bf16[2,64,48,128]{3,0,2,1:T(2,128)(2,1)} %copy.47), calls=%async_computation.2 | async-start | bytes 3145728 | tf_op jit(solution)/shard_map/all_to_all | solution.py:108
  133.5 0.5 reshape.263
  134.0 0.2 copy.46
  134.2 0.7 gather_fusion.3
  134.9 34.9 %all-to-all-done.2 = bf16[2,64,48,128]{3,0,2,1:T(2,128)(2,1)} async-done(((bf16[2,64,48,128]{3,0,2,1:T(2,128)(2,1)}), bf16[2,64,48,128]{3,0,2,1:T(2,128)(2,1)}, u32[]{:S(2)}, u32[]{:S(2)}) %all-to-all-start.2) | async-done | bytes 1572896 | tf_op jit(solution)/shard_map/all_to_all | solution.py:108
  169.8 1.6 copy.48
  171.4 0.2 copy.49
  171.6 1.0 copy.50
  172.6 1.7 gather_fusion.5
  174.3 1.7 fusion.26
  176.1 1.3 collective-permute-start.2
  177.4 4.6 %collective-permute-start.3 = (bf16[2,16,12,128]{3,2,1,0:T(8,128)(2,1)S(1)}, bf16[2,16,12,128]{3,2,1,0:T(8,128)(2,1)}, u32[]{:S(2)}, u32[]{:S(2)}) collective-permute-start(bf16[2,16,12,128]{3,2,1,0:T(8,128)(2,1)S(1)} %get-tuple-element.19), channel_id=1, source_target_pairs={{1,0},{3,2},{5,4},{7,6},{9,8},{11,10},{13,12},{15,14},{17,16},{19,... | collective-permute-start | bytes 294920 | tf_op jit(solution)/shard_map/ppermute | solution.py:17
  182.0 0.2 select_bitcast_fusion.1
  182.2 1.3 copy.52
  183.5 2.8 %convolution_convert_fusion.1 = bf16[2,16,128,128]{3,2,1,0:T(8,128)(2,1)} fusion(bf16[2,16,12,128]{3,2,1,0:T(8,128)(2,1)} %collective-permute-done.3, bf16[2,16,128,128]{3,2,1,0:T(8,128)(2,1)S(1)} %fusion.26, bf16[2,16,12,128]{3,2,1,0:T(8,128)(2,1)} %collective-permute-done.2, bf16[152,128]{1,0:T(8,128)(2,1)S(1)} %get-tuple-element.12, ...), kind=kOutput, calls=%fused_computation.27 | convolution fusion | flops 298385408 | bytes 2365440 | tf_op jit(solution)/shard_map/dot_general | solution.py:118
  (45 shorter events, 0.6 us)
Async XLA Ops:
  7.2 1.2 copy-start
  7.2 6.1 %copy-start.5 = (s32[128,1]{0,1:T(1,128)S(1)}, s32[128,1]{0,1:T(1,128)}, u32[]{:S(2)}) copy-start(s32[128,1]{0,1:T(1,128)} %param.11) | copy-start | bytes 1540
  7.2 6.6 %copy-start.4 = (s32[128,128]{1,0:T(8,128)S(1)}, s32[128,128]{1,0:T(8,128)}, u32[]{:S(2)}) copy-start(s32[128,128]{1,0:T(8,128)} %param.10) | copy-start | bytes 196612
  8.4 5.5 %copy-start.7 = (f32[25]{0:T(128)S(1)}, f32[25]{0:T(128)}, u32[]{:S(2)}) copy-start(f32[25]{0:T(128)} %param.14) | copy-start | bytes 304
  8.9 5.5 %collective-permute-start = (bf16[2,16,12,128]{3,2,1,0:T(8,128)(2,1)S(1)}, bf16[2,16,12,128]{3,2,1,0:T(8,128)(2,1)S(1)}, u32[]{:S(2)}, u32[]{:S(2)}) collective-permute-start(bf16[2,16,12,128]{3,2,1,0:T(8,128)(2,1)S(1)} %get-tuple-element.20), channel_id=1, source_target_pairs={{0,1},{2,3},{4,5},{6,7},{8,9},{10,11},{12,13},{14,15},{16,17},{18,... | collective-permute-start | bytes 294920 | tf_op jit(solution)/shard_map/ppermute | solution.py:15
  10.2 4.2 %collective-permute-start.1 = (bf16[2,16,12,128]{3,2,1,0:T(8,128)(2,1)S(1)}, bf16[2,16,12,128]{3,2,1,0:T(8,128)(2,1)S(1)}, u32[]{:S(2)}, u32[]{:S(2)}) collective-permute-start(bf16[2,16,12,128]{3,2,1,0:T(8,128)(2,1)S(1)} %get-tuple-element.21), channel_id=1, source_target_pairs={{1,0},{3,2},{5,4},{7,6},{9,8},{11,10},{13,12},{15,14},{17,16},{19,... | collective-permute-start | bytes 294920 | tf_op jit(solution)/shard_map/ppermute | solution.py:17
  20.6 5.6 %copy-start.6 = (f32[1,3,65]{2,0,1:T(1,128)S(1)}, f32[1,3,65]{2,0,1:T(1,128)}, u32[]{:S(2)}) copy-start(f32[1,3,65]{2,0,1:T(1,128)} %param.16) | copy-start | bytes 2344
  20.7 5.6 %copy-start.8 = (s32[1,3]{1,0:T(1,128)S(1)}, s32[1,3]{1,0:T(1,128)}, u32[]{:S(2)}) copy-start(s32[1,3]{1,0:T(1,128)} %param.17) | copy-start | bytes 40
  20.7 6.3 %copy-start.3 = (s32[128,128]{1,0:T(8,128)S(1)}, s32[128,128]{1,0:T(8,128)}, u32[]{:S(2)}) copy-start(s32[128,128]{1,0:T(8,128)} %param.12) | copy-start | bytes 196612
  20.7 6.9 %copy-start.1 = (bf16[512,2,128]{2,1,0:T(2,128)(2,1)S(1)}, bf16[512,2,128]{2,1,0:T(2,128)(2,1)}, u32[]{:S(2)}) copy-start(bf16[512,2,128]{2,1,0:T(2,128)(2,1)} %param.13) | copy-start | bytes 786436
  20.7 47.1 %all-to-all-start = ((bf16[2,16,192,128]{3,1,0,2:T(8,128)(2,1)}), bf16[2,16,192,128]{3,1,0,2:T(8,128)(2,1)S(1)}, u32[]{:S(2)}, u32[]{:S(2)}) async-start(bf16[2,16,192,128]{3,1,0,2:T(8,128)(2,1)} %select_bitcast_fusion), calls=%async_computation | async-start | bytes 3145728 | tf_op jit(solution)/shard_map/all_to_all | solution.py:90
  26.2 84.0 %all-reduce.2.cloned.1.call-start = ((), (), s32[]{:S(2)}) async-start(), calls=%async_computation.3 | async-start | bytes 1572864 | tf_op jit(solution)/shard_map/psum | solution.py:100
  111.8 6.2 %copy-start.2 = (bf16[2,16,4,48,128]{4,1,2,0,3:T(8,128)(2,1)S(1)}, bf16[2,16,4,48,128]{4,1,2,0,3:T(8,128)(2,1)}, u32[]{:S(2)}) copy-start(bf16[2,16,4,48,128]{4,1,2,0,3:T(8,128)(2,1)} %copy.44) | copy-start | bytes 4718596
  113.7 15.2 %all-to-all-start.1 = ((bf16[4,2,24576]{2,1,0:T(2,128)(2,1)}), bf16[4,2,24576]{2,1,0:T(2,128)(2,1)S(1)}, u32[]{:S(2)}, u32[]{:S(2)}) async-start(bf16[4,2,24576]{2,1,0:T(2,128)(2,1)} %reshape.262), calls=%async_computation.1 | async-start | bytes 786432 | tf_op jit(solution)/shard_map/all_to_all | solution.py:110
  128.9 40.9 %all-to-all-start.2 = ((bf16[2,64,48,128]{3,0,2,1:T(2,128)(2,1)}), bf16[2,64,48,128]{3,0,2,1:T(2,128)(2,1)}, u32[]{:S(2)}, u32[]{:S(2)}) async-start(bf16[2,64,48,128]{3,0,2,1:T(2,128)(2,1)} %copy.47), calls=%async_computation.2 | async-start | bytes 3145728 | tf_op jit(solution)/shard_map/all_to_all | solution.py:108
  176.1 7.4 %collective-permute-start.2 = (bf16[2,16,12,128]{3,2,1,0:T(8,128)(2,1)S(1)}, bf16[2,16,12,128]{3,2,1,0:T(8,128)(2,1)}, u32[]{:S(2)}, u32[]{:S(2)}) collective-permute-start(bf16[2,16,12,128]{3,2,1,0:T(8,128)(2,1)S(1)} %get-tuple-element.18), channel_id=1, source_target_pairs={{0,1},{2,3},{4,5},{6,7},{8,9},{10,11},{12,13},{14,15},{16,17},{18,... | collective-permute-start | bytes 294920 | tf_op jit(solution)/shard_map/ppermute | solution.py:15
  177.4 6.1 %collective-permute-start.3 = (bf16[2,16,12,128]{3,2,1,0:T(8,128)(2,1)S(1)}, bf16[2,16,12,128]{3,2,1,0:T(8,128)(2,1)}, u32[]{:S(2)}, u32[]{:S(2)}) collective-permute-start(bf16[2,16,12,128]{3,2,1,0:T(8,128)(2,1)S(1)} %get-tuple-element.19), channel_id=1, source_target_pairs={{1,0},{3,2},{5,4},{7,6},{9,8},{11,10},{13,12},{15,14},{17,16},{19,... | collective-permute-start | bytes 294920 | tf_op jit(solution)/shard_map/ppermute | solution.py:17
Sparse Core Ops, SparseCore 0:
  74.6 35.5 all-reduce.1
where the time goes:
time: 194 us; the launch traced here: 193 us
  waiting for transfers between devices  74.7 us (39%)
  local copies, waits for them, and re-layouts  58.2 us (30%)
  starting transfers between devices  24.7 us (13%)
  between operations  14.4 us (7%)
  matrix products  12.3 us (6%)
  other arithmetic  8.88 us (5%)
    gather x2, local copies, waits for them, and re-layouts, on_device(): shapes = jnp.take(templates, jnp.take(support, my_sources, axis=0), axis=0)  40.7 us
    psum x1, waiting for transfers between devices, on_device(): lax.psum(partial_scores.astype(jnp.bfloat16), 'planes').astype(jnp.float32)  35.2 us
    all_to_all x1, waiting for transfers between devices, on_device(): lax.all_to_all(resid_cols, 'wide', split_axis=1, concat_axis=2, tiled=True)  34.9 us
    ppermute x2, starting transfers between devices, extended(): lax.ppermute(head, axis, [((i + 1) % count, i) for i in range(ends)])  7.68 us
    all_to_all x1, starting transfers between devices, on_device(): lax.all_to_all(packed, 'wide', split_axis=2, concat_axis=1, tiled=True)  5.55 us
    dot_general x1, matrix products, on_device(): jnp.einsum('cjpw,ptcw->cjt', shapes, mixed_cols, preferred_element_type=j...  5.01 us
    all_to_all x1, waiting for transfers between devices, on_device(): lax.all_to_all(trace_share, 'wide', split_axis=2, concat_axis=0, tiled=True)  4.58 us
    all_to_all x1, starting transfers between devices, on_device(): lax.all_to_all(resid_cols, 'wide', split_axis=1, concat_axis=2, tiled=True)  4.53 us
  transfers between devices with their start and end apart: 8, of which 3 were waited for; matrix products, arithmetic and copies ran while one was open for 27% of the time, Pallas kernels for 0%

commit v1 on v0

v1 whole, which is shorter than its diff:
```python
import functools

import jax
import jax.numpy as jnp
from jax import lax
from jax.experimental import pallas as pl
from jax.experimental.pallas import tpu as pltpu
from jax.sharding import PartitionSpec as P

BLOCK = 16
LANES = 128
F32 = jnp.float32
BF16 = jnp.bfloat16


def halo_pair(cells, axis, dim, width):
    count = lax.axis_size(axis)
    extent = cells.shape[dim]
    if count == 2:
        start = jnp.where(lax.axis_index(axis) == 0, extent - width, 0)
        edge = lax.dynamic_slice_in_dim(cells, start, width, axis=dim)
        other = lax.ppermute(edge, axis, [(0, 1), (1, 0)])
        return other, other
    head = lax.slice_in_dim(cells, 0, width, axis=dim)
    tail = lax.slice_in_dim(cells, extent - width, extent, axis=dim)
    above = lax.ppermute(tail, axis, [(i, i + 1) for i in range(count - 1)])
    below = lax.ppermute(head, axis, [(i + 1, i) for i in range(count - 1)])
    return above, below


def iota(shape, dim):
    return lax.broadcasted_iota(jnp.int32, shape, dim)


def column_band(lane_taps, rim):
    shape = (LANES, LANES)
    rolled = pltpu.roll(jnp.broadcast_to(lane_taps, shape), 0, 1, stride=1, stride_axis=0)
    gap = iota(shape, 1) - iota(shape, 0)
    return jnp.where(jnp.abs(gap) <= rim, rolled, 0.0).astype(BF16)


def row_band(lane_taps):
    rolled = pltpu.roll(
        jnp.broadcast_to(lane_taps, (BLOCK, LANES)), 0, 1, stride=1, stride_axis=0
    )
    return rolled[:, : 3 * BLOCK].astype(BF16)


def expand_forward(band, frames):
    out_rows, depth, span = BLOCK * frames, 3 * BLOCK * frames, 3 * BLOCK
    left = (iota((out_rows, BLOCK), 0) // frames == iota((out_rows, BLOCK), 1)).astype(BF16)
    right = (lax.rem(iota((span, depth), 1), span) == iota((span, depth), 0)).astype(BF16)
    wide_rows = jnp.dot(left, band, preferred_element_type=F32).astype(BF16)
    spread = jnp.dot(wide_rows, right, preferred_element_type=F32)
    start = iota((out_rows, depth), 1) - span * lax.rem(iota((out_rows, depth), 0), frames)
    return jnp.where((start >= 0) & (start < span), spread, 0.0).astype(BF16)


def expand_adjoint(band, frames):
    out_rows, depth, span = BLOCK * frames, 3 * BLOCK * frames, 3 * BLOCK
    left = (lax.rem(iota((out_rows, BLOCK), 0), BLOCK) == iota((out_rows, BLOCK), 1)).astype(BF16)
    right = (iota((span, depth), 1) // frames == iota((span, depth), 0)).astype(BF16)
    wide_rows = jnp.dot(left, band, preferred_element_type=F32).astype(BF16)
    spread = jnp.dot(wide_rows, right, preferred_element_type=F32)
    same = lax.rem(iota((out_rows, depth), 1), frames) == iota((out_rows, depth), 0) // BLOCK
    return jnp.where(same, spread, 0.0).astype(BF16)


def per_frame(rows, frames, copies):
    tall = jnp.broadcast_to(rows[:, None, :], (BLOCK, frames, LANES)).reshape(BLOCK * frames, LANES)
    return tall if copies == 1 else jnp.concatenate([tall] * copies, axis=1)


def forward_kernel(
    rim, ends_ref, movie_ref, above_ref, below_ref, col_ref, row_ref, mask_ref, support_ref,
    templates_ref, filtered_ref, projected_ref, smooth_ref,
):
    planes, frames, rows, _ = movie_ref.shape
    col_fwd = column_band(col_ref[...], rim)
    row_fwd = expand_forward(row_band(row_ref[...]), frames)
    for p in range(planes):
        lanes = slice(p * LANES, (p + 1) * LANES)

        @pl.loop(0, frames)
        def _(f):
            smooth_ref[f, BLOCK : BLOCK + rows, lanes] = jnp.dot(
                movie_ref[p, f], col_fwd, preferred_element_type=F32
            ).astype(BF16)

        for ref, spot, flag in ((above_ref, 0, 0), (below_ref, BLOCK + rows, 1)):
            edge = jnp.dot(
                ref[p].reshape(frames * BLOCK, LANES), col_fwd, preferred_element_type=F32
            )
            edge = jnp.where(ends_ref[flag] > 0, edge, 0.0).astype(BF16)
            smooth_ref[:, spot : spot + BLOCK, lanes] = edge.reshape(frames, BLOCK, LANES)

    tiles = templates_ref.shape[0] // LANES

    @pl.loop(0, rows // BLOCK)
    def _(b):
        top = pl.multiple_of(b * BLOCK, BLOCK)
        near = smooth_ref[:, pl.ds(top, 3 * BLOCK), :].reshape(
            frames * 3 * BLOCK, planes * LANES
        )
        along = jnp.dot(row_fwd, near, preferred_element_type=F32)
        mask = per_frame(mask_ref[pl.ds(top, BLOCK), :].astype(F32), frames, planes)
        filtered = (along * mask).astype(BF16)
        out_rows = pl.ds(pl.multiple_of(top * frames, BLOCK * frames), BLOCK * frames)
        filtered_ref[out_rows, :] = filtered
        dense = lax.dot_general(
            filtered, templates_ref[...], (((1,), (1,)), ((), ())), preferred_element_type=F32
        )
        picked = per_frame(support_ref[pl.ds(top, BLOCK), :], frames, 1)
        lane, tile = picked & (LANES - 1), picked // LANES
        chosen = jnp.zeros(picked.shape, F32)
        for t in range(tiles):
            found = jnp.take_along_axis(
                dense[:, t * LANES : (t + 1) * LANES], lane, axis=1, mode="promise_in_bounds"
            )
            chosen = jnp.where(tile == t, found, chosen)
        projected_ref[out_rows, :] = chosen.astype(BF16)


def mix_kernel(lag_ref, parts_ref, out_ref):
    planes, wide, rows, frames, lanes = parts_ref.shape

    @pl.loop(0, rows)
    def _(h):
        lag = lag_ref[h]
        total = None
        for p in range(planes):
            cells = parts_ref[p, :, h].reshape(wide * frames, lanes)
            term = jnp.dot(lag, cells, preferred_element_type=F32)
            total = term if total is None else total + term
        traces = jnp.maximum(total, 0.0).astype(BF16).reshape(wide, frames, lanes)
        for p in range(planes):
            out_ref[p, :, h] = traces


def shapes_kernel(support_ref, templates_ref, shapes_ref):
    pairs = shapes_ref.shape[0]
    count = templates_ref.shape[1]
    for i in range(pairs):
        both = jnp.concatenate(
            [support_ref[2 * i : 2 * i + 1, :], support_ref[2 * i + 1 : 2 * i + 2, :]], axis=1
        )
        hits = iota((count, 2 * LANES), 0) == jnp.broadcast_to(both, (count, 2 * LANES))
        shapes_ref[i] = jnp.dot(
            templates_ref[...], hits.astype(BF16), preferred_element_type=F32
        ).astype(BF16)


def residual_kernel(traces_ref, shapes_ref, filtered_ref, mask_ref, out_ref):
    rows, frames, lanes = traces_ref.shape
    copies = filtered_ref.shape[1] // LANES
    mask = mask_ref[...].astype(F32)
    for h in range(rows):
        shape = shapes_ref[h // 2, :, (h % 2) * lanes : (h % 2 + 1) * lanes]
        model = lax.dot_general(
            traces_ref[h], shape, (((1,), (1,)), ((), ())), preferred_element_type=F32
        )
        row = jnp.concatenate([mask[h : h + 1, :]] * copies, axis=1)
        spot = slice(h * frames, (h + 1) * frames)
        out_ref[spot, :] = (filtered_ref[spot, :].astype(F32) - row * model).astype(BF16)


def backward_kernel(
    rim, ends_ref, resid_ref, above_ref, below_ref, col_ref, row_ref, out_ref, padded_ref
):
    planes, frames, rows, _ = out_ref.shape
    edge = BLOCK * frames
    col_adj = column_band(col_ref[...], rim)
    row_adj = expand_adjoint(row_band(row_ref[...]), frames)
    padded_ref[:edge, :] = jnp.where(ends_ref[0] > 0, above_ref[...], jnp.zeros_like(above_ref))
    padded_ref[edge : edge + rows * frames, :] = resid_ref[...]
    padded_ref[edge + rows * frames :, :] = jnp.where(
        ends_ref[1] > 0, below_ref[...], jnp.zeros_like(below_ref)
    )

    @pl.loop(0, rows // BLOCK)
    def _(b):
        near = padded_ref[pl.ds(pl.multiple_of(b * edge, edge), 3 * edge), :]
        back = jnp.dot(row_adj, near, preferred_element_type=F32).astype(BF16)
        top = pl.multiple_of(b * BLOCK, BLOCK)
        for p in range(planes):
            full = jnp.dot(
                back[:, p * LANES : (p + 1) * LANES], col_adj, preferred_element_type=F32
            ).astype(BF16)
            out_ref[p, :, pl.ds(top, BLOCK), :] = full.reshape(frames, BLOCK, LANES)


def vmem(count):
    return [pl.BlockSpec(memory_space=pltpu.VMEM)] * count


def params():
    return pltpu.CompilerParams(vmem_limit_bytes=48 * 1024 * 1024)


def lag_kernel_values(gains, lags, frame_count):
    taps = gains.shape[1]
    lag_values = jnp.arange(2 * frame_count - 1, dtype=jnp.int32) - (frame_count - 1)
    offsets = jnp.arange(taps, dtype=jnp.int32) - (taps - 1) // 2
    hits = lag_values[None, :, None] == lags[:, None, None] * offsets[None, None, :]
    spread = jnp.where(hits, gains[:, None, :], jnp.zeros((), gains.dtype))
    return jnp.sum(spread, axis=(0, 2)).astype(BF16)


def lag_tables(kernels, frame_count):
    rows = kernels.shape[0]
    ext = jnp.pad(kernels, ((0, 0), (0, 1)))
    flat = jnp.broadcast_to(ext[:, None, :], (rows, frame_count, 2 * frame_count))
    flat = flat.reshape(rows, -1)[:, : frame_count * (2 * frame_count - 1)]
    return flat.reshape(rows, frame_count, 2 * frame_count - 1)[:, :, frame_count - 1 :]


def on_device(
    movie_frames, pixel_mask, tile_owner, support, templates, row_taps, col_taps, lag_gains, dilations
):
    planes, frames, rows, cols = movie_frames.shape
    wide, plane_count = lax.axis_size("wide"), lax.axis_size("planes")
    rim = (row_taps.shape[0] - 1) // 2
    total_frames = frames * wide
    share = rows // (wide * plane_count)
    rep, rep_count = lax.axis_index("rep"), lax.axis_size("rep")
    ends = jnp.stack([rep > 0, rep < rep_count - 1]).astype(jnp.int32)
    smem = pl.BlockSpec(memory_space=pltpu.SMEM)

    def around(taps):
        row = jnp.zeros((1, LANES), F32)
        row = lax.dynamic_update_slice(row, taps[None, rim:], (0, 0))
        return lax.dynamic_update_slice(row, taps[None, :rim], (0, LANES - rim))

    def placed(taps):
        spot = BLOCK - rim
        return jnp.pad(taps[None, :], ((0, 0), (spot, LANES - spot - taps.shape[0])))

    above, below = halo_pair(movie_frames, "rep", 2, BLOCK)
    kernel_row = lag_kernel_values(lag_gains[0], dilations[0], total_frames)
    kernels = lax.all_gather(kernel_row, "wide", axis=0)
    flat_templates = templates.reshape(templates.shape[0], planes * cols)

    filtered, projected = pl.pallas_call(
        functools.partial(forward_kernel, rim),
        out_shape=(
            jax.ShapeDtypeStruct((rows * frames, planes * cols), BF16),
            jax.ShapeDtypeStruct((rows * frames, support.shape[1]), BF16),
        ),
        in_specs=[smem] + vmem(8),
        out_specs=tuple(vmem(2)),
        scratch_shapes=[pltpu.VMEM((frames, rows + 2 * BLOCK, planes * cols), BF16)],
        compiler_params=params(),
        cost_estimate=pl.CostEstimate(flops=1700000000, bytes_accessed=4000000, transcendentals=0),
        name="forward",
    )(
        ends, movie_frames, above, below, around(col_taps[::-1]), placed(row_taps), pixel_mask, support,
        flat_templates,
    )
    parts = lax.all_to_all(
        projected.reshape(rows, frames, -1), ("planes", "wide"), split_axis=0, concat_axis=0, tiled=True
    )
    parts = parts.reshape(plane_count, wide, share, frames, -1)

    late_support, late_templates, _ = lax.optimization_barrier((support, flat_templates, projected))
    pairs = rows // 2
    steps = 8
    shapes = pl.pallas_call(
        shapes_kernel,
        grid=(steps,),
        out_shape=jax.ShapeDtypeStruct((pairs, planes * cols, 2 * LANES), BF16),
        in_specs=[
            pl.BlockSpec((rows // steps, LANES), lambda i: (i, 0)),
            pl.BlockSpec((planes * cols, templates.shape[0]), lambda i: (0, 0)),
        ],
        out_specs=pl.BlockSpec((pairs // steps, planes * cols, 2 * LANES), lambda i: (i, 0, 0)),
        compiler_params=params(),
        cost_estimate=pl.CostEstimate(flops=4300000000, bytes_accessed=9000000, transcendentals=0),
        name="shapes",
    )(late_support, late_templates.T)

    here = lax.axis_index("planes") * wide + lax.axis_index("wide")
    owners = lax.dynamic_slice_in_dim(tile_owner[:, 0], here * share, share, 0)
    tables = lag_tables(jnp.take(kernels, owners, axis=0), total_frames)
    traces = pl.pallas_call(
        mix_kernel,
        out_shape=jax.ShapeDtypeStruct(parts.shape, BF16),
        in_specs=vmem(2),
        out_specs=vmem(1)[0],
        compiler_params=params(),
        cost_estimate=pl.CostEstimate(flops=40000000, bytes_accessed=1200000, transcendentals=0),
        name="mix",
    )(tables, parts)
    traces = lax.all_to_all(
        traces.reshape(rows, frames, -1), ("planes", "wide"), split_axis=0, concat_axis=0, tiled=True
    )

    step_rows = BLOCK
    residual = pl.pallas_call(
        residual_kernel,
        grid=(rows // step_rows,),
        out_shape=jax.ShapeDtypeStruct((rows * frames, planes * cols), BF16),
        in_specs=[
            pl.BlockSpec((step_rows, frames, LANES), lambda i: (i, 0, 0)),
            pl.BlockSpec((step_rows // 2, planes * cols, 2 * LANES), lambda i: (i, 0, 0)),
            pl.BlockSpec((step_rows * frames, planes * cols), lambda i: (i, 0)),
            pl.BlockSpec((step_rows, cols), lambda i: (i, 0)),
        ],
        out_specs=pl.BlockSpec((step_rows * frames, planes * cols), lambda i: (i, 0)),
        compiler_params=params(),
        cost_estimate=pl.CostEstimate(flops=140000000, bytes_accessed=10000000, transcendentals=0),
        name="residual",
    )(traces, shapes, filtered, pixel_mask)

    above_back, below_back = halo_pair(residual, "rep", 0, BLOCK * frames)
    foot_share = support.shape[1] // plane_count
    mine = lax.dynamic_slice_in_dim(traces, lax.axis_index("planes") * foot_share, foot_share, 2)
    trace_out = jnp.transpose(mine, (2, 1, 0))
    back_projected = pl.pallas_call(
        functools.partial(backward_kernel, rim),
        out_shape=jax.ShapeDtypeStruct(movie_frames.shape, BF16),
        in_specs=[smem] + vmem(5),
        out_specs=vmem(1)[0],
        scratch_shapes=[pltpu.VMEM(((rows + 2 * BLOCK) * frames, planes * cols), BF16)],
        compiler_params=params(),
        cost_estimate=pl.CostEstimate(flops=1000000000, bytes_accessed=3000000, transcendentals=0),
        name="backward",
    )(ends, residual, above_back, below_back, around(col_taps), placed(row_taps[::-1]))
    return trace_out, back_projected


def solution(mesh):
    return jax.shard_map(
        on_device,
        mesh=mesh,
        in_specs=(
            P("planes", ("groups", "wide"), "rep", None),
            P("rep", None),
            P("rep", None),
            P("rep", None),
            P(None, "planes", None),
            P(),
            P(),
            P("wide", None, None),
            P("wide", None),
        ),
        out_specs=(
            P("planes", ("groups", "wide"), "rep"),
            P("planes", ("groups", "wide"), "rep", None),
        ),
        check_vma=False,
    )
```

time: 194 us -> 84.1 us (0.43)
  waiting for transfers between devices: 74.7 us -> 3.94 us
  local copies, waits for them, and re-layouts: 58.2 us -> 12.5 us
  Pallas kernels: 0 us -> 34.9 us
  between operations: 14.4 us -> 1.5 us
  blocking collectives: 0 us -> 12.4 us
  matrix products: 12.3 us -> 0 us
  other arithmetic: 8.88 us -> 0.45 us
  starting transfers between devices: 24.7 us -> 17.7 us
    gather x6 -> x1, local copies, waits for them, and re-layouts: 45.8 us -> 0.58 us  [on_device(): tables = lag_tables(jnp.take(kernels, owners, axis=0), total_frames)]
    all_to_all x3 -> x2, waiting for transfers between devices: 39.5 us -> 3.94 us  [the longest x1 3.94 us: on_device(): lax.all_to_all(traces.reshape(rows, frames, -1), ('planes', 'wide'), spli...]
    psum x1 -> x0, waiting for transfers between devices: 35.2 us -> none  [on_device(): lax.psum(partial_scores.astype(jnp.bfloat16), 'planes').astype(jnp.float32)]
    pallas_call x0 -> x5, Pallas kernels: none -> 34.9 us  [the longest x1 11.6 us: on_device(): pl.pallas_call(functools.partial(forward_kernel, rim), out_shape=(jax.Sha...]
    unnamed x0 -> x1, blocking collectives: none -> 12.4 us
    dot_general x5 -> x0, matrix products: 12.3 us -> none  [the longest x1 5.01 us: on_device(): jnp.einsum('cjpw,ptcw->cjt', shapes, mixed_cols, preferred_element_type=j...]
    ppermute x4 -> x2, starting transfers between devices: 10.3 us -> 4.93 us  [halo_pair(): other = lax.ppermute(edge, axis, [(0, 1), (1, 0)])]
    select_n x5 -> x1, other arithmetic: 4.81 us -> 0.08 us  [on_device(): tables = lag_tables(jnp.take(kernels, owners, axis=0), total_frames)]
  transfers between devices with their start and end apart: 8 -> 4, of which waited for: 3 -> 1; matrix products, arithmetic and copies ran while one was open for 27% -> 11% of each run, Pallas kernels for 0% -> 9%
where the time goes in v1:
time: 84.1 us; the launch traced here: 83.4 us
  Pallas kernels  34.9 us (41%)
  starting transfers between devices  17.7 us (21%)
  local copies, waits for them, and re-layouts  12.5 us (15%)
  blocking collectives  12.4 us (15%)
  waiting for transfers between devices  3.94 us (5%)
  between operations  1.5 us (2%)
    unnamed x1, blocking collectives  12.4 us
    pallas_call x1, Pallas kernels, on_device(): pl.pallas_call(functools.partial(forward_kernel, rim), out_shape=(jax.Sha...  11.6 us
    pallas_call x1, Pallas kernels, on_device(): pl.pallas_call(shapes_kernel, grid=(steps,), out_shape=jax.ShapeDtypeStru...  7.65 us
    pallas_call x1, Pallas kernels, on_device(): pl.pallas_call(residual_kernel, grid=(rows // step_rows,), out_shape=jax....  7.07 us
    all_to_all x1, starting transfers between devices, on_device(): lax.all_to_all(projected.reshape(rows, frames, -1), ('planes', 'wide'), s...  6.96 us
    unnamed x27, local copies, waits for them, and re-layouts  6.35 us
    all_to_all x1, starting transfers between devices, on_device(): lax.all_to_all(traces.reshape(rows, frames, -1), ('planes', 'wide'), spli...  5.79 us
    pallas_call x1, Pallas kernels, on_device(): pl.pallas_call(functools.partial(backward_kernel, rim), out_shape=jax.Sha...  5.6 us
  transfers between devices with their start and end apart: 4, of which 1 were waited for; matrix products, arithmetic and copies ran while one was open for 11% of the time, Pallas kernels for 9%

profile of v1, /device:TPU:1, one launch (start us, length us, event | category | flops | bytes accessed | tf_op | source)
XLA Modules:
  0.0 83.4 jit_solution(4742112119812840615)
XLA Ops:
  0.6 0.0 copy-start.9
  0.6 0.0 copy-start.4
  0.7 1.0 %constant_dynamic-slice_fusion.1 = bf16[2,16,16,128]{3,2,1,0:T(8,128)(2,1)S(1)} fusion(bf16[2,16,128,128]{3,2,1,0:T(8,128)(2,1)} %movie_ref.1, s32[]{:T(128)S(6)} %select_n.34), kind=kLoop, calls=%fused_computation.12 | loop fusion | bytes 262148 | tf_op jit(solution)/shard_map/dynamic_slice | solution.py:21
  1.7 0.1 collective-permute-start
  1.8 0.8 slice_bitcast_fusion.1
  2.6 0.8 slice_bitcast_fusion
  3.4 0.1 slice.27
  3.5 0.1 slice.29
  3.6 1.1 %copy.14 = bf16[512,2,128]{0,2,1:T(8,128)(2,1)S(1)} copy(bf16[512,2,128]{2,1,0:T(2,128)(2,1)} %param.13) | data formatting | bytes 524288 | tf_op args[4]
  4.7 0.1 copy.15.templates_ref
  4.8 0.7 pad.14.row_ref
  5.6 0.2 dynamic_update_slice.13.col_ref
  5.8 0.1 add_convert_fusion.ends_ref
  5.8 0.0 collective-permute-done.above_ref.below_ref
  5.8 0.8 %copy-done = s32[128,128]{1,0:T(8,128)S(1)} copy-done((s32[128,128]{1,0:T(8,128)S(1)}, s32[128,128]{1,0:T(8,128)}, u32[]{:S(2)}) %copy-start) | copy-done | bytes 65560
  6.7 1.2 %copy-done.2 = bf16[2,16,128,128]{3,2,1,0:T(8,128)(2,1)S(1)} copy-done((bf16[2,16,128,128]{3,2,1,0:T(8,128)(2,1)S(1)}, bf16[2,16,128,128]{3,2,1,0:T(8,128)(2,1)}, u32[]{:S(2)}) %copy-start.2) | copy-done | bytes 1048600
  7.9 0.8 %copy-done.3 = s32[128,128]{1,0:T(8,128)S(1)} copy-done((s32[128,128]{1,0:T(8,128)S(1)}, s32[128,128]{1,0:T(8,128)}, u32[]{:S(2)}) %copy-start.3) | copy-done | bytes 65560
  8.8 11.6 %forward.1 = (bf16[2048,256]{1,0:T(8,128)(2,1)S(1)}, bf16[2048,128]{1,0:T(8,128)(2,1)}) custom-call(s32[2]{0:T(128)S(1)} %add_convert_fusion.ends_ref, bf16[2,16,128,128]{3,2,1,0:T(8,128)(2,1)S(1)} %copy-done.2, bf16[2,16,16,128]{3,2,1,0:T(8,128)(2,1)S(1)} %collective-permute-done.above_ref.below_ref, ...), custom_call_target="tpu_custom_call" | custom-call | flops 1700000000 | bytes 4000000 | tf_op jit(solution)/shard_map/forward/pallas_call | solution.py:243
  20.4 7.0 %all-to-all-start = ((bf16[128,16,128]{2,1,0:T(8,128)(2,1)}), bf16[128,16,128]{2,1,0:T(8,128)(2,1)S(1)}, u32[]{:S(2)}, u32[]{:S(2)}) async-start(bf16[128,16,128]{2,1,0:T(8,128)(2,1)} %bitcast.10), calls=%async_computation | async-start | bytes 1048576 | tf_op jit(solution)/shard_map/all_to_all | solution.py:259
  27.4 0.0 copy-done.5
  27.4 0.6 dynamic-slice.1
  28.7 0.0 copy-done.6
  28.7 0.1 broadcast_multiply_fusion
  28.7 0.1 select_reduce_fusion
  28.9 0.2 dynamic-update-slice
  29.1 12.4 %all-reduce.5 = bf16[508]{0:T(512)(128)(2,1)S(1)} all-reduce(bf16[508]{0:T(512)(128)(2,1)S(1)} %dynamic-update-slice), channel_id=2, replica_groups=mesh['groups'=2,'wide'=4,'planes'=2,'rep'=2] {'wide'}, use_global_device_ids=true, to_apply=%add.5 | all-reduce | flops 508 | bytes 2032
  41.6 0.1 reshape.91
  41.7 0.0 copy-done.7
  41.7 0.1 and_bitcast_fusion
  41.7 0.6 gather_fusion
  42.3 0.1 broadcast_select_fusion
  42.4 0.2 copy.21
  42.6 0.9 %reshape.78 = bf16[16,64,127]{2,1,0:T(8,128)(2,1)S(1)} reshape(bf16[16,8128]{1,0:T(8,128)(2,1)S(1)} %bitcast.34) | data formatting | bytes 520192 | tf_op jit(solution)/shard_map/reshape | solution.py:214
  43.6 0.1 slice.35.lag_ref
  43.7 0.0 all-to-all-done
  43.7 2.9 %mix.1 = bf16[2,4,16,16,128]{4,3,2,1,0:T(8,128)(2,1)} custom-call(bf16[16,64,64]{2,1,0:T(8,128)(2,1)S(1)} %slice.35.lag_ref, bf16[2,4,16,16,128]{4,3,2,1,0:T(8,128)(2,1)S(1)} %bitcast.30), custom_call_target="tpu_custom_call" | custom-call | flops 40000000 | bytes 1200000 | tf_op jit(solution)/shard_map/mix/pallas_call | solution.py:284
  46.6 5.8 %all-to-all-start.1 = ((bf16[128,16,128]{2,1,0:T(8,128)(2,1)}), bf16[128,16,128]{2,1,0:T(8,128)(2,1)S(1)}, u32[]{:S(2)}, u32[]{:S(2)}) async-start(bf16[128,16,128]{2,1,0:T(8,128)(2,1)} %bitcast.12), calls=%async_computation.1 | async-start | bytes 1048576 | tf_op jit(solution)/shard_map/all_to_all | solution.py:293
  52.4 7.7 %shapes.1.shapes_ref = bf16[64,256,256]{2,1,0:T(8,128)(2,1)} custom-call(s32[128,128]{1,0:T(8,128)S(1)} %copy-done.4, bf16[256,512]{1,0:T(8,128)(2,1)S(1)} %bitcast.32), custom_call_target="tpu_custom_call" | custom-call | flops 4300000256 | bytes 9000000 | tf_op jit(solution)/shard_map/shapes/pallas_call | solution.py:267
  60.1 3.9 %all-to-all-done.1.traces_ref = bf16[128,16,128]{2,1,0:T(8,128)(2,1)S(1)} async-done(((bf16[128,16,128]{2,1,0:T(8,128)(2,1)}), bf16[128,16,128]{2,1,0:T(8,128)(2,1)S(1)}, u32[]{:S(2)}, u32[]{:S(2)}) %all-to-all-start.1) | async-done | bytes 524320 | tf_op jit(solution)/shard_map/all_to_all | solution.py:293
  64.0 7.1 %residual.1.resid_ref = bf16[2048,256]{1,0:T(8,128)(2,1)S(1)} custom-call(bf16[128,16,128]{2,1,0:T(8,128)(2,1)S(1)} %all-to-all-done.1.traces_ref, bf16[64,256,256]{2,1,0:T(8,128)(2,1)} %shapes.1.shapes_ref, bf16[2048,256]{1,0:T(8,128)(2,1)S(1)} %get-tuple-element.9.filtered_ref, s32[128,128]{1,0:T(8,128)S(1)} %copy-done.1), custom_call_target="tpu_custom_call" | custom-call | flops 140000000 | bytes 10000000 | tf_op jit(solution)/shard_map/residual/pallas_call | solution.py:298
  71.1 4.8 %collective-permute-start.1 = (bf16[256,256]{1,0:T(8,128)(2,1)S(1)}, bf16[256,256]{1,0:T(8,128)(2,1)S(1)}, u32[]{:S(2)}, u32[]{:S(2)}) collective-permute-start(bf16[256,256]{1,0:T(8,128)(2,1)S(1)} %constant_dynamic-slice_fusion), channel_id=1, source_target_pairs={{0,1},{1,0},{2,3},{3,2},{4,5},{5,4},{6,7},{7,6},{8,9},{9,8},{10,11... | collective-permute-start | bytes 393224 | tf_op jit(solution)/shard_map/ppermute | solution.py:22
  76.0 0.1 rev.4
  76.1 0.1 pad.15.row_ref
  76.1 0.2 dynamic_update_slice.15.col_ref
  76.3 0.2 dynamic-slice_bitcast_fusion
  76.5 1.3 %copy.16 = bf16[64,16,128]{2,1,0:T(8,128)(2,1)} copy(bf16[64,16,128]{0,1,2:T(8,128)(2,1)S(1)} %dynamic-slice_bitcast_fusion) | data formatting | bytes 524288
  77.8 0.0 collective-permute-done.1.above_ref.below_ref
  77.8 5.6 %backward.1 = bf16[2,16,128,128]{3,2,1,0:T(8,128)(2,1)} custom-call(s32[2]{0:T(128)S(1)} %add_convert_fusion.ends_ref, bf16[2048,256]{1,0:T(8,128)(2,1)S(1)} %residual.1.resid_ref, bf16[256,256]{1,0:T(8,128)(2,1)S(1)} %collective-permute-done.1.above_ref.below_ref, bf16[256,256]{1,0:T(8,128)(2,1)S(1)} %collective-permute-done.1.above_ref.below_ref, ...), custom_call_target="tpu_custom_call" | custom-call | flops 1000000000 | bytes 3000000 | tf_op jit(solution)/shard_map/backward/pallas_call | solution.py:318
  (22 shorter events, 0.1 us)
Async XLA Ops:
  0.6 26.8 %copy-start.9 = (u32[32]{0:T(128)S(1)}, u32[32]{0:T(128)}, u32[]{:S(2)}) copy-start(u32[32]{0:T(128)} %constant.73) | copy-start | bytes 388
  0.6 51.8 %copy-start.4 = (s32[128,128]{1,0:T(8,128)S(1)}, s32[128,128]{1,0:T(8,128)}, u32[]{:S(2)}) copy-start(s32[128,128]{1,0:T(8,128)} %support_ref.2) | copy-start | bytes 196612
  0.7 26.7 %copy-start.5 = (f32[1,3,65]{2,0,1:T(1,128)S(1)}, f32[1,3,65]{2,0,1:T(1,128)}, u32[]{:S(2)}) copy-start(f32[1,3,65]{2,0,1:T(1,128)} %param.16) | copy-start | bytes 2344
  0.7 28.0 %copy-start.6 = (s32[1,3]{1,0:T(1,128)S(1)}, s32[1,3]{1,0:T(1,128)}, u32[]{:S(2)}) copy-start(s32[1,3]{1,0:T(1,128)} %param.17) | copy-start | bytes 40
  0.7 41.0 %copy-start.7 = (s32[128,1]{0,1:T(1,128)S(1)}, s32[128,1]{0,1:T(1,128)}, u32[]{:S(2)}) copy-start(s32[128,1]{0,1:T(1,128)} %param.11) | copy-start | bytes 1540
  1.7 4.2 %collective-permute-start = (bf16[2,16,16,128]{3,2,1,0:T(8,128)(2,1)S(1)}, bf16[2,16,16,128]{3,2,1,0:T(8,128)(2,1)S(1)}, u32[]{:S(2)}, u32[]{:S(2)}) collective-permute-start(bf16[2,16,16,128]{3,2,1,0:T(8,128)(2,1)S(1)} %constant_dynamic-slice_fusion.1), channel_id=1, source_target_pairs={{0,1},{1,0},{2,3},{3,2},{4,5},{5,4},{6,7},{7,6},{8,9},{9,8},{10,11... | collective-permute-start | bytes 393224 | tf_op jit(solution)/shard_map/ppermute | solution.py:22
  5.8 0.8 %copy-start = (s32[128,128]{1,0:T(8,128)S(1)}, s32[128,128]{1,0:T(8,128)}, u32[]{:S(2)}) copy-start(s32[128,128]{1,0:T(8,128)} %mask_ref.3) | copy-start | bytes 196612
  6.7 1.2 %copy-start.2 = (bf16[2,16,128,128]{3,2,1,0:T(8,128)(2,1)S(1)}, bf16[2,16,128,128]{3,2,1,0:T(8,128)(2,1)}, u32[]{:S(2)}) copy-start(bf16[2,16,128,128]{3,2,1,0:T(8,128)(2,1)} %movie_ref.1) | copy-start | bytes 3145732
  7.9 0.8 %copy-start.3 = (s32[128,128]{1,0:T(8,128)S(1)}, s32[128,128]{1,0:T(8,128)}, u32[]{:S(2)}) copy-start(s32[128,128]{1,0:T(8,128)} %support_ref.2) | copy-start | bytes 196612
  20.4 23.3 %all-to-all-start = ((bf16[128,16,128]{2,1,0:T(8,128)(2,1)}), bf16[128,16,128]{2,1,0:T(8,128)(2,1)S(1)}, u32[]{:S(2)}, u32[]{:S(2)}) async-start(bf16[128,16,128]{2,1,0:T(8,128)(2,1)} %bitcast.10), calls=%async_computation | async-start | bytes 1048576 | tf_op jit(solution)/shard_map/all_to_all | solution.py:259
  46.6 17.4 %copy-start.1 = (s32[128,128]{1,0:T(8,128)S(1)}, s32[128,128]{1,0:T(8,128)}, u32[]{:S(2)}) copy-start(s32[128,128]{1,0:T(8,128)} %mask_ref.3) | copy-start | bytes 196612
  46.6 17.4 %all-to-all-start.1 = ((bf16[128,16,128]{2,1,0:T(8,128)(2,1)}), bf16[128,16,128]{2,1,0:T(8,128)(2,1)S(1)}, u32[]{:S(2)}, u32[]{:S(2)}) async-start(bf16[128,16,128]{2,1,0:T(8,128)(2,1)} %bitcast.12), calls=%async_computation.1 | async-start | bytes 1048576 | tf_op jit(solution)/shard_map/all_to_all | solution.py:293
  60.1 15.9 %copy-start.8 = (f32[25]{0:T(128)S(1)}, f32[25]{0:T(128)}, u32[]{:S(2)}) copy-start(f32[25]{0:T(128)} %param.14) | copy-start | bytes 304
  71.1 6.7 %collective-permute-start.1 = (bf16[256,256]{1,0:T(8,128)(2,1)S(1)}, bf16[256,256]{1,0:T(8,128)(2,1)S(1)}, u32[]{:S(2)}, u32[]{:S(2)}) collective-permute-start(bf16[256,256]{1,0:T(8,128)(2,1)S(1)} %constant_dynamic-slice_fusion), channel_id=1, source_target_pairs={{0,1},{1,0},{2,3},{3,2},{4,5},{5,4},{6,7},{7,6},{8,9},{9,8},{10,11... | collective-permute-start | bytes 393224 | tf_op jit(solution)/shard_map/ppermute | solution.py:22

commit v2 on v0

v2 whole, which is shorter than its diff:
```python
import functools

import jax
import jax.numpy as jnp
from jax import lax
from jax.experimental import pallas as pl
from jax.experimental.pallas import tpu as pltpu
from jax.sharding import PartitionSpec as P

BLOCK = 16
LANES = 128
F32 = jnp.float32
BF16 = jnp.bfloat16
REP, PLANE, WIDE = 0, 1, 2


def exchange(cells, axis, flip):
    count = lax.axis_size(axis)
    return lax.ppermute(cells, axis, [(i, i ^ flip) for i in range(count)])


def iota(shape, dim):
    return lax.broadcasted_iota(jnp.int32, shape, dim)


def tap_row(taps_ref, place):
    lane = iota((8, LANES), 1)
    row = jnp.zeros((8, LANES), F32)
    for k in range(taps_ref.shape[0]):
        row = jnp.where(lane == place(k) % LANES, taps_ref[k], row)
    return row[:1]


def toeplitz(row, count, shift=0):
    return pltpu.roll(
        jnp.broadcast_to(row, (count, row.shape[1])), shift, 1, stride=1, stride_axis=0
    )


def column_band(taps_ref, rim, sign):
    rolled = toeplitz(tap_row(taps_ref, lambda k: sign * (k - rim)), LANES)
    gap = iota((LANES, LANES), 1) - iota((LANES, LANES), 0)
    return jnp.where(jnp.abs(gap) <= rim, rolled, 0.0).astype(BF16)


def row_band_forward(taps_ref, rim, frames):
    out_rows, depth, span = BLOCK * frames, 3 * BLOCK * frames, 3 * BLOCK
    band = toeplitz(tap_row(taps_ref, lambda k: k + BLOCK - rim), BLOCK)[:, :span].astype(BF16)
    left = (iota((out_rows, BLOCK), 0) // frames == iota((out_rows, BLOCK), 1)).astype(BF16)
    right = (lax.rem(iota((span, depth), 1), span) == iota((span, depth), 0)).astype(BF16)
    tall = jnp.dot(left, band, preferred_element_type=F32).astype(BF16)
    spread = jnp.dot(tall, right, preferred_element_type=F32)
    start = iota((out_rows, depth), 1) - span * lax.rem(iota((out_rows, depth), 0), frames)
    return jnp.where((start >= 0) & (start < span), spread, 0.0).astype(BF16)


def row_band_adjoint(taps_ref, rim, frames):
    out_rows, depth, span = BLOCK * frames, 3 * BLOCK * frames, 3 * BLOCK
    band = toeplitz(tap_row(taps_ref, lambda k: BLOCK + rim - k), BLOCK)[:, :span].astype(BF16)
    left = (lax.rem(iota((out_rows, BLOCK), 0), BLOCK) == iota((out_rows, BLOCK), 1)).astype(BF16)
    right = (iota((span, depth), 1) // frames == iota((span, depth), 0)).astype(BF16)
    tall = jnp.dot(left, band, preferred_element_type=F32).astype(BF16)
    spread = jnp.dot(tall, right, preferred_element_type=F32)
    same = lax.rem(iota((out_rows, depth), 1), frames) == iota((out_rows, depth), 0) // BLOCK
    return jnp.where(same, spread, 0.0).astype(BF16)


def per_frame(rows, frames, copies):
    tall = jnp.broadcast_to(rows[:, None, :], (BLOCK, frames, LANES)).reshape(BLOCK * frames, LANES)
    return tall if copies == 1 else jnp.concatenate([tall] * copies, axis=1)


def smooth_kernel(rim, frames, col_ref, row_ref, movie_ref, smooth_ref, col_fwd_ref, row_fwd_ref):
    @pl.when((pl.program_id(0) == 0) & (pl.program_id(1) == 0))
    def _():
        col_fwd_ref[...] = column_band(col_ref, rim, -1)
        row_fwd_ref[...] = row_band_forward(row_ref, rim, frames)

    _, some, rows, _ = movie_ref.shape
    full = jnp.dot(
        movie_ref[0].reshape(some * rows, LANES), col_fwd_ref[...], preferred_element_type=F32
    )
    smooth_ref[:, BLOCK : BLOCK + rows, :] = full.astype(BF16).reshape(some, rows, LANES)


def forward_kernel(
    flip, fill, place_ref, smooth_in_ref, edge_ref, col_fwd_ref, row_fwd_ref, code_ref,
    templates_ref, smooth_ref, filtered_ref, projected_ref,
):
    frames, padded_rows, width = smooth_ref.shape
    planes, rows = width // LANES, padded_rows - 2 * BLOCK
    if fill:
        for p in range(planes):
            edge = jnp.dot(
                edge_ref[p].reshape(frames * BLOCK, LANES), col_fwd_ref[...],
                preferred_element_type=F32,
            ).reshape(frames, BLOCK, LANES)
            lanes = slice(p * LANES, (p + 1) * LANES)
            above = jnp.where(place_ref[REP] > 0, edge, 0.0).astype(BF16)
            below = jnp.where(place_ref[REP] > 0, 0.0, edge).astype(BF16)
            smooth_ref[:, :BLOCK, lanes] = above
            smooth_ref[:, BLOCK + rows :, lanes] = below
    here = filtered_ref.shape[0] // frames
    first = (place_ref[PLANE] ^ flip) * here
    tiles = templates_ref.shape[1] // LANES
    for b in range(here // BLOCK):
        top = pl.multiple_of(first + b * BLOCK, BLOCK)
        near = smooth_ref[:, pl.ds(top, 3 * BLOCK), :].reshape(frames * 3 * BLOCK, width)
        along = jnp.dot(row_fwd_ref[...], near, preferred_element_type=F32)
        code = code_ref[pl.ds(top, BLOCK), :]
        mask = per_frame((code & 1).astype(F32), frames, planes)
        filtered = (along * mask).astype(BF16)
        spot = slice(b * BLOCK * frames, (b + 1) * BLOCK * frames)
        filtered_ref[spot, :] = filtered
        dense = jnp.dot(filtered, templates_ref[...], preferred_element_type=F32)
        picked = per_frame(code >> 1, frames, 1)
        lane, tile = picked & (LANES - 1), picked // LANES
        chosen = jnp.zeros(picked.shape, F32)
        for t in range(tiles):
            found = jnp.take_along_axis(
                dense[:, t * LANES : (t + 1) * LANES], lane, axis=1, mode="promise_in_bounds"
            )
            chosen = jnp.where(tile == t, found, chosen)
        projected_ref[spot, :] = chosen.astype(BF16)


def split_kernel(count, place_ref, lag_ref, *refs):
    parts, outs = refs[:count], refs[count:]
    rows = parts[0].shape[0] // len(outs)
    for k, out_ref in enumerate(outs):
        start = pl.multiple_of((place_ref[WIDE] ^ k) * rows, rows)
        total = parts[0][pl.ds(start, rows), :].astype(F32)
        for part in parts[1:]:
            total = total + part[pl.ds(start, rows), :].astype(F32)
        out_ref[:rows, :] = total.astype(BF16)
        out_ref[rows:, :] = lag_ref[...]


def mix_kernel(wide, place_ref, owner_ref, *refs):
    blocks, outs = refs[:wide], refs[wide : 2 * wide]
    cells_ref, kernels_ref, traces_ref, tables_ref = refs[2 * wide :]
    _, share, frames, lanes = cells_ref.shape
    total = wide * frames
    here = place_ref[WIDE]
    for k, block in enumerate(blocks):
        cells_ref[here ^ k] = block[: share * frames, :].reshape(share, frames, lanes)
        kernels_ref[here ^ k] = block[share * frames :, :].astype(F32)

    def table(values):
        row = jnp.concatenate([values[i : i + 1, :] for i in range(2 * total // LANES)], axis=1)
        return toeplitz(row, total, total + 1)[:, :total].astype(BF16)

    if wide <= share:
        for d in range(wide):
            tables_ref[d] = table(kernels_ref[d])
    first = (place_ref[PLANE] * wide + here) * share
    for h in range(share):
        owner = owner_ref[first + h]
        lag = tables_ref[owner] if wide <= share else table(kernels_ref[owner])
        mixed = jnp.dot(lag, cells_ref[:, h].reshape(total, lanes), preferred_element_type=F32)
        traces_ref[:, h] = jnp.maximum(mixed, 0.0).astype(BF16).reshape(wide, frames, lanes)
    for k, out_ref in enumerate(outs):
        out_ref[...] = traces_ref[here ^ k]


def shapes_kernel(
    rim, frames, col_ref, row_ref, code_ref, templates_ref, shapes_ref, col_adj_ref, row_adj_ref
):
    @pl.when(pl.program_id(0) == 0)
    def _():
        col_adj_ref[...] = column_band(col_ref, rim, 1)
        row_adj_ref[...] = row_band_adjoint(row_ref, rim, frames)

    count = templates_ref.shape[1]
    support = code_ref[...] >> 1
    for i in range(0, shapes_ref.shape[0], 2):
        both = jnp.concatenate([support[i : i + 1, :], support[i + 1 : i + 2, :]], axis=1)
        hits = iota((count, 2 * LANES), 0) == jnp.broadcast_to(both, (count, 2 * LANES))
        pair = jnp.dot(
            templates_ref[...], hits.astype(BF16), preferred_element_type=F32
        ).astype(BF16)
        shapes_ref[i] = pair[:, :LANES]
        shapes_ref[i + 1] = pair[:, LANES:]


def residual_kernel(
    flip, place_ref, traces_ref, shapes_ref, filtered_ref, code_ref, out_ref, edge_ref, ordered_ref
):
    wide, share, frames, lanes = traces_ref.shape
    copies = filtered_ref.shape[1] // LANES
    base = (place_ref[PLANE] ^ flip) * wide * share
    for k in range(wide):
        block = place_ref[WIDE] ^ k
        for h in range(share):
            row = block * share + h
            model = lax.dot_general(
                traces_ref[k, h], shapes_ref[base + row], (((1,), (1,)), ((), ())),
                preferred_element_type=F32,
            )
            mask = (code_ref[pl.ds(base + row, 1), :] & 1).astype(F32)
            spot = pl.ds(pl.multiple_of(row * frames, frames), frames)
            out_ref[spot, :] = (
                filtered_ref[spot, :].astype(F32) - jnp.concatenate([mask] * copies, axis=1) * model
            ).astype(BF16)
        ordered_ref[pl.ds(block * share, share)] = traces_ref[k]
    edge = edge_ref.shape[0]
    start = jnp.where(place_ref[REP] > 0, 0, out_ref.shape[0] - edge)
    edge_ref[...] = out_ref[pl.ds(pl.multiple_of(start, edge), edge), :]


def backward_kernel(count, place_ref, edge_ref, col_adj_ref, row_adj_ref, *refs):
    parts, (out_ref, padded_ref) = refs[:count], refs[count:]
    planes, frames, rows, _ = out_ref.shape
    edge, size = BLOCK * frames, parts[0].shape[0]
    zero = jnp.zeros_like(edge_ref)
    padded_ref[:edge, :] = jnp.where(place_ref[REP] > 0, edge_ref[...], zero)
    padded_ref[edge + rows * frames :, :] = jnp.where(place_ref[REP] > 0, zero, edge_ref[...])
    for flip, part in enumerate(parts):
        spot = pl.multiple_of(edge + (place_ref[PLANE] ^ flip) * size, edge)
        padded_ref[pl.ds(spot, size), :] = part[...]
    for b in range(rows // BLOCK):
        near = padded_ref[b * edge : (b + 3) * edge, :]
        back = jnp.dot(row_adj_ref[...], near, preferred_element_type=F32).astype(BF16)
        for p in range(planes):
            full = jnp.dot(
                back[:, p * LANES : (p + 1) * LANES], col_adj_ref[...], preferred_element_type=F32
            ).astype(BF16)
            out_ref[p, :, b * BLOCK : (b + 1) * BLOCK, :] = full.reshape(frames, BLOCK, LANES)


VMEM = pl.BlockSpec(memory_space=pltpu.VMEM)
SMEM = pl.BlockSpec(memory_space=pltpu.SMEM)


def shaped(shape):
    return jax.ShapeDtypeStruct(shape, BF16)


def call(kernel, name, outs, smem, vmem, flops, moved, scratch=(), aliases=None):
    return pl.pallas_call(
        kernel,
        out_shape=tuple(shaped(s) for s in outs),
        in_specs=[SMEM] * smem + [VMEM] * vmem,
        out_specs=(VMEM,) * len(outs),
        scratch_shapes=scratch,
        input_output_aliases=aliases or {},
        compiler_params=pltpu.CompilerParams(vmem_limit_bytes=32 * 1024 * 1024),
        cost_estimate=pl.CostEstimate(flops=flops, bytes_accessed=moved, transcendentals=0),
        name=name,
    )


def lag_kernel_values(gains, lags, frame_count):
    taps = gains.shape[1]
    lag_values = jnp.arange(2 * frame_count, dtype=jnp.int32) - (frame_count - 1)
    offsets = jnp.arange(taps, dtype=jnp.int32) - (taps - 1) // 2
    hits = lag_values[None, :, None] == lags[:, None, None] * offsets[None, None, :]
    spread = jnp.where(hits, gains[:, None, :], jnp.zeros((), gains.dtype))
    return jnp.sum(spread, axis=(0, 2)).astype(BF16)


def on_device(
    movie_frames, pixel_mask, tile_owner, support, templates, row_taps, col_taps, lag_gains, dilations
):
    planes, frames, rows, cols = movie_frames.shape
    wide, plane_count = lax.axis_size("wide"), lax.axis_size("planes")
    rim = (row_taps.shape[0] - 1) // 2
    total_frames, width = frames * wide, planes * cols
    here = rows // plane_count
    share = here // wide
    edge = BLOCK * frames
    rep, plane, spot = lax.axis_index("rep"), lax.axis_index("planes"), lax.axis_index("wide")
    place = jnp.stack([rep, plane, spot]).astype(jnp.int32)
    mib = 1 << 20

    start = jnp.where(rep == 0, rows - BLOCK, 0)
    rim_rows = exchange(lax.dynamic_slice_in_dim(movie_frames, start, BLOCK, axis=2), "rep", 1)
    code = support * 2 + pixel_mask
    tall_templates = jnp.transpose(templates, (1, 2, 0)).reshape(width, -1)
    kernel_row = lag_kernel_values(lag_gains[0], dilations[0], total_frames)
    lag_rows = -(-2 * total_frames // (LANES * BLOCK)) * BLOCK
    kernel_row = jnp.pad(kernel_row, (0, lag_rows * LANES - 2 * total_frames)).reshape(lag_rows, LANES)

    half = frames // 2
    depth = 3 * BLOCK * frames
    smooth, col_fwd, row_fwd = pl.pallas_call(
        functools.partial(smooth_kernel, rim, frames),
        grid=(2, planes),
        out_shape=(
            shaped((frames, rows + 2 * BLOCK, width)), shaped((cols, cols)), shaped((edge, depth))
        ),
        in_specs=[SMEM, SMEM, pl.BlockSpec((1, half, rows, cols), lambda i, p: (p, i, 0, 0))],
        out_specs=(
            pl.BlockSpec((half, rows + 2 * BLOCK, cols), lambda i, p: (i, 0, p)),
            pl.BlockSpec((cols, cols), lambda i, p: (0, 0)),
            pl.BlockSpec((edge, depth), lambda i, p: (0, 0)),
        ),
        compiler_params=pltpu.CompilerParams(vmem_limit_bytes=32 * 1024 * 1024),
        cost_estimate=pl.CostEstimate(flops=200000000, bytes_accessed=3 * mib, transcendentals=0),
        name="smooth",
    )(col_taps, row_taps, movie_frames)

    filtered, projected = [None] * plane_count, [None] * plane_count
    for turn in range(plane_count):
        flip = (turn + 1) % plane_count
        smooth, filtered[flip], mine = call(
            functools.partial(forward_kernel, flip, turn == 0), "forward",
            [smooth.shape, (here * frames, width), (here * frames, support.shape[1])],
            1, 6, 800000000, 3 * mib, aliases={1: 0},
        )(place, smooth, rim_rows, col_fwd, row_fwd, code, tall_templates)
        projected[flip] = exchange(mine, "planes", flip) if flip else mine

    block_rows = share * frames + lag_rows
    blocks = call(
        functools.partial(split_kernel, plane_count), "split", [(block_rows, LANES)] * wide,
        1, 1 + plane_count, 1000000, mib,
    )(place, kernel_row, *projected)
    blocks = [exchange(block, "wide", k) if k else block for k, block in enumerate(blocks)]

    late_code, late_templates, _ = lax.optimization_barrier((code, tall_templates, blocks[0]))
    steps = 8
    shapes, col_adj, row_adj = pl.pallas_call(
        functools.partial(shapes_kernel, rim, frames),
        grid=(steps,),
        out_shape=(shaped((rows, width, LANES)), shaped((cols, cols)), shaped((edge, depth))),
        in_specs=[
            SMEM,
            SMEM,
            pl.BlockSpec((rows // steps, LANES), lambda i: (i, 0)),
            pl.BlockSpec((width, templates.shape[0]), lambda i: (0, 0)),
        ],
        out_specs=(
            pl.BlockSpec((rows // steps, width, LANES), lambda i: (i, 0, 0)),
            pl.BlockSpec((cols, cols), lambda i: (0, 0)),
            pl.BlockSpec((edge, depth), lambda i: (0, 0)),
        ),
        compiler_params=pltpu.CompilerParams(vmem_limit_bytes=32 * 1024 * 1024),
        cost_estimate=pl.CostEstimate(flops=4300000000, bytes_accessed=9 * mib, transcendentals=0),
        name="shapes",
    )(col_taps, row_taps, late_code, late_templates)

    cell_shape = (wide, share, frames, LANES)
    tables = (wide, total_frames, total_frames) if wide <= share else (1, BLOCK, LANES)
    traces = call(
        functools.partial(mix_kernel, wide), "mix", [cell_shape[1:]] * wide, 2, wide, 20000000, mib,
        scratch=[
            pltpu.VMEM(cell_shape, BF16), pltpu.VMEM((wide, lag_rows, LANES), F32),
            pltpu.VMEM(cell_shape, BF16), pltpu.VMEM(tables, BF16),
        ],
    )(place, tile_owner[:, 0], *blocks)
    traces = jnp.stack([exchange(cells, "wide", k) if k else cells for k, cells in enumerate(traces)])

    residual, edges, ordered = [], [], []
    for flip in range(plane_count):
        got = exchange(traces, "planes", flip) if flip else traces
        part, tip, sorted_rows = call(
            functools.partial(residual_kernel, flip), "residual",
            [(here * frames, width), (edge, width), (here, frames, LANES)], 1, 4, 70000000, 6 * mib,
        )(place, got, shapes, filtered[flip], code)
        residual.append(part)
        edges.append(tip)
        ordered.append(sorted_rows)

    outer = plane ^ jnp.where(rep == 0, plane_count - 1, 0)
    tip = edges[0]
    for flip in range(1, plane_count):
        tip = jnp.where(outer == flip, edges[flip], tip)
    tip = exchange(tip, "rep", 1)

    foot_share = support.shape[1] // plane_count
    in_order = []
    for q in range(plane_count):
        rows_q = ordered[0]
        for flip in range(1, plane_count):
            rows_q = jnp.where(plane ^ q == flip, ordered[flip], rows_q)
        in_order.append(rows_q)
    mine = lax.dynamic_slice_in_dim(jnp.concatenate(in_order), plane * foot_share, foot_share, 2)
    trace_out = jnp.transpose(mine, (2, 1, 0))

    (back_projected,) = call(
        functools.partial(backward_kernel, plane_count), "backward", [movie_frames.shape],
        1, 3 + plane_count, 1000000000, 3 * mib,
        scratch=[pltpu.VMEM(((rows + 2 * BLOCK) * frames, width), BF16)],
    )(place, tip, col_adj, row_adj, *residual)
    return trace_out, back_projected


def solution(mesh):
    return jax.shard_map(
        on_device,
        mesh=mesh,
        in_specs=(
            P("planes", ("groups", "wide"), "rep", None),
            P("rep", None),
            P("rep", None),
            P("rep", None),
            P(None, "planes", None),
            P(),
            P(),
            P("wide", None, None),
            P("wide", None),
        ),
        out_specs=(
            P("planes", ("groups", "wide"), "rep"),
            P("planes", ("groups", "wide"), "rep", None),
        ),
        check_vma=False,
    )
```

time: 194 us -> 61.2 us (0.32)
  waiting for transfers between devices: 74.7 us -> 14.1 us
  local copies, waits for them, and re-layouts: 58.2 us -> 6.56 us
  Pallas kernels: 0 us -> 23.5 us
  between operations: 14.4 us -> 0.78 us
  matrix products: 12.3 us -> 0 us
  starting transfers between devices: 24.7 us -> 13.9 us
  other arithmetic: 8.88 us -> 2.13 us
    gather x6 -> x0, local copies, waits for them, and re-layouts: 45.8 us -> none  [the longest x2 40.7 us: on_device(): shapes = jnp.take(templates, jnp.take(support, my_sources, axis=0), axis=0)]
    all_to_all x3 -> x0, waiting for transfers between devices: 39.5 us -> none  [the longest x1 34.9 us: on_device(): lax.all_to_all(resid_cols, 'wide', split_axis=1, concat_axis=2, tiled=True)]
    psum x1 -> x0, waiting for transfers between devices: 35.2 us -> none  [on_device(): lax.psum(partial_scores.astype(jnp.bfloat16), 'planes').astype(jnp.float32)]
    pallas_call x0 -> x9, Pallas kernels: none -> 23.5 us  [the longest x1 6.94 us: on_device(): pl.pallas_call(functools.partial(shapes_kernel, rim, frames), grid=(steps...]
    all_to_all x3 -> x0, starting transfers between devices: 14.4 us -> none  [the longest x1 5.55 us: on_device(): lax.all_to_all(packed, 'wide', split_axis=2, concat_axis=1, tiled=True)]
    ppermute x4 -> x10, waiting for transfers between devices: 0.01 us -> 14.1 us  [exchange(): return lax.ppermute(cells, axis, [(i, i ^ flip) for i in range(count)])]
    dot_general x5 -> x0, matrix products: 12.3 us -> none  [the longest x1 5.01 us: on_device(): jnp.einsum('cjpw,ptcw->cjt', shapes, mixed_cols, preferred_element_type=j...]
    select_n x5 -> x2, other arithmetic: 4.81 us -> 0.06 us  [the longest x1 0.04 us: on_device(): rows_q = jnp.where(plane ^ q == flip, ordered[flip], rows_q)]
  transfers between devices with their start and end apart: 8 -> 10, of which waited for: 3 -> 5; matrix products, arithmetic and copies ran while one was open for 27% -> 8% of each run, Pallas kernels for 0% -> 22%
where the time goes in v2:
time: 61.2 us; the launch traced here: 60.9 us
  Pallas kernels  23.5 us (38%)
  waiting for transfers between devices  14.1 us (23%)
  starting transfers between devices  13.9 us (23%)
  local copies, waits for them, and re-layouts  6.56 us (11%)
  other arithmetic  2.13 us (3%)
  between operations  0.78 us (1%)
    ppermute x10, waiting for transfers between devices, exchange(): return lax.ppermute(cells, axis, [(i, i ^ flip) for i in range(count)])  14.1 us
    ppermute x10, starting transfers between devices, exchange(): return lax.ppermute(cells, axis, [(i, i ^ flip) for i in range(count)])  13.9 us
    pallas_call x1, Pallas kernels, on_device(): pl.pallas_call(functools.partial(shapes_kernel, rim, frames), grid=(steps...  6.94 us
    pallas_call x2, Pallas kernels, on_device(): call(functools.partial(forward_kernel, flip, turn == 0), 'forward', [smoo...  4.89 us
    unnamed x14, local copies, waits for them, and re-layouts  4.52 us
    pallas_call x1, Pallas kernels, on_device(): call(functools.partial(backward_kernel, plane_count), 'backward', [movie_...  4.43 us
    pallas_call x2, Pallas kernels, on_device(): call(functools.partial(residual_kernel, flip), 'residual', [(here * frame...  3.54 us
    pallas_call x1, Pallas kernels, on_device(): pl.pallas_call(functools.partial(smooth_kernel, rim, frames), grid=(2, pl...  2.2 us
  transfers between devices with their start and end apart: 10, of which 5 were waited for; matrix products, arithmetic and copies ran while one was open for 8% of the time, Pallas kernels for 22%

profile of v2, /device:TPU:1, one launch (start us, length us, event | category | flops | bytes accessed | tf_op | source)
XLA Modules:
  0.0 60.9 jit_solution(17656525243909960716)
XLA Ops:
  0.6 0.9 %constant_dynamic-slice_fusion = bf16[2,16,16,128]{3,2,1,0:T(8,128)(2,1)S(1)} fusion(bf16[2,16,128,128]{3,2,1,0:T(8,128)(2,1)} %movie_ref.1, s32[]{:T(128)S(6)} %select_n.39), kind=kLoop, calls=%fused_computation.11 | loop fusion | bytes 262148 | tf_op jit(solution)/shard_map/dynamic_slice | solution.py:277
  1.6 0.1 collective-permute-start
  1.7 1.1 %copy.15 = bf16[2,128,512]{2,1,0:T(8,128)(2,1)S(1)} copy(bf16[2,128,512]{1,0,2:T(2,128)(2,1)} %bitcast.23) | data formatting | bytes 524288 | tf_op jit(solution)/shard_map/transpose | solution.py:279
  2.8 0.7 %copy.19 = f32[1,3,65]{2,1,0:T(4,128)S(1)} copy(f32[1,3,65]{2,0,1:T(1,128)} %param.16) | data formatting | bytes 1560
  3.5 0.9 %multiply_add_fusion.code_ref = s32[128,128]{1,0:T(8,128)S(1)} fusion(s32[128,128]{1,0:T(8,128)} %param.10, s32[128,128]{1,0:T(8,128)} %param.12), kind=kLoop, calls=%fused_computation.7 | loop fusion | flops 32768 | bytes 196608 | tf_op jit(solution)/shard_map/add | solution.py:278
  4.4 0.7 %broadcast_multiply_fusion = s32[3,65]{1,0:T(4,128)S(1)} fusion(s32[65]{0:T(128)S(1)} %iota_add_fusion, s32[3]{0:T(128)} %bitcast.28), kind=kLoop, calls=%fused_computation.10 | loop fusion | flops 195 | bytes 1052 | tf_op jit(solution)/shard_map/mul | solution.py:257
  5.1 0.0 copy-start
  5.1 1.2 %copy-done = bf16[2,16,128,128]{3,2,1,0:T(8,128)(2,1)S(1)} copy-done((bf16[2,16,128,128]{3,2,1,0:T(8,128)(2,1)S(1)}, bf16[2,16,128,128]{3,2,1,0:T(8,128)(2,1)}, u32[]{:S(2)}) %copy-start) | copy-done | bytes 1048600
  6.3 0.7 %copy-done.1 = f32[25]{0:T(128)S(1)} copy-done((f32[25]{0:T(128)S(1)}, f32[25]{0:T(128)}, u32[]{:S(2)}) %copy-start.1) | copy-done | bytes 124
  7.0 0.7 %copy-done.3 = f32[25]{0:T(128)S(1)} copy-done((f32[25]{0:T(128)S(1)}, f32[25]{0:T(128)}, u32[]{:S(2)}) %copy-start.3) | copy-done | bytes 124
  7.6 2.2 %smooth.1 = (bf16[16,160,256]{2,1,0:T(8,128)(2,1)S(1)}, bf16[128,128]{1,0:T(8,128)(2,1)S(1)}, bf16[256,768]{1,0:T(8,128)(2,1)S(1)}) custom-call(f32[25]{0:T(128)S(1)} %copy-done.1, f32[25]{0:T(128)S(1)} %copy-done.3, bf16[2,16,128,128]{3,2,1,0:T(8,128)(2,1)S(1)} %copy-done), custom_call_target="tpu_custom_call" | custom-call | flops 200000000 | bytes 3145728 | tf_op jit(solution)/shard_map/smooth/pallas_call | solution.py:286
  9.9 0.1 pad_add_fusion.place_ref
  9.9 0.0 collective-permute-done.edge_ref
  9.9 2.5 %forward.2 = (bf16[16,160,256]{2,1,0:T(8,128)(2,1)S(1)}, bf16[1024,256]{1,0:T(8,128)(2,1)S(1)}, bf16[1024,128]{1,0:T(8,128)(2,1)S(1)}) custom-call(s32[3]{0:T(128)S(1)} %pad_add_fusion.place_ref, bf16[16,160,256]{2,1,0:T(8,128)(2,1)S(1)} %get-tuple-element.29.smooth_in_ref, ...), custom_call_target="tpu_custom_call", output_to_operand_aliasing={{0}: (1, {})} | custom-call | flops 800000000 | bytes 3145728 | tf_op jit(solution)/shard_map/forward/pallas_call | solution.py:306
  12.5 2.7 %collective-permute-start.1 = (bf16[1024,128]{1,0:T(8,128)(2,1)S(1)}, bf16[1024,128]{1,0:T(8,128)(2,1)S(1)}, u32[]{:S(2)}, u32[]{:S(2)}) collective-permute-start(bf16[1024,128]{1,0:T(8,128)(2,1)S(1)} %get-tuple-element.34), channel_id=1, source_target_pairs={{0,2},{2,0},{1,3},{3,1},{4,6},{6,4},{5,7},{7,5},{8,10},{10,8},{9,1... | collective-permute-start | bytes 786440 | tf_op jit(solution)/shard_map/ppermute | solution.py:19
  15.2 0.1 select_reduce_fusion
  15.3 0.0 copy-start.5
  15.4 2.4 %forward.3 = (bf16[16,160,256]{2,1,0:T(8,128)(2,1)S(1)}, bf16[1024,256]{1,0:T(8,128)(2,1)S(1)}, bf16[1024,128]{1,0:T(8,128)(2,1)S(1)}) custom-call(s32[3]{0:T(128)S(1)} %pad_add_fusion.place_ref, bf16[16,160,256]{2,1,0:T(8,128)(2,1)S(1)} %get-tuple-element.32.smooth_in_ref, ...), custom_call_target="tpu_custom_call", output_to_operand_aliasing={{0}: (1, {})} | custom-call | flops 800000000 | bytes 3145728 | tf_op jit(solution)/shard_map/forward/pallas_call | solution.py:306
  17.7 0.0 copy-start.2
  17.7 0.0 copy-start.4
  17.7 4.1 %collective-permute-done.1.refs_1_ = bf16[1024,128]{1,0:T(8,128)(2,1)S(1)} collective-permute-done((bf16[1024,128]{1,0:T(8,128)(2,1)S(1)}, bf16[1024,128]{1,0:T(8,128)(2,1)S(1)}, u32[]{:S(2)}, u32[]{:S(2)}) %collective-permute-start.1) | collective-permute-done | bytes 262176 | tf_op jit(solution)/shard_map/ppermute | solution.py:19
  21.8 0.6 split.1
  22.5 1.4 %collective-permute-start.2 = (bf16[272,128]{1,0:T(8,128)(2,1)S(1)}, bf16[272,128]{1,0:T(8,128)(2,1)S(1)}, u32[]{:S(2)}, u32[]{:S(2)}) collective-permute-start(bf16[272,128]{1,0:T(8,128)(2,1)S(1)} %get-tuple-element.36), channel_id=1, source_target_pairs={{0,4},{4,0},{8,12},{12,8},{1,5},{5,1},{9,13},{13,9},{2,6},{6,2},{1... | collective-permute-start | bytes 208904 | tf_op jit(solution)/shard_map/ppermute | solution.py:19
  23.9 2.3 %collective-permute-start.3 = (bf16[272,128]{1,0:T(8,128)(2,1)S(1)}, bf16[272,128]{1,0:T(8,128)(2,1)S(1)}, u32[]{:S(2)}, u32[]{:S(2)}) collective-permute-start(bf16[272,128]{1,0:T(8,128)(2,1)S(1)} %get-tuple-element.37), channel_id=1, source_target_pairs={{0,8},{4,12},{8,0},{12,4},{1,9},{5,13},{9,1},{13,5},{2,10},{6,14},... | collective-permute-start | bytes 208904 | tf_op jit(solution)/shard_map/ppermute | solution.py:19
  26.2 0.0 collective-permute-start.4
  26.2 0.0 collective-permute-done.2.refs_1_
  26.2 2.4 %collective-permute-done.3.refs_2_ = bf16[272,128]{1,0:T(8,128)(2,1)S(1)} collective-permute-done((bf16[272,128]{1,0:T(8,128)(2,1)S(1)}, bf16[272,128]{1,0:T(8,128)(2,1)S(1)}, u32[]{:S(2)}, u32[]{:S(2)}) %collective-permute-start.3) | collective-permute-done | bytes 69664 | tf_op jit(solution)/shard_map/ppermute | solution.py:19
  28.6 2.5 %collective-permute-done.4.refs_3_ = bf16[272,128]{1,0:T(8,128)(2,1)S(1)} collective-permute-done((bf16[272,128]{1,0:T(8,128)(2,1)S(1)}, bf16[272,128]{1,0:T(8,128)(2,1)S(1)}, u32[]{:S(2)}, u32[]{:S(2)}) %collective-permute-start.4) | collective-permute-done | bytes 69664 | tf_op jit(solution)/shard_map/ppermute | solution.py:19
  31.2 0.0 copy-done.5
  31.2 0.9 %mix.1 = (bf16[16,16,128]{2,1,0:T(8,128)(2,1)S(1)}, bf16[16,16,128]{2,1,0:T(8,128)(2,1)S(1)}, bf16[16,16,128]{2,1,0:T(8,128)(2,1)S(1)}, bf16[16,16,128]{2,1,0:T(8,128)(2,1)S(1)}) custom-call(s32[3]{0:T(128)S(1)} %pad_add_fusion.place_ref, s32[128]{0:T(128)S(1)} %bitcast.22, bf16[272,128]{1,0:T(8,128)(2,1)S(1)} %get-tuple-element.35.refs_0_, ...), custom_call_target="tpu_custom_call" | custom-call | flops 20000000 | bytes 1048576 | tf_op jit(solution)/shard_map/mix/pallas_call | solution.py:344
  32.0 2.2 %collective-permute-start.6 = (bf16[16,16,128]{2,1,0:T(8,128)(2,1)S(1)}, bf16[16,16,128]{2,1,0:T(8,128)(2,1)S(1)}, u32[]{:S(2)}, u32[]{:S(2)}) collective-permute-start(bf16[16,16,128]{2,1,0:T(8,128)(2,1)S(1)} %get-tuple-element.41), channel_id=1, source_target_pairs={{0,8},{4,12},{8,0},{12,4},{1,9},{5,13},{9,1},{13,5},{2,10},{6,14},... | collective-permute-start | bytes 196616 | tf_op jit(solution)/shard_map/ppermute | solution.py:19
  34.2 0.6 collective-permute-start.7
  34.8 0.0 collective-permute-start.5
  34.8 2.0 %collective-permute-done.6 = bf16[16,16,128]{2,1,0:T(8,128)(2,1)S(1)} collective-permute-done((bf16[16,16,128]{2,1,0:T(8,128)(2,1)S(1)}, bf16[16,16,128]{2,1,0:T(8,128)(2,1)S(1)}, u32[]{:S(2)}, u32[]{:S(2)}) %collective-permute-start.6) | collective-permute-done | bytes 65568 | tf_op jit(solution)/shard_map/ppermute | solution.py:19
  36.8 3.0 %collective-permute-done.7 = bf16[16,16,128]{2,1,0:T(8,128)(2,1)S(1)} collective-permute-done((bf16[16,16,128]{2,1,0:T(8,128)(2,1)S(1)}, bf16[16,16,128]{2,1,0:T(8,128)(2,1)S(1)}, u32[]{:S(2)}, u32[]{:S(2)}) %collective-permute-start.7) | collective-permute-done | bytes 65568 | tf_op jit(solution)/shard_map/ppermute | solution.py:19
  39.8 0.0 collective-permute-done.5
  39.9 1.3 %collective-permute-start.8 = (bf16[4,16,16,128]{3,2,1,0:T(8,128)(2,1)S(1)}, bf16[4,16,16,128]{3,2,1,0:T(8,128)(2,1)S(1)}, u32[]{:S(2)}, u32[]{:S(2)}) collective-permute-start(bf16[4,16,16,128]{3,2,1,0:T(8,128)(2,1)S(1)} %pad_maximum_fusion.traces_ref), channel_id=1, source_target_pairs={{0,2},{2,0},{1,3},{3,1},{4,6},{6,4},{5,7},{7,5},{8,10},{10,8},{9,1... | collective-permute-start | bytes 786440 | tf_op jit(solution)/shard_map/ppermute | solution.py:19
  41.2 0.0 copy-done.2
  41.2 0.0 copy-done.4
  41.2 6.9 %shapes.1 = (bf16[128,256,128]{2,1,0:T(8,128)(2,1)S(1)}, bf16[128,128]{1,0:T(8,128)(2,1)S(1)}, bf16[256,768]{1,0:T(8,128)(2,1)S(1)}) custom-call(f32[25]{0:T(128)S(1)} %copy-done.2, f32[25]{0:T(128)S(1)} %copy-done.4, s32[128,128]{1,0:T(8,128)S(1)} %multiply_add_fusion.code_ref, bf16[256,512]{1,0:T(8,128)(2,1)S(1)} %bitcast.20), custom_call_target="tpu_custom_call" | custom-call | flops 4300000256 | bytes 9437184 | tf_op jit(solution)/shard_map/shapes/pallas_call | solution.py:322
  48.1 1.8 %residual.3 = (bf16[1024,256]{1,0:T(8,128)(2,1)S(1)}, bf16[256,256]{1,0:T(8,128)(2,1)S(1)}, bf16[64,16,128]{2,1,0:T(8,128)(2,1)S(1)}) custom-call(s32[3]{0:T(128)S(1)} %pad_add_fusion.place_ref, bf16[4,16,16,128]{3,2,1,0:T(8,128)(2,1)S(1)} %pad_maximum_fusion.traces_ref, bf16[128,256,128]{2,1,0:T(8,128)(2,1)S(1)} %get-tuple-element.45.shapes_ref, ...), custom_call_target="tpu_custom_call" | custom-call | flops 70000000 | bytes 6291456 | tf_op jit(solution)/shard_map/residual/pallas_call | solution.py:356
  49.9 0.0 collective-permute-done.8.traces_ref
  49.9 1.8 %residual.2 = (bf16[1024,256]{1,0:T(8,128)(2,1)S(1)}, bf16[256,256]{1,0:T(8,128)(2,1)S(1)}, bf16[64,16,128]{2,1,0:T(8,128)(2,1)S(1)}) custom-call(s32[3]{0:T(128)S(1)} %pad_add_fusion.place_ref, bf16[4,16,16,128]{3,2,1,0:T(8,128)(2,1)S(1)} %collective-permute-done.8.traces_ref, bf16[128,256,128]{2,1,0:T(8,128)(2,1)S(1)} %get-tuple-element.45.shapes_ref, ...), custom_call_target="tpu_custom_call" | custom-call | flops 70000000 | bytes 6291456 | tf_op jit(solution)/shard_map/residual/pallas_call | solution.py:356
  51.7 3.2 %collective-permute-start.9 = (bf16[256,256]{1,0:T(8,128)(2,1)S(1)}, bf16[256,256]{1,0:T(8,128)(2,1)S(1)}, u32[]{:S(2)}, u32[]{:S(2)}) collective-permute-start(bf16[256,256]{1,0:T(8,128)(2,1)S(1)} %broadcast_select_fusion.2), channel_id=1, source_target_pairs={{0,1},{1,0},{2,3},{3,2},{4,5},{5,4},{6,7},{7,6},{8,9},{9,8},{10,11... | collective-permute-start | bytes 393224 | tf_op jit(solution)/shard_map/ppermute | solution.py:19
  54.9 0.2 fusion
  55.2 1.3 %copy.16 = bf16[64,16,128]{2,1,0:T(8,128)(2,1)} copy(bf16[64,16,128]{0,1,2:T(8,128)(2,1)S(1)} %fusion) | data formatting | bytes 524288
  56.4 0.0 collective-permute-done.9.edge_ref
  56.4 4.4 %backward.1 = bf16[2,16,128,128]{3,2,1,0:T(8,128)(2,1)} custom-call(s32[3]{0:T(128)S(1)} %pad_add_fusion.place_ref, bf16[256,256]{1,0:T(8,128)(2,1)S(1)} %collective-permute-done.9.edge_ref, bf16[128,128]{1,0:T(8,128)(2,1)S(1)} %get-tuple-element.52.col_adj_ref, bf16[256,768]{1,0:T(8,128)(2,1)S(1)} %get-tuple-element.53.row_adj_ref, ...), custom_call_target="tpu_custom_call" | custom-call | flops 1000000000 | bytes 3145728 | tf_op jit(solution)/shard_map/backward/pallas_call | solution.py:380
  (8 shorter events, 0.1 us)
Async XLA Ops:
  1.6 8.4 %collective-permute-start = (bf16[2,16,16,128]{3,2,1,0:T(8,128)(2,1)S(1)}, bf16[2,16,16,128]{3,2,1,0:T(8,128)(2,1)S(1)}, u32[]{:S(2)}, u32[]{:S(2)}) collective-permute-start(bf16[2,16,16,128]{3,2,1,0:T(8,128)(2,1)S(1)} %constant_dynamic-slice_fusion), channel_id=1, source_target_pairs={{0,1},{1,0},{2,3},{3,2},{4,5},{5,4},{6,7},{7,6},{8,9},{9,8},{10,11... | collective-permute-start | bytes 393224 | tf_op jit(solution)/shard_map/ppermute | solution.py:19
  5.1 1.2 %copy-start = (bf16[2,16,128,128]{3,2,1,0:T(8,128)(2,1)S(1)}, bf16[2,16,128,128]{3,2,1,0:T(8,128)(2,1)}, u32[]{:S(2)}) copy-start(bf16[2,16,128,128]{3,2,1,0:T(8,128)(2,1)} %movie_ref.1) | copy-start | bytes 3145732
  6.3 0.7 %copy-start.1 = (f32[25]{0:T(128)S(1)}, f32[25]{0:T(128)}, u32[]{:S(2)}) copy-start(f32[25]{0:T(128)} %col_ref.3) | copy-start | bytes 304
  7.0 0.7 %copy-start.3 = (f32[25]{0:T(128)S(1)}, f32[25]{0:T(128)}, u32[]{:S(2)}) copy-start(f32[25]{0:T(128)} %row_ref.3) | copy-start | bytes 304
  12.5 9.4 %collective-permute-start.1 = (bf16[1024,128]{1,0:T(8,128)(2,1)S(1)}, bf16[1024,128]{1,0:T(8,128)(2,1)S(1)}, u32[]{:S(2)}, u32[]{:S(2)}) collective-permute-start(bf16[1024,128]{1,0:T(8,128)(2,1)S(1)} %get-tuple-element.34), channel_id=1, source_target_pairs={{0,2},{2,0},{1,3},{3,1},{4,6},{6,4},{5,7},{7,5},{8,10},{10,8},{9,1... | collective-permute-start | bytes 786440 | tf_op jit(solution)/shard_map/ppermute | solution.py:19
  15.3 15.8 %copy-start.5 = (s32[128,1]{0,1:T(1,128)S(1)}, s32[128,1]{0,1:T(1,128)}, u32[]{:S(2)}) copy-start(s32[128,1]{0,1:T(1,128)} %param.11) | copy-start | bytes 1540
  17.7 23.5 %copy-start.2 = (f32[25]{0:T(128)S(1)}, f32[25]{0:T(128)}, u32[]{:S(2)}) copy-start(f32[25]{0:T(128)} %col_ref.3) | copy-start | bytes 304
  17.7 23.5 %copy-start.4 = (f32[25]{0:T(128)S(1)}, f32[25]{0:T(128)}, u32[]{:S(2)}) copy-start(f32[25]{0:T(128)} %row_ref.3) | copy-start | bytes 304
  22.5 3.7 %collective-permute-start.2 = (bf16[272,128]{1,0:T(8,128)(2,1)S(1)}, bf16[272,128]{1,0:T(8,128)(2,1)S(1)}, u32[]{:S(2)}, u32[]{:S(2)}) collective-permute-start(bf16[272,128]{1,0:T(8,128)(2,1)S(1)} %get-tuple-element.36), channel_id=1, source_target_pairs={{0,4},{4,0},{8,12},{12,8},{1,5},{5,1},{9,13},{13,9},{2,6},{6,2},{1... | collective-permute-start | bytes 208904 | tf_op jit(solution)/shard_map/ppermute | solution.py:19
  23.9 4.8 %collective-permute-start.3 = (bf16[272,128]{1,0:T(8,128)(2,1)S(1)}, bf16[272,128]{1,0:T(8,128)(2,1)S(1)}, u32[]{:S(2)}, u32[]{:S(2)}) collective-permute-start(bf16[272,128]{1,0:T(8,128)(2,1)S(1)} %get-tuple-element.37), channel_id=1, source_target_pairs={{0,8},{4,12},{8,0},{12,4},{1,9},{5,13},{9,1},{13,5},{2,10},{6,14},... | collective-permute-start | bytes 208904 | tf_op jit(solution)/shard_map/ppermute | solution.py:19
  26.2 5.0 %collective-permute-start.4 = (bf16[272,128]{1,0:T(8,128)(2,1)S(1)}, bf16[272,128]{1,0:T(8,128)(2,1)S(1)}, u32[]{:S(2)}, u32[]{:S(2)}) collective-permute-start(bf16[272,128]{1,0:T(8,128)(2,1)S(1)} %get-tuple-element.38), channel_id=1, source_target_pairs={{0,12},{4,8},{8,4},{12,0},{1,13},{5,9},{9,5},{13,1},{2,14},{6,10},... | collective-permute-start | bytes 208904 | tf_op jit(solution)/shard_map/ppermute | solution.py:19
  32.0 4.8 %collective-permute-start.6 = (bf16[16,16,128]{2,1,0:T(8,128)(2,1)S(1)}, bf16[16,16,128]{2,1,0:T(8,128)(2,1)S(1)}, u32[]{:S(2)}, u32[]{:S(2)}) collective-permute-start(bf16[16,16,128]{2,1,0:T(8,128)(2,1)S(1)} %get-tuple-element.41), channel_id=1, source_target_pairs={{0,8},{4,12},{8,0},{12,4},{1,9},{5,13},{9,1},{13,5},{2,10},{6,14},... | collective-permute-start | bytes 196616 | tf_op jit(solution)/shard_map/ppermute | solution.py:19
  34.2 5.6 %collective-permute-start.7 = (bf16[16,16,128]{2,1,0:T(8,128)(2,1)S(1)}, bf16[16,16,128]{2,1,0:T(8,128)(2,1)S(1)}, u32[]{:S(2)}, u32[]{:S(2)}) collective-permute-start(bf16[16,16,128]{2,1,0:T(8,128)(2,1)S(1)} %get-tuple-element.42), channel_id=1, source_target_pairs={{0,12},{4,8},{8,4},{12,0},{1,13},{5,9},{9,5},{13,1},{2,14},{6,10},... | collective-permute-start | bytes 196616 | tf_op jit(solution)/shard_map/ppermute | solution.py:19
  34.8 5.0 %collective-permute-start.5 = (bf16[16,16,128]{2,1,0:T(8,128)(2,1)S(1)}, bf16[16,16,128]{2,1,0:T(8,128)(2,1)S(1)}, u32[]{:S(2)}, u32[]{:S(2)}) collective-permute-start(bf16[16,16,128]{2,1,0:T(8,128)(2,1)S(1)} %get-tuple-element.40), channel_id=1, source_target_pairs={{0,4},{4,0},{8,12},{12,8},{1,5},{5,1},{9,13},{13,9},{2,6},{6,2},{1... | collective-permute-start | bytes 196616 | tf_op jit(solution)/shard_map/ppermute | solution.py:19
  39.9 10.0 %collective-permute-start.8 = (bf16[4,16,16,128]{3,2,1,0:T(8,128)(2,1)S(1)}, bf16[4,16,16,128]{3,2,1,0:T(8,128)(2,1)S(1)}, u32[]{:S(2)}, u32[]{:S(2)}) collective-permute-start(bf16[4,16,16,128]{3,2,1,0:T(8,128)(2,1)S(1)} %pad_maximum_fusion.traces_ref), channel_id=1, source_target_pairs={{0,2},{2,0},{1,3},{3,1},{4,6},{6,4},{5,7},{7,5},{8,10},{10,8},{9,1... | collective-permute-start | bytes 786440 | tf_op jit(solution)/shard_map/ppermute | solution.py:19
  51.7 4.7 %collective-permute-start.9 = (bf16[256,256]{1,0:T(8,128)(2,1)S(1)}, bf16[256,256]{1,0:T(8,128)(2,1)S(1)}, u32[]{:S(2)}, u32[]{:S(2)}) collective-permute-start(bf16[256,256]{1,0:T(8,128)(2,1)S(1)} %broadcast_select_fusion.2), channel_id=1, source_target_pairs={{0,1},{1,0},{2,3},{3,2},{4,5},{5,4},{6,7},{7,6},{8,9},{9,8},{10,11... | collective-permute-start | bytes 393224 | tf_op jit(solution)/shard_map/ppermute | solution.py:19

commit v3 on v2

--- a/solution.py
+++ b/solution.py
@@ -70,23 +70,59 @@
     return tall if copies == 1 else jnp.concatenate([tall] * copies, axis=1)
 
 
-def smooth_kernel(rim, frames, col_ref, row_ref, movie_ref, smooth_ref, col_fwd_ref, row_fwd_ref):
-    @pl.when((pl.program_id(0) == 0) & (pl.program_id(1) == 0))
-    def _():
-        col_fwd_ref[...] = column_band(col_ref, rim, -1)
-        row_fwd_ref[...] = row_band_forward(row_ref, rim, frames)
-
-    _, some, rows, _ = movie_ref.shape
-    full = jnp.dot(
-        movie_ref[0].reshape(some * rows, LANES), col_fwd_ref[...], preferred_element_type=F32
-    )
-    smooth_ref[:, BLOCK : BLOCK + rows, :] = full.astype(BF16).reshape(some, rows, LANES)
+def prepare_kernel(
+    rim, cuts, col_hbm, row_hbm, movie_hbm, mask_hbm, support_hbm, templates_hbm,
+    smooth_ref, col_fwd_ref, row_fwd_ref, code_ref, templates_ref,
+    movie_ref, mask_ref, support_ref, packed_ref, loose_ref, col_ref, row_ref, sems,
+):
+    planes, frames, rows, _ = movie_ref.shape
+    some = frames // cuts
+
+    def fetch(n, source, target):
+        copy = pltpu.make_async_copy(source, target, sems.at[n])
+        copy.start()
+        return copy
+
+    tap_copies = [fetch(0, col_hbm, col_ref), fetch(1, row_hbm, row_ref)]
+    movie_copies = []
+    for n in range(planes * cuts):
+        piece = (n // cuts, pl.ds(n % cuts * some, some))
+        movie_copies.append(fetch(5 + n, movie_hbm.at[piece], movie_ref.at[piece]))
+    packed_copy = fetch(2, templates_hbm, packed_ref)
+    code_copies = [fetch(3, mask_hbm, mask_ref), fetch(4, support_hbm, support_ref)]
+    for copy in tap_copies:
+        copy.wait()
+    col_fwd = column_band(col_ref, rim, -1)
+    col_fwd_ref[...] = col_fwd
+    row_fwd_ref[...] = row_band_forward(row_ref, rim, frames)
+    for n, copy in enumerate(movie_copies):
+        p, first = n // cuts, n % cuts * some
+        copy.wait()
+        full = jnp.dot(
+            movie_ref[p, first : first + some].reshape(some * rows, LANES), col_fwd,
+            preferred_element_type=F32,
+        )
+        smooth_ref[first : first + some, BLOCK : BLOCK + rows, p * LANES : (p + 1) * LANES] = (
+            full.astype(BF16).reshape(some, rows, LANES)
+        )
+    packed_copy.wait()
+    loose_ref[...] = packed_ref[...].astype(F32)
+    unit = (iota((LANES, LANES), 0) == iota((LANES, LANES), 1)).astype(BF16)
+    for p in range(planes):
+        shapes = loose_ref[pl.ds(p, templates_ref.shape[1], stride=planes), :].astype(BF16)
+        templates_ref[p * LANES : (p + 1) * LANES, :] = lax.dot_general(
+            unit, shapes, (((1,), (1,)), ((), ())), preferred_element_type=F32
+        ).astype(BF16)
+    for copy in code_copies:
+        copy.wait()
+    code_ref[...] = support_ref[...] * 2 + mask_ref[...]
 
 
 def forward_kernel(
     flip, fill, place_ref, smooth_in_ref, edge_ref, col_fwd_ref, row_fwd_ref, code_ref,
-    templates_ref, smooth_ref, filtered_ref, projected_ref,
+    templates_ref, smooth_ref, filtered_ref, *refs
 ):
+    outs, projected_ref = refs[:-1], refs[-1]
     frames, padded_rows, width = smooth_ref.shape
     planes, rows = width // LANES, padded_rows - 2 * BLOCK
     if fill:
@@ -122,27 +158,36 @@
             )
             chosen = jnp.where(tile == t, found, chosen)
         projected_ref[spot, :] = chosen.astype(BF16)
-
-
-def split_kernel(count, place_ref, lag_ref, *refs):
-    parts, outs = refs[:count], refs[count:]
-    rows = parts[0].shape[0] // len(outs)
+    size = outs[0].shape[0]
     for k, out_ref in enumerate(outs):
-        start = pl.multiple_of((place_ref[WIDE] ^ k) * rows, rows)
-        total = parts[0][pl.ds(start, rows), :].astype(F32)
-        for part in parts[1:]:
-            total = total + part[pl.ds(start, rows), :].astype(F32)
-        out_ref[:rows, :] = total.astype(BF16)
-        out_ref[rows:, :] = lag_ref[...]
-
-
-def mix_kernel(wide, place_ref, owner_ref, *refs):
-    blocks, outs = refs[:wide], refs[wide : 2 * wide]
-    cells_ref, kernels_ref, traces_ref, tables_ref = refs[2 * wide :]
+        start = pl.multiple_of((place_ref[WIDE] ^ k) * size, size)
+        out_ref[...] = projected_ref[pl.ds(start, size), :]
+
+
+def add_all(parts):
+    total = parts[0][...].astype(F32)
+    for part in parts[1:]:
+        total = total + part[...].astype(F32)
+    return total.astype(BF16)
+
+
+def sum_kernel(lag_ref, *refs):
+    parts, out_ref = refs[:-1], refs[-1]
+    rows = parts[0].shape[0]
+    out_ref[:rows, :] = add_all(parts)
+    out_ref[rows:, :] = lag_ref[...]
+
+
+def mix_kernel(wide, count, place_ref, owner_ref, lag_ref, *refs):
+    parts, refs = refs[:count], refs[count:]
+    blocks, outs = refs[: wide - 1], refs[wide - 1 : 2 * wide - 1]
+    cells_ref, kernels_ref, traces_ref, tables_ref = refs[2 * wide - 1 :]
     _, share, frames, lanes = cells_ref.shape
     total = wide * frames
     here = place_ref[WIDE]
-    for k, block in enumerate(blocks):
+    cells_ref[here] = add_all(parts).reshape(share, frames, lanes)
+    kernels_ref[here] = lag_ref[...].astype(F32)
+    for k, block in enumerate(blocks, 1):
         cells_ref[here ^ k] = block[: share * frames, :].reshape(share, frames, lanes)
         kernels_ref[here ^ k] = block[share * frames :, :].astype(F32)
 
@@ -163,30 +208,40 @@
         out_ref[...] = traces_ref[here ^ k]
 
 
-def shapes_kernel(
-    rim, frames, col_ref, row_ref, code_ref, templates_ref, shapes_ref, col_adj_ref, row_adj_ref
+def shapes_kernel(flip, rim, frames, place_ref, *refs):
+    if rim:
+        col_ref, row_ref, code_ref, templates_ref, shapes_ref, col_adj_ref, row_adj_ref = refs
+        band = column_band(col_ref, rim, 1)
+        planes = templates_ref.shape[0] // LANES
+        col_adj_ref[...] = jnp.zeros_like(col_adj_ref)
+        for p in range(planes):
+            lanes = slice(p * LANES, (p + 1) * LANES)
+            col_adj_ref[lanes, lanes] = band
+        row_adj_ref[...] = row_band_adjoint(row_ref, rim, frames)
+    else:
+        code_ref, templates_ref, shapes_ref = refs
+    count, here = templates_ref.shape[1], shapes_ref.shape[0]
+    first = pl.multiple_of((place_ref[PLANE] ^ flip) * here, here)
+
+    @pl.loop(0, here // 8)
+    def _(g):
+        support = code_ref[pl.ds(pl.multiple_of(first + g * 8, 8), 8), :] >> 1
+        for i in range(0, 8, 2):
+            both = jnp.concatenate([support[i : i + 1, :], support[i + 1 : i + 2, :]], axis=1)
+            hits = iota((count, 2 * LANES), 0) == jnp.broadcast_to(both, (count, 2 * LANES))
+            pair = jnp.dot(
+                templates_ref[...], hits.astype(BF16), preferred_element_type=F32
+            ).astype(BF16)
+            shapes_ref[g * 8 + i] = pair[:, :LANES]
+            shapes_ref[g * 8 + i + 1] = pair[:, LANES:]
+
+
+def residual_kernel(
+    flip, place_ref, shapes_ref, filtered_ref, code_ref, *refs
 ):
-    @pl.when(pl.program_id(0) == 0)
-    def _():
-        col_adj_ref[...] = column_band(col_ref, rim, 1)
-        row_adj_ref[...] = row_band_adjoint(row_ref, rim, frames)
-
-    count = templates_ref.shape[1]
-    support = code_ref[...] >> 1
-    for i in range(0, shapes_ref.shape[0], 2):
-        both = jnp.concatenate([support[i : i + 1, :], support[i + 1 : i + 2, :]], axis=1)
-        hits = iota((count, 2 * LANES), 0) == jnp.broadcast_to(both, (count, 2 * LANES))
-        pair = jnp.dot(
-            templates_ref[...], hits.astype(BF16), preferred_element_type=F32
-        ).astype(BF16)
-        shapes_ref[i] = pair[:, :LANES]
-        shapes_ref[i + 1] = pair[:, LANES:]
-
-
-def residual_kernel(
-    flip, place_ref, traces_ref, shapes_ref, filtered_ref, code_ref, out_ref, edge_ref, ordered_ref
-):
-    wide, share, frames, lanes = traces_ref.shape
+    traces, (out_ref, edge_ref, ordered_ref) = refs[:-3], refs[-3:]
+    wide = len(traces)
+    share, frames, lanes = traces[0].shape
     copies = filtered_ref.shape[1] // LANES
     base = (place_ref[PLANE] ^ flip) * wide * share
     for k in range(wide):
@@ -194,7 +249,7 @@
         for h in range(share):
             row = block * share + h
             model = lax.dot_general(
-                traces_ref[k, h], shapes_ref[base + row], (((1,), (1,)), ((), ())),
+                traces[k][h], shapes_ref[row], (((1,), (1,)), ((), ())),
                 preferred_element_type=F32,
             )
             mask = (code_ref[pl.ds(base + row, 1), :] & 1).astype(F32)
@@ -202,14 +257,14 @@
             out_ref[spot, :] = (
                 filtered_ref[spot, :].astype(F32) - jnp.concatenate([mask] * copies, axis=1) * model
             ).astype(BF16)
-        ordered_ref[pl.ds(block * share, share)] = traces_ref[k]
+        ordered_ref[pl.ds(block * share, share)] = traces[k][...]
     edge = edge_ref.shape[0]
     start = jnp.where(place_ref[REP] > 0, 0, out_ref.shape[0] - edge)
     edge_ref[...] = out_ref[pl.ds(pl.multiple_of(start, edge), edge), :]
 
 
 def backward_kernel(count, place_ref, edge_ref, col_adj_ref, row_adj_ref, *refs):
-    parts, (out_ref, padded_ref) = refs[:count], refs[count:]
+    parts, (out_hbm, padded_ref, out_ref, sems) = refs[:count], refs[count:]
     planes, frames, rows, _ = out_ref.shape
     edge, size = BLOCK * frames, parts[0].shape[0]
     zero = jnp.zeros_like(edge_ref)
@@ -218,18 +273,26 @@
     for flip, part in enumerate(parts):
         spot = pl.multiple_of(edge + (place_ref[PLANE] ^ flip) * size, edge)
         padded_ref[pl.ds(spot, size), :] = part[...]
+    copies = []
     for b in range(rows // BLOCK):
         near = padded_ref[b * edge : (b + 3) * edge, :]
         back = jnp.dot(row_adj_ref[...], near, preferred_element_type=F32).astype(BF16)
+        full = jnp.dot(back, col_adj_ref[...], preferred_element_type=F32).astype(BF16)
+        piece = (slice(None), slice(None), pl.ds(b * BLOCK, BLOCK))
         for p in range(planes):
-            full = jnp.dot(
-                back[:, p * LANES : (p + 1) * LANES], col_adj_ref[...], preferred_element_type=F32
-            ).astype(BF16)
-            out_ref[p, :, b * BLOCK : (b + 1) * BLOCK, :] = full.reshape(frames, BLOCK, LANES)
+            out_ref[p, :, b * BLOCK : (b + 1) * BLOCK, :] = full[
+                :, p * LANES : (p + 1) * LANES
+            ].reshape(frames, BLOCK, LANES)
+        copy = pltpu.make_async_copy(out_ref.at[piece], out_hbm.at[piece], sems.at[b])
+        copy.start()
+        copies.append(copy)
+    for copy in copies:
+        copy.wait()
 
 
 VMEM = pl.BlockSpec(memory_space=pltpu.VMEM)
 SMEM = pl.BlockSpec(memory_space=pltpu.SMEM)
+HBM = pl.BlockSpec(memory_space=pltpu.HBM)
 
 
 def shaped(shape):
@@ -275,88 +338,111 @@
 
     start = jnp.where(rep == 0, rows - BLOCK, 0)
     rim_rows = exchange(lax.dynamic_slice_in_dim(movie_frames, start, BLOCK, axis=2), "rep", 1)
-    code = support * 2 + pixel_mask
-    tall_templates = jnp.transpose(templates, (1, 2, 0)).reshape(width, -1)
-    kernel_row = lag_kernel_values(lag_gains[0], dilations[0], total_frames)
-    lag_rows = -(-2 * total_frames // (LANES * BLOCK)) * BLOCK
-    kernel_row = jnp.pad(kernel_row, (0, lag_rows * LANES - 2 * total_frames)).reshape(lag_rows, LANES)
-
-    half = frames // 2
-    depth = 3 * BLOCK * frames
-    smooth, col_fwd, row_fwd = pl.pallas_call(
-        functools.partial(smooth_kernel, rim, frames),
-        grid=(2, planes),
+    cuts = 2
+    depth, names = 3 * BLOCK * frames, templates.shape[0]
+    smooth, col_fwd, row_fwd, code, tall_templates = pl.pallas_call(
+        functools.partial(prepare_kernel, rim, cuts),
         out_shape=(
-            shaped((frames, rows + 2 * BLOCK, width)), shaped((cols, cols)), shaped((edge, depth))
+            shaped((frames, rows + 2 * BLOCK, width)), shaped((cols, cols)), shaped((edge, depth)),
+            jax.ShapeDtypeStruct(support.shape, jnp.int32), shaped((width, names)),
         ),
-        in_specs=[SMEM, SMEM, pl.BlockSpec((1, half, rows, cols), lambda i, p: (p, i, 0, 0))],
-        out_specs=(
-            pl.BlockSpec((half, rows + 2 * BLOCK, cols), lambda i, p: (i, 0, p)),
-            pl.BlockSpec((cols, cols), lambda i, p: (0, 0)),
-            pl.BlockSpec((edge, depth), lambda i, p: (0, 0)),
-        ),
-        compiler_params=pltpu.CompilerParams(vmem_limit_bytes=32 * 1024 * 1024),
+        in_specs=[HBM] * 6,
+        out_specs=(VMEM,) * 5,
+        scratch_shapes=[
+            pltpu.VMEM(movie_frames.shape, BF16),
+            pltpu.VMEM(pixel_mask.shape, jnp.int32),
+            pltpu.VMEM(support.shape, jnp.int32),
+            pltpu.VMEM((names * planes, cols), BF16),
+            pltpu.VMEM((names * planes, cols), F32),
+            pltpu.SMEM(col_taps.shape, F32),
+            pltpu.SMEM(row_taps.shape, F32),
+            pltpu.SemaphoreType.DMA((5 + planes * cuts,)),
+        ],
+        compiler_params=pltpu.CompilerParams(vmem_limit_bytes=32 * mib),
         cost_estimate=pl.CostEstimate(flops=200000000, bytes_accessed=3 * mib, transcendentals=0),
-        name="smooth",
-    )(col_taps, row_taps, movie_frames)
-
+        name="prepare",
+    )(
+        *[
+            pltpu.with_memory_space_constraint(x, pltpu.HBM)
+            for x in (
+                col_taps, row_taps, movie_frames, pixel_mask, support,
+                templates.reshape(names * planes, cols),
+            )
+        ]
+    )
+
+    order = list(range(wide // 2, wide)) + list(range(1, wide // 2)) + [0]
     filtered, projected = [None] * plane_count, [None] * plane_count
     for turn in range(plane_count):
         flip = (turn + 1) % plane_count
-        smooth, filtered[flip], mine = call(
+        smooth, filtered[flip], *mine = call(
             functools.partial(forward_kernel, flip, turn == 0), "forward",
-            [smooth.shape, (here * frames, width), (here * frames, support.shape[1])],
+            [smooth.shape, (here * frames, width)] + [(share * frames, LANES)] * wide,
             1, 6, 800000000, 3 * mib, aliases={1: 0},
+            scratch=[pltpu.VMEM((here * frames, LANES), BF16)],
         )(place, smooth, rim_rows, col_fwd, row_fwd, code, tall_templates)
-        projected[flip] = exchange(mine, "planes", flip) if flip else mine
+        projected[flip] = {k: exchange(mine[k], "planes", flip) if flip else mine[k] for k in order}
+        if turn == 0:
+            gains, lags, _ = lax.optimization_barrier((lag_gains[0], dilations[0], mine[0]))
+            kernel_row = lag_kernel_values(gains, lags, total_frames)
+            lag_rows = -(-2 * total_frames // (LANES * BLOCK)) * BLOCK
+            kernel_row = jnp.pad(kernel_row, (0, lag_rows * LANES - 2 * total_frames))
+            kernel_row = kernel_row.reshape(lag_rows, LANES)
 
     block_rows = share * frames + lag_rows
-    blocks = call(
-        functools.partial(split_kernel, plane_count), "split", [(block_rows, LANES)] * wide,
-        1, 1 + plane_count, 1000000, mib,
-    )(place, kernel_row, *projected)
-    blocks = [exchange(block, "wide", k) if k else block for k, block in enumerate(blocks)]
-
-    late_code, late_templates, _ = lax.optimization_barrier((code, tall_templates, blocks[0]))
-    steps = 8
-    shapes, col_adj, row_adj = pl.pallas_call(
-        functools.partial(shapes_kernel, rim, frames),
-        grid=(steps,),
-        out_shape=(shaped((rows, width, LANES)), shaped((cols, cols)), shaped((edge, depth))),
-        in_specs=[
-            SMEM,
-            SMEM,
-            pl.BlockSpec((rows // steps, LANES), lambda i: (i, 0)),
-            pl.BlockSpec((width, templates.shape[0]), lambda i: (0, 0)),
-        ],
-        out_specs=(
-            pl.BlockSpec((rows // steps, width, LANES), lambda i: (i, 0, 0)),
-            pl.BlockSpec((cols, cols), lambda i: (0, 0)),
-            pl.BlockSpec((edge, depth), lambda i: (0, 0)),
-        ),
-        compiler_params=pltpu.CompilerParams(vmem_limit_bytes=32 * 1024 * 1024),
-        cost_estimate=pl.CostEstimate(flops=4300000000, bytes_accessed=9 * mib, transcendentals=0),
-        name="shapes",
-    )(col_taps, row_taps, late_code, late_templates)
+    sums, blocks = {}, {}
+    for k in order[:-1]:
+        (sums[k],) = call(
+            sum_kernel, "sum", [(block_rows, LANES)], 0, 1 + plane_count, 100000, mib // 4
+        )(kernel_row, *[part[k] for part in projected])
+        blocks[k] = exchange(sums[k], "wide", k)
+
+    def make_shapes(flip, after, bands):
+        late_code, late_templates, _ = lax.optimization_barrier((code, tall_templates, after))
+        outs = [(here, width, LANES)]
+        taps = ()
+        if bands:
+            outs += [(width, width), (edge, depth)]
+            taps = (col_taps, row_taps)
+        return call(
+            functools.partial(shapes_kernel, flip, rim if bands else 0, frames), "shapes",
+            outs, 1 + len(taps), 2, 2150000000, 5 * mib,
+        )(place, *taps, late_code, late_templates)
+
+    shapes = [None] * plane_count
+    shapes[0], col_adj, row_adj = make_shapes(0, [sums[k] for k in order[:-1]], True)
+    first, col_adj = lax.optimization_barrier((projected[0][0], col_adj))
 
     cell_shape = (wide, share, frames, LANES)
     tables = (wide, total_frames, total_frames) if wide <= share else (1, BLOCK, LANES)
     traces = call(
-        functools.partial(mix_kernel, wide), "mix", [cell_shape[1:]] * wide, 2, wide, 20000000, mib,
+        functools.partial(mix_kernel, wide, plane_count), "mix", [cell_shape[1:]] * wide,
+        2, wide + plane_count, 20000000, mib,
         scratch=[
             pltpu.VMEM(cell_shape, BF16), pltpu.VMEM((wide, lag_rows, LANES), F32),
             pltpu.VMEM(cell_shape, BF16), pltpu.VMEM(tables, BF16),
         ],
-    )(place, tile_owner[:, 0], *blocks)
-    traces = jnp.stack([exchange(cells, "wide", k) if k else cells for k, cells in enumerate(traces)])
+    )(
+        place, tile_owner[:, 0], kernel_row, first, *[part[0] for part in projected[1:]],
+        *[blocks[k] for k in range(1, wide)],
+    )
+    for flip in range(1, plane_count):
+        (shapes[flip],) = make_shapes(flip, traces[0], False)
+    swapped = {k: exchange(traces[k], "wide", k) if k else traces[0] for k in order}
+    for k in range(1, wide):
+        swapped[k], _ = lax.optimization_barrier((swapped[k], shapes[1:]))
+    passed = [swapped] + [
+        {k: exchange(swapped[k], "planes", flip) for k in order[::-1]}
+        for flip in range(1, plane_count)
+    ]
 
     residual, edges, ordered = [], [], []
     for flip in range(plane_count):
-        got = exchange(traces, "planes", flip) if flip else traces
         part, tip, sorted_rows = call(
             functools.partial(residual_kernel, flip), "residual",
-            [(here * frames, width), (edge, width), (here, frames, LANES)], 1, 4, 70000000, 6 * mib,
-        )(place, got, shapes, filtered[flip], code)
+            [(here * frames, width), (edge, width), (here, frames, LANES)],
+            1, 3 + wide, 70000000, 6 * mib,
+        )(place, shapes[flip], filtered[flip], code, *[passed[flip][k] for k in range(wide)])
         residual.append(part)
         edges.append(tip)
         ordered.append(sorted_rows)
@@ -377,10 +463,19 @@
     mine = lax.dynamic_slice_in_dim(jnp.concatenate(in_order), plane * foot_share, foot_share, 2)
     trace_out = jnp.transpose(mine, (2, 1, 0))
 
-    (back_projected,) = call(
-        functools.partial(backward_kernel, plane_count), "backward", [movie_frames.shape],
-        1, 3 + plane_count, 1000000000, 3 * mib,
-        scratch=[pltpu.VMEM(((rows + 2 * BLOCK) * frames, width), BF16)],
+    back_projected = pl.pallas_call(
+        functools.partial(backward_kernel, plane_count),
+        out_shape=shaped(movie_frames.shape),
+        in_specs=[SMEM] + [VMEM] * (3 + plane_count),
+        out_specs=HBM,
+        scratch_shapes=[
+            pltpu.VMEM(((rows + 2 * BLOCK) * frames, width), BF16),
+            pltpu.VMEM(movie_frames.shape, BF16),
+            pltpu.SemaphoreType.DMA((rows // BLOCK,)),
+        ],
+        compiler_params=pltpu.CompilerParams(vmem_limit_bytes=32 * mib),
+        cost_estimate=pl.CostEstimate(flops=1000000000, bytes_accessed=3 * mib, transcendentals=0),
+        name="backward",
     )(place, tip, col_adj, row_adj, *residual)
     return trace_out, back_projected
 

time: 61.2 us -> 55.4 us (0.905)
  waiting for transfers between devices: 14.1 us -> 0.04 us
  starting transfers between devices: 13.9 us -> 19.5 us
  local copies, waits for them, and re-layouts: 6.56 us -> 9.43 us
  other arithmetic: 2.13 us -> 0.56 us
  Pallas kernels: 23.5 us -> 24.8 us
    ppermute x10 -> x16, waiting for transfers between devices: 14.1 us -> 0.04 us  [exchange(): return lax.ppermute(cells, axis, [(i, i ^ flip) for i in range(count)])]
    ppermute x10 -> x16, starting transfers between devices: 13.9 us -> 19.5 us  [exchange(): return lax.ppermute(cells, axis, [(i, i ^ flip) for i in range(count)])]
    unnamed x14 -> x18, local copies, waits for them, and re-layouts: 4.52 us -> 8.5 us
    pallas_call x5 -> x8, Pallas kernels: 15.1 us -> 16.4 us  [the longest x2 8.69 us: make_shapes(): call(functools.partial(shapes_kernel, flip, rim if bands else 0, frames),...]
    transpose x1 -> x0, local copies, waits for them, and re-layouts: 1.11 us -> none  [on_device(): tall_templates = jnp.transpose(templates, (1, 2, 0)).reshape(width, -1)]
    add x1 -> x0, other arithmetic: 0.88 us -> none  [on_device(): code = support * 2 + pixel_mask]
    mul x1, other arithmetic: 0.73 us -> 0.07 us  [lag_kernel_values(): lags[:, None, None] * offsets[None, None, :]]
  transfers between devices with their start and end apart: 10 -> 16, of which waited for: 5 -> 0; matrix products, arithmetic and copies ran while one was open for 8% -> 5% of each run, Pallas kernels for 22% -> 28%
where the time goes in v3:
time: 55.4 us; the launch traced here: 55.2 us
  Pallas kernels  24.8 us (45%)
  starting transfers between devices  19.5 us (35%)
  local copies, waits for them, and re-layouts  9.43 us (17%)
  between operations  0.84 us (2%)
  other arithmetic  0.56 us (1%)
    ppermute x16, starting transfers between devices, exchange(): return lax.ppermute(cells, axis, [(i, i ^ flip) for i in range(count)])  19.5 us
    pallas_call x2, Pallas kernels, make_shapes(): call(functools.partial(shapes_kernel, flip, rim if bands else 0, frames),...  8.69 us
    unnamed x18, local copies, waits for them, and re-layouts  8.5 us
    pallas_call x2, Pallas kernels, on_device(): call(functools.partial(forward_kernel, flip, turn == 0), 'forward', [smoo...  4.91 us
    pallas_call x1, Pallas kernels, on_device(): pl.pallas_call(functools.partial(backward_kernel, plane_count), out_shape...  4.1 us
    pallas_call x2, Pallas kernels, on_device(): call(functools.partial(residual_kernel, flip), 'residual', [(here * frame...  3.55 us
    pallas_call x1, Pallas kernels, on_device(): pl.pallas_call(functools.partial(prepare_kernel, rim, cuts), out_shape=(s...  2.62 us
  transfers between devices with their start and end apart: 16, of which 0 were waited for; matrix products, arithmetic and copies ran while one was open for 5% of the time, Pallas kernels for 28%

profile of v3, /device:TPU:1, one launch (start us, length us, event | category | flops | bytes accessed | tf_op | source)
XLA Modules:
  0.0 55.2 jit_solution(8052291287875075191)
XLA Ops:
  0.6 0.9 %constant_dynamic-slice_fusion = bf16[2,16,16,128]{3,2,1,0:T(8,128)(2,1)S(1)} fusion(bf16[2,16,128,128]{3,2,1,0:T(8,128)(2,1)} %movie_hbm.1, s32[]{:T(128)S(6)} %select_n.38), kind=kLoop, calls=%fused_computation.9 | loop fusion | bytes 262148 | tf_op jit(solution)/shard_map/dynamic_slice | solution.py:340
  1.6 0.1 collective-permute-start
  1.7 0.7 %copy.17 = f32[1,3,65]{2,1,0:T(4,128)S(1)} copy(f32[1,3,65]{2,0,1:T(1,128)} %param.16) | data formatting | bytes 1560
  2.4 2.6 %prepare.1 = (bf16[16,160,256]{2,1,0:T(8,128)(2,1)S(1)}, bf16[128,128]{1,0:T(8,128)(2,1)S(1)}, bf16[256,768]{1,0:T(8,128)(2,1)S(1)}, s32[128,128]{1,0:T(8,128)S(1)}, bf16[256,512]{1,0:T(8,128)(2,1)S(1)}) custom-call(f32[25]{0:T(128)} %refs_0_.1, f32[25]{0:T(128)} %refs_1_.1, bf16[2,16,128,128]{3,2,1,0:T(8,128)(2,1)} %movie_hbm.1, s32[128,128]{1,0:T(8,128)} %mask_hbm.1, ...), custom_call_target="tpu_custom_call" | custom-call | flops 200000000 | bytes 3145728 | tf_op jit(solution)/shard_map/prepare/pallas_call | solution.py:343
  5.0 0.1 pad_add_fusion.place_ref
  5.1 0.0 collective-permute-done.edge_ref
  5.1 2.5 %forward.2 = (bf16[16,160,256]{2,1,0:T(8,128)(2,1)S(1)}, bf16[1024,256]{1,0:T(8,128)(2,1)S(1)}, bf16[256,128]{1,0:T(8,128)(2,1)S(1)}, bf16[256,128]{1,0:T(8,128)...) custom-call(s32[3]{0:T(128)S(1)} %pad_add_fusion.place_ref, ...), custom_call_target="tpu_custom_call", output_to_operand_aliasing={{0}: (1, {})} | custom-call | flops 800000000 | bytes 3145728 | tf_op jit(solution)/shard_map/forward/pallas_call | solution.py:378
  7.7 2.7 %collective-permute-start.4 = (bf16[256,128]{1,0:T(8,128)(2,1)S(1)}, bf16[256,128]{1,0:T(8,128)(2,1)S(1)}, u32[]{:S(2)}, u32[]{:S(2)}) collective-permute-start(bf16[256,128]{1,0:T(8,128)(2,1)S(1)} %get-tuple-element.47), channel_id=1, source_target_pairs={{0,2},{2,0},{1,3},{3,1},{4,6},{6,4},{5,7},{7,5},{8,10},{10,8},{9,1... | collective-permute-start | bytes 196616 | tf_op jit(solution)/shard_map/ppermute | solution.py:19
  10.4 0.1 broadcast_multiply_fusion
  10.4 0.1 select_reduce_fusion
  10.6 0.1 collective-permute-start.3
  10.7 1.4 %collective-permute-start.2 = (bf16[256,128]{1,0:T(8,128)(2,1)S(1)}, bf16[256,128]{1,0:T(8,128)(2,1)S(1)}, u32[]{:S(2)}, u32[]{:S(2)}) collective-permute-start(bf16[256,128]{1,0:T(8,128)(2,1)S(1)} %get-tuple-element.55), channel_id=1, source_target_pairs={{0,2},{2,0},{1,3},{3,1},{4,6},{6,4},{5,7},{7,5},{8,10},{10,8},{9,1... | collective-permute-start | bytes 196616 | tf_op jit(solution)/shard_map/ppermute | solution.py:19
  12.1 0.1 collective-permute-start.1
  12.2 2.4 %forward.3 = (bf16[16,160,256]{2,1,0:T(8,128)(2,1)S(1)}, bf16[1024,256]{1,0:T(8,128)(2,1)S(1)}, bf16[256,128]{1,0:T(8,128)(2,1)S(1)}, bf16[256,128]{1,0:T(8,128)...) custom-call(s32[3]{0:T(128)S(1)} %pad_add_fusion.place_ref, ...), custom_call_target="tpu_custom_call", output_to_operand_aliasing={{0}: (1, {})} | custom-call | flops 800000000 | bytes 3145728 | tf_op jit(solution)/shard_map/forward/pallas_call | solution.py:378
  14.6 0.0 collective-permute-done.3.refs_1_
  14.6 1.5 %collective-permute-start.5 = (bf16[272,128]{1,0:T(8,128)(2,1)S(1)}, bf16[272,128]{1,0:T(8,128)(2,1)S(1)}, u32[]{:S(2)}, u32[]{:S(2)}) collective-permute-start(bf16[272,128]{1,0:T(8,128)(2,1)S(1)} %sum.5), channel_id=1, source_target_pairs={{0,4},{4,0},{8,12},{12,8},{1,5},{5,1},{9,13},{13,9},{2,6},{6,2},{1... | collective-permute-start | bytes 208904 | tf_op jit(solution)/shard_map/ppermute | solution.py:19
  16.2 0.0 collective-permute-done.2.refs_1_
  16.2 2.6 %collective-permute-start.7 = (bf16[272,128]{1,0:T(8,128)(2,1)S(1)}, bf16[272,128]{1,0:T(8,128)(2,1)S(1)}, u32[]{:S(2)}, u32[]{:S(2)}) collective-permute-start(bf16[272,128]{1,0:T(8,128)(2,1)S(1)} %sum.4), channel_id=1, source_target_pairs={{0,12},{4,8},{8,4},{12,0},{1,13},{5,9},{9,5},{13,1},{2,14},{6,10},... | collective-permute-start | bytes 208904 | tf_op jit(solution)/shard_map/ppermute | solution.py:19
  18.8 0.0 collective-permute-done.1.refs_1_
  18.9 0.0 copy-start.6
  18.9 0.4 collective-permute-start.6
  19.3 4.6 %shapes.2 = (bf16[64,256,128]{2,1,0:T(8,128)(2,1)S(1)}, bf16[256,256]{1,0:T(8,128)(2,1)S(1)}, bf16[256,768]{1,0:T(8,128)(2,1)S(1)}) custom-call(s32[3]{0:T(128)S(1)} %pad_add_fusion.place_ref, f32[25]{0:T(128)S(1)} %copy-done.4, f32[25]{0:T(128)S(1)} %copy-done.5, s32[128,128]{1,0:T(8,128)S(1)} %get-tuple-element.63.code_ref.refs_2_.refs_0_, ...), custom_call_target="tpu_custom_call" | custom-call | flops 2150000128 | bytes 5242880 | tf_op jit(solution)/shard_map/shapes/pallas_call | solution.py:407
  23.9 2.0 %copy-done = bf16[64,256,128]{2,1,0:T(8,128)(2,1)} copy-done((bf16[64,256,128]{2,1,0:T(8,128)(2,1)}, bf16[64,256,128]{2,1,0:T(8,128)(2,1)S(1)}, u32[]{:S(2)}) %copy-start) | copy-done | bytes 4194328
  25.9 0.0 collective-permute-done.4.refs_1_
  25.9 0.0 collective-permute-done.5.refs_2_
  25.9 0.0 collective-permute-done.7.refs_4_
  25.9 0.0 collective-permute-done.6.refs_3_
  25.9 0.9 %mix.1 = (bf16[16,16,128]{2,1,0:T(8,128)(2,1)S(1)}, bf16[16,16,128]{2,1,0:T(8,128)(2,1)S(1)}, bf16[16,16,128]{2,1,0:T(8,128)(2,1)S(1)}, bf16[16,16,128]{2,1,0:T(8,128)(2,1)S(1)}) custom-call(s32[3]{0:T(128)S(1)} %pad_add_fusion.place_ref, s32[128]{0:T(128)S(1)} %bitcast.13, bf16[16,128]{1,0:T(8,128)(2,1)S(1)} %pad_bitcast_fusion.lag_ref, ...), custom_call_target="tpu_custom_call" | custom-call | flops 20000000 | bytes 1048576 | tf_op jit(solution)/shard_map/mix/pallas_call | solution.py:418
  26.8 1.5 %collective-permute-start.8 = (bf16[16,16,128]{2,1,0:T(8,128)(2,1)S(1)}, bf16[16,16,128]{2,1,0:T(8,128)(2,1)S(1)}, u32[]{:S(2)}, u32[]{:S(2)}) collective-permute-start(bf16[16,16,128]{2,1,0:T(8,128)(2,1)S(1)} %get-tuple-element.62.refs_0_), channel_id=1, source_target_pairs={{0,2},{2,0},{1,3},{3,1},{4,6},{6,4},{5,7},{7,5},{8,10},{10,8},{9,1... | collective-permute-start | bytes 196616 | tf_op jit(solution)/shard_map/ppermute | solution.py:19
  28.3 1.6 %collective-permute-start.13 = (bf16[16,16,128]{2,1,0:T(8,128)(2,1)S(1)}, bf16[16,16,128]{2,1,0:T(8,128)(2,1)S(1)}, u32[]{:S(2)}, u32[]{:S(2)}) collective-permute-start(bf16[16,16,128]{2,1,0:T(8,128)(2,1)S(1)} %get-tuple-element.70), channel_id=1, source_target_pairs={{0,12},{4,8},{8,4},{12,0},{1,13},{5,9},{9,5},{13,1},{2,14},{6,10},... | collective-permute-start | bytes 196616 | tf_op jit(solution)/shard_map/ppermute | solution.py:19
  29.9 0.8 %collective-permute-start.11 = (bf16[16,16,128]{2,1,0:T(8,128)(2,1)S(1)}, bf16[16,16,128]{2,1,0:T(8,128)(2,1)S(1)}, u32[]{:S(2)}, u32[]{:S(2)}) collective-permute-start(bf16[16,16,128]{2,1,0:T(8,128)(2,1)S(1)} %get-tuple-element.68), channel_id=1, source_target_pairs={{0,8},{4,12},{8,0},{12,4},{1,9},{5,13},{9,1},{13,5},{2,10},{6,14},... | collective-permute-start | bytes 196616 | tf_op jit(solution)/shard_map/ppermute | solution.py:19
  30.8 1.1 %collective-permute-start.9 = (bf16[16,16,128]{2,1,0:T(8,128)(2,1)S(1)}, bf16[16,16,128]{2,1,0:T(8,128)(2,1)S(1)}, u32[]{:S(2)}, u32[]{:S(2)}) collective-permute-start(bf16[16,16,128]{2,1,0:T(8,128)(2,1)S(1)} %get-tuple-element.66), channel_id=1, source_target_pairs={{0,4},{4,0},{8,12},{12,8},{1,5},{5,1},{9,13},{13,9},{2,6},{6,2},{1... | collective-permute-start | bytes 196616 | tf_op jit(solution)/shard_map/ppermute | solution.py:19
  31.8 4.1 %shapes.3.shapes_ref = bf16[64,256,128]{2,1,0:T(8,128)(2,1)S(1)} custom-call(s32[3]{0:T(128)S(1)} %pad_add_fusion.place_ref, s32[128,128]{1,0:T(8,128)S(1)} %get-tuple-element.63.code_ref.refs_2_.refs_0_, bf16[256,512]{1,0:T(8,128)(2,1)S(1)} %get-tuple-element.64.templates_ref.refs_3_.refs_1_), custom_call_target="tpu_custom_call" | custom-call | flops 2150000128 | bytes 5242880 | tf_op jit(solution)/shard_map/shapes/pallas_call | solution.py:407
  36.0 1.9 %copy-done.2 = bf16[64,256,128]{2,1,0:T(8,128)(2,1)} copy-done((bf16[64,256,128]{2,1,0:T(8,128)(2,1)}, bf16[64,256,128]{2,1,0:T(8,128)(2,1)S(1)}, u32[]{:S(2)}) %copy-start.2) | copy-done | bytes 4194328
  37.9 0.0 collective-permute-done.13.refs_3_
  37.9 0.1 collective-permute-start.14
  38.1 1.4 %collective-permute-start.12 = (bf16[16,16,128]{2,1,0:T(8,128)(2,1)S(1)}, bf16[16,16,128]{2,1,0:T(8,128)(2,1)S(1)}, u32[]{:S(2)}, u32[]{:S(2)}) collective-permute-start(bf16[16,16,128]{2,1,0:T(8,128)(2,1)S(1)} %collective-permute-done.11.refs_2_), channel_id=1, source_target_pairs={{0,2},{2,0},{1,3},{3,1},{4,6},{6,4},{5,7},{7,5},{8,10},{10,8},{9,1... | collective-permute-start | bytes 196616 | tf_op jit(solution)/shard_map/ppermute | solution.py:19
  39.5 0.1 collective-permute-start.10
  39.5 2.2 %copy-done.1 = bf16[64,256,128]{2,1,0:T(8,128)(2,1)S(1)} copy-done((bf16[64,256,128]{2,1,0:T(8,128)(2,1)S(1)}, bf16[64,256,128]{2,1,0:T(8,128)(2,1)}, u32[]{:S(2)}) %copy-start.1) | copy-done | bytes 4194328
  41.7 1.8 %residual.3 = (bf16[1024,256]{1,0:T(8,128)(2,1)S(1)}, bf16[256,256]{1,0:T(8,128)(2,1)S(1)}, bf16[64,16,128]{2,1,0:T(8,128)(2,1)S(1)}) custom-call(s32[3]{0:T(128)S(1)} %pad_add_fusion.place_ref, bf16[64,256,128]{2,1,0:T(8,128)(2,1)S(1)} %copy-done.1, bf16[1024,256]{1,0:T(8,128)(2,1)S(1)} %get-tuple-element.74.filtered_ref, ...), custom_call_target="tpu_custom_call" | custom-call | flops 70000000 | bytes 6291456 | tf_op jit(solution)/shard_map/residual/pallas_call | solution.py:441
  43.5 0.0 collective-permute-done.14.refs_3_
  43.5 0.0 collective-permute-done.12.refs_2_
  43.6 0.4 copy-done.3
  43.9 1.8 %residual.2 = (bf16[1024,256]{1,0:T(8,128)(2,1)S(1)}, bf16[256,256]{1,0:T(8,128)(2,1)S(1)}, bf16[64,16,128]{2,1,0:T(8,128)(2,1)S(1)}) custom-call(s32[3]{0:T(128)S(1)} %pad_add_fusion.place_ref, bf16[64,256,128]{2,1,0:T(8,128)(2,1)S(1)} %copy-done.3, bf16[1024,256]{1,0:T(8,128)(2,1)S(1)} %get-tuple-element.65.filtered_ref, ...), custom_call_target="tpu_custom_call" | custom-call | flops 70000000 | bytes 6291456 | tf_op jit(solution)/shard_map/residual/pallas_call | solution.py:441
  45.7 3.8 %collective-permute-start.15 = (bf16[256,256]{1,0:T(8,128)(2,1)S(1)}, bf16[256,256]{1,0:T(8,128)(2,1)S(1)}, u32[]{:S(2)}, u32[]{:S(2)}) collective-permute-start(bf16[256,256]{1,0:T(8,128)(2,1)S(1)} %broadcast_select_fusion.2), channel_id=1, source_target_pairs={{0,1},{1,0},{2,3},{3,2},{4,5},{5,4},{6,7},{7,6},{8,9},{9,8},{10,11... | collective-permute-start | bytes 393224 | tf_op jit(solution)/shard_map/ppermute | solution.py:19
  49.6 0.2 fusion
  49.8 1.3 %copy.14 = bf16[64,16,128]{2,1,0:T(8,128)(2,1)} copy(bf16[64,16,128]{0,1,2:T(8,128)(2,1)S(1)} %fusion) | data formatting | bytes 524288
  51.1 4.1 %backward.1 = bf16[2,16,128,128]{3,2,1,0:T(8,128)(2,1)} custom-call(s32[3]{0:T(128)S(1)} %pad_add_fusion.place_ref, bf16[256,256]{1,0:T(8,128)(2,1)S(1)} %collective-permute-done.15.edge_ref, bf16[256,256]{1,0:T(8,128)(2,1)S(1)} %get-tuple-element.78.col_adj_ref, bf16[256,768]{1,0:T(8,128)(2,1)S(1)} %get-tuple-element.79.row_adj_ref, ...), custom_call_target="tpu_custom_call" | custom-call | flops 1000000000 | bytes 3145728 | tf_op jit(solution)/shard_map/backward/pallas_call | solution.py:466
  (24 shorter events, 0.2 us)
Async XLA Ops:
  1.6 3.5 %collective-permute-start = (bf16[2,16,16,128]{3,2,1,0:T(8,128)(2,1)S(1)}, bf16[2,16,16,128]{3,2,1,0:T(8,128)(2,1)S(1)}, u32[]{:S(2)}, u32[]{:S(2)}) collective-permute-start(bf16[2,16,16,128]{3,2,1,0:T(8,128)(2,1)S(1)} %constant_dynamic-slice_fusion), channel_id=1, source_target_pairs={{0,1},{1,0},{2,3},{3,2},{4,5},{5,4},{6,7},{7,6},{8,9},{9,8},{10,11... | collective-permute-start | bytes 393224 | tf_op jit(solution)/shard_map/ppermute | solution.py:19
  5.1 5.3 %copy-start.7 = (s32[1,3]{1,0:T(1,128)S(1)}, s32[1,3]{1,0:T(1,128)}, u32[]{:S(2)}) copy-start(s32[1,3]{1,0:T(1,128)} %param.17) | copy-start | bytes 40
  7.7 18.2 %collective-permute-start.4 = (bf16[256,128]{1,0:T(8,128)(2,1)S(1)}, bf16[256,128]{1,0:T(8,128)(2,1)S(1)}, u32[]{:S(2)}, u32[]{:S(2)}) collective-permute-start(bf16[256,128]{1,0:T(8,128)(2,1)S(1)} %get-tuple-element.47), channel_id=1, source_target_pairs={{0,2},{2,0},{1,3},{3,1},{4,6},{6,4},{5,7},{7,5},{8,10},{10,8},{9,1... | collective-permute-start | bytes 196616 | tf_op jit(solution)/shard_map/ppermute | solution.py:19
  10.6 4.0 %collective-permute-start.3 = (bf16[256,128]{1,0:T(8,128)(2,1)S(1)}, bf16[256,128]{1,0:T(8,128)(2,1)S(1)}, u32[]{:S(2)}, u32[]{:S(2)}) collective-permute-start(bf16[256,128]{1,0:T(8,128)(2,1)S(1)} %get-tuple-element.57), channel_id=1, source_target_pairs={{0,2},{2,0},{1,3},{3,1},{4,6},{6,4},{5,7},{7,5},{8,10},{10,8},{9,1... | collective-permute-start | bytes 196616 | tf_op jit(solution)/shard_map/ppermute | solution.py:19
  10.7 5.5 %collective-permute-start.2 = (bf16[256,128]{1,0:T(8,128)(2,1)S(1)}, bf16[256,128]{1,0:T(8,128)(2,1)S(1)}, u32[]{:S(2)}, u32[]{:S(2)}) collective-permute-start(bf16[256,128]{1,0:T(8,128)(2,1)S(1)} %get-tuple-element.55), channel_id=1, source_target_pairs={{0,2},{2,0},{1,3},{3,1},{4,6},{6,4},{5,7},{7,5},{8,10},{10,8},{9,1... | collective-permute-start | bytes 196616 | tf_op jit(solution)/shard_map/ppermute | solution.py:19
  12.1 6.7 %collective-permute-start.1 = (bf16[256,128]{1,0:T(8,128)(2,1)S(1)}, bf16[256,128]{1,0:T(8,128)(2,1)S(1)}, u32[]{:S(2)}, u32[]{:S(2)}) collective-permute-start(bf16[256,128]{1,0:T(8,128)(2,1)S(1)} %get-tuple-element.53), channel_id=1, source_target_pairs={{0,2},{2,0},{1,3},{3,1},{4,6},{6,4},{5,7},{7,5},{8,10},{10,8},{9,1... | collective-permute-start | bytes 196616 | tf_op jit(solution)/shard_map/ppermute | solution.py:19
  12.2 7.0 %copy-start.4 = (f32[25]{0:T(128)S(1)}, f32[25]{0:T(128)}, u32[]{:S(2)}) copy-start(f32[25]{0:T(128)} %refs_0_.1) | copy-start | bytes 304
  12.2 7.0 %copy-start.5 = (f32[25]{0:T(128)S(1)}, f32[25]{0:T(128)}, u32[]{:S(2)}) copy-start(f32[25]{0:T(128)} %refs_1_.1) | copy-start | bytes 304
  14.6 11.3 %collective-permute-start.5 = (bf16[272,128]{1,0:T(8,128)(2,1)S(1)}, bf16[272,128]{1,0:T(8,128)(2,1)S(1)}, u32[]{:S(2)}, u32[]{:S(2)}) collective-permute-start(bf16[272,128]{1,0:T(8,128)(2,1)S(1)} %sum.5), channel_id=1, source_target_pairs={{0,4},{4,0},{8,12},{12,8},{1,5},{5,1},{9,13},{13,9},{2,6},{6,2},{1... | collective-permute-start | bytes 208904 | tf_op jit(solution)/shard_map/ppermute | solution.py:19
  16.2 9.7 %collective-permute-start.7 = (bf16[272,128]{1,0:T(8,128)(2,1)S(1)}, bf16[272,128]{1,0:T(8,128)(2,1)S(1)}, u32[]{:S(2)}, u32[]{:S(2)}) collective-permute-start(bf16[272,128]{1,0:T(8,128)(2,1)S(1)} %sum.4), channel_id=1, source_target_pairs={{0,12},{4,8},{8,4},{12,0},{1,13},{5,9},{9,5},{13,1},{2,14},{6,10},... | collective-permute-start | bytes 208904 | tf_op jit(solution)/shard_map/ppermute | solution.py:19
  18.9 7.0 %copy-start.6 = (s32[128,1]{0,1:T(1,128)S(1)}, s32[128,1]{0,1:T(1,128)}, u32[]{:S(2)}) copy-start(s32[128,1]{0,1:T(1,128)} %param.11) | copy-start | bytes 1540
  18.9 7.0 %collective-permute-start.6 = (bf16[272,128]{1,0:T(8,128)(2,1)S(1)}, bf16[272,128]{1,0:T(8,128)(2,1)S(1)}, u32[]{:S(2)}, u32[]{:S(2)}) collective-permute-start(bf16[272,128]{1,0:T(8,128)(2,1)S(1)} %sum.3), channel_id=1, source_target_pairs={{0,8},{4,12},{8,0},{12,4},{1,9},{5,13},{9,1},{13,5},{2,10},{6,14},... | collective-permute-start | bytes 208904 | tf_op jit(solution)/shard_map/ppermute | solution.py:19
  23.8 2.0 %copy-start = (bf16[64,256,128]{2,1,0:T(8,128)(2,1)}, bf16[64,256,128]{2,1,0:T(8,128)(2,1)S(1)}, u32[]{:S(2)}) copy-start(bf16[64,256,128]{2,1,0:T(8,128)(2,1)S(1)} %get-tuple-element.73.shapes_ref) | copy-start | bytes 12582916
  26.8 16.7 %collective-permute-start.8 = (bf16[16,16,128]{2,1,0:T(8,128)(2,1)S(1)}, bf16[16,16,128]{2,1,0:T(8,128)(2,1)S(1)}, u32[]{:S(2)}, u32[]{:S(2)}) collective-permute-start(bf16[16,16,128]{2,1,0:T(8,128)(2,1)S(1)} %get-tuple-element.62.refs_0_), channel_id=1, source_target_pairs={{0,2},{2,0},{1,3},{3,1},{4,6},{6,4},{5,7},{7,5},{8,10},{10,8},{9,1... | collective-permute-start | bytes 196616 | tf_op jit(solution)/shard_map/ppermute | solution.py:19
  28.3 9.6 %collective-permute-start.13 = (bf16[16,16,128]{2,1,0:T(8,128)(2,1)S(1)}, bf16[16,16,128]{2,1,0:T(8,128)(2,1)S(1)}, u32[]{:S(2)}, u32[]{:S(2)}) collective-permute-start(bf16[16,16,128]{2,1,0:T(8,128)(2,1)S(1)} %get-tuple-element.70), channel_id=1, source_target_pairs={{0,12},{4,8},{8,4},{12,0},{1,13},{5,9},{9,5},{13,1},{2,14},{6,10},... | collective-permute-start | bytes 196616 | tf_op jit(solution)/shard_map/ppermute | solution.py:19
  29.9 8.0 %collective-permute-start.11 = (bf16[16,16,128]{2,1,0:T(8,128)(2,1)S(1)}, bf16[16,16,128]{2,1,0:T(8,128)(2,1)S(1)}, u32[]{:S(2)}, u32[]{:S(2)}) collective-permute-start(bf16[16,16,128]{2,1,0:T(8,128)(2,1)S(1)} %get-tuple-element.68), channel_id=1, source_target_pairs={{0,8},{4,12},{8,0},{12,4},{1,9},{5,13},{9,1},{13,5},{2,10},{6,14},... | collective-permute-start | bytes 196616 | tf_op jit(solution)/shard_map/ppermute | solution.py:19
  30.8 7.2 %collective-permute-start.9 = (bf16[16,16,128]{2,1,0:T(8,128)(2,1)S(1)}, bf16[16,16,128]{2,1,0:T(8,128)(2,1)S(1)}, u32[]{:S(2)}, u32[]{:S(2)}) collective-permute-start(bf16[16,16,128]{2,1,0:T(8,128)(2,1)S(1)} %get-tuple-element.66), channel_id=1, source_target_pairs={{0,4},{4,0},{8,12},{12,8},{1,5},{5,1},{9,13},{13,9},{2,6},{6,2},{1... | collective-permute-start | bytes 196616 | tf_op jit(solution)/shard_map/ppermute | solution.py:19
  36.0 2.0 %copy-start.2 = (bf16[64,256,128]{2,1,0:T(8,128)(2,1)}, bf16[64,256,128]{2,1,0:T(8,128)(2,1)S(1)}, u32[]{:S(2)}) copy-start(bf16[64,256,128]{2,1,0:T(8,128)(2,1)S(1)} %shapes.3.shapes_ref) | copy-start | bytes 12582916
  37.9 5.6 %collective-permute-start.14 = (bf16[16,16,128]{2,1,0:T(8,128)(2,1)S(1)}, bf16[16,16,128]{2,1,0:T(8,128)(2,1)S(1)}, u32[]{:S(2)}, u32[]{:S(2)}) collective-permute-start(bf16[16,16,128]{2,1,0:T(8,128)(2,1)S(1)} %collective-permute-done.13.refs_3_), channel_id=1, source_target_pairs={{0,2},{2,0},{1,3},{3,1},{4,6},{6,4},{5,7},{7,5},{8,10},{10,8},{9,1... | collective-permute-start | bytes 196616 | tf_op jit(solution)/shard_map/ppermute | solution.py:19
  38.1 5.5 %collective-permute-start.12 = (bf16[16,16,128]{2,1,0:T(8,128)(2,1)S(1)}, bf16[16,16,128]{2,1,0:T(8,128)(2,1)S(1)}, u32[]{:S(2)}, u32[]{:S(2)}) collective-permute-start(bf16[16,16,128]{2,1,0:T(8,128)(2,1)S(1)} %collective-permute-done.11.refs_2_), channel_id=1, source_target_pairs={{0,2},{2,0},{1,3},{3,1},{4,6},{6,4},{5,7},{7,5},{8,10},{10,8},{9,1... | collective-permute-start | bytes 196616 | tf_op jit(solution)/shard_map/ppermute | solution.py:19
  39.5 4.1 %collective-permute-start.10 = (bf16[16,16,128]{2,1,0:T(8,128)(2,1)S(1)}, bf16[16,16,128]{2,1,0:T(8,128)(2,1)S(1)}, u32[]{:S(2)}, u32[]{:S(2)}) collective-permute-start(bf16[16,16,128]{2,1,0:T(8,128)(2,1)S(1)} %collective-permute-done.9.refs_1_), channel_id=1, source_target_pairs={{0,2},{2,0},{1,3},{3,1},{4,6},{6,4},{5,7},{7,5},{8,10},{10,8},{9,1... | collective-permute-start | bytes 196616 | tf_op jit(solution)/shard_map/ppermute | solution.py:19
  39.5 2.2 %copy-start.1 = (bf16[64,256,128]{2,1,0:T(8,128)(2,1)S(1)}, bf16[64,256,128]{2,1,0:T(8,128)(2,1)}, u32[]{:S(2)}) copy-start(bf16[64,256,128]{2,1,0:T(8,128)(2,1)} %copy-done) | copy-start | bytes 12582916
  41.7 2.2 %copy-start.3 = (bf16[64,256,128]{2,1,0:T(8,128)(2,1)S(1)}, bf16[64,256,128]{2,1,0:T(8,128)(2,1)}, u32[]{:S(2)}) copy-start(bf16[64,256,128]{2,1,0:T(8,128)(2,1)} %copy-done.2) | copy-start | bytes 12582916
  45.7 5.4 %collective-permute-start.15 = (bf16[256,256]{1,0:T(8,128)(2,1)S(1)}, bf16[256,256]{1,0:T(8,128)(2,1)S(1)}, u32[]{:S(2)}, u32[]{:S(2)}) collective-permute-start(bf16[256,256]{1,0:T(8,128)(2,1)S(1)} %broadcast_select_fusion.2), channel_id=1, source_target_pairs={{0,1},{1,0},{2,3},{3,2},{4,5},{5,4},{6,7},{7,6},{8,9},{9,8},{10,11... | collective-permute-start | bytes 393224 | tf_op jit(solution)/shard_map/ppermute | solution.py:19

commit v4 on v3

--- a/solution.py
+++ b/solution.py
@@ -72,7 +72,7 @@
 
 def prepare_kernel(
     rim, cuts, col_hbm, row_hbm, movie_hbm, mask_hbm, support_hbm, templates_hbm,
-    smooth_ref, col_fwd_ref, row_fwd_ref, code_ref, templates_ref,
+    smooth_ref, col_fwd_ref, row_fwd_ref, code_ref, templates_ref, flat_ref,
     movie_ref, mask_ref, support_ref, packed_ref, loose_ref, col_ref, row_ref, sems,
 ):
     planes, frames, rows, _ = movie_ref.shape
@@ -110,6 +110,7 @@
     unit = (iota((LANES, LANES), 0) == iota((LANES, LANES), 1)).astype(BF16)
     for p in range(planes):
         shapes = loose_ref[pl.ds(p, templates_ref.shape[1], stride=planes), :].astype(BF16)
+        flat_ref[:, p * LANES : (p + 1) * LANES] = shapes
         templates_ref[p * LANES : (p + 1) * LANES, :] = lax.dot_general(
             unit, shapes, (((1,), (1,)), ((), ())), preferred_element_type=F32
         ).astype(BF16)
@@ -212,7 +213,7 @@
     if rim:
         col_ref, row_ref, code_ref, templates_ref, shapes_ref, col_adj_ref, row_adj_ref = refs
         band = column_band(col_ref, rim, 1)
-        planes = templates_ref.shape[0] // LANES
+        planes = templates_ref.shape[1] // LANES
         col_adj_ref[...] = jnp.zeros_like(col_adj_ref)
         for p in range(planes):
             lanes = slice(p * LANES, (p + 1) * LANES)
@@ -220,20 +221,19 @@
         row_adj_ref[...] = row_band_adjoint(row_ref, rim, frames)
     else:
         code_ref, templates_ref, shapes_ref = refs
-    count, here = templates_ref.shape[1], shapes_ref.shape[0]
+    count, here = templates_ref.shape[0], shapes_ref.shape[0]
     first = pl.multiple_of((place_ref[PLANE] ^ flip) * here, here)
 
     @pl.loop(0, here // 8)
     def _(g):
         support = code_ref[pl.ds(pl.multiple_of(first + g * 8, 8), 8), :] >> 1
-        for i in range(0, 8, 2):
-            both = jnp.concatenate([support[i : i + 1, :], support[i + 1 : i + 2, :]], axis=1)
-            hits = iota((count, 2 * LANES), 0) == jnp.broadcast_to(both, (count, 2 * LANES))
-            pair = jnp.dot(
-                templates_ref[...], hits.astype(BF16), preferred_element_type=F32
+        columns = jnp.transpose(support)
+        lane = iota((LANES, count), 1)
+        for i in range(8):
+            named = jnp.broadcast_to(columns[:, i : i + 1], (LANES, count))
+            shapes_ref[g * 8 + i] = jnp.dot(
+                (lane == named).astype(BF16), templates_ref[...], preferred_element_type=F32
             ).astype(BF16)
-            shapes_ref[g * 8 + i] = pair[:, :LANES]
-            shapes_ref[g * 8 + i + 1] = pair[:, LANES:]
 
 
 def residual_kernel(
@@ -248,10 +248,7 @@
         block = place_ref[WIDE] ^ k
         for h in range(share):
             row = block * share + h
-            model = lax.dot_general(
-                traces[k][h], shapes_ref[row], (((1,), (1,)), ((), ())),
-                preferred_element_type=F32,
-            )
+            model = jnp.dot(traces[k][h], shapes_ref[row], preferred_element_type=F32)
             mask = (code_ref[pl.ds(base + row, 1), :] & 1).astype(F32)
             spot = pl.ds(pl.multiple_of(row * frames, frames), frames)
             out_ref[spot, :] = (
@@ -273,19 +270,24 @@
     for flip, part in enumerate(parts):
         spot = pl.multiple_of(edge + (place_ref[PLANE] ^ flip) * size, edge)
         padded_ref[pl.ds(spot, size), :] = part[...]
+    def along(b):
+        near = padded_ref[b * edge : (b + 3) * edge, :]
+        return jnp.dot(row_adj_ref[...], near, preferred_element_type=F32).astype(BF16)
+
     copies = []
+    back = along(0)
     for b in range(rows // BLOCK):
-        near = padded_ref[b * edge : (b + 3) * edge, :]
-        back = jnp.dot(row_adj_ref[...], near, preferred_element_type=F32).astype(BF16)
+        ahead = along(b + 1) if b + 1 < rows // BLOCK else None
         full = jnp.dot(back, col_adj_ref[...], preferred_element_type=F32).astype(BF16)
-        piece = (slice(None), slice(None), pl.ds(b * BLOCK, BLOCK))
         for p in range(planes):
             out_ref[p, :, b * BLOCK : (b + 1) * BLOCK, :] = full[
                 :, p * LANES : (p + 1) * LANES
             ].reshape(frames, BLOCK, LANES)
+        piece = (slice(None), slice(None), pl.ds(b * BLOCK, BLOCK))
         copy = pltpu.make_async_copy(out_ref.at[piece], out_hbm.at[piece], sems.at[b])
         copy.start()
         copies.append(copy)
+        back = ahead
     for copy in copies:
         copy.wait()
 
@@ -302,7 +304,7 @@
 def call(kernel, name, outs, smem, vmem, flops, moved, scratch=(), aliases=None):
     return pl.pallas_call(
         kernel,
-        out_shape=tuple(shaped(s) for s in outs),
+        out_shape=tuple(shaped(s) if isinstance(s, tuple) else s for s in outs),
         in_specs=[SMEM] * smem + [VMEM] * vmem,
         out_specs=(VMEM,) * len(outs),
         scratch_shapes=scratch,
@@ -340,14 +342,15 @@
     rim_rows = exchange(lax.dynamic_slice_in_dim(movie_frames, start, BLOCK, axis=2), "rep", 1)
     cuts = 2
     depth, names = 3 * BLOCK * frames, templates.shape[0]
-    smooth, col_fwd, row_fwd, code, tall_templates = pl.pallas_call(
+    smooth, col_fwd, row_fwd, code, tall_templates, flat_templates = pl.pallas_call(
         functools.partial(prepare_kernel, rim, cuts),
         out_shape=(
             shaped((frames, rows + 2 * BLOCK, width)), shaped((cols, cols)), shaped((edge, depth)),
             jax.ShapeDtypeStruct(support.shape, jnp.int32), shaped((width, names)),
+            shaped((names, width)),
         ),
         in_specs=[HBM] * 6,
-        out_specs=(VMEM,) * 5,
+        out_specs=(VMEM,) * 6,
         scratch_shapes=[
             pltpu.VMEM(movie_frames.shape, BF16),
             pltpu.VMEM(pixel_mask.shape, jnp.int32),
@@ -381,10 +384,17 @@
             1, 6, 800000000, 3 * mib, aliases={1: 0},
             scratch=[pltpu.VMEM((here * frames, LANES), BF16)],
         )(place, smooth, rim_rows, col_fwd, row_fwd, code, tall_templates)
-        projected[flip] = {k: exchange(mine[k], "planes", flip) if flip else mine[k] for k in order}
+        if flip:
+            halves = [order[: wide // 2], order[wide // 2 :]]
+            mine = dict(enumerate(mine))
+            for ks in halves:
+                both = exchange(jnp.concatenate([mine[k] for k in ks]), "planes", flip)
+                for i, k in enumerate(ks):
+                    mine[k] = both[i * share * frames : (i + 1) * share * frames]
+        projected[flip] = mine
         if turn == 0:
-            gains, lags, _ = lax.optimization_barrier((lag_gains[0], dilations[0], mine[0]))
-            kernel_row = lag_kernel_values(gains, lags, total_frames)
+            gains, lags, _ = lax.optimization_barrier((lag_gains, dilations, smooth))
+            kernel_row = lag_kernel_values(gains[0], lags[0], total_frames)
             lag_rows = -(-2 * total_frames // (LANES * BLOCK)) * BLOCK
             kernel_row = jnp.pad(kernel_row, (0, lag_rows * LANES - 2 * total_frames))
             kernel_row = kernel_row.reshape(lag_rows, LANES)
@@ -398,8 +408,8 @@
         blocks[k] = exchange(sums[k], "wide", k)
 
     def make_shapes(flip, after, bands):
-        late_code, late_templates, _ = lax.optimization_barrier((code, tall_templates, after))
-        outs = [(here, width, LANES)]
+        late_code, late_templates, _ = lax.optimization_barrier((code, flat_templates, after))
+        outs = [pltpu.VMEM((here, LANES, width), BF16)]
         taps = ()
         if bands:
             outs += [(width, width), (edge, depth)]

time: 55.4 us -> 56 us (1.011)
  waiting for transfers between devices: 0.04 us -> 2.48 us
  starting transfers between devices: 19.5 us -> 17.6 us
    ppermute x16 -> x14, waiting for transfers between devices: 0.04 us -> 2.48 us  [exchange(): return lax.ppermute(cells, axis, [(i, i ^ flip) for i in range(count)])]
    pallas_call x2, Pallas kernels: 8.69 us -> 11 us  [make_shapes(): call(functools.partial(shapes_kernel, flip, rim if bands else 0, frames),...]
    ppermute x16 -> x14, starting transfers between devices: 19.5 us -> 17.6 us  [exchange(): return lax.ppermute(cells, axis, [(i, i ^ flip) for i in range(count)])]
    pallas_call x1, Pallas kernels: 4.1 us -> 2.92 us  [on_device(): pl.pallas_call(functools.partial(backward_kernel, plane_count), out_shape...]
    pallas_call x2, Pallas kernels: 3.55 us -> 2.47 us  [on_device(): call(functools.partial(residual_kernel, flip), 'residual', [(here * frame...]
    unnamed x18 -> x20, local copies, waits for them, and re-layouts: 8.5 us -> 8.36 us
  transfers between devices with their start and end apart: 16 -> 14, of which waited for: 0 -> 2; matrix products, arithmetic and copies ran while one was open for 5% -> 3% of each run, Pallas kernels for 28% -> 31%
where the time goes in v4:
time: 56 us; the launch traced here: 55.8 us
  Pallas kernels  24.9 us (44%)
  starting transfers between devices  17.6 us (31%)
  local copies, waits for them, and re-layouts  9.31 us (17%)
  waiting for transfers between devices  2.48 us (4%)
  between operations  0.9 us (2%)
  other arithmetic  0.58 us (1%)
    ppermute x14, starting transfers between devices, exchange(): return lax.ppermute(cells, axis, [(i, i ^ flip) for i in range(count)])  17.6 us
    pallas_call x2, Pallas kernels, make_shapes(): call(functools.partial(shapes_kernel, flip, rim if bands else 0, frames),...  11 us
    unnamed x20, local copies, waits for them, and re-layouts  8.36 us
    pallas_call x2, Pallas kernels, on_device(): call(functools.partial(forward_kernel, flip, turn == 0), 'forward', [smoo...  4.92 us
    pallas_call x1, Pallas kernels, on_device(): pl.pallas_call(functools.partial(backward_kernel, plane_count), out_shape...  2.92 us
    pallas_call x1, Pallas kernels, on_device(): pl.pallas_call(functools.partial(prepare_kernel, rim, cuts), out_shape=(s...  2.67 us
    ppermute x14, waiting for transfers between devices, exchange(): return lax.ppermute(cells, axis, [(i, i ^ flip) for i in range(count)])  2.48 us
    pallas_call x2, Pallas kernels, on_device(): call(functools.partial(residual_kernel, flip), 'residual', [(here * frame...  2.47 us
  transfers between devices with their start and end apart: 14, of which 2 were waited for; matrix products, arithmetic and copies ran while one was open for 3% of the time, Pallas kernels for 31%

profile of v4, /device:TPU:1, one launch (start us, length us, event | category | flops | bytes accessed | tf_op | source)
XLA Modules:
  0.0 55.8 jit_solution(6983900176733565662)
XLA Ops:
  0.6 0.9 %constant_dynamic-slice_fusion = bf16[2,16,16,128]{3,2,1,0:T(8,128)(2,1)S(1)} fusion(bf16[2,16,128,128]{3,2,1,0:T(8,128)(2,1)} %movie_hbm.1, s32[]{:T(128)S(6)} %select_n.38), kind=kLoop, calls=%fused_computation.11 | loop fusion | bytes 262148 | tf_op jit(solution)/shard_map/dynamic_slice | solution.py:342
  1.6 0.1 collective-permute-start
  1.7 2.7 %prepare.1 = (bf16[16,160,256]{2,1,0:T(8,128)(2,1)S(1)}, bf16[128,128]{1,0:T(8,128)(2,1)S(1)}, bf16[256,768]{1,0:T(8,128)(2,1)S(1)}, s32[128,128]{1,0:T(8,128)S(...) custom-call(f32[25]{0:T(128)} %refs_0_.1, f32[25]{0:T(128)} %refs_1_.1, ...), custom_call_target="tpu_custom_call" | custom-call | flops 200000000 | bytes 3145728 | tf_op jit(solution)/shard_map/prepare/pallas_call | solution.py:345
  4.4 0.1 pad_add_fusion.place_ref
  4.5 0.0 collective-permute-done.edge_ref
  4.5 2.5 %forward.2 = (bf16[16,160,256]{2,1,0:T(8,128)(2,1)S(1)}, bf16[1024,256]{1,0:T(8,128)(2,1)S(1)}, bf16[256,128]{1,0:T(8,128)(2,1)S(1)}, bf16[256,128]{1,0:T(8,128)...) custom-call(s32[3]{0:T(128)S(1)} %pad_add_fusion.place_ref, ...), custom_call_target="tpu_custom_call", output_to_operand_aliasing={{0}: (1, {})} | custom-call | flops 800000000 | bytes 3145728 | tf_op jit(solution)/shard_map/forward/pallas_call | solution.py:381
  7.1 2.7 %collective-permute-start.2 = (bf16[512,128]{1,0:T(8,128)(2,1)S(1)}, bf16[512,128]{1,0:T(8,128)(2,1)S(1)}, u32[]{:S(2)}, u32[]{:S(2)}) collective-permute-start(bf16[512,128]{1,0:T(8,128)(2,1)S(1)} %pad_maximum_fusion.1), channel_id=1, source_target_pairs={{0,2},{2,0},{1,3},{3,1},{4,6},{6,4},{5,7},{7,5},{8,10},{10,8},{9,1... | collective-permute-start | bytes 393224 | tf_op jit(solution)/shard_map/ppermute | solution.py:19
  9.8 0.1 collective-permute-start.1
  9.9 0.1 broadcast_multiply_fusion
  10.0 0.1 select_reduce_fusion
  10.1 0.0 copy-start.5
  10.1 2.4 %forward.3 = (bf16[16,160,256]{2,1,0:T(8,128)(2,1)S(1)}, bf16[1024,256]{1,0:T(8,128)(2,1)S(1)}, bf16[256,128]{1,0:T(8,128)(2,1)S(1)}, bf16[256,128]{1,0:T(8,128)...) custom-call(s32[3]{0:T(128)S(1)} %pad_add_fusion.place_ref, ...), custom_call_target="tpu_custom_call", output_to_operand_aliasing={{0}: (1, {})} | custom-call | flops 800000000 | bytes 3145728 | tf_op jit(solution)/shard_map/forward/pallas_call | solution.py:381
  12.5 1.1 %collective-permute-done.2 = bf16[512,128]{1,0:T(8,128)(2,1)S(1)} collective-permute-done((bf16[512,128]{1,0:T(8,128)(2,1)S(1)}, bf16[512,128]{1,0:T(8,128)(2,1)S(1)}, u32[]{:S(2)}, u32[]{:S(2)}) %collective-permute-start.2) | collective-permute-done | bytes 131104 | tf_op jit(solution)/shard_map/ppermute | solution.py:19
  13.6 1.4 %collective-permute-start.3 = (bf16[272,128]{1,0:T(8,128)(2,1)S(1)}, bf16[272,128]{1,0:T(8,128)(2,1)S(1)}, u32[]{:S(2)}, u32[]{:S(2)}) collective-permute-start(bf16[272,128]{1,0:T(8,128)(2,1)S(1)} %sum.5), channel_id=1, source_target_pairs={{0,4},{4,0},{8,12},{12,8},{1,5},{5,1},{9,13},{13,9},{2,6},{6,2},{1... | collective-permute-start | bytes 208904 | tf_op jit(solution)/shard_map/ppermute | solution.py:19
  15.1 1.4 %collective-permute-done.1 = bf16[512,128]{1,0:T(8,128)(2,1)S(1)} collective-permute-done((bf16[512,128]{1,0:T(8,128)(2,1)S(1)}, bf16[512,128]{1,0:T(8,128)(2,1)S(1)}, u32[]{:S(2)}, u32[]{:S(2)}) %collective-permute-start.1) | collective-permute-done | bytes 131104 | tf_op jit(solution)/shard_map/ppermute | solution.py:19
  16.5 3.4 %collective-permute-start.5 = (bf16[272,128]{1,0:T(8,128)(2,1)S(1)}, bf16[272,128]{1,0:T(8,128)(2,1)S(1)}, u32[]{:S(2)}, u32[]{:S(2)}) collective-permute-start(bf16[272,128]{1,0:T(8,128)(2,1)S(1)} %sum.4), channel_id=1, source_target_pairs={{0,12},{4,8},{8,4},{12,0},{1,13},{5,9},{9,5},{13,1},{2,14},{6,10},... | collective-permute-start | bytes 208904 | tf_op jit(solution)/shard_map/ppermute | solution.py:19
  19.9 0.1 collective-permute-start.4
  20.0 0.0 copy-start.6
  20.0 5.7 %shapes.2 = (bf16[64,128,256]{2,1,0:T(8,128)(2,1)S(1)}, bf16[256,256]{1,0:T(8,128)(2,1)S(1)}, bf16[256,768]{1,0:T(8,128)(2,1)S(1)}) custom-call(s32[3]{0:T(128)S(1)} %pad_add_fusion.place_ref, f32[25]{0:T(128)S(1)} %copy-done.4, f32[25]{0:T(128)S(1)} %copy-done.5, s32[128,128]{1,0:T(8,128)S(1)} %get-tuple-element.65.code_ref.refs_2_.refs_0_, ...), custom_call_target="tpu_custom_call" | custom-call | flops 2150000128 | bytes 5242880 | tf_op jit(solution)/shard_map/shapes/pallas_call | solution.py:417
  25.8 2.0 %copy-done = bf16[64,128,256]{2,1,0:T(8,128)(2,1)} copy-done((bf16[64,128,256]{2,1,0:T(8,128)(2,1)}, bf16[64,128,256]{2,1,0:T(8,128)(2,1)S(1)}, u32[]{:S(2)}) %copy-start) | copy-done | bytes 4194328
  27.8 0.0 collective-permute-done.3.refs_2_
  27.8 0.0 collective-permute-done.5.refs_4_
  27.8 0.0 collective-permute-done.4.refs_3_
  27.8 0.9 %mix.1 = (bf16[16,16,128]{2,1,0:T(8,128)(2,1)S(1)}, bf16[16,16,128]{2,1,0:T(8,128)(2,1)S(1)}, bf16[16,16,128]{2,1,0:T(8,128)(2,1)S(1)}, bf16[16,16,128]{2,1,0:T(8,128)(2,1)S(1)}) custom-call(s32[3]{0:T(128)S(1)} %pad_add_fusion.place_ref, s32[128]{0:T(128)S(1)} %bitcast.13, bf16[16,128]{1,0:T(8,128)(2,1)S(1)} %pad_bitcast_fusion.lag_ref, ...), custom_call_target="tpu_custom_call" | custom-call | flops 20000000 | bytes 1048576 | tf_op jit(solution)/shard_map/mix/pallas_call | solution.py:428
  28.7 1.3 %collective-permute-start.6 = (bf16[16,16,128]{2,1,0:T(8,128)(2,1)S(1)}, bf16[16,16,128]{2,1,0:T(8,128)(2,1)S(1)}, u32[]{:S(2)}, u32[]{:S(2)}) collective-permute-start(bf16[16,16,128]{2,1,0:T(8,128)(2,1)S(1)} %get-tuple-element.64.refs_0_), channel_id=1, source_target_pairs={{0,2},{2,0},{1,3},{3,1},{4,6},{6,4},{5,7},{7,5},{8,10},{10,8},{9,1... | collective-permute-start | bytes 196616 | tf_op jit(solution)/shard_map/ppermute | solution.py:19
  30.0 1.3 %collective-permute-start.11 = (bf16[16,16,128]{2,1,0:T(8,128)(2,1)S(1)}, bf16[16,16,128]{2,1,0:T(8,128)(2,1)S(1)}, u32[]{:S(2)}, u32[]{:S(2)}) collective-permute-start(bf16[16,16,128]{2,1,0:T(8,128)(2,1)S(1)} %get-tuple-element.72), channel_id=1, source_target_pairs={{0,12},{4,8},{8,4},{12,0},{1,13},{5,9},{9,5},{13,1},{2,14},{6,10},... | collective-permute-start | bytes 196616 | tf_op jit(solution)/shard_map/ppermute | solution.py:19
  31.3 1.0 %collective-permute-start.9 = (bf16[16,16,128]{2,1,0:T(8,128)(2,1)S(1)}, bf16[16,16,128]{2,1,0:T(8,128)(2,1)S(1)}, u32[]{:S(2)}, u32[]{:S(2)}) collective-permute-start(bf16[16,16,128]{2,1,0:T(8,128)(2,1)S(1)} %get-tuple-element.70), channel_id=1, source_target_pairs={{0,8},{4,12},{8,0},{12,4},{1,9},{5,13},{9,1},{13,5},{2,10},{6,14},... | collective-permute-start | bytes 196616 | tf_op jit(solution)/shard_map/ppermute | solution.py:19
  32.3 1.2 %collective-permute-start.7 = (bf16[16,16,128]{2,1,0:T(8,128)(2,1)S(1)}, bf16[16,16,128]{2,1,0:T(8,128)(2,1)S(1)}, u32[]{:S(2)}, u32[]{:S(2)}) collective-permute-start(bf16[16,16,128]{2,1,0:T(8,128)(2,1)S(1)} %get-tuple-element.68), channel_id=1, source_target_pairs={{0,4},{4,0},{8,12},{12,8},{1,5},{5,1},{9,13},{13,9},{2,6},{6,2},{1... | collective-permute-start | bytes 196616 | tf_op jit(solution)/shard_map/ppermute | solution.py:19
  33.5 5.3 %shapes.3.shapes_ref = bf16[64,128,256]{2,1,0:T(8,128)(2,1)S(1)} custom-call(s32[3]{0:T(128)S(1)} %pad_add_fusion.place_ref, s32[128,128]{1,0:T(8,128)S(1)} %get-tuple-element.65.code_ref.refs_2_.refs_0_, bf16[512,256]{1,0:T(8,128)(2,1)S(1)} %get-tuple-element.66.refs_3_.refs_1_), custom_call_target="tpu_custom_call" | custom-call | flops 2150000128 | bytes 5242880 | tf_op jit(solution)/shard_map/shapes/pallas_call | solution.py:417
  38.8 1.9 %copy-done.2 = bf16[64,128,256]{2,1,0:T(8,128)(2,1)} copy-done((bf16[64,128,256]{2,1,0:T(8,128)(2,1)}, bf16[64,128,256]{2,1,0:T(8,128)(2,1)S(1)}, u32[]{:S(2)}) %copy-start.2) | copy-done | bytes 4194328
  40.7 0.0 collective-permute-done.11.refs_3_
  40.8 0.0 collective-permute-done.9.refs_2_
  40.8 0.0 collective-permute-done.7.refs_1_
  40.8 0.3 collective-permute-start.12
  41.1 1.2 %collective-permute-start.10 = (bf16[16,16,128]{2,1,0:T(8,128)(2,1)S(1)}, bf16[16,16,128]{2,1,0:T(8,128)(2,1)S(1)}, u32[]{:S(2)}, u32[]{:S(2)}) collective-permute-start(bf16[16,16,128]{2,1,0:T(8,128)(2,1)S(1)} %collective-permute-done.9.refs_2_), channel_id=1, source_target_pairs={{0,2},{2,0},{1,3},{3,1},{4,6},{6,4},{5,7},{7,5},{8,10},{10,8},{9,1... | collective-permute-start | bytes 196616 | tf_op jit(solution)/shard_map/ppermute | solution.py:19
  42.3 0.2 collective-permute-start.8
  42.5 2.2 %copy-done.1 = bf16[64,128,256]{2,1,0:T(8,128)(2,1)S(1)} copy-done((bf16[64,128,256]{2,1,0:T(8,128)(2,1)S(1)}, bf16[64,128,256]{2,1,0:T(8,128)(2,1)}, u32[]{:S(2)}) %copy-start.1) | copy-done | bytes 4194328
  44.7 1.2 %residual.3 = (bf16[1024,256]{1,0:T(8,128)(2,1)S(1)}, bf16[256,256]{1,0:T(8,128)(2,1)S(1)}, bf16[64,16,128]{2,1,0:T(8,128)(2,1)S(1)}) custom-call(s32[3]{0:T(128)S(1)} %pad_add_fusion.place_ref, bf16[64,128,256]{2,1,0:T(8,128)(2,1)S(1)} %copy-done.1, bf16[1024,256]{1,0:T(8,128)(2,1)S(1)} %get-tuple-element.76.filtered_ref, ...), custom_call_target="tpu_custom_call" | custom-call | flops 70000000 | bytes 6291456 | tf_op jit(solution)/shard_map/residual/pallas_call | solution.py:451
  46.0 0.0 collective-permute-done.6.refs_0_
  46.0 0.0 collective-permute-done.10.refs_2_
  46.0 0.0 collective-permute-done.8.refs_1_
  46.0 0.9 %copy-done.3 = bf16[64,128,256]{2,1,0:T(8,128)(2,1)S(1)} copy-done((bf16[64,128,256]{2,1,0:T(8,128)(2,1)S(1)}, bf16[64,128,256]{2,1,0:T(8,128)(2,1)}, u32[]{:S(2)}) %copy-start.3) | copy-done | bytes 4194328
  46.9 1.2 %residual.2 = (bf16[1024,256]{1,0:T(8,128)(2,1)S(1)}, bf16[256,256]{1,0:T(8,128)(2,1)S(1)}, bf16[64,16,128]{2,1,0:T(8,128)(2,1)S(1)}) custom-call(s32[3]{0:T(128)S(1)} %pad_add_fusion.place_ref, bf16[64,128,256]{2,1,0:T(8,128)(2,1)S(1)} %copy-done.3, bf16[1024,256]{1,0:T(8,128)(2,1)S(1)} %get-tuple-element.67.filtered_ref, ...), custom_call_target="tpu_custom_call" | custom-call | flops 70000000 | bytes 6291456 | tf_op jit(solution)/shard_map/residual/pallas_call | solution.py:451
  48.2 3.1 %collective-permute-start.13 = (bf16[256,256]{1,0:T(8,128)(2,1)S(1)}, bf16[256,256]{1,0:T(8,128)(2,1)S(1)}, u32[]{:S(2)}, u32[]{:S(2)}) collective-permute-start(bf16[256,256]{1,0:T(8,128)(2,1)S(1)} %broadcast_select_fusion.2), channel_id=1, source_target_pairs={{0,1},{1,0},{2,3},{3,2},{4,5},{5,4},{6,7},{7,6},{8,9},{9,8},{10,11... | collective-permute-start | bytes 393224 | tf_op jit(solution)/shard_map/ppermute | solution.py:19
  51.4 0.2 fusion
  51.6 1.3 %copy.14 = bf16[64,16,128]{2,1,0:T(8,128)(2,1)} copy(bf16[64,16,128]{0,1,2:T(8,128)(2,1)S(1)} %fusion) | data formatting | bytes 524288
  52.9 0.0 collective-permute-done.13.edge_ref
  52.9 2.9 %backward.1 = bf16[2,16,128,128]{3,2,1,0:T(8,128)(2,1)} custom-call(s32[3]{0:T(128)S(1)} %pad_add_fusion.place_ref, bf16[256,256]{1,0:T(8,128)(2,1)S(1)} %collective-permute-done.13.edge_ref, bf16[256,256]{1,0:T(8,128)(2,1)S(1)} %get-tuple-element.80.col_adj_ref, bf16[256,768]{1,0:T(8,128)(2,1)S(1)} %get-tuple-element.81.row_adj_ref, ...), custom_call_target="tpu_custom_call" | custom-call | flops 1000000000 | bytes 3145728 | tf_op jit(solution)/shard_map/backward/pallas_call | solution.py:476
  (26 shorter events, 0.2 us)
Async XLA Ops:
  1.6 2.9 %collective-permute-start = (bf16[2,16,16,128]{3,2,1,0:T(8,128)(2,1)S(1)}, bf16[2,16,16,128]{3,2,1,0:T(8,128)(2,1)S(1)}, u32[]{:S(2)}, u32[]{:S(2)}) collective-permute-start(bf16[2,16,16,128]{3,2,1,0:T(8,128)(2,1)S(1)} %constant_dynamic-slice_fusion), channel_id=1, source_target_pairs={{0,1},{1,0},{2,3},{3,2},{4,5},{5,4},{6,7},{7,6},{8,9},{9,8},{10,11... | collective-permute-start | bytes 393224 | tf_op jit(solution)/shard_map/ppermute | solution.py:19
  4.5 2.6 %copy-start.7 = (f32[1,3,65]{2,0,1:T(1,128)S(1)}, f32[1,3,65]{2,0,1:T(1,128)}, u32[]{:S(2)}) copy-start(f32[1,3,65]{2,0,1:T(1,128)} %param.16) | copy-start | bytes 2344
  4.5 5.4 %copy-start.8 = (s32[1,3]{1,0:T(1,128)S(1)}, s32[1,3]{1,0:T(1,128)}, u32[]{:S(2)}) copy-start(s32[1,3]{1,0:T(1,128)} %param.17) | copy-start | bytes 40
  7.1 6.5 %collective-permute-start.2 = (bf16[512,128]{1,0:T(8,128)(2,1)S(1)}, bf16[512,128]{1,0:T(8,128)(2,1)S(1)}, u32[]{:S(2)}, u32[]{:S(2)}) collective-permute-start(bf16[512,128]{1,0:T(8,128)(2,1)S(1)} %pad_maximum_fusion.1), channel_id=1, source_target_pairs={{0,2},{2,0},{1,3},{3,1},{4,6},{6,4},{5,7},{7,5},{8,10},{10,8},{9,1... | collective-permute-start | bytes 393224 | tf_op jit(solution)/shard_map/ppermute | solution.py:19
  9.8 6.6 %collective-permute-start.1 = (bf16[512,128]{1,0:T(8,128)(2,1)S(1)}, bf16[512,128]{1,0:T(8,128)(2,1)S(1)}, u32[]{:S(2)}, u32[]{:S(2)}) collective-permute-start(bf16[512,128]{1,0:T(8,128)(2,1)S(1)} %pad_maximum_fusion), channel_id=1, source_target_pairs={{0,2},{2,0},{1,3},{3,1},{4,6},{6,4},{5,7},{7,5},{8,10},{10,8},{9,1... | collective-permute-start | bytes 393224 | tf_op jit(solution)/shard_map/ppermute | solution.py:19
  10.1 9.9 %copy-start.4 = (f32[25]{0:T(128)S(1)}, f32[25]{0:T(128)}, u32[]{:S(2)}) copy-start(f32[25]{0:T(128)} %refs_0_.1) | copy-start | bytes 304
  10.1 9.9 %copy-start.5 = (f32[25]{0:T(128)S(1)}, f32[25]{0:T(128)}, u32[]{:S(2)}) copy-start(f32[25]{0:T(128)} %refs_1_.1) | copy-start | bytes 304
  13.6 14.1 %collective-permute-start.3 = (bf16[272,128]{1,0:T(8,128)(2,1)S(1)}, bf16[272,128]{1,0:T(8,128)(2,1)S(1)}, u32[]{:S(2)}, u32[]{:S(2)}) collective-permute-start(bf16[272,128]{1,0:T(8,128)(2,1)S(1)} %sum.5), channel_id=1, source_target_pairs={{0,4},{4,0},{8,12},{12,8},{1,5},{5,1},{9,13},{13,9},{2,6},{6,2},{1... | collective-permute-start | bytes 208904 | tf_op jit(solution)/shard_map/ppermute | solution.py:19
  16.5 11.3 %collective-permute-start.5 = (bf16[272,128]{1,0:T(8,128)(2,1)S(1)}, bf16[272,128]{1,0:T(8,128)(2,1)S(1)}, u32[]{:S(2)}, u32[]{:S(2)}) collective-permute-start(bf16[272,128]{1,0:T(8,128)(2,1)S(1)} %sum.4), channel_id=1, source_target_pairs={{0,12},{4,8},{8,4},{12,0},{1,13},{5,9},{9,5},{13,1},{2,14},{6,10},... | collective-permute-start | bytes 208904 | tf_op jit(solution)/shard_map/ppermute | solution.py:19
  19.9 7.9 %collective-permute-start.4 = (bf16[272,128]{1,0:T(8,128)(2,1)S(1)}, bf16[272,128]{1,0:T(8,128)(2,1)S(1)}, u32[]{:S(2)}, u32[]{:S(2)}) collective-permute-start(bf16[272,128]{1,0:T(8,128)(2,1)S(1)} %sum.3), channel_id=1, source_target_pairs={{0,8},{4,12},{8,0},{12,4},{1,9},{5,13},{9,1},{13,5},{2,10},{6,14},... | collective-permute-start | bytes 208904 | tf_op jit(solution)/shard_map/ppermute | solution.py:19
  20.0 7.8 %copy-start.6 = (s32[128,1]{0,1:T(1,128)S(1)}, s32[128,1]{0,1:T(1,128)}, u32[]{:S(2)}) copy-start(s32[128,1]{0,1:T(1,128)} %param.11) | copy-start | bytes 1540
  25.8 2.0 %copy-start = (bf16[64,128,256]{2,1,0:T(8,128)(2,1)}, bf16[64,128,256]{2,1,0:T(8,128)(2,1)S(1)}, u32[]{:S(2)}) copy-start(bf16[64,128,256]{2,1,0:T(8,128)(2,1)S(1)} %get-tuple-element.75.shapes_ref) | copy-start | bytes 12582916
  28.7 17.3 %collective-permute-start.6 = (bf16[16,16,128]{2,1,0:T(8,128)(2,1)S(1)}, bf16[16,16,128]{2,1,0:T(8,128)(2,1)S(1)}, u32[]{:S(2)}, u32[]{:S(2)}) collective-permute-start(bf16[16,16,128]{2,1,0:T(8,128)(2,1)S(1)} %get-tuple-element.64.refs_0_), channel_id=1, source_target_pairs={{0,2},{2,0},{1,3},{3,1},{4,6},{6,4},{5,7},{7,5},{8,10},{10,8},{9,1... | collective-permute-start | bytes 196616 | tf_op jit(solution)/shard_map/ppermute | solution.py:19
  30.0 10.8 %collective-permute-start.11 = (bf16[16,16,128]{2,1,0:T(8,128)(2,1)S(1)}, bf16[16,16,128]{2,1,0:T(8,128)(2,1)S(1)}, u32[]{:S(2)}, u32[]{:S(2)}) collective-permute-start(bf16[16,16,128]{2,1,0:T(8,128)(2,1)S(1)} %get-tuple-element.72), channel_id=1, source_target_pairs={{0,12},{4,8},{8,4},{12,0},{1,13},{5,9},{9,5},{13,1},{2,14},{6,10},... | collective-permute-start | bytes 196616 | tf_op jit(solution)/shard_map/ppermute | solution.py:19
  31.3 9.5 %collective-permute-start.9 = (bf16[16,16,128]{2,1,0:T(8,128)(2,1)S(1)}, bf16[16,16,128]{2,1,0:T(8,128)(2,1)S(1)}, u32[]{:S(2)}, u32[]{:S(2)}) collective-permute-start(bf16[16,16,128]{2,1,0:T(8,128)(2,1)S(1)} %get-tuple-element.70), channel_id=1, source_target_pairs={{0,8},{4,12},{8,0},{12,4},{1,9},{5,13},{9,1},{13,5},{2,10},{6,14},... | collective-permute-start | bytes 196616 | tf_op jit(solution)/shard_map/ppermute | solution.py:19
  32.3 8.5 %collective-permute-start.7 = (bf16[16,16,128]{2,1,0:T(8,128)(2,1)S(1)}, bf16[16,16,128]{2,1,0:T(8,128)(2,1)S(1)}, u32[]{:S(2)}, u32[]{:S(2)}) collective-permute-start(bf16[16,16,128]{2,1,0:T(8,128)(2,1)S(1)} %get-tuple-element.68), channel_id=1, source_target_pairs={{0,4},{4,0},{8,12},{12,8},{1,5},{5,1},{9,13},{13,9},{2,6},{6,2},{1... | collective-permute-start | bytes 196616 | tf_op jit(solution)/shard_map/ppermute | solution.py:19
  38.8 2.0 %copy-start.2 = (bf16[64,128,256]{2,1,0:T(8,128)(2,1)}, bf16[64,128,256]{2,1,0:T(8,128)(2,1)S(1)}, u32[]{:S(2)}) copy-start(bf16[64,128,256]{2,1,0:T(8,128)(2,1)S(1)} %shapes.3.shapes_ref) | copy-start | bytes 12582916
  40.8 5.2 %collective-permute-start.12 = (bf16[16,16,128]{2,1,0:T(8,128)(2,1)S(1)}, bf16[16,16,128]{2,1,0:T(8,128)(2,1)S(1)}, u32[]{:S(2)}, u32[]{:S(2)}) collective-permute-start(bf16[16,16,128]{2,1,0:T(8,128)(2,1)S(1)} %collective-permute-done.11.refs_3_), channel_id=1, source_target_pairs={{0,2},{2,0},{1,3},{3,1},{4,6},{6,4},{5,7},{7,5},{8,10},{10,8},{9,1... | collective-permute-start | bytes 196616 | tf_op jit(solution)/shard_map/ppermute | solution.py:19
  41.1 4.9 %collective-permute-start.10 = (bf16[16,16,128]{2,1,0:T(8,128)(2,1)S(1)}, bf16[16,16,128]{2,1,0:T(8,128)(2,1)S(1)}, u32[]{:S(2)}, u32[]{:S(2)}) collective-permute-start(bf16[16,16,128]{2,1,0:T(8,128)(2,1)S(1)} %collective-permute-done.9.refs_2_), channel_id=1, source_target_pairs={{0,2},{2,0},{1,3},{3,1},{4,6},{6,4},{5,7},{7,5},{8,10},{10,8},{9,1... | collective-permute-start | bytes 196616 | tf_op jit(solution)/shard_map/ppermute | solution.py:19
  42.3 3.7 %collective-permute-start.8 = (bf16[16,16,128]{2,1,0:T(8,128)(2,1)S(1)}, bf16[16,16,128]{2,1,0:T(8,128)(2,1)S(1)}, u32[]{:S(2)}, u32[]{:S(2)}) collective-permute-start(bf16[16,16,128]{2,1,0:T(8,128)(2,1)S(1)} %collective-permute-done.7.refs_1_), channel_id=1, source_target_pairs={{0,2},{2,0},{1,3},{3,1},{4,6},{6,4},{5,7},{7,5},{8,10},{10,8},{9,1... | collective-permute-start | bytes 196616 | tf_op jit(solution)/shard_map/ppermute | solution.py:19
  42.5 2.2 %copy-start.1 = (bf16[64,128,256]{2,1,0:T(8,128)(2,1)S(1)}, bf16[64,128,256]{2,1,0:T(8,128)(2,1)}, u32[]{:S(2)}) copy-start(bf16[64,128,256]{2,1,0:T(8,128)(2,1)} %copy-done) | copy-start | bytes 12582916
  44.7 2.2 %copy-start.3 = (bf16[64,128,256]{2,1,0:T(8,128)(2,1)S(1)}, bf16[64,128,256]{2,1,0:T(8,128)(2,1)}, u32[]{:S(2)}) copy-start(bf16[64,128,256]{2,1,0:T(8,128)(2,1)} %copy-done.2) | copy-start | bytes 12582916
  48.2 4.7 %collective-permute-start.13 = (bf16[256,256]{1,0:T(8,128)(2,1)S(1)}, bf16[256,256]{1,0:T(8,128)(2,1)S(1)}, u32[]{:S(2)}, u32[]{:S(2)}) collective-permute-start(bf16[256,256]{1,0:T(8,128)(2,1)S(1)} %broadcast_select_fusion.2), channel_id=1, source_target_pairs={{0,1},{1,0},{2,3},{3,2},{4,5},{5,4},{6,7},{7,6},{8,9},{9,8},{10,11... | collective-permute-start | bytes 393224 | tf_op jit(solution)/shard_map/ppermute | solution.py:19

commit v5 on v4

--- a/solution.py
+++ b/solution.py
@@ -209,51 +209,61 @@
         out_ref[...] = traces_ref[here ^ k]
 
 
-def shapes_kernel(flip, rim, frames, place_ref, *refs):
-    if rim:
-        col_ref, row_ref, code_ref, templates_ref, shapes_ref, col_adj_ref, row_adj_ref = refs
-        band = column_band(col_ref, rim, 1)
-        planes = templates_ref.shape[1] // LANES
-        col_adj_ref[...] = jnp.zeros_like(col_adj_ref)
-        for p in range(planes):
-            lanes = slice(p * LANES, (p + 1) * LANES)
-            col_adj_ref[lanes, lanes] = band
-        row_adj_ref[...] = row_band_adjoint(row_ref, rim, frames)
-    else:
-        code_ref, templates_ref, shapes_ref = refs
-    count, here = templates_ref.shape[0], shapes_ref.shape[0]
-    first = pl.multiple_of((place_ref[PLANE] ^ flip) * here, here)
-
-    @pl.loop(0, here // 8)
-    def _(g):
-        support = code_ref[pl.ds(pl.multiple_of(first + g * 8, 8), 8), :] >> 1
-        columns = jnp.transpose(support)
-        lane = iota((LANES, count), 1)
-        for i in range(8):
-            named = jnp.broadcast_to(columns[:, i : i + 1], (LANES, count))
-            shapes_ref[g * 8 + i] = jnp.dot(
-                (lane == named).astype(BF16), templates_ref[...], preferred_element_type=F32
-            ).astype(BF16)
-
-
-def residual_kernel(
-    flip, place_ref, shapes_ref, filtered_ref, code_ref, *refs
-):
-    traces, (out_ref, edge_ref, ordered_ref) = refs[:-3], refs[-3:]
+def bands_kernel(rim, frames, col_ref, row_ref, col_adj_ref, row_adj_ref):
+    band = column_band(col_ref, rim, 1)
+    col_adj_ref[...] = jnp.zeros_like(col_adj_ref)
+    for p in range(col_adj_ref.shape[0] // LANES):
+        lanes = slice(p * LANES, (p + 1) * LANES)
+        col_adj_ref[lanes, lanes] = band
+    row_adj_ref[...] = row_band_adjoint(row_ref, rim, frames)
+
+
+def residual_kernel(flip, place_ref, filtered_ref, code_ref, templates_ref, *refs):
+    traces, (out_ref, edge_ref, ordered_ref, slots_ref) = refs[:-4], refs[-4:]
     wide = len(traces)
     share, frames, lanes = traces[0].shape
-    copies = filtered_ref.shape[1] // LANES
+    names, width = templates_ref.shape
+    tile = 2 * LANES
     base = (place_ref[PLANE] ^ flip) * wide * share
+    marks = iota((lanes, tile), 1).astype(F32).astype(BF16)
+    group = min(8, share)
     for k in range(wide):
         block = place_ref[WIDE] ^ k
-        for h in range(share):
-            row = block * share + h
-            model = jnp.dot(traces[k][h], shapes_ref[row], preferred_element_type=F32)
-            mask = (code_ref[pl.ds(base + row, 1), :] & 1).astype(F32)
-            spot = pl.ds(pl.multiple_of(row * frames, frames), frames)
-            out_ref[spot, :] = (
-                filtered_ref[spot, :].astype(F32) - jnp.concatenate([mask] * copies, axis=1) * model
-            ).astype(BF16)
+        top = base + block * share
+        for g in range(share // group):
+            support = code_ref[pl.ds(top + g * group, group), :] >> 1
+            support = jnp.concatenate([support] * (8 // group), axis=0)
+            columns = [
+                jnp.transpose(
+                    jnp.where(support // tile == t, support & (tile - 1), -1).astype(F32)
+                )
+                for t in range(names // tile)
+            ]
+            for i in range(group):
+                h = g * group + i
+                hits = jnp.concatenate(
+                    [
+                        jnp.where(
+                            marks
+                            == jnp.broadcast_to(column[:, i : i + 1], (lanes, tile)).astype(BF16),
+                            jnp.ones((), BF16), jnp.zeros((), BF16),
+                        )
+                        for column in columns
+                    ],
+                    axis=1,
+                )
+                slots_ref[k, h * frames : (h + 1) * frames, :] = jnp.dot(
+                    traces[k][h], hits, preferred_element_type=F32
+                ).astype(BF16)
+        model = jnp.dot(slots_ref[k], templates_ref[...], preferred_element_type=F32)
+        mask = (code_ref[pl.ds(top, share), :] & 1).astype(F32)
+        mask = jnp.broadcast_to(mask[:, None, :], (share, frames, lanes)).reshape(-1, lanes)
+        size = share * frames
+        spot = pl.ds(pl.multiple_of(block * size, size), size)
+        out_ref[spot, :] = (
+            filtered_ref[spot, :].astype(F32)
+            - jnp.concatenate([mask] * (width // lanes), axis=1) * model
+        ).astype(BF16)
         ordered_ref[pl.ds(block * share, share)] = traces[k][...]
     edge = edge_ref.shape[0]
     start = jnp.where(place_ref[REP] > 0, 0, out_ref.shape[0] - edge)
@@ -407,21 +417,14 @@
         )(kernel_row, *[part[k] for part in projected])
         blocks[k] = exchange(sums[k], "wide", k)
 
-    def make_shapes(flip, after, bands):
-        late_code, late_templates, _ = lax.optimization_barrier((code, flat_templates, after))
-        outs = [pltpu.VMEM((here, LANES, width), BF16)]
-        taps = ()
-        if bands:
-            outs += [(width, width), (edge, depth)]
-            taps = (col_taps, row_taps)
-        return call(
-            functools.partial(shapes_kernel, flip, rim if bands else 0, frames), "shapes",
-            outs, 1 + len(taps), 2, 2150000000, 5 * mib,
-        )(place, *taps, late_code, late_templates)
-
-    shapes = [None] * plane_count
-    shapes[0], col_adj, row_adj = make_shapes(0, [sums[k] for k in order[:-1]], True)
-    first, col_adj = lax.optimization_barrier((projected[0][0], col_adj))
+    late_col, late_row, _ = lax.optimization_barrier(
+        (col_taps, row_taps, [sums[k] for k in order[:-1]])
+    )
+    col_adj, row_adj = call(
+        functools.partial(bands_kernel, rim, frames), "bands", [(width, width), (edge, depth)],
+        2, 0, 10000000, mib,
+    )(late_col, late_row)
+    first, col_adj, row_adj = lax.optimization_barrier((projected[0][0], col_adj, row_adj))
 
     cell_shape = (wide, share, frames, LANES)
     tables = (wide, total_frames, total_frames) if wide <= share else (1, BLOCK, LANES)
@@ -436,11 +439,7 @@
         place, tile_owner[:, 0], kernel_row, first, *[part[0] for part in projected[1:]],
         *[blocks[k] for k in range(1, wide)],
     )
-    for flip in range(1, plane_count):
-        (shapes[flip],) = make_shapes(flip, traces[0], False)
     swapped = {k: exchange(traces[k], "wide", k) if k else traces[0] for k in order}
-    for k in range(1, wide):
-        swapped[k], _ = lax.optimization_barrier((swapped[k], shapes[1:]))
     passed = [swapped] + [
         {k: exchange(swapped[k], "planes", flip) for k in order[::-1]}
         for flip in range(1, plane_count)
@@ -451,8 +450,9 @@
         part, tip, sorted_rows = call(
             functools.partial(residual_kernel, flip), "residual",
             [(here * frames, width), (edge, width), (here, frames, LANES)],
-            1, 3 + wide, 70000000, 6 * mib,
-        )(place, shapes[flip], filtered[flip], code, *[passed[flip][k] for k in range(wide)])
+            1, 3 + wide, 500000000, 2 * mib,
+            scratch=[pltpu.VMEM((wide, share * frames, names), BF16)],
+        )(place, filtered[flip], code, flat_templates, *[passed[flip][k] for k in range(wide)])
         residual.append(part)
         edges.append(tip)
         ordered.append(sorted_rows)

time: 56 us -> 49.6 us (0.89)
  local copies, waits for them, and re-layouts: 9.31 us -> 2.26 us
  Pallas kernels: 24.9 us -> 18.5 us
  waiting for transfers between devices: 2.48 us -> 7.73 us
  starting transfers between devices: 17.6 us -> 19.6 us
    pallas_call x2 -> x1, Pallas kernels: 11 us -> 1 us  [on_device(): call(functools.partial(bands_kernel, rim, frames), 'bands', [(width, widt...]
    unnamed x20 -> x12, local copies, waits for them, and re-layouts: 8.36 us -> 1.31 us
    ppermute x14, waiting for transfers between devices: 2.48 us -> 7.73 us  [exchange(): return lax.ppermute(cells, axis, [(i, i ^ flip) for i in range(count)])]
    pallas_call x2, Pallas kernels: 2.47 us -> 6.01 us  [on_device(): call(functools.partial(residual_kernel, flip), 'residual', [(here * frame...]
    ppermute x14, starting transfers between devices: 17.6 us -> 19.6 us  [exchange(): return lax.ppermute(cells, axis, [(i, i ^ flip) for i in range(count)])]
  transfers between devices with their start and end apart: 14 -> 14, of which waited for: 2 -> 5; matrix products, arithmetic and copies ran while one was open for 3% -> 4% of each run, Pallas kernels for 31% -> 18%
where the time goes in v5:
time: 49.6 us; the launch traced here: 49.5 us
  starting transfers between devices  19.6 us (40%)
  Pallas kernels  18.5 us (37%)
  waiting for transfers between devices  7.73 us (16%)
  local copies, waits for them, and re-layouts  2.26 us (5%)
  between operations  0.87 us (2%)
  other arithmetic  0.58 us (1%)
    ppermute x14, starting transfers between devices, exchange(): return lax.ppermute(cells, axis, [(i, i ^ flip) for i in range(count)])  19.6 us
    ppermute x14, waiting for transfers between devices, exchange(): return lax.ppermute(cells, axis, [(i, i ^ flip) for i in range(count)])  7.73 us
    pallas_call x2, Pallas kernels, on_device(): call(functools.partial(residual_kernel, flip), 'residual', [(here * frame...  6.01 us
    pallas_call x2, Pallas kernels, on_device(): call(functools.partial(forward_kernel, flip, turn == 0), 'forward', [smoo...  4.92 us
    pallas_call x1, Pallas kernels, on_device(): pl.pallas_call(functools.partial(backward_kernel, plane_count), out_shape...  2.92 us
    pallas_call x1, Pallas kernels, on_device(): pl.pallas_call(functools.partial(prepare_kernel, rim, cuts), out_shape=(s...  2.67 us
    unnamed x12, local copies, waits for them, and re-layouts  1.31 us
    pallas_call x1, Pallas kernels, on_device(): call(functools.partial(bands_kernel, rim, frames), 'bands', [(width, widt...  1 us
  transfers between devices with their start and end apart: 14, of which 5 were waited for; matrix products, arithmetic and copies ran while one was open for 4% of the time, Pallas kernels for 18%

profile of v5, /device:TPU:1, one launch (start us, length us, event | category | flops | bytes accessed | tf_op | source)
XLA Modules:
  0.0 49.5 jit_solution(14896122082240175397)
XLA Ops:
  0.6 0.9 %constant_dynamic-slice_fusion = bf16[2,16,16,128]{3,2,1,0:T(8,128)(2,1)S(1)} fusion(bf16[2,16,128,128]{3,2,1,0:T(8,128)(2,1)} %movie_hbm.1, s32[]{:T(128)S(6)} %select_n.38), kind=kLoop, calls=%fused_computation.11 | loop fusion | bytes 262148 | tf_op jit(solution)/shard_map/dynamic_slice | solution.py:352
  1.6 0.1 collective-permute-start
  1.7 2.7 %prepare.1 = (bf16[16,160,256]{2,1,0:T(8,128)(2,1)S(1)}, bf16[128,128]{1,0:T(8,128)(2,1)S(1)}, bf16[256,768]{1,0:T(8,128)(2,1)S(1)}, s32[128,128]{1,0:T(8,128)S(...) custom-call(f32[25]{0:T(128)} %col_ref, f32[25]{0:T(128)} %row_ref, bf16[2,16,128,128]{3,2,1,0:T(8,128)(2,1)} %movie_hbm.1, ...), custom_call_target="tpu_custom_call" | custom-call | flops 200000000 | bytes 3145728 | tf_op jit(solution)/shard_map/prepare/pallas_call | solution.py:355
  4.4 0.1 pad_add_fusion.place_ref
  4.5 0.0 collective-permute-done.edge_ref
  4.5 2.5 %forward.2 = (bf16[16,160,256]{2,1,0:T(8,128)(2,1)S(1)}, bf16[1024,256]{1,0:T(8,128)(2,1)S(1)}, bf16[256,128]{1,0:T(8,128)(2,1)S(1)}, bf16[256,128]{1,0:T(8,128)...) custom-call(s32[3]{0:T(128)S(1)} %pad_add_fusion.place_ref, ...), custom_call_target="tpu_custom_call", output_to_operand_aliasing={{0}: (1, {})} | custom-call | flops 800000000 | bytes 3145728 | tf_op jit(solution)/shard_map/forward/pallas_call | solution.py:391
  7.0 0.0 copy-done.3
  7.1 2.7 %collective-permute-start.2 = (bf16[512,128]{1,0:T(8,128)(2,1)S(1)}, bf16[512,128]{1,0:T(8,128)(2,1)S(1)}, u32[]{:S(2)}, u32[]{:S(2)}) collective-permute-start(bf16[512,128]{1,0:T(8,128)(2,1)S(1)} %pad_maximum_fusion.1), channel_id=1, source_target_pairs={{0,2},{2,0},{1,3},{3,1},{4,6},{6,4},{5,7},{7,5},{8,10},{10,8},{9,1... | collective-permute-start | bytes 393224 | tf_op jit(solution)/shard_map/ppermute | solution.py:19
  9.8 0.1 collective-permute-start.1
  9.9 0.0 copy-done.4
  9.9 0.1 broadcast_multiply_fusion
  10.0 0.1 select_reduce_fusion
  10.1 0.0 copy-start
  10.1 0.0 copy-start.1
  10.1 0.0 copy-start.2
  10.1 2.4 %forward.3 = (bf16[16,160,256]{2,1,0:T(8,128)(2,1)S(1)}, bf16[1024,256]{1,0:T(8,128)(2,1)S(1)}, bf16[256,128]{1,0:T(8,128)(2,1)S(1)}, bf16[256,128]{1,0:T(8,128)...) custom-call(s32[3]{0:T(128)S(1)} %pad_add_fusion.place_ref, ...), custom_call_target="tpu_custom_call", output_to_operand_aliasing={{0}: (1, {})} | custom-call | flops 800000000 | bytes 3145728 | tf_op jit(solution)/shard_map/forward/pallas_call | solution.py:391
  12.5 1.1 %collective-permute-done.2 = bf16[512,128]{1,0:T(8,128)(2,1)S(1)} collective-permute-done((bf16[512,128]{1,0:T(8,128)(2,1)S(1)}, bf16[512,128]{1,0:T(8,128)(2,1)S(1)}, u32[]{:S(2)}, u32[]{:S(2)}) %collective-permute-start.2) | collective-permute-done | bytes 131104 | tf_op jit(solution)/shard_map/ppermute | solution.py:19
  13.7 1.4 %collective-permute-start.3 = (bf16[272,128]{1,0:T(8,128)(2,1)S(1)}, bf16[272,128]{1,0:T(8,128)(2,1)S(1)}, u32[]{:S(2)}, u32[]{:S(2)}) collective-permute-start(bf16[272,128]{1,0:T(8,128)(2,1)S(1)} %sum.5), channel_id=1, source_target_pairs={{0,4},{4,0},{8,12},{12,8},{1,5},{5,1},{9,13},{13,9},{2,6},{6,2},{1... | collective-permute-start | bytes 208904 | tf_op jit(solution)/shard_map/ppermute | solution.py:19
  15.1 1.4 %collective-permute-done.1 = bf16[512,128]{1,0:T(8,128)(2,1)S(1)} collective-permute-done((bf16[512,128]{1,0:T(8,128)(2,1)S(1)}, bf16[512,128]{1,0:T(8,128)(2,1)S(1)}, u32[]{:S(2)}, u32[]{:S(2)}) %collective-permute-start.1) | collective-permute-done | bytes 131104 | tf_op jit(solution)/shard_map/ppermute | solution.py:19
  16.5 3.4 %collective-permute-start.5 = (bf16[272,128]{1,0:T(8,128)(2,1)S(1)}, bf16[272,128]{1,0:T(8,128)(2,1)S(1)}, u32[]{:S(2)}, u32[]{:S(2)}) collective-permute-start(bf16[272,128]{1,0:T(8,128)(2,1)S(1)} %sum.4), channel_id=1, source_target_pairs={{0,12},{4,8},{8,4},{12,0},{1,13},{5,9},{9,5},{13,1},{2,14},{6,10},... | collective-permute-start | bytes 208904 | tf_op jit(solution)/shard_map/ppermute | solution.py:19
  19.9 0.1 collective-permute-start.4
  20.0 1.0 %bands.1 = (bf16[256,256]{1,0:T(8,128)(2,1)S(1)}, bf16[256,768]{1,0:T(8,128)(2,1)S(1)}) custom-call(f32[25]{0:T(128)S(1)} %copy-done, f32[25]{0:T(128)S(1)} %copy-done.1), custom_call_target="tpu_custom_call" | custom-call | flops 10000000 | bytes 1048576 | tf_op jit(solution)/shard_map/bands/pallas_call | solution.py:423
  21.0 0.0 collective-permute-done.3.refs_2_
  21.0 0.6 %collective-permute-done.5.refs_4_ = bf16[272,128]{1,0:T(8,128)(2,1)S(1)} collective-permute-done((bf16[272,128]{1,0:T(8,128)(2,1)S(1)}, bf16[272,128]{1,0:T(8,128)(2,1)S(1)}, u32[]{:S(2)}, u32[]{:S(2)}) %collective-permute-start.5) | collective-permute-done | bytes 69664 | tf_op jit(solution)/shard_map/ppermute | solution.py:19
  21.6 4.3 %collective-permute-done.4.refs_3_ = bf16[272,128]{1,0:T(8,128)(2,1)S(1)} collective-permute-done((bf16[272,128]{1,0:T(8,128)(2,1)S(1)}, bf16[272,128]{1,0:T(8,128)(2,1)S(1)}, u32[]{:S(2)}, u32[]{:S(2)}) %collective-permute-start.4) | collective-permute-done | bytes 69664 | tf_op jit(solution)/shard_map/ppermute | solution.py:19
  25.9 0.0 copy-done.2
  25.9 0.9 %mix.1 = (bf16[16,16,128]{2,1,0:T(8,128)(2,1)S(1)}, bf16[16,16,128]{2,1,0:T(8,128)(2,1)S(1)}, bf16[16,16,128]{2,1,0:T(8,128)(2,1)S(1)}, bf16[16,16,128]{2,1,0:T(8,128)(2,1)S(1)}) custom-call(s32[3]{0:T(128)S(1)} %pad_add_fusion.place_ref, s32[128]{0:T(128)S(1)} %bitcast.13, bf16[16,128]{1,0:T(8,128)(2,1)S(1)} %pad_bitcast_fusion.lag_ref, ...), custom_call_target="tpu_custom_call" | custom-call | flops 20000000 | bytes 1048576 | tf_op jit(solution)/shard_map/mix/pallas_call | solution.py:431
  26.8 0.1 collective-permute-start.9
  26.9 1.8 %collective-permute-start.11 = (bf16[16,16,128]{2,1,0:T(8,128)(2,1)S(1)}, bf16[16,16,128]{2,1,0:T(8,128)(2,1)S(1)}, u32[]{:S(2)}, u32[]{:S(2)}) collective-permute-start(bf16[16,16,128]{2,1,0:T(8,128)(2,1)S(1)} %get-tuple-element.64), channel_id=1, source_target_pairs={{0,12},{4,8},{8,4},{12,0},{1,13},{5,9},{9,5},{13,1},{2,14},{6,10},... | collective-permute-start | bytes 196616 | tf_op jit(solution)/shard_map/ppermute | solution.py:19
  28.6 0.9 %collective-permute-start.7 = (bf16[16,16,128]{2,1,0:T(8,128)(2,1)S(1)}, bf16[16,16,128]{2,1,0:T(8,128)(2,1)S(1)}, u32[]{:S(2)}, u32[]{:S(2)}) collective-permute-start(bf16[16,16,128]{2,1,0:T(8,128)(2,1)S(1)} %get-tuple-element.62), channel_id=1, source_target_pairs={{0,4},{4,0},{8,12},{12,8},{1,5},{5,1},{9,13},{13,9},{2,6},{6,2},{1... | collective-permute-start | bytes 196616 | tf_op jit(solution)/shard_map/ppermute | solution.py:19
  29.5 1.4 %collective-permute-start.6 = (bf16[16,16,128]{2,1,0:T(8,128)(2,1)S(1)}, bf16[16,16,128]{2,1,0:T(8,128)(2,1)S(1)}, u32[]{:S(2)}, u32[]{:S(2)}) collective-permute-start(bf16[16,16,128]{2,1,0:T(8,128)(2,1)S(1)} %get-tuple-element.61.refs_0_), channel_id=1, source_target_pairs={{0,2},{2,0},{1,3},{3,1},{4,6},{6,4},{5,7},{7,5},{8,10},{10,8},{9,1... | collective-permute-start | bytes 196616 | tf_op jit(solution)/shard_map/ppermute | solution.py:19
  30.9 0.0 collective-permute-done.9.refs_2_
  30.9 1.3 %collective-permute-start.10 = (bf16[16,16,128]{2,1,0:T(8,128)(2,1)S(1)}, bf16[16,16,128]{2,1,0:T(8,128)(2,1)S(1)}, u32[]{:S(2)}, u32[]{:S(2)}) collective-permute-start(bf16[16,16,128]{2,1,0:T(8,128)(2,1)S(1)} %collective-permute-done.9.refs_2_), channel_id=1, source_target_pairs={{0,2},{2,0},{1,3},{3,1},{4,6},{6,4},{5,7},{7,5},{8,10},{10,8},{9,1... | collective-permute-start | bytes 196616 | tf_op jit(solution)/shard_map/ppermute | solution.py:19
  32.2 0.3 collective-permute-done.11.refs_3_
  32.5 1.5 %collective-permute-start.12 = (bf16[16,16,128]{2,1,0:T(8,128)(2,1)S(1)}, bf16[16,16,128]{2,1,0:T(8,128)(2,1)S(1)}, u32[]{:S(2)}, u32[]{:S(2)}) collective-permute-start(bf16[16,16,128]{2,1,0:T(8,128)(2,1)S(1)} %collective-permute-done.11.refs_3_), channel_id=1, source_target_pairs={{0,2},{2,0},{1,3},{3,1},{4,6},{6,4},{5,7},{7,5},{8,10},{10,8},{9,1... | collective-permute-start | bytes 196616 | tf_op jit(solution)/shard_map/ppermute | solution.py:19
  34.0 0.0 collective-permute-done.7.refs_1_
  34.0 0.0 collective-permute-start.8
  34.0 3.0 %residual.3 = (bf16[1024,256]{1,0:T(8,128)(2,1)S(1)}, bf16[256,256]{1,0:T(8,128)(2,1)S(1)}, bf16[64,16,128]{2,1,0:T(8,128)(2,1)S(1)}) custom-call(s32[3]{0:T(128)S(1)} %pad_add_fusion.place_ref, bf16[1024,256]{1,0:T(8,128)(2,1)S(1)} %get-tuple-element.66.filtered_ref, s32[128,128]{1,0:T(8,128)S(1)} %get-tuple-element.41.code_ref, ...), custom_call_target="tpu_custom_call" | custom-call | flops 500000000 | bytes 2097152 | tf_op jit(solution)/shard_map/residual/pallas_call | solution.py:450
  37.1 0.0 collective-permute-done.6.refs_0_
  37.1 0.0 collective-permute-done.10.refs_2_
  37.1 0.0 collective-permute-done.12.refs_3_
  37.1 0.0 collective-permute-done.8.refs_1_
  37.1 3.0 %residual.2 = (bf16[1024,256]{1,0:T(8,128)(2,1)S(1)}, bf16[256,256]{1,0:T(8,128)(2,1)S(1)}, bf16[64,16,128]{2,1,0:T(8,128)(2,1)S(1)}) custom-call(s32[3]{0:T(128)S(1)} %pad_add_fusion.place_ref, bf16[1024,256]{1,0:T(8,128)(2,1)S(1)} %get-tuple-element.43.filtered_ref, s32[128,128]{1,0:T(8,128)S(1)} %get-tuple-element.41.code_ref, ...), custom_call_target="tpu_custom_call" | custom-call | flops 500000000 | bytes 2097152 | tf_op jit(solution)/shard_map/residual/pallas_call | solution.py:450
  40.2 4.9 %collective-permute-start.13 = (bf16[256,256]{1,0:T(8,128)(2,1)S(1)}, bf16[256,256]{1,0:T(8,128)(2,1)S(1)}, u32[]{:S(2)}, u32[]{:S(2)}) collective-permute-start(bf16[256,256]{1,0:T(8,128)(2,1)S(1)} %broadcast_select_fusion.2), channel_id=1, source_target_pairs={{0,1},{1,0},{2,3},{3,2},{4,5},{5,4},{6,7},{7,6},{8,9},{9,8},{10,11... | collective-permute-start | bytes 393224 | tf_op jit(solution)/shard_map/ppermute | solution.py:19
  45.1 0.2 fusion
  45.3 1.3 %copy.14 = bf16[64,16,128]{2,1,0:T(8,128)(2,1)} copy(bf16[64,16,128]{0,1,2:T(8,128)(2,1)S(1)} %fusion) | data formatting | bytes 524288
  46.6 0.0 collective-permute-done.13.edge_ref
  46.6 2.9 %backward.1 = bf16[2,16,128,128]{3,2,1,0:T(8,128)(2,1)} custom-call(s32[3]{0:T(128)S(1)} %pad_add_fusion.place_ref, bf16[256,256]{1,0:T(8,128)(2,1)S(1)} %collective-permute-done.13.edge_ref, bf16[256,256]{1,0:T(8,128)(2,1)S(1)} %get-tuple-element.70.col_adj_ref, bf16[256,768]{1,0:T(8,128)(2,1)S(1)} %get-tuple-element.71.row_adj_ref, ...), custom_call_target="tpu_custom_call" | custom-call | flops 1000000000 | bytes 3145728 | tf_op jit(solution)/shard_map/backward/pallas_call | solution.py:476
  (17 shorter events, 0.2 us)
Async XLA Ops:
  1.6 2.9 %collective-permute-start = (bf16[2,16,16,128]{3,2,1,0:T(8,128)(2,1)S(1)}, bf16[2,16,16,128]{3,2,1,0:T(8,128)(2,1)S(1)}, u32[]{:S(2)}, u32[]{:S(2)}) collective-permute-start(bf16[2,16,16,128]{3,2,1,0:T(8,128)(2,1)S(1)} %constant_dynamic-slice_fusion), channel_id=1, source_target_pairs={{0,1},{1,0},{2,3},{3,2},{4,5},{5,4},{6,7},{7,6},{8,9},{9,8},{10,11... | collective-permute-start | bytes 393224 | tf_op jit(solution)/shard_map/ppermute | solution.py:19
  4.5 2.6 %copy-start.3 = (f32[1,3,65]{2,0,1:T(1,128)S(1)}, f32[1,3,65]{2,0,1:T(1,128)}, u32[]{:S(2)}) copy-start(f32[1,3,65]{2,0,1:T(1,128)} %param.16) | copy-start | bytes 2344
  4.5 5.4 %copy-start.4 = (s32[1,3]{1,0:T(1,128)S(1)}, s32[1,3]{1,0:T(1,128)}, u32[]{:S(2)}) copy-start(s32[1,3]{1,0:T(1,128)} %param.17) | copy-start | bytes 40
  7.1 6.6 %collective-permute-start.2 = (bf16[512,128]{1,0:T(8,128)(2,1)S(1)}, bf16[512,128]{1,0:T(8,128)(2,1)S(1)}, u32[]{:S(2)}, u32[]{:S(2)}) collective-permute-start(bf16[512,128]{1,0:T(8,128)(2,1)S(1)} %pad_maximum_fusion.1), channel_id=1, source_target_pairs={{0,2},{2,0},{1,3},{3,1},{4,6},{6,4},{5,7},{7,5},{8,10},{10,8},{9,1... | collective-permute-start | bytes 393224 | tf_op jit(solution)/shard_map/ppermute | solution.py:19
  9.8 6.6 %collective-permute-start.1 = (bf16[512,128]{1,0:T(8,128)(2,1)S(1)}, bf16[512,128]{1,0:T(8,128)(2,1)S(1)}, u32[]{:S(2)}, u32[]{:S(2)}) collective-permute-start(bf16[512,128]{1,0:T(8,128)(2,1)S(1)} %pad_maximum_fusion), channel_id=1, source_target_pairs={{0,2},{2,0},{1,3},{3,1},{4,6},{6,4},{5,7},{7,5},{8,10},{10,8},{9,1... | collective-permute-start | bytes 393224 | tf_op jit(solution)/shard_map/ppermute | solution.py:19
  10.1 9.9 %copy-start = (f32[25]{0:T(128)S(1)}, f32[25]{0:T(128)}, u32[]{:S(2)}) copy-start(f32[25]{0:T(128)} %col_ref) | copy-start | bytes 304
  10.1 9.9 %copy-start.1 = (f32[25]{0:T(128)S(1)}, f32[25]{0:T(128)}, u32[]{:S(2)}) copy-start(f32[25]{0:T(128)} %row_ref) | copy-start | bytes 304
  10.1 15.8 %copy-start.2 = (s32[128,1]{0,1:T(1,128)S(1)}, s32[128,1]{0,1:T(1,128)}, u32[]{:S(2)}) copy-start(s32[128,1]{0,1:T(1,128)} %param.11) | copy-start | bytes 1540
  13.7 7.4 %collective-permute-start.3 = (bf16[272,128]{1,0:T(8,128)(2,1)S(1)}, bf16[272,128]{1,0:T(8,128)(2,1)S(1)}, u32[]{:S(2)}, u32[]{:S(2)}) collective-permute-start(bf16[272,128]{1,0:T(8,128)(2,1)S(1)} %sum.5), channel_id=1, source_target_pairs={{0,4},{4,0},{8,12},{12,8},{1,5},{5,1},{9,13},{13,9},{2,6},{6,2},{1... | collective-permute-start | bytes 208904 | tf_op jit(solution)/shard_map/ppermute | solution.py:19
  16.5 5.2 %collective-permute-start.5 = (bf16[272,128]{1,0:T(8,128)(2,1)S(1)}, bf16[272,128]{1,0:T(8,128)(2,1)S(1)}, u32[]{:S(2)}, u32[]{:S(2)}) collective-permute-start(bf16[272,128]{1,0:T(8,128)(2,1)S(1)} %sum.4), channel_id=1, source_target_pairs={{0,12},{4,8},{8,4},{12,0},{1,13},{5,9},{9,5},{13,1},{2,14},{6,10},... | collective-permute-start | bytes 208904 | tf_op jit(solution)/shard_map/ppermute | solution.py:19
  19.9 6.0 %collective-permute-start.4 = (bf16[272,128]{1,0:T(8,128)(2,1)S(1)}, bf16[272,128]{1,0:T(8,128)(2,1)S(1)}, u32[]{:S(2)}, u32[]{:S(2)}) collective-permute-start(bf16[272,128]{1,0:T(8,128)(2,1)S(1)} %sum.3), channel_id=1, source_target_pairs={{0,8},{4,12},{8,0},{12,4},{1,9},{5,13},{9,1},{13,5},{2,10},{6,14},... | collective-permute-start | bytes 208904 | tf_op jit(solution)/shard_map/ppermute | solution.py:19
  26.8 4.1 %collective-permute-start.9 = (bf16[16,16,128]{2,1,0:T(8,128)(2,1)S(1)}, bf16[16,16,128]{2,1,0:T(8,128)(2,1)S(1)}, u32[]{:S(2)}, u32[]{:S(2)}) collective-permute-start(bf16[16,16,128]{2,1,0:T(8,128)(2,1)S(1)} %get-tuple-element.63), channel_id=1, source_target_pairs={{0,8},{4,12},{8,0},{12,4},{1,9},{5,13},{9,1},{13,5},{2,10},{6,14},... | collective-permute-start | bytes 196616 | tf_op jit(solution)/shard_map/ppermute | solution.py:19
  26.9 5.6 %collective-permute-start.11 = (bf16[16,16,128]{2,1,0:T(8,128)(2,1)S(1)}, bf16[16,16,128]{2,1,0:T(8,128)(2,1)S(1)}, u32[]{:S(2)}, u32[]{:S(2)}) collective-permute-start(bf16[16,16,128]{2,1,0:T(8,128)(2,1)S(1)} %get-tuple-element.64), channel_id=1, source_target_pairs={{0,12},{4,8},{8,4},{12,0},{1,13},{5,9},{9,5},{13,1},{2,14},{6,10},... | collective-permute-start | bytes 196616 | tf_op jit(solution)/shard_map/ppermute | solution.py:19
  28.6 5.4 %collective-permute-start.7 = (bf16[16,16,128]{2,1,0:T(8,128)(2,1)S(1)}, bf16[16,16,128]{2,1,0:T(8,128)(2,1)S(1)}, u32[]{:S(2)}, u32[]{:S(2)}) collective-permute-start(bf16[16,16,128]{2,1,0:T(8,128)(2,1)S(1)} %get-tuple-element.62), channel_id=1, source_target_pairs={{0,4},{4,0},{8,12},{12,8},{1,5},{5,1},{9,13},{13,9},{2,6},{6,2},{1... | collective-permute-start | bytes 196616 | tf_op jit(solution)/shard_map/ppermute | solution.py:19
  29.5 7.5 %collective-permute-start.6 = (bf16[16,16,128]{2,1,0:T(8,128)(2,1)S(1)}, bf16[16,16,128]{2,1,0:T(8,128)(2,1)S(1)}, u32[]{:S(2)}, u32[]{:S(2)}) collective-permute-start(bf16[16,16,128]{2,1,0:T(8,128)(2,1)S(1)} %get-tuple-element.61.refs_0_), channel_id=1, source_target_pairs={{0,2},{2,0},{1,3},{3,1},{4,6},{6,4},{5,7},{7,5},{8,10},{10,8},{9,1... | collective-permute-start | bytes 196616 | tf_op jit(solution)/shard_map/ppermute | solution.py:19
  30.9 6.2 %collective-permute-start.10 = (bf16[16,16,128]{2,1,0:T(8,128)(2,1)S(1)}, bf16[16,16,128]{2,1,0:T(8,128)(2,1)S(1)}, u32[]{:S(2)}, u32[]{:S(2)}) collective-permute-start(bf16[16,16,128]{2,1,0:T(8,128)(2,1)S(1)} %collective-permute-done.9.refs_2_), channel_id=1, source_target_pairs={{0,2},{2,0},{1,3},{3,1},{4,6},{6,4},{5,7},{7,5},{8,10},{10,8},{9,1... | collective-permute-start | bytes 196616 | tf_op jit(solution)/shard_map/ppermute | solution.py:19
  32.5 4.6 %collective-permute-start.12 = (bf16[16,16,128]{2,1,0:T(8,128)(2,1)S(1)}, bf16[16,16,128]{2,1,0:T(8,128)(2,1)S(1)}, u32[]{:S(2)}, u32[]{:S(2)}) collective-permute-start(bf16[16,16,128]{2,1,0:T(8,128)(2,1)S(1)} %collective-permute-done.11.refs_3_), channel_id=1, source_target_pairs={{0,2},{2,0},{1,3},{3,1},{4,6},{6,4},{5,7},{7,5},{8,10},{10,8},{9,1... | collective-permute-start | bytes 196616 | tf_op jit(solution)/shard_map/ppermute | solution.py:19
  34.0 3.1 %collective-permute-start.8 = (bf16[16,16,128]{2,1,0:T(8,128)(2,1)S(1)}, bf16[16,16,128]{2,1,0:T(8,128)(2,1)S(1)}, u32[]{:S(2)}, u32[]{:S(2)}) collective-permute-start(bf16[16,16,128]{2,1,0:T(8,128)(2,1)S(1)} %collective-permute-done.7.refs_1_), channel_id=1, source_target_pairs={{0,2},{2,0},{1,3},{3,1},{4,6},{6,4},{5,7},{7,5},{8,10},{10,8},{9,1... | collective-permute-start | bytes 196616 | tf_op jit(solution)/shard_map/ppermute | solution.py:19
  40.2 6.4 %collective-permute-start.13 = (bf16[256,256]{1,0:T(8,128)(2,1)S(1)}, bf16[256,256]{1,0:T(8,128)(2,1)S(1)}, u32[]{:S(2)}, u32[]{:S(2)}) collective-permute-start(bf16[256,256]{1,0:T(8,128)(2,1)S(1)} %broadcast_select_fusion.2), channel_id=1, source_target_pairs={{0,1},{1,0},{2,3},{3,2},{4,5},{5,4},{6,7},{7,6},{8,9},{9,8},{10,11... | collective-permute-start | bytes 393224 | tf_op jit(solution)/shard_map/ppermute | solution.py:19

commit v6 on v5

--- a/solution.py
+++ b/solution.py
@@ -17,6 +17,16 @@
 def exchange(cells, axis, flip):
     count = lax.axis_size(axis)
     return lax.ppermute(cells, axis, [(i, i ^ flip) for i in range(count)])
+
+
+def crossed(cells, plane_flip, wide_flip):
+    count, size = lax.axis_size("planes"), lax.axis_size("wide")
+    pairs = [
+        (w * count + p, (w ^ wide_flip) * count + (p ^ plane_flip))
+        for w in range(size)
+        for p in range(count)
+    ]
+    return lax.ppermute(cells, ("wide", "planes"), pairs)
 
 
 def iota(shape, dim):
@@ -63,6 +73,10 @@
     spread = jnp.dot(tall, right, preferred_element_type=F32)
     same = lax.rem(iota((out_rows, depth), 1), frames) == iota((out_rows, depth), 0) // BLOCK
     return jnp.where(same, spread, 0.0).astype(BF16)
+
+
+def half_of(place_ref, flip, far, wide):
+    return (place_ref[PLANE] ^ flip) * 2 + ((place_ref[WIDE] // (wide // 2)) ^ far)
 
 
 def per_frame(rows, frames, copies):
@@ -120,10 +134,9 @@
 
 
 def forward_kernel(
-    flip, fill, place_ref, smooth_in_ref, edge_ref, col_fwd_ref, row_fwd_ref, code_ref,
-    templates_ref, smooth_ref, filtered_ref, *refs
+    flip, far, fill, wide, ks, place_ref, smooth_in_ref, edge_ref, col_fwd_ref, row_fwd_ref, code_ref,
+    templates_ref, smooth_ref, filtered_ref, out_ref, projected_ref,
 ):
-    outs, projected_ref = refs[:-1], refs[-1]
     frames, padded_rows, width = smooth_ref.shape
     planes, rows = width // LANES, padded_rows - 2 * BLOCK
     if fill:
@@ -138,18 +151,22 @@
             smooth_ref[:, :BLOCK, lanes] = above
             smooth_ref[:, BLOCK + rows :, lanes] = below
     here = filtered_ref.shape[0] // frames
-    first = (place_ref[PLANE] ^ flip) * here
+    first = half_of(place_ref, flip, far, wide) * here
     tiles = templates_ref.shape[1] // LANES
+    def along(b):
+        near = smooth_ref[:, pl.ds(pl.multiple_of(first + b * BLOCK, BLOCK), 3 * BLOCK), :]
+        near = near.reshape(frames * 3 * BLOCK, width)
+        return jnp.dot(row_fwd_ref[...], near, preferred_element_type=F32)
+
+    cells = along(0)
     for b in range(here // BLOCK):
-        top = pl.multiple_of(first + b * BLOCK, BLOCK)
-        near = smooth_ref[:, pl.ds(top, 3 * BLOCK), :].reshape(frames * 3 * BLOCK, width)
-        along = jnp.dot(row_fwd_ref[...], near, preferred_element_type=F32)
-        code = code_ref[pl.ds(top, BLOCK), :]
+        code = code_ref[pl.ds(pl.multiple_of(first + b * BLOCK, BLOCK), BLOCK), :]
         mask = per_frame((code & 1).astype(F32), frames, planes)
-        filtered = (along * mask).astype(BF16)
+        filtered = (cells * mask).astype(BF16)
         spot = slice(b * BLOCK * frames, (b + 1) * BLOCK * frames)
         filtered_ref[spot, :] = filtered
         dense = jnp.dot(filtered, templates_ref[...], preferred_element_type=F32)
+        cells = along(b + 1) if b + 1 < here // BLOCK else None
         picked = per_frame(code >> 1, frames, 1)
         lane, tile = picked & (LANES - 1), picked // LANES
         chosen = jnp.zeros(picked.shape, F32)
@@ -159,34 +176,35 @@
             )
             chosen = jnp.where(tile == t, found, chosen)
         projected_ref[spot, :] = chosen.astype(BF16)
-    size = outs[0].shape[0]
-    for k, out_ref in enumerate(outs):
-        start = pl.multiple_of((place_ref[WIDE] ^ k) * size, size)
-        out_ref[...] = projected_ref[pl.ds(start, size), :]
-
-
-def add_all(parts):
-    total = parts[0][...].astype(F32)
-    for part in parts[1:]:
-        total = total + part[...].astype(F32)
+    size = out_ref.shape[0] // len(ks)
+    for i, k in enumerate(ks):
+        start = pl.multiple_of(((place_ref[WIDE] ^ k) & (wide // 2 - 1)) * size, size)
+        out_ref[i * size : (i + 1) * size, :] = projected_ref[pl.ds(start, size), :]
+
+
+def add_all(parts, spots, rows):
+    total = None
+    for part, spot in zip(parts, spots):
+        term = part[spot * rows : (spot + 1) * rows, :].astype(F32)
+        total = term if total is None else total + term
     return total.astype(BF16)
 
 
-def sum_kernel(lag_ref, *refs):
+def sum_kernel(spots, lag_ref, *refs):
     parts, out_ref = refs[:-1], refs[-1]
-    rows = parts[0].shape[0]
-    out_ref[:rows, :] = add_all(parts)
+    rows = out_ref.shape[0] - lag_ref.shape[0]
+    out_ref[:rows, :] = add_all(parts, spots, rows)
     out_ref[rows:, :] = lag_ref[...]
 
 
-def mix_kernel(wide, count, place_ref, owner_ref, lag_ref, *refs):
-    parts, refs = refs[:count], refs[count:]
+def mix_kernel(wide, spots, place_ref, owner_ref, lag_ref, *refs):
+    parts, refs = refs[: len(spots)], refs[len(spots) :]
     blocks, outs = refs[: wide - 1], refs[wide - 1 : 2 * wide - 1]
     cells_ref, kernels_ref, traces_ref, tables_ref = refs[2 * wide - 1 :]
     _, share, frames, lanes = cells_ref.shape
     total = wide * frames
     here = place_ref[WIDE]
-    cells_ref[here] = add_all(parts).reshape(share, frames, lanes)
+    cells_ref[here] = add_all(parts, spots, share * frames).reshape(share, frames, lanes)
     kernels_ref[here] = lag_ref[...].astype(F32)
     for k, block in enumerate(blocks, 1):
         cells_ref[here ^ k] = block[: share * frames, :].reshape(share, frames, lanes)
@@ -218,17 +236,18 @@
     row_adj_ref[...] = row_band_adjoint(row_ref, rim, frames)
 
 
-def residual_kernel(flip, place_ref, filtered_ref, code_ref, templates_ref, *refs):
+def residual_kernel(flip, far, wide, spots, place_ref, filtered_ref, code_ref, templates_ref, *refs):
     traces, (out_ref, edge_ref, ordered_ref, slots_ref) = refs[:-4], refs[-4:]
-    wide = len(traces)
-    share, frames, lanes = traces[0].shape
+    _, frames, lanes = traces[0].shape
+    share = ordered_ref.shape[0] // len(spots)
     names, width = templates_ref.shape
     tile = 2 * LANES
-    base = (place_ref[PLANE] ^ flip) * wide * share
+    base = half_of(place_ref, flip, far, wide) * len(spots) * share
     marks = iota((lanes, tile), 1).astype(F32).astype(BF16)
     group = min(8, share)
-    for k in range(wide):
-        block = place_ref[WIDE] ^ k
+    for n, (k, source, offset) in enumerate(spots):
+        block = (place_ref[WIDE] ^ k) & (wide // 2 - 1)
+        source, offset = traces[source], offset * share
         top = base + block * share
         for g in range(share // group):
             support = code_ref[pl.ds(top + g * group, group), :] >> 1
@@ -252,10 +271,10 @@
                     ],
                     axis=1,
                 )
-                slots_ref[k, h * frames : (h + 1) * frames, :] = jnp.dot(
-                    traces[k][h], hits, preferred_element_type=F32
+                slots_ref[n, h * frames : (h + 1) * frames, :] = jnp.dot(
+                    source[offset + h], hits, preferred_element_type=F32
                 ).astype(BF16)
-        model = jnp.dot(slots_ref[k], templates_ref[...], preferred_element_type=F32)
+        model = jnp.dot(slots_ref[n], templates_ref[...], preferred_element_type=F32)
         mask = (code_ref[pl.ds(top, share), :] & 1).astype(F32)
         mask = jnp.broadcast_to(mask[:, None, :], (share, frames, lanes)).reshape(-1, lanes)
         size = share * frames
@@ -264,21 +283,21 @@
             filtered_ref[spot, :].astype(F32)
             - jnp.concatenate([mask] * (width // lanes), axis=1) * model
         ).astype(BF16)
-        ordered_ref[pl.ds(block * share, share)] = traces[k][...]
+        ordered_ref[pl.ds(block * share, share)] = source[offset : offset + share]
     edge = edge_ref.shape[0]
     start = jnp.where(place_ref[REP] > 0, 0, out_ref.shape[0] - edge)
     edge_ref[...] = out_ref[pl.ds(pl.multiple_of(start, edge), edge), :]
 
 
-def backward_kernel(count, place_ref, edge_ref, col_adj_ref, row_adj_ref, *refs):
-    parts, (out_hbm, padded_ref, out_ref, sems) = refs[:count], refs[count:]
+def backward_kernel(keys, wide, place_ref, edge_ref, col_adj_ref, row_adj_ref, *refs):
+    parts, (out_hbm, padded_ref, out_ref, sems) = refs[: len(keys)], refs[len(keys) :]
     planes, frames, rows, _ = out_ref.shape
     edge, size = BLOCK * frames, parts[0].shape[0]
     zero = jnp.zeros_like(edge_ref)
     padded_ref[:edge, :] = jnp.where(place_ref[REP] > 0, edge_ref[...], zero)
     padded_ref[edge + rows * frames :, :] = jnp.where(place_ref[REP] > 0, zero, edge_ref[...])
-    for flip, part in enumerate(parts):
-        spot = pl.multiple_of(edge + (place_ref[PLANE] ^ flip) * size, edge)
+    for (flip, far), part in zip(keys, parts):
+        spot = pl.multiple_of(edge + half_of(place_ref, flip, far, wide) * size, edge)
         padded_ref[pl.ds(spot, size), :] = part[...]
     def along(b):
         near = padded_ref[b * edge : (b + 3) * edge, :]
@@ -311,7 +330,7 @@
     return jax.ShapeDtypeStruct(shape, BF16)
 
 
-def call(kernel, name, outs, smem, vmem, flops, moved, scratch=(), aliases=None):
+def call(kernel, name, outs, smem, vmem, scratch=(), aliases=None):
     return pl.pallas_call(
         kernel,
         out_shape=tuple(shaped(s) if isinstance(s, tuple) else s for s in outs),
@@ -320,7 +339,6 @@
         scratch_shapes=scratch,
         input_output_aliases=aliases or {},
         compiler_params=pltpu.CompilerParams(vmem_limit_bytes=32 * 1024 * 1024),
-        cost_estimate=pl.CostEstimate(flops=flops, bytes_accessed=moved, transcendentals=0),
         name=name,
     )
 
@@ -372,7 +390,6 @@
             pltpu.SemaphoreType.DMA((5 + planes * cuts,)),
         ],
         compiler_params=pltpu.CompilerParams(vmem_limit_bytes=32 * mib),
-        cost_estimate=pl.CostEstimate(flops=200000000, bytes_accessed=3 * mib, transcendentals=0),
         name="prepare",
     )(
         *[
@@ -384,24 +401,19 @@
         ]
     )
 
-    order = list(range(wide // 2, wide)) + list(range(1, wide // 2)) + [0]
-    filtered, projected = [None] * plane_count, [None] * plane_count
-    for turn in range(plane_count):
-        flip = (turn + 1) % plane_count
-        smooth, filtered[flip], *mine = call(
-            functools.partial(forward_kernel, flip, turn == 0), "forward",
-            [smooth.shape, (here * frames, width)] + [(share * frames, LANES)] * wide,
-            1, 6, 800000000, 3 * mib, aliases={1: 0},
-            scratch=[pltpu.VMEM((here * frames, LANES), BF16)],
+    near_ks, far_ks = list(range(wide // 2)), list(range(wide // 2, wide))
+    halves = {1: far_ks, 0: near_ks[::-1]}
+    half_rows = here // 2
+    filtered, projected = {}, {}
+    keys = [((turn + 1) % plane_count, far) for turn in range(plane_count) for far in (0, 1)]
+    for turn, (flip, far) in enumerate(keys):
+        smooth, filtered[flip, far], mine = call(
+            functools.partial(forward_kernel, flip, far, turn == 0, wide, halves[far]), "forward",
+            [smooth.shape, (half_rows * frames, width), (half_rows * frames, LANES)],
+            1, 6, aliases={1: 0},
+            scratch=[pltpu.VMEM((half_rows * frames, LANES), BF16)],
         )(place, smooth, rim_rows, col_fwd, row_fwd, code, tall_templates)
-        if flip:
-            halves = [order[: wide // 2], order[wide // 2 :]]
-            mine = dict(enumerate(mine))
-            for ks in halves:
-                both = exchange(jnp.concatenate([mine[k] for k in ks]), "planes", flip)
-                for i, k in enumerate(ks):
-                    mine[k] = both[i * share * frames : (i + 1) * share * frames]
-        projected[flip] = mine
+        projected[flip, far] = exchange(mine, "planes", flip) if flip else mine
         if turn == 0:
             gains, lags, _ = lax.optimization_barrier((lag_gains, dilations, smooth))
             kernel_row = lag_kernel_values(gains[0], lags[0], total_frames)
@@ -411,72 +423,87 @@
 
     block_rows = share * frames + lag_rows
     sums, blocks = {}, {}
-    for k in order[:-1]:
+
+    def parts_of(k):
+        far = int(k in far_ks)
+        spots = [halves[far].index(k)] * plane_count
+        return spots, [projected[flip, far] for flip in range(plane_count)]
+
+    for k in near_ks[1:] + far_ks:
+        spots, parts = parts_of(k)
         (sums[k],) = call(
-            sum_kernel, "sum", [(block_rows, LANES)], 0, 1 + plane_count, 100000, mib // 4
-        )(kernel_row, *[part[k] for part in projected])
+            functools.partial(sum_kernel, spots), "sum", [(block_rows, LANES)],
+            0, 1 + plane_count,
+        )(kernel_row, *parts)
         blocks[k] = exchange(sums[k], "wide", k)
 
     late_col, late_row, _ = lax.optimization_barrier(
-        (col_taps, row_taps, [sums[k] for k in order[:-1]])
+        (col_taps, row_taps, list(sums.values()))
     )
     col_adj, row_adj = call(
         functools.partial(bands_kernel, rim, frames), "bands", [(width, width), (edge, depth)],
-        2, 0, 10000000, mib,
+        2, 0,
     )(late_col, late_row)
-    first, col_adj, row_adj = lax.optimization_barrier((projected[0][0], col_adj, row_adj))
+    own_spots, own_parts = parts_of(0)
+    own_parts[0], col_adj, row_adj = lax.optimization_barrier((own_parts[0], col_adj, row_adj))
 
     cell_shape = (wide, share, frames, LANES)
     tables = (wide, total_frames, total_frames) if wide <= share else (1, BLOCK, LANES)
     traces = call(
-        functools.partial(mix_kernel, wide, plane_count), "mix", [cell_shape[1:]] * wide,
-        2, wide + plane_count, 20000000, mib,
+        functools.partial(mix_kernel, wide, own_spots), "mix", [cell_shape[1:]] * wide,
+        2, wide + plane_count,
         scratch=[
             pltpu.VMEM(cell_shape, BF16), pltpu.VMEM((wide, lag_rows, LANES), F32),
             pltpu.VMEM(cell_shape, BF16), pltpu.VMEM(tables, BF16),
         ],
     )(
-        place, tile_owner[:, 0], kernel_row, first, *[part[0] for part in projected[1:]],
-        *[blocks[k] for k in range(1, wide)],
-    )
-    swapped = {k: exchange(traces[k], "wide", k) if k else traces[0] for k in order}
-    passed = [swapped] + [
-        {k: exchange(swapped[k], "planes", flip) for k in order[::-1]}
-        for flip in range(1, plane_count)
-    ]
-
-    residual, edges, ordered = [], [], []
-    for flip in range(plane_count):
-        part, tip, sorted_rows = call(
-            functools.partial(residual_kernel, flip), "residual",
-            [(here * frames, width), (edge, width), (here, frames, LANES)],
-            1, 3 + wide, 500000000, 2 * mib,
-            scratch=[pltpu.VMEM((wide, share * frames, names), BF16)],
-        )(place, filtered[flip], code, flat_templates, *[passed[flip][k] for k in range(wide)])
-        residual.append(part)
-        edges.append(tip)
-        ordered.append(sorted_rows)
-
-    outer = plane ^ jnp.where(rep == 0, plane_count - 1, 0)
-    tip = edges[0]
-    for flip in range(1, plane_count):
-        tip = jnp.where(outer == flip, edges[flip], tip)
+        place, tile_owner[:, 0], kernel_row, *own_parts, *[blocks[k] for k in range(1, wide)],
+    )
+    swapped = {k: exchange(traces[k], "wide", k) for k in far_ks + near_ks[1:]}
+    swapped[0] = traces[0]
+    late = range(1, plane_count)
+    direct = {flip: [crossed(traces[k], flip, k) for k in near_ks] for flip in late}
+
+    residual, edges, ordered = {}, {}, {}
+    back_keys = [(flip, far) for flip in range(plane_count) for far in (0, 1)]
+
+    def subtract(flip, far, groups, got):
+        spots = [(k, n, i) for n, ks in enumerate(groups) for i, k in enumerate(ks)]
+        residual[flip, far], edges[flip, far], ordered[flip, far] = call(
+            functools.partial(residual_kernel, flip, far, wide, spots), "residual",
+            [(half_rows * frames, width), (edge, width), (half_rows, frames, LANES)],
+            1, 3 + len(got), scratch=[pltpu.VMEM((len(spots), share * frames, names), BF16)],
+        )(place, filtered[flip, far], code, flat_templates, *got)
+
+    subtract(0, 0, [[k] for k in near_ks], [swapped[k] for k in near_ks])
+    distant, direct, _ = lax.optimization_barrier(
+        ([swapped[k] for k in far_ks], direct, edges[0, 0])
+    )
+    joined = jnp.concatenate(distant)
+    subtract(0, 1, [[k] for k in far_ks], distant)
+    for flip in late:
+        subtract(flip, 0, [[k] for k in near_ks], direct[flip])
+        subtract(flip, 1, [far_ks], [exchange(joined, "planes", flip)])
+
+    def pick(table, part, half):
+        found = table[0, 0]
+        for flip, far in back_keys[1:]:
+            here_it_is = ((plane ^ part) == flip) & ((spot // (wide // 2) ^ half) == far)
+            found = jnp.where(here_it_is, table[flip, far], found)
+        return found
+
+    tip = pick(edges, jnp.where(rep == 0, plane_count - 1, 0), jnp.where(rep == 0, 1, 0))
     tip = exchange(tip, "rep", 1)
 
     foot_share = support.shape[1] // plane_count
-    in_order = []
-    for q in range(plane_count):
-        rows_q = ordered[0]
-        for flip in range(1, plane_count):
-            rows_q = jnp.where(plane ^ q == flip, ordered[flip], rows_q)
-        in_order.append(rows_q)
+    in_order = [pick(ordered, q, half) for q in range(plane_count) for half in (0, 1)]
     mine = lax.dynamic_slice_in_dim(jnp.concatenate(in_order), plane * foot_share, foot_share, 2)
     trace_out = jnp.transpose(mine, (2, 1, 0))
 
     back_projected = pl.pallas_call(
-        functools.partial(backward_kernel, plane_count),
+        functools.partial(backward_kernel, back_keys, wide),
         out_shape=shaped(movie_frames.shape),
-        in_specs=[SMEM] + [VMEM] * (3 + plane_count),
+        in_specs=[SMEM] + [VMEM] * (3 + len(back_keys)),
         out_specs=HBM,
         scratch_shapes=[
             pltpu.VMEM(((rows + 2 * BLOCK) * frames, width), BF16),
@@ -484,9 +511,8 @@
             pltpu.SemaphoreType.DMA((rows // BLOCK,)),
         ],
         compiler_params=pltpu.CompilerParams(vmem_limit_bytes=32 * mib),
-        cost_estimate=pl.CostEstimate(flops=1000000000, bytes_accessed=3 * mib, transcendentals=0),
         name="backward",
-    )(place, tip, col_adj, row_adj, *residual)
+    )(place, tip, col_adj, row_adj, *[residual[key] for key in back_keys])
     return trace_out, back_projected
 
 

time: 49.6 us -> 49 us (0.988)
  Pallas kernels: 18.5 us -> 21.9 us
  starting transfers between devices: 19.6 us -> 16.7 us
  waiting for transfers between devices: 7.73 us -> 6.44 us
    ppermute x14 -> x11, starting transfers between devices: 19.6 us -> 15.5 us  [exchange(): return lax.ppermute(cells, axis, [(i, i ^ flip) for i in range(count)])]
    pallas_call x9 -> x13, Pallas kernels: 14.8 us -> 18.2 us  [the longest x4 7.79 us: subtract(): call(functools.partial(residual_kernel, flip, far, wide, spots), 'residua...]
    ppermute x14 -> x11, waiting for transfers between devices: 7.73 us -> 4.36 us  [exchange(): return lax.ppermute(cells, axis, [(i, i ^ flip) for i in range(count)])]
    ppermute x0 -> x2, waiting for transfers between devices: none -> 2.08 us  [crossed(): return lax.ppermute(cells, ('wide', 'planes'), pairs)]
    ppermute x0 -> x2, starting transfers between devices: none -> 1.22 us  [crossed(): return lax.ppermute(cells, ('wide', 'planes'), pairs)]
  transfers between devices with their start and end apart: 14 -> 13, of which waited for: 5 -> 5; matrix products, arithmetic and copies ran while one was open for 4% -> 4% of each run, Pallas kernels for 18% -> 26%
where the time goes in v6:
time: 49 us; the launch traced here: 48.8 us
  Pallas kernels  21.9 us (45%)
  starting transfers between devices  16.7 us (34%)
  waiting for transfers between devices  6.44 us (13%)
  local copies, waits for them, and re-layouts  2.24 us (5%)
  between operations  0.85 us (2%)
  other arithmetic  0.63 us (1%)
    ppermute x11, starting transfers between devices, exchange(): return lax.ppermute(cells, axis, [(i, i ^ flip) for i in range(count)])  15.5 us
    pallas_call x4, Pallas kernels, subtract(): call(functools.partial(residual_kernel, flip, far, wide, spots), 'residua...  7.79 us
    pallas_call x4, Pallas kernels, on_device(): call(functools.partial(forward_kernel, flip, far, turn == 0, wide, halves...  6.58 us
    ppermute x11, waiting for transfers between devices, exchange(): return lax.ppermute(cells, axis, [(i, i ^ flip) for i in range(count)])  4.36 us
    pallas_call x1, Pallas kernels, on_device(): pl.pallas_call(functools.partial(backward_kernel, back_keys, wide), out_s...  2.91 us
    pallas_call x1, Pallas kernels, on_device(): pl.pallas_call(functools.partial(prepare_kernel, rim, cuts), out_shape=(s...  2.67 us
    ppermute x2, waiting for transfers between devices, crossed(): return lax.ppermute(cells, ('wide', 'planes'), pairs)  2.08 us
    unnamed x12, local copies, waits for them, and re-layouts  1.31 us
  transfers between devices with their start and end apart: 13, of which 5 were waited for; matrix products, arithmetic and copies ran while one was open for 4% of the time, Pallas kernels for 26%

profile of v6, /device:TPU:1, one launch (start us, length us, event | category | flops | bytes accessed | tf_op | source)
XLA Modules:
  0.0 48.8 jit_solution(13604196501516412939)
XLA Ops:
  0.6 0.9 %constant_dynamic-slice_fusion = bf16[2,16,16,128]{3,2,1,0:T(8,128)(2,1)S(1)} fusion(bf16[2,16,128,128]{3,2,1,0:T(8,128)(2,1)} %movie_hbm.1, s32[]{:T(128)S(6)} %select_n.131), kind=kLoop, calls=%fused_computation.13 | loop fusion | bytes 262148 | tf_op jit(solution)/shard_map/dynamic_slice | solution.py:370
  1.6 0.1 collective-permute-start
  1.7 2.7 %prepare.1 = (bf16[16,160,256]{2,1,0:T(8,128)(2,1)S(1)}, bf16[128,128]{1,0:T(8,128)(2,1)S(1)}, bf16[256,768]{1,0:T(8,128)(2,1)S(1)}, s32[128,128]{1,0:T(8,128)S(...) custom-call(f32[25]{0:T(128)} %col_ref, f32[25]{0:T(128)} %row_ref, bf16[2,16,128,128]{3,2,1,0:T(8,128)(2,1)} %movie_hbm.1, ...), custom_call_target="tpu_custom_call" | custom-call | tf_op jit(solution)/shard_map/prepare/pallas_call | solution.py:373
  4.4 0.0 copy-start.3
  4.4 0.1 pad_add_fusion.place_ref
  4.5 0.0 collective-permute-done.edge_ref
  4.5 1.8 %forward.4 = (bf16[16,160,256]{2,1,0:T(8,128)(2,1)S(1)}, bf16[512,256]{1,0:T(8,128)(2,1)S(1)}, bf16[512,128]{1,0:T(8,128)(2,1)S(1)}) custom-call(s32[3]{0:T(128)S(1)} %pad_add_fusion.place_ref, bf16[16,160,256]{2,1,0:T(8,128)(2,1)S(1)} %get-tuple-element.48.smooth_in_ref, ...), custom_call_target="tpu_custom_call", output_to_operand_aliasing={{0}: (1, {})} | custom-call | tf_op jit(solution)/shard_map/forward/pallas_call | solution.py:410
  6.2 0.0 copy-start.4
  6.3 1.6 %forward.5 = (bf16[16,160,256]{2,1,0:T(8,128)(2,1)S(1)}, bf16[512,256]{1,0:T(8,128)(2,1)S(1)}, bf16[512,128]{1,0:T(8,128)(2,1)S(1)}) custom-call(s32[3]{0:T(128)S(1)} %pad_add_fusion.place_ref, bf16[16,160,256]{2,1,0:T(8,128)(2,1)S(1)} %get-tuple-element.53.smooth_in_ref, ...), custom_call_target="tpu_custom_call", output_to_operand_aliasing={{0}: (1, {})} | custom-call | tf_op jit(solution)/shard_map/forward/pallas_call | solution.py:410
  7.9 2.7 %collective-permute-start.2 = (bf16[512,128]{1,0:T(8,128)(2,1)S(1)}, bf16[512,128]{1,0:T(8,128)(2,1)S(1)}, u32[]{:S(2)}, u32[]{:S(2)}) collective-permute-start(bf16[512,128]{1,0:T(8,128)(2,1)S(1)} %get-tuple-element.63), channel_id=1, source_target_pairs={{0,2},{2,0},{1,3},{3,1},{4,6},{6,4},{5,7},{7,5},{8,10},{10,8},{9,1... | collective-permute-start | bytes 393224 | tf_op jit(solution)/shard_map/ppermute | solution.py:19
  10.6 0.1 collective-permute-start.1
  10.7 0.1 broadcast_multiply_fusion
  10.8 0.1 select_reduce_fusion
  10.9 1.6 %forward.6 = (bf16[16,160,256]{2,1,0:T(8,128)(2,1)S(1)}, bf16[512,256]{1,0:T(8,128)(2,1)S(1)}, bf16[512,128]{1,0:T(8,128)(2,1)S(1)}) custom-call(s32[3]{0:T(128)S(1)} %pad_add_fusion.place_ref, bf16[16,160,256]{2,1,0:T(8,128)(2,1)S(1)} %get-tuple-element.58.smooth_in_ref, ...), custom_call_target="tpu_custom_call", output_to_operand_aliasing={{0}: (1, {})} | custom-call | tf_op jit(solution)/shard_map/forward/pallas_call | solution.py:410
  12.5 0.0 copy-start.1
  12.5 0.0 copy-start.2
  12.5 1.6 %forward.7 = (bf16[16,160,256]{2,1,0:T(8,128)(2,1)S(1)}, bf16[512,256]{1,0:T(8,128)(2,1)S(1)}, bf16[512,128]{1,0:T(8,128)(2,1)S(1)}) custom-call(s32[3]{0:T(128)S(1)} %pad_add_fusion.place_ref, bf16[16,160,256]{2,1,0:T(8,128)(2,1)S(1)} %get-tuple-element.61.smooth_in_ref, ...), custom_call_target="tpu_custom_call", output_to_operand_aliasing={{0}: (1, {})} | custom-call | tf_op jit(solution)/shard_map/forward/pallas_call | solution.py:410
  14.2 0.3 collective-permute-done.2.refs_1_
  14.5 3.4 %collective-permute-start.5 = (bf16[272,128]{1,0:T(8,128)(2,1)S(1)}, bf16[272,128]{1,0:T(8,128)(2,1)S(1)}, u32[]{:S(2)}, u32[]{:S(2)}) collective-permute-start(bf16[272,128]{1,0:T(8,128)(2,1)S(1)} %sum.5), channel_id=1, source_target_pairs={{0,12},{4,8},{8,4},{12,0},{1,13},{5,9},{9,5},{13,1},{2,14},{6,10},... | collective-permute-start | bytes 208904 | tf_op jit(solution)/shard_map/ppermute | solution.py:19
  17.9 0.1 collective-permute-start.4
  18.0 0.0 collective-permute-done.1.refs_1_
  18.0 0.6 %collective-permute-start.3 = (bf16[272,128]{1,0:T(8,128)(2,1)S(1)}, bf16[272,128]{1,0:T(8,128)(2,1)S(1)}, u32[]{:S(2)}, u32[]{:S(2)}) collective-permute-start(bf16[272,128]{1,0:T(8,128)(2,1)S(1)} %sum.3), channel_id=1, source_target_pairs={{0,4},{4,0},{8,12},{12,8},{1,5},{5,1},{9,13},{13,9},{2,6},{6,2},{1... | collective-permute-start | bytes 208904 | tf_op jit(solution)/shard_map/ppermute | solution.py:19
  18.7 1.0 %bands.1 = (bf16[256,256]{1,0:T(8,128)(2,1)S(1)}, bf16[256,768]{1,0:T(8,128)(2,1)S(1)}) custom-call(f32[25]{0:T(128)S(1)} %copy-done, f32[25]{0:T(128)S(1)} %copy-done.1), custom_call_target="tpu_custom_call" | custom-call | tf_op jit(solution)/shard_map/bands/pallas_call | solution.py:443
  19.7 0.0 collective-permute-done.5.refs_4_
  19.7 3.7 %collective-permute-done.4.refs_3_ = bf16[272,128]{1,0:T(8,128)(2,1)S(1)} collective-permute-done((bf16[272,128]{1,0:T(8,128)(2,1)S(1)}, bf16[272,128]{1,0:T(8,128)(2,1)S(1)}, u32[]{:S(2)}, u32[]{:S(2)}) %collective-permute-start.4) | collective-permute-done | bytes 69664 | tf_op jit(solution)/shard_map/ppermute | solution.py:19
  23.4 0.0 collective-permute-done.3.refs_2_
  23.4 0.9 %mix.1 = (bf16[16,16,128]{2,1,0:T(8,128)(2,1)S(1)}, bf16[16,16,128]{2,1,0:T(8,128)(2,1)S(1)}, bf16[16,16,128]{2,1,0:T(8,128)(2,1)S(1)}, bf16[16,16,128]{2,1,0:T(8,128)(2,1)S(1)}) custom-call(s32[3]{0:T(128)S(1)} %pad_add_fusion.place_ref, s32[128]{0:T(128)S(1)} %bitcast.13, bf16[16,128]{1,0:T(8,128)(2,1)S(1)} %pad_bitcast_fusion.lag_ref, ...), custom_call_target="tpu_custom_call" | custom-call | tf_op jit(solution)/shard_map/mix/pallas_call | solution.py:452
  24.3 0.1 collective-permute-start.10
  24.4 1.0 %collective-permute-start.6 = (bf16[16,16,128]{2,1,0:T(8,128)(2,1)S(1)}, bf16[16,16,128]{2,1,0:T(8,128)(2,1)S(1)}, u32[]{:S(2)}, u32[]{:S(2)}) collective-permute-start(bf16[16,16,128]{2,1,0:T(8,128)(2,1)S(1)} %get-tuple-element.69), channel_id=1, source_target_pairs={{0,8},{4,12},{8,0},{12,4},{1,9},{5,13},{9,1},{13,5},{2,10},{6,14},... | collective-permute-start | bytes 196616 | tf_op jit(solution)/shard_map/ppermute | solution.py:19
  25.4 2.5 %collective-permute-start.7 = (bf16[16,16,128]{2,1,0:T(8,128)(2,1)S(1)}, bf16[16,16,128]{2,1,0:T(8,128)(2,1)S(1)}, u32[]{:S(2)}, u32[]{:S(2)}) collective-permute-start(bf16[16,16,128]{2,1,0:T(8,128)(2,1)S(1)} %get-tuple-element.70), channel_id=1, source_target_pairs={{0,12},{4,8},{8,4},{12,0},{1,13},{5,9},{9,5},{13,1},{2,14},{6,10},... | collective-permute-start | bytes 196616 | tf_op jit(solution)/shard_map/ppermute | solution.py:19
  27.9 1.2 %collective-permute-start.8 = (bf16[16,16,128]{2,1,0:T(8,128)(2,1)S(1)}, bf16[16,16,128]{2,1,0:T(8,128)(2,1)S(1)}, u32[]{:S(2)}, u32[]{:S(2)}) collective-permute-start(bf16[16,16,128]{2,1,0:T(8,128)(2,1)S(1)} %get-tuple-element.71.refs_0_), channel_id=1, source_target_pairs={{0,2},{2,0},{4,6},{6,4},{8,10},{10,8},{12,14},{14,12},{1,3},{3,1},... | collective-permute-start | bytes 196616 | tf_op jit(solution)/shard_map/ppermute | solution.py:29
  29.1 0.0 collective-permute-start.9
  29.1 0.0 collective-permute-done.10.refs_1_
  29.1 1.9 %residual.4 = (bf16[512,256]{1,0:T(8,128)(2,1)S(1)}, bf16[256,256]{1,0:T(8,128)(2,1)S(1)}, bf16[32,16,128]{2,1,0:T(8,128)(2,1)S(1)}) custom-call(s32[3]{0:T(128)S(1)} %pad_add_fusion.place_ref, bf16[512,256]{1,0:T(8,128)(2,1)S(1)} %get-tuple-element.73.filtered_ref, s32[128,128]{1,0:T(8,128)S(1)} %get-tuple-element.51.code_ref, ...), custom_call_target="tpu_custom_call" | custom-call | tf_op jit(solution)/shard_map/residual/pallas_call | solution.py:472
  31.1 0.0 collective-permute-done.6.refs_0_
  31.1 0.0 collective-permute-done.7.refs_1_
  31.1 0.2 collective-permute-done.8.refs_0_
  31.3 1.9 %collective-permute-done.9.refs_1_ = bf16[16,16,128]{2,1,0:T(8,128)(2,1)S(1)} collective-permute-done((bf16[16,16,128]{2,1,0:T(8,128)(2,1)S(1)}, bf16[16,16,128]{2,1,0:T(8,128)(2,1)S(1)}, u32[]{:S(2)}, u32[]{:S(2)}) %collective-permute-start.9) | collective-permute-done | bytes 65568 | tf_op jit(solution)/shard_map/ppermute | solution.py:29
  33.2 0.3 collective-permute-start.11
  33.5 1.9 %residual.7 = (bf16[512,256]{1,0:T(8,128)(2,1)S(1)}, bf16[256,256]{1,0:T(8,128)(2,1)S(1)}, bf16[32,16,128]{2,1,0:T(8,128)(2,1)S(1)}) custom-call(s32[3]{0:T(128)S(1)} %pad_add_fusion.place_ref, bf16[512,256]{1,0:T(8,128)(2,1)S(1)} %get-tuple-element.82.filtered_ref, s32[128,128]{1,0:T(8,128)S(1)} %get-tuple-element.51.code_ref, ...), custom_call_target="tpu_custom_call" | custom-call | tf_op jit(solution)/shard_map/residual/pallas_call | solution.py:472
  35.5 1.9 %residual.6 = (bf16[512,256]{1,0:T(8,128)(2,1)S(1)}, bf16[256,256]{1,0:T(8,128)(2,1)S(1)}, bf16[32,16,128]{2,1,0:T(8,128)(2,1)S(1)}) custom-call(s32[3]{0:T(128)S(1)} %pad_add_fusion.place_ref, bf16[512,256]{1,0:T(8,128)(2,1)S(1)} %get-tuple-element.78.filtered_ref, s32[128,128]{1,0:T(8,128)S(1)} %get-tuple-element.51.code_ref, ...), custom_call_target="tpu_custom_call" | custom-call | tf_op jit(solution)/shard_map/residual/pallas_call | solution.py:472
  37.4 0.4 collective-permute-done.11.refs_0_
  37.8 1.9 %residual.5 = (bf16[512,256]{1,0:T(8,128)(2,1)S(1)}, bf16[256,256]{1,0:T(8,128)(2,1)S(1)}, bf16[32,16,128]{2,1,0:T(8,128)(2,1)S(1)}) custom-call(s32[3]{0:T(128)S(1)} %pad_add_fusion.place_ref, bf16[512,256]{1,0:T(8,128)(2,1)S(1)} %get-tuple-element.54.filtered_ref, s32[128,128]{1,0:T(8,128)S(1)} %get-tuple-element.51.code_ref, ...), custom_call_target="tpu_custom_call" | custom-call | tf_op jit(solution)/shard_map/residual/pallas_call | solution.py:472
  39.8 4.5 %collective-permute-start.12 = (bf16[256,256]{1,0:T(8,128)(2,1)S(1)}, bf16[256,256]{1,0:T(8,128)(2,1)S(1)}, u32[]{:S(2)}, u32[]{:S(2)}) collective-permute-start(bf16[256,256]{1,0:T(8,128)(2,1)S(1)} %select_select_fusion), channel_id=1, source_target_pairs={{0,1},{1,0},{2,3},{3,2},{4,5},{5,4},{6,7},{7,6},{8,9},{9,8},{10,11... | collective-permute-start | bytes 393224 | tf_op jit(solution)/shard_map/ppermute | solution.py:19
  44.3 0.1 select_select_fusion.4
  44.4 0.2 fusion
  44.6 1.3 %copy.16 = bf16[64,16,128]{2,1,0:T(8,128)(2,1)} copy(bf16[64,16,128]{0,1,2:T(8,128)(2,1)S(1)} %fusion) | data formatting | bytes 524288
  45.9 2.9 %backward.1 = bf16[2,16,128,128]{3,2,1,0:T(8,128)(2,1)} custom-call(s32[3]{0:T(128)S(1)} %pad_add_fusion.place_ref, bf16[256,256]{1,0:T(8,128)(2,1)S(1)} %collective-permute-done.12.edge_ref, bf16[256,256]{1,0:T(8,128)(2,1)S(1)} %get-tuple-element.88.col_adj_ref, bf16[256,768]{1,0:T(8,128)(2,1)S(1)} %get-tuple-element.89.row_adj_ref, ...), custom_call_target="tpu_custom_call" | custom-call | tf_op jit(solution)/shard_map/backward/pallas_call | solution.py:503
  (16 shorter events, 0.1 us)
Async XLA Ops:
  1.6 2.9 %collective-permute-start = (bf16[2,16,16,128]{3,2,1,0:T(8,128)(2,1)S(1)}, bf16[2,16,16,128]{3,2,1,0:T(8,128)(2,1)S(1)}, u32[]{:S(2)}, u32[]{:S(2)}) collective-permute-start(bf16[2,16,16,128]{3,2,1,0:T(8,128)(2,1)S(1)} %constant_dynamic-slice_fusion), channel_id=1, source_target_pairs={{0,1},{1,0},{2,3},{3,2},{4,5},{5,4},{6,7},{7,6},{8,9},{9,8},{10,11... | collective-permute-start | bytes 393224 | tf_op jit(solution)/shard_map/ppermute | solution.py:19
  4.4 1.9 %copy-start.3 = (f32[1,3,65]{2,0,1:T(1,128)S(1)}, f32[1,3,65]{2,0,1:T(1,128)}, u32[]{:S(2)}) copy-start(f32[1,3,65]{2,0,1:T(1,128)} %param.16) | copy-start | bytes 2344
  6.2 4.4 %copy-start.4 = (s32[1,3]{1,0:T(1,128)S(1)}, s32[1,3]{1,0:T(1,128)}, u32[]{:S(2)}) copy-start(s32[1,3]{1,0:T(1,128)} %param.17) | copy-start | bytes 40
  7.9 6.5 %collective-permute-start.2 = (bf16[512,128]{1,0:T(8,128)(2,1)S(1)}, bf16[512,128]{1,0:T(8,128)(2,1)S(1)}, u32[]{:S(2)}, u32[]{:S(2)}) collective-permute-start(bf16[512,128]{1,0:T(8,128)(2,1)S(1)} %get-tuple-element.63), channel_id=1, source_target_pairs={{0,2},{2,0},{1,3},{3,1},{4,6},{6,4},{5,7},{7,5},{8,10},{10,8},{9,1... | collective-permute-start | bytes 393224 | tf_op jit(solution)/shard_map/ppermute | solution.py:19
  10.6 7.4 %collective-permute-start.1 = (bf16[512,128]{1,0:T(8,128)(2,1)S(1)}, bf16[512,128]{1,0:T(8,128)(2,1)S(1)}, u32[]{:S(2)}, u32[]{:S(2)}) collective-permute-start(bf16[512,128]{1,0:T(8,128)(2,1)S(1)} %get-tuple-element.60), channel_id=1, source_target_pairs={{0,2},{2,0},{1,3},{3,1},{4,6},{6,4},{5,7},{7,5},{8,10},{10,8},{9,1... | collective-permute-start | bytes 393224 | tf_op jit(solution)/shard_map/ppermute | solution.py:19
  12.5 6.2 %copy-start = (f32[25]{0:T(128)S(1)}, f32[25]{0:T(128)}, u32[]{:S(2)}) copy-start(f32[25]{0:T(128)} %col_ref) | copy-start | bytes 304
  12.5 6.2 %copy-start.1 = (f32[25]{0:T(128)S(1)}, f32[25]{0:T(128)}, u32[]{:S(2)}) copy-start(f32[25]{0:T(128)} %row_ref) | copy-start | bytes 304
  12.5 10.9 %copy-start.2 = (s32[128,1]{0,1:T(1,128)S(1)}, s32[128,1]{0,1:T(1,128)}, u32[]{:S(2)}) copy-start(s32[128,1]{0,1:T(1,128)} %param.11) | copy-start | bytes 1540
  14.5 5.2 %collective-permute-start.5 = (bf16[272,128]{1,0:T(8,128)(2,1)S(1)}, bf16[272,128]{1,0:T(8,128)(2,1)S(1)}, u32[]{:S(2)}, u32[]{:S(2)}) collective-permute-start(bf16[272,128]{1,0:T(8,128)(2,1)S(1)} %sum.5), channel_id=1, source_target_pairs={{0,12},{4,8},{8,4},{12,0},{1,13},{5,9},{9,5},{13,1},{2,14},{6,10},... | collective-permute-start | bytes 208904 | tf_op jit(solution)/shard_map/ppermute | solution.py:19
  17.9 5.5 %collective-permute-start.4 = (bf16[272,128]{1,0:T(8,128)(2,1)S(1)}, bf16[272,128]{1,0:T(8,128)(2,1)S(1)}, u32[]{:S(2)}, u32[]{:S(2)}) collective-permute-start(bf16[272,128]{1,0:T(8,128)(2,1)S(1)} %sum.4), channel_id=1, source_target_pairs={{0,8},{4,12},{8,0},{12,4},{1,9},{5,13},{9,1},{13,5},{2,10},{6,14},... | collective-permute-start | bytes 208904 | tf_op jit(solution)/shard_map/ppermute | solution.py:19
  18.0 5.4 %collective-permute-start.3 = (bf16[272,128]{1,0:T(8,128)(2,1)S(1)}, bf16[272,128]{1,0:T(8,128)(2,1)S(1)}, u32[]{:S(2)}, u32[]{:S(2)}) collective-permute-start(bf16[272,128]{1,0:T(8,128)(2,1)S(1)} %sum.3), channel_id=1, source_target_pairs={{0,4},{4,0},{8,12},{12,8},{1,5},{5,1},{9,13},{13,9},{2,6},{6,2},{1... | collective-permute-start | bytes 208904 | tf_op jit(solution)/shard_map/ppermute | solution.py:19
  24.3 4.8 %collective-permute-start.10 = (bf16[16,16,128]{2,1,0:T(8,128)(2,1)S(1)}, bf16[16,16,128]{2,1,0:T(8,128)(2,1)S(1)}, u32[]{:S(2)}, u32[]{:S(2)}) collective-permute-start(bf16[16,16,128]{2,1,0:T(8,128)(2,1)S(1)} %get-tuple-element.72), channel_id=1, source_target_pairs={{0,4},{4,0},{8,12},{12,8},{1,5},{5,1},{9,13},{13,9},{2,6},{6,2},{1... | collective-permute-start | bytes 196616 | tf_op jit(solution)/shard_map/ppermute | solution.py:19
  24.4 6.7 %collective-permute-start.6 = (bf16[16,16,128]{2,1,0:T(8,128)(2,1)S(1)}, bf16[16,16,128]{2,1,0:T(8,128)(2,1)S(1)}, u32[]{:S(2)}, u32[]{:S(2)}) collective-permute-start(bf16[16,16,128]{2,1,0:T(8,128)(2,1)S(1)} %get-tuple-element.69), channel_id=1, source_target_pairs={{0,8},{4,12},{8,0},{12,4},{1,9},{5,13},{9,1},{13,5},{2,10},{6,14},... | collective-permute-start | bytes 196616 | tf_op jit(solution)/shard_map/ppermute | solution.py:19
  25.4 5.7 %collective-permute-start.7 = (bf16[16,16,128]{2,1,0:T(8,128)(2,1)S(1)}, bf16[16,16,128]{2,1,0:T(8,128)(2,1)S(1)}, u32[]{:S(2)}, u32[]{:S(2)}) collective-permute-start(bf16[16,16,128]{2,1,0:T(8,128)(2,1)S(1)} %get-tuple-element.70), channel_id=1, source_target_pairs={{0,12},{4,8},{8,4},{12,0},{1,13},{5,9},{9,5},{13,1},{2,14},{6,10},... | collective-permute-start | bytes 196616 | tf_op jit(solution)/shard_map/ppermute | solution.py:19
  27.9 3.4 %collective-permute-start.8 = (bf16[16,16,128]{2,1,0:T(8,128)(2,1)S(1)}, bf16[16,16,128]{2,1,0:T(8,128)(2,1)S(1)}, u32[]{:S(2)}, u32[]{:S(2)}) collective-permute-start(bf16[16,16,128]{2,1,0:T(8,128)(2,1)S(1)} %get-tuple-element.71.refs_0_), channel_id=1, source_target_pairs={{0,2},{2,0},{4,6},{6,4},{8,10},{10,8},{12,14},{14,12},{1,3},{3,1},... | collective-permute-start | bytes 196616 | tf_op jit(solution)/shard_map/ppermute | solution.py:29
  29.1 4.1 %collective-permute-start.9 = (bf16[16,16,128]{2,1,0:T(8,128)(2,1)S(1)}, bf16[16,16,128]{2,1,0:T(8,128)(2,1)S(1)}, u32[]{:S(2)}, u32[]{:S(2)}) collective-permute-start(bf16[16,16,128]{2,1,0:T(8,128)(2,1)S(1)} %get-tuple-element.72), channel_id=1, source_target_pairs={{0,6},{2,4},{4,2},{6,0},{8,14},{10,12},{12,10},{14,8},{1,7},{3,5},... | collective-permute-start | bytes 196616 | tf_op jit(solution)/shard_map/ppermute | solution.py:29
  33.2 4.6 %collective-permute-start.11 = (bf16[32,16,128]{2,1,0:T(8,128)(2,1)S(1)}, bf16[32,16,128]{2,1,0:T(8,128)(2,1)S(1)}, u32[]{:S(2)}, u32[]{:S(2)}) collective-permute-start(bf16[32,16,128]{2,1,0:T(8,128)(2,1)S(1)} %pad_maximum_fusion), channel_id=1, source_target_pairs={{0,2},{2,0},{1,3},{3,1},{4,6},{6,4},{5,7},{7,5},{8,10},{10,8},{9,1... | collective-permute-start | bytes 393224 | tf_op jit(solution)/shard_map/ppermute | solution.py:19
  39.8 6.1 %collective-permute-start.12 = (bf16[256,256]{1,0:T(8,128)(2,1)S(1)}, bf16[256,256]{1,0:T(8,128)(2,1)S(1)}, u32[]{:S(2)}, u32[]{:S(2)}) collective-permute-start(bf16[256,256]{1,0:T(8,128)(2,1)S(1)} %select_select_fusion), channel_id=1, source_target_pairs={{0,1},{1,0},{2,3},{3,2},{4,5},{5,4},{6,7},{7,6},{8,9},{9,8},{10,11... | collective-permute-start | bytes 393224 | tf_op jit(solution)/shard_map/ppermute | solution.py:19

commit v7 on v6

--- a/solution.py
+++ b/solution.py
@@ -11,7 +11,7 @@
 LANES = 128
 F32 = jnp.float32
 BF16 = jnp.bfloat16
-REP, PLANE, WIDE = 0, 1, 2
+REP, PLANE, WIDE = "rep", "planes", "wide"
 
 
 def exchange(cells, axis, flip):
@@ -41,6 +41,16 @@
     return row[:1]
 
 
+def quotient(x, n):
+    if n & (n - 1) == 0:
+        return lax.shift_right_logical(x, n.bit_length() - 1)
+    return lax.shift_right_logical(x * (65536 // n + 1), 16)
+
+
+def remainder(x, n):
+    return x & (n - 1) if n & (n - 1) == 0 else x - n * quotient(x, n)
+
+
 def toeplitz(row, count, shift=0):
     return pltpu.roll(
         jnp.broadcast_to(row, (count, row.shape[1])), shift, 1, stride=1, stride_axis=0
@@ -56,27 +66,27 @@
 def row_band_forward(taps_ref, rim, frames):
     out_rows, depth, span = BLOCK * frames, 3 * BLOCK * frames, 3 * BLOCK
     band = toeplitz(tap_row(taps_ref, lambda k: k + BLOCK - rim), BLOCK)[:, :span].astype(BF16)
-    left = (iota((out_rows, BLOCK), 0) // frames == iota((out_rows, BLOCK), 1)).astype(BF16)
-    right = (lax.rem(iota((span, depth), 1), span) == iota((span, depth), 0)).astype(BF16)
+    left = (quotient(iota((out_rows, BLOCK), 0), frames) == iota((out_rows, BLOCK), 1)).astype(BF16)
+    right = (remainder(iota((span, depth), 1), span) == iota((span, depth), 0)).astype(BF16)
     tall = jnp.dot(left, band, preferred_element_type=F32).astype(BF16)
     spread = jnp.dot(tall, right, preferred_element_type=F32)
-    start = iota((out_rows, depth), 1) - span * lax.rem(iota((out_rows, depth), 0), frames)
+    start = iota((out_rows, depth), 1) - span * remainder(iota((out_rows, depth), 0), frames)
     return jnp.where((start >= 0) & (start < span), spread, 0.0).astype(BF16)
 
 
 def row_band_adjoint(taps_ref, rim, frames):
     out_rows, depth, span = BLOCK * frames, 3 * BLOCK * frames, 3 * BLOCK
     band = toeplitz(tap_row(taps_ref, lambda k: BLOCK + rim - k), BLOCK)[:, :span].astype(BF16)
-    left = (lax.rem(iota((out_rows, BLOCK), 0), BLOCK) == iota((out_rows, BLOCK), 1)).astype(BF16)
-    right = (iota((span, depth), 1) // frames == iota((span, depth), 0)).astype(BF16)
+    left = (remainder(iota((out_rows, BLOCK), 0), BLOCK) == iota((out_rows, BLOCK), 1)).astype(BF16)
+    right = (quotient(iota((span, depth), 1), frames) == iota((span, depth), 0)).astype(BF16)
     tall = jnp.dot(left, band, preferred_element_type=F32).astype(BF16)
     spread = jnp.dot(tall, right, preferred_element_type=F32)
-    same = lax.rem(iota((out_rows, depth), 1), frames) == iota((out_rows, depth), 0) // BLOCK
+    same = remainder(iota((out_rows, depth), 1), frames) == quotient(iota((out_rows, depth), 0), BLOCK)
     return jnp.where(same, spread, 0.0).astype(BF16)
 
 
-def half_of(place_ref, flip, far, wide):
-    return (place_ref[PLANE] ^ flip) * 2 + ((place_ref[WIDE] // (wide // 2)) ^ far)
+def half_of(flip, far, wide):
+    return (lax.axis_index(PLANE) ^ flip) * 2 + (quotient(lax.axis_index(WIDE), wide // 2) ^ far)
 
 
 def per_frame(rows, frames, copies):
@@ -134,7 +144,7 @@
 
 
 def forward_kernel(
-    flip, far, fill, wide, ks, place_ref, smooth_in_ref, edge_ref, col_fwd_ref, row_fwd_ref, code_ref,
+    flip, far, fill, wide, ks, smooth_in_ref, edge_ref, col_fwd_ref, row_fwd_ref, code_ref,
     templates_ref, smooth_ref, filtered_ref, out_ref, projected_ref,
 ):
     frames, padded_rows, width = smooth_ref.shape
@@ -146,12 +156,12 @@
                 preferred_element_type=F32,
             ).reshape(frames, BLOCK, LANES)
             lanes = slice(p * LANES, (p + 1) * LANES)
-            above = jnp.where(place_ref[REP] > 0, edge, 0.0).astype(BF16)
-            below = jnp.where(place_ref[REP] > 0, 0.0, edge).astype(BF16)
+            above = jnp.where(lax.axis_index(REP) > 0, edge, 0.0).astype(BF16)
+            below = jnp.where(lax.axis_index(REP) > 0, 0.0, edge).astype(BF16)
             smooth_ref[:, :BLOCK, lanes] = above
             smooth_ref[:, BLOCK + rows :, lanes] = below
     here = filtered_ref.shape[0] // frames
-    first = half_of(place_ref, flip, far, wide) * here
+    first = half_of(flip, far, wide) * here
     tiles = templates_ref.shape[1] // LANES
     def along(b):
         near = smooth_ref[:, pl.ds(pl.multiple_of(first + b * BLOCK, BLOCK), 3 * BLOCK), :]
@@ -168,7 +178,7 @@
         dense = jnp.dot(filtered, templates_ref[...], preferred_element_type=F32)
         cells = along(b + 1) if b + 1 < here // BLOCK else None
         picked = per_frame(code >> 1, frames, 1)
-        lane, tile = picked & (LANES - 1), picked // LANES
+        lane, tile = picked & (LANES - 1), quotient(picked, LANES)
         chosen = jnp.zeros(picked.shape, F32)
         for t in range(tiles):
             found = jnp.take_along_axis(
@@ -178,7 +188,7 @@
         projected_ref[spot, :] = chosen.astype(BF16)
     size = out_ref.shape[0] // len(ks)
     for i, k in enumerate(ks):
-        start = pl.multiple_of(((place_ref[WIDE] ^ k) & (wide // 2 - 1)) * size, size)
+        start = pl.multiple_of(((lax.axis_index(WIDE) ^ k) & (wide // 2 - 1)) * size, size)
         out_ref[i * size : (i + 1) * size, :] = projected_ref[pl.ds(start, size), :]
 
 
@@ -197,30 +207,32 @@
     out_ref[rows:, :] = lag_ref[...]
 
 
-def mix_kernel(wide, spots, place_ref, owner_ref, lag_ref, *refs):
+def mix_kernel(wide, spots, owner_ref, lag_ref, *refs):
     parts, refs = refs[: len(spots)], refs[len(spots) :]
     blocks, outs = refs[: wide - 1], refs[wide - 1 : 2 * wide - 1]
-    cells_ref, kernels_ref, traces_ref, tables_ref = refs[2 * wide - 1 :]
+    cells_ref, kernels_ref, traces_ref = refs[2 * wide - 1 :]
     _, share, frames, lanes = cells_ref.shape
     total = wide * frames
-    here = place_ref[WIDE]
+    here = lax.axis_index(WIDE)
     cells_ref[here] = add_all(parts, spots, share * frames).reshape(share, frames, lanes)
     kernels_ref[here] = lag_ref[...].astype(F32)
     for k, block in enumerate(blocks, 1):
         cells_ref[here ^ k] = block[: share * frames, :].reshape(share, frames, lanes)
         kernels_ref[here ^ k] = block[share * frames :, :].astype(F32)
-
-    def table(values):
-        row = jnp.concatenate([values[i : i + 1, :] for i in range(2 * total // LANES)], axis=1)
-        return toeplitz(row, total, total + 1)[:, :total].astype(BF16)
-
-    if wide <= share:
-        for d in range(wide):
-            tables_ref[d] = table(kernels_ref[d])
-    first = (place_ref[PLANE] * wide + here) * share
+    first = (lax.axis_index(PLANE) * wide + here) * share
+    owners = owner_ref[...]
+    lane = iota(owners.shape, 1)
     for h in range(share):
-        owner = owner_ref[first + h]
-        lag = tables_ref[owner] if wide <= share else table(kernels_ref[owner])
+        owner = jnp.sum(jnp.where(lane == first + h, owners, 0), axis=1, keepdims=True)
+        owner = jnp.broadcast_to(owner, (8, lanes))
+        row = []
+        for i in range(0, kernels_ref.shape[1], 8):
+            values = jnp.zeros((8, lanes), F32)
+            for d in range(wide):
+                values = jnp.where(owner == d, kernels_ref[d, i : i + 8, :], values)
+            row += [values[n : n + 1, :] for n in range(8)]
+        row = jnp.concatenate(row[: 2 * total // lanes], axis=1)
+        lag = toeplitz(row, total, total + 1)[:, :total].astype(BF16)
         mixed = jnp.dot(lag, cells_ref[:, h].reshape(total, lanes), preferred_element_type=F32)
         traces_ref[:, h] = jnp.maximum(mixed, 0.0).astype(BF16).reshape(wide, frames, lanes)
     for k, out_ref in enumerate(outs):
@@ -236,17 +248,17 @@
     row_adj_ref[...] = row_band_adjoint(row_ref, rim, frames)
 
 
-def residual_kernel(flip, far, wide, spots, place_ref, filtered_ref, code_ref, templates_ref, *refs):
+def residual_kernel(flip, far, wide, spots, filtered_ref, code_ref, templates_ref, *refs):
     traces, (out_ref, edge_ref, ordered_ref, slots_ref) = refs[:-4], refs[-4:]
     _, frames, lanes = traces[0].shape
     share = ordered_ref.shape[0] // len(spots)
     names, width = templates_ref.shape
     tile = 2 * LANES
-    base = half_of(place_ref, flip, far, wide) * len(spots) * share
+    base = half_of(flip, far, wide) * len(spots) * share
     marks = iota((lanes, tile), 1).astype(F32).astype(BF16)
     group = min(8, share)
     for n, (k, source, offset) in enumerate(spots):
-        block = (place_ref[WIDE] ^ k) & (wide // 2 - 1)
+        block = (lax.axis_index(WIDE) ^ k) & (wide // 2 - 1)
         source, offset = traces[source], offset * share
         top = base + block * share
         for g in range(share // group):
@@ -254,7 +266,7 @@
             support = jnp.concatenate([support] * (8 // group), axis=0)
             columns = [
                 jnp.transpose(
-                    jnp.where(support // tile == t, support & (tile - 1), -1).astype(F32)
+                    jnp.where(quotient(support, tile) == t, support & (tile - 1), -1).astype(F32)
                 )
                 for t in range(names // tile)
             ]
@@ -285,19 +297,19 @@
         ).astype(BF16)
         ordered_ref[pl.ds(block * share, share)] = source[offset : offset + share]
     edge = edge_ref.shape[0]
-    start = jnp.where(place_ref[REP] > 0, 0, out_ref.shape[0] - edge)
+    start = jnp.where(lax.axis_index(REP) > 0, 0, out_ref.shape[0] - edge)
     edge_ref[...] = out_ref[pl.ds(pl.multiple_of(start, edge), edge), :]
 
 
-def backward_kernel(keys, wide, place_ref, edge_ref, col_adj_ref, row_adj_ref, *refs):
+def backward_kernel(keys, wide, edge_ref, col_adj_ref, row_adj_ref, *refs):
     parts, (out_hbm, padded_ref, out_ref, sems) = refs[: len(keys)], refs[len(keys) :]
     planes, frames, rows, _ = out_ref.shape
     edge, size = BLOCK * frames, parts[0].shape[0]
     zero = jnp.zeros_like(edge_ref)
-    padded_ref[:edge, :] = jnp.where(place_ref[REP] > 0, edge_ref[...], zero)
-    padded_ref[edge + rows * frames :, :] = jnp.where(place_ref[REP] > 0, zero, edge_ref[...])
+    padded_ref[:edge, :] = jnp.where(lax.axis_index(REP) > 0, edge_ref[...], zero)
+    padded_ref[edge + rows * frames :, :] = jnp.where(lax.axis_index(REP) > 0, zero, edge_ref[...])
     for (flip, far), part in zip(keys, parts):
-        spot = pl.multiple_of(edge + half_of(place_ref, flip, far, wide) * size, edge)
+        spot = pl.multiple_of(edge + half_of(flip, far, wide) * size, edge)
         padded_ref[pl.ds(spot, size), :] = part[...]
     def along(b):
         near = padded_ref[b * edge : (b + 3) * edge, :]
@@ -363,7 +375,6 @@
     share = here // wide
     edge = BLOCK * frames
     rep, plane, spot = lax.axis_index("rep"), lax.axis_index("planes"), lax.axis_index("wide")
-    place = jnp.stack([rep, plane, spot]).astype(jnp.int32)
     mib = 1 << 20
 
     start = jnp.where(rep == 0, rows - BLOCK, 0)
@@ -410,9 +421,9 @@
         smooth, filtered[flip, far], mine = call(
             functools.partial(forward_kernel, flip, far, turn == 0, wide, halves[far]), "forward",
             [smooth.shape, (half_rows * frames, width), (half_rows * frames, LANES)],
-            1, 6, aliases={1: 0},
+            0, 6, aliases={0: 0},
             scratch=[pltpu.VMEM((half_rows * frames, LANES), BF16)],
-        )(place, smooth, rim_rows, col_fwd, row_fwd, code, tall_templates)
+        )(smooth, rim_rows, col_fwd, row_fwd, code, tall_templates)
         projected[flip, far] = exchange(mine, "planes", flip) if flip else mine
         if turn == 0:
             gains, lags, _ = lax.optimization_barrier((lag_gains, dilations, smooth))
@@ -448,16 +459,15 @@
     own_parts[0], col_adj, row_adj = lax.optimization_barrier((own_parts[0], col_adj, row_adj))
 
     cell_shape = (wide, share, frames, LANES)
-    tables = (wide, total_frames, total_frames) if wide <= share else (1, BLOCK, LANES)
     traces = call(
         functools.partial(mix_kernel, wide, own_spots), "mix", [cell_shape[1:]] * wide,
-        2, wide + plane_count,
+        0, 1 + wide + plane_count,
         scratch=[
             pltpu.VMEM(cell_shape, BF16), pltpu.VMEM((wide, lag_rows, LANES), F32),
-            pltpu.VMEM(cell_shape, BF16), pltpu.VMEM(tables, BF16),
+            pltpu.VMEM(cell_shape, BF16),
         ],
     )(
-        place, tile_owner[:, 0], kernel_row, *own_parts, *[blocks[k] for k in range(1, wide)],
+        tile_owner.reshape(1, rows), kernel_row, *own_parts, *[blocks[k] for k in range(1, wide)],
     )
     swapped = {k: exchange(traces[k], "wide", k) for k in far_ks + near_ks[1:]}
     swapped[0] = traces[0]
@@ -472,8 +482,8 @@
         residual[flip, far], edges[flip, far], ordered[flip, far] = call(
             functools.partial(residual_kernel, flip, far, wide, spots), "residual",
             [(half_rows * frames, width), (edge, width), (half_rows, frames, LANES)],
-            1, 3 + len(got), scratch=[pltpu.VMEM((len(spots), share * frames, names), BF16)],
-        )(place, filtered[flip, far], code, flat_templates, *got)
+            0, 3 + len(got), scratch=[pltpu.VMEM((len(spots), share * frames, names), BF16)],
+        )(filtered[flip, far], code, flat_templates, *got)
 
     subtract(0, 0, [[k] for k in near_ks], [swapped[k] for k in near_ks])
     distant, direct, _ = lax.optimization_barrier(
@@ -503,7 +513,7 @@
     back_projected = pl.pallas_call(
         functools.partial(backward_kernel, back_keys, wide),
         out_shape=shaped(movie_frames.shape),
-        in_specs=[SMEM] + [VMEM] * (3 + len(back_keys)),
+        in_specs=[VMEM] * (3 + len(back_keys)),
         out_specs=HBM,
         scratch_shapes=[
             pltpu.VMEM(((rows + 2 * BLOCK) * frames, width), BF16),
@@ -512,7 +522,7 @@
         ],
         compiler_params=pltpu.CompilerParams(vmem_limit_bytes=32 * mib),
         name="backward",
-    )(place, tip, col_adj, row_adj, *[residual[key] for key in back_keys])
+    )(tip, col_adj, row_adj, *[residual[key] for key in back_keys])
     return trace_out, back_projected
 
 

time: 49 us -> 46.6 us (0.951)
  Pallas kernels: 21.9 us -> 16.9 us
  waiting for transfers between devices: 6.44 us -> 9.22 us
    ppermute x11, waiting for transfers between devices: 4.36 us -> 6.84 us  [exchange(): return lax.ppermute(cells, axis, [(i, i ^ flip) for i in range(count)])]
    pallas_call x4, Pallas kernels: 7.79 us -> 5.58 us  [subtract(): call(functools.partial(residual_kernel, flip, far, wide, spots), 'residua...]
    pallas_call x4, Pallas kernels: 6.58 us -> 4.42 us  [on_device(): call(functools.partial(forward_kernel, flip, far, turn == 0, wide, halves...]
    pallas_call x1, Pallas kernels: 2.91 us -> 2.37 us  [on_device(): pl.pallas_call(functools.partial(backward_kernel, back_keys, wide), out_s...]
  transfers between devices with their start and end apart: 13 -> 13, of which waited for: 5 -> 6; matrix products, arithmetic and copies ran while one was open for 4% -> 4% of each run, Pallas kernels for 26% -> 22%
where the time goes in v7:
time: 46.6 us; the launch traced here: 46.4 us
  Pallas kernels  16.9 us (36%)
  starting transfers between devices  16.6 us (36%)
  waiting for transfers between devices  9.22 us (20%)
  local copies, waits for them, and re-layouts  2.24 us (5%)
  between operations  0.86 us (2%)
  other arithmetic  0.54 us (1%)
    ppermute x11, starting transfers between devices, exchange(): return lax.ppermute(cells, axis, [(i, i ^ flip) for i in range(count)])  15.4 us
    ppermute x11, waiting for transfers between devices, exchange(): return lax.ppermute(cells, axis, [(i, i ^ flip) for i in range(count)])  6.84 us
    pallas_call x4, Pallas kernels, subtract(): call(functools.partial(residual_kernel, flip, far, wide, spots), 'residua...  5.58 us
    pallas_call x4, Pallas kernels, on_device(): call(functools.partial(forward_kernel, flip, far, turn == 0, wide, halves...  4.42 us
    pallas_call x1, Pallas kernels, on_device(): pl.pallas_call(functools.partial(prepare_kernel, rim, cuts), out_shape=(s...  2.66 us
    ppermute x2, waiting for transfers between devices, crossed(): return lax.ppermute(cells, ('wide', 'planes'), pairs)  2.37 us
    pallas_call x1, Pallas kernels, on_device(): pl.pallas_call(functools.partial(backward_kernel, back_keys, wide), out_s...  2.37 us
    unnamed x12, local copies, waits for them, and re-layouts  1.31 us
  transfers between devices with their start and end apart: 13, of which 6 were waited for; matrix products, arithmetic and copies ran while one was open for 4% of the time, Pallas kernels for 22%

profile of v7, /device:TPU:1, one launch (start us, length us, event | category | flops | bytes accessed | tf_op | source)
XLA Modules:
  0.0 46.4 jit_solution(10358626592810024520)
XLA Ops:
  0.6 0.9 %constant_dynamic-slice_fusion = bf16[2,16,16,128]{3,2,1,0:T(8,128)(2,1)S(1)} fusion(bf16[2,16,128,128]{3,2,1,0:T(8,128)(2,1)} %movie_hbm.1, s32[]{:T(128)S(6)} %select_n.131), kind=kLoop, calls=%fused_computation.13 | loop fusion | bytes 262148 | tf_op jit(solution)/shard_map/dynamic_slice | solution.py:381
  1.6 0.1 collective-permute-start
  1.7 2.7 %prepare.1 = (bf16[16,160,256]{2,1,0:T(8,128)(2,1)S(1)}, bf16[128,128]{1,0:T(8,128)(2,1)S(1)}, bf16[256,768]{1,0:T(8,128)(2,1)S(1)}, s32[128,128]{1,0:T(8,128)S(...) custom-call(f32[25]{0:T(128)} %col_ref, f32[25]{0:T(128)} %row_ref, bf16[2,16,128,128]{3,2,1,0:T(8,128)(2,1)} %movie_hbm.1, ...), custom_call_target="tpu_custom_call" | custom-call | tf_op jit(solution)/shard_map/prepare/pallas_call | solution.py:384
  4.4 0.0 copy-start.3
  4.4 0.0 collective-permute-done.edge_ref
  4.4 1.2 %forward.4 = (bf16[16,160,256]{2,1,0:T(8,128)(2,1)S(1)}, bf16[512,256]{1,0:T(8,128)(2,1)S(1)}, bf16[512,128]{1,0:T(8,128)(2,1)S(1)}) custom-call(bf16[16,160,256]{2,1,0:T(8,128)(2,1)S(1)} %get-tuple-element.48.smooth_in_ref, bf16[2,16,16,128]{3,2,1,0:T(8,128)(2,1)S(1)} %collective-permute-done.edge_ref, ...), custom_call_target="tpu_custom_call", output_to_operand_aliasing={{0}: (0, {})} | custom-call | tf_op jit(solution)/shard_map/forward/pallas_call | solution.py:421
  5.7 1.1 %forward.5 = (bf16[16,160,256]{2,1,0:T(8,128)(2,1)S(1)}, bf16[512,256]{1,0:T(8,128)(2,1)S(1)}, bf16[512,128]{1,0:T(8,128)(2,1)S(1)}) custom-call(bf16[16,160,256]{2,1,0:T(8,128)(2,1)S(1)} %get-tuple-element.53.smooth_in_ref, bf16[2,16,16,128]{3,2,1,0:T(8,128)(2,1)S(1)} %collective-permute-done.edge_ref, ...), custom_call_target="tpu_custom_call", output_to_operand_aliasing={{0}: (0, {})} | custom-call | tf_op jit(solution)/shard_map/forward/pallas_call | solution.py:421
  6.7 2.8 %collective-permute-start.2 = (bf16[512,128]{1,0:T(8,128)(2,1)S(1)}, bf16[512,128]{1,0:T(8,128)(2,1)S(1)}, u32[]{:S(2)}, u32[]{:S(2)}) collective-permute-start(bf16[512,128]{1,0:T(8,128)(2,1)S(1)} %get-tuple-element.63), channel_id=1, source_target_pairs={{0,2},{2,0},{1,3},{3,1},{4,6},{6,4},{5,7},{7,5},{8,10},{10,8},{9,1... | collective-permute-start | bytes 393224 | tf_op jit(solution)/shard_map/ppermute | solution.py:19
  9.5 0.1 collective-permute-start.1
  9.5 0.1 broadcast_multiply_fusion
  9.6 0.1 select_reduce_fusion
  9.7 1.1 %forward.6 = (bf16[16,160,256]{2,1,0:T(8,128)(2,1)S(1)}, bf16[512,256]{1,0:T(8,128)(2,1)S(1)}, bf16[512,128]{1,0:T(8,128)(2,1)S(1)}) custom-call(bf16[16,160,256]{2,1,0:T(8,128)(2,1)S(1)} %get-tuple-element.58.smooth_in_ref, bf16[2,16,16,128]{3,2,1,0:T(8,128)(2,1)S(1)} %collective-permute-done.edge_ref, ...), custom_call_target="tpu_custom_call", output_to_operand_aliasing={{0}: (0, {})} | custom-call | tf_op jit(solution)/shard_map/forward/pallas_call | solution.py:421
  10.8 0.0 copy-start.1
  10.8 0.0 copy-start.2
  10.8 1.1 %forward.7 = (bf16[16,160,256]{2,1,0:T(8,128)(2,1)S(1)}, bf16[512,256]{1,0:T(8,128)(2,1)S(1)}, bf16[512,128]{1,0:T(8,128)(2,1)S(1)}) custom-call(bf16[16,160,256]{2,1,0:T(8,128)(2,1)S(1)} %get-tuple-element.61.smooth_in_ref, bf16[2,16,16,128]{3,2,1,0:T(8,128)(2,1)S(1)} %collective-permute-done.edge_ref, ...), custom_call_target="tpu_custom_call", output_to_operand_aliasing={{0}: (0, {})} | custom-call | tf_op jit(solution)/shard_map/forward/pallas_call | solution.py:421
  11.9 1.4 %collective-permute-done.2.refs_1_ = bf16[512,128]{1,0:T(8,128)(2,1)S(1)} collective-permute-done((bf16[512,128]{1,0:T(8,128)(2,1)S(1)}, bf16[512,128]{1,0:T(8,128)(2,1)S(1)}, u32[]{:S(2)}, u32[]{:S(2)}) %collective-permute-start.2) | collective-permute-done | bytes 131104 | tf_op jit(solution)/shard_map/ppermute | solution.py:19
  13.3 3.4 %collective-permute-start.5 = (bf16[272,128]{1,0:T(8,128)(2,1)S(1)}, bf16[272,128]{1,0:T(8,128)(2,1)S(1)}, u32[]{:S(2)}, u32[]{:S(2)}) collective-permute-start(bf16[272,128]{1,0:T(8,128)(2,1)S(1)} %sum.5), channel_id=1, source_target_pairs={{0,12},{4,8},{8,4},{12,0},{1,13},{5,9},{9,5},{13,1},{2,14},{6,10},... | collective-permute-start | bytes 208904 | tf_op jit(solution)/shard_map/ppermute | solution.py:19
  16.8 0.1 collective-permute-start.4
  16.9 0.0 collective-permute-done.1.refs_1_
  16.9 0.6 %collective-permute-start.3 = (bf16[272,128]{1,0:T(8,128)(2,1)S(1)}, bf16[272,128]{1,0:T(8,128)(2,1)S(1)}, u32[]{:S(2)}, u32[]{:S(2)}) collective-permute-start(bf16[272,128]{1,0:T(8,128)(2,1)S(1)} %sum.3), channel_id=1, source_target_pairs={{0,4},{4,0},{8,12},{12,8},{1,5},{5,1},{9,13},{13,9},{2,6},{6,2},{1... | collective-permute-start | bytes 208904 | tf_op jit(solution)/shard_map/ppermute | solution.py:19
  17.5 0.0 copy-done
  17.5 1.0 %bands.1 = (bf16[256,256]{1,0:T(8,128)(2,1)S(1)}, bf16[256,768]{1,0:T(8,128)(2,1)S(1)}) custom-call(f32[25]{0:T(128)S(1)} %copy-done, f32[25]{0:T(128)S(1)} %copy-done.1), custom_call_target="tpu_custom_call" | custom-call | tf_op jit(solution)/shard_map/bands/pallas_call | solution.py:454
  18.5 0.0 collective-permute-done.5.refs_4_
  18.6 4.0 %collective-permute-done.4.refs_3_ = bf16[272,128]{1,0:T(8,128)(2,1)S(1)} collective-permute-done((bf16[272,128]{1,0:T(8,128)(2,1)S(1)}, bf16[272,128]{1,0:T(8,128)(2,1)S(1)}, u32[]{:S(2)}, u32[]{:S(2)}) %collective-permute-start.4) | collective-permute-done | bytes 69664 | tf_op jit(solution)/shard_map/ppermute | solution.py:19
  22.6 0.0 collective-permute-done.3.refs_2_
  22.6 0.8 %mix.1 = (bf16[16,16,128]{2,1,0:T(8,128)(2,1)S(1)}, bf16[16,16,128]{2,1,0:T(8,128)(2,1)S(1)}, bf16[16,16,128]{2,1,0:T(8,128)(2,1)S(1)}, bf16[16,16,128]{2,1,0:T(8,128)(2,1)S(1)}) custom-call(s32[1,128]{1,0:T(1,128)S(1)} %bitcast.10, bf16[16,128]{1,0:T(8,128)(2,1)S(1)} %pad_bitcast_fusion.lag_ref, bf16[512,128]{1,0:T(8,128)(2,1)S(1)} %get-tuple-element.68.refs_0_, ...), custom_call_target="tpu_custom_call" | custom-call | tf_op jit(solution)/shard_map/mix/pallas_call | solution.py:462
  23.4 0.1 collective-permute-start.10
  23.5 0.8 %collective-permute-start.6 = (bf16[16,16,128]{2,1,0:T(8,128)(2,1)S(1)}, bf16[16,16,128]{2,1,0:T(8,128)(2,1)S(1)}, u32[]{:S(2)}, u32[]{:S(2)}) collective-permute-start(bf16[16,16,128]{2,1,0:T(8,128)(2,1)S(1)} %get-tuple-element.69), channel_id=1, source_target_pairs={{0,8},{4,12},{8,0},{12,4},{1,9},{5,13},{9,1},{13,5},{2,10},{6,14},... | collective-permute-start | bytes 196616 | tf_op jit(solution)/shard_map/ppermute | solution.py:19
  24.3 2.7 %collective-permute-start.7 = (bf16[16,16,128]{2,1,0:T(8,128)(2,1)S(1)}, bf16[16,16,128]{2,1,0:T(8,128)(2,1)S(1)}, u32[]{:S(2)}, u32[]{:S(2)}) collective-permute-start(bf16[16,16,128]{2,1,0:T(8,128)(2,1)S(1)} %get-tuple-element.70), channel_id=1, source_target_pairs={{0,12},{4,8},{8,4},{12,0},{1,13},{5,9},{9,5},{13,1},{2,14},{6,10},... | collective-permute-start | bytes 196616 | tf_op jit(solution)/shard_map/ppermute | solution.py:19
  27.0 1.2 %collective-permute-start.8 = (bf16[16,16,128]{2,1,0:T(8,128)(2,1)S(1)}, bf16[16,16,128]{2,1,0:T(8,128)(2,1)S(1)}, u32[]{:S(2)}, u32[]{:S(2)}) collective-permute-start(bf16[16,16,128]{2,1,0:T(8,128)(2,1)S(1)} %get-tuple-element.71.refs_0_), channel_id=1, source_target_pairs={{0,2},{2,0},{4,6},{6,4},{8,10},{10,8},{12,14},{14,12},{1,3},{3,1},... | collective-permute-start | bytes 196616 | tf_op jit(solution)/shard_map/ppermute | solution.py:29
  28.2 0.0 collective-permute-start.9
  28.2 0.0 collective-permute-done.10.refs_1_
  28.2 1.4 %residual.4 = (bf16[512,256]{1,0:T(8,128)(2,1)S(1)}, bf16[256,256]{1,0:T(8,128)(2,1)S(1)}, bf16[32,16,128]{2,1,0:T(8,128)(2,1)S(1)}) custom-call(bf16[512,256]{1,0:T(8,128)(2,1)S(1)} %get-tuple-element.73.filtered_ref, s32[128,128]{1,0:T(8,128)S(1)} %get-tuple-element.51.code_ref, bf16[512,256]{1,0:T(8,128)(2,1)S(1)} %get-tuple-element.55.templates_ref, ...), custom_call_target="tpu_custom_call" | custom-call | tf_op jit(solution)/shard_map/residual/pallas_call | solution.py:482
  29.6 0.0 collective-permute-done.6.refs_0_
  29.6 0.2 collective-permute-done.7.refs_1_
  29.9 0.5 %collective-permute-done.8.refs_0_ = bf16[16,16,128]{2,1,0:T(8,128)(2,1)S(1)} collective-permute-done((bf16[16,16,128]{2,1,0:T(8,128)(2,1)S(1)}, bf16[16,16,128]{2,1,0:T(8,128)(2,1)S(1)}, u32[]{:S(2)}, u32[]{:S(2)}) %collective-permute-start.8) | collective-permute-done | bytes 65568 | tf_op jit(solution)/shard_map/ppermute | solution.py:29
  30.4 1.8 %collective-permute-done.9.refs_1_ = bf16[16,16,128]{2,1,0:T(8,128)(2,1)S(1)} collective-permute-done((bf16[16,16,128]{2,1,0:T(8,128)(2,1)S(1)}, bf16[16,16,128]{2,1,0:T(8,128)(2,1)S(1)}, u32[]{:S(2)}, u32[]{:S(2)}) %collective-permute-start.9) | collective-permute-done | bytes 65568 | tf_op jit(solution)/shard_map/ppermute | solution.py:29
  32.3 0.3 collective-permute-start.11
  32.6 1.4 %residual.7 = (bf16[512,256]{1,0:T(8,128)(2,1)S(1)}, bf16[256,256]{1,0:T(8,128)(2,1)S(1)}, bf16[32,16,128]{2,1,0:T(8,128)(2,1)S(1)}) custom-call(bf16[512,256]{1,0:T(8,128)(2,1)S(1)} %get-tuple-element.82.filtered_ref, s32[128,128]{1,0:T(8,128)S(1)} %get-tuple-element.51.code_ref, bf16[512,256]{1,0:T(8,128)(2,1)S(1)} %get-tuple-element.55.templates_ref, ...), custom_call_target="tpu_custom_call" | custom-call | tf_op jit(solution)/shard_map/residual/pallas_call | solution.py:482
  34.0 1.4 %residual.6 = (bf16[512,256]{1,0:T(8,128)(2,1)S(1)}, bf16[256,256]{1,0:T(8,128)(2,1)S(1)}, bf16[32,16,128]{2,1,0:T(8,128)(2,1)S(1)}) custom-call(bf16[512,256]{1,0:T(8,128)(2,1)S(1)} %get-tuple-element.78.filtered_ref, s32[128,128]{1,0:T(8,128)S(1)} %get-tuple-element.51.code_ref, bf16[512,256]{1,0:T(8,128)(2,1)S(1)} %get-tuple-element.55.templates_ref, ...), custom_call_target="tpu_custom_call" | custom-call | tf_op jit(solution)/shard_map/residual/pallas_call | solution.py:482
  35.4 1.2 %collective-permute-done.11.refs_0_ = bf16[32,16,128]{2,1,0:T(8,128)(2,1)S(1)} collective-permute-done((bf16[32,16,128]{2,1,0:T(8,128)(2,1)S(1)}, bf16[32,16,128]{2,1,0:T(8,128)(2,1)S(1)}, u32[]{:S(2)}, u32[]{:S(2)}) %collective-permute-start.11) | collective-permute-done | bytes 131104 | tf_op jit(solution)/shard_map/ppermute | solution.py:19
  36.6 1.4 %residual.5 = (bf16[512,256]{1,0:T(8,128)(2,1)S(1)}, bf16[256,256]{1,0:T(8,128)(2,1)S(1)}, bf16[32,16,128]{2,1,0:T(8,128)(2,1)S(1)}) custom-call(bf16[512,256]{1,0:T(8,128)(2,1)S(1)} %get-tuple-element.54.filtered_ref, s32[128,128]{1,0:T(8,128)S(1)} %get-tuple-element.51.code_ref, bf16[512,256]{1,0:T(8,128)(2,1)S(1)} %get-tuple-element.55.templates_ref, ...), custom_call_target="tpu_custom_call" | custom-call | tf_op jit(solution)/shard_map/residual/pallas_call | solution.py:482
  38.0 4.5 %collective-permute-start.12 = (bf16[256,256]{1,0:T(8,128)(2,1)S(1)}, bf16[256,256]{1,0:T(8,128)(2,1)S(1)}, u32[]{:S(2)}, u32[]{:S(2)}) collective-permute-start(bf16[256,256]{1,0:T(8,128)(2,1)S(1)} %select_select_fusion), channel_id=1, source_target_pairs={{0,1},{1,0},{2,3},{3,2},{4,5},{5,4},{6,7},{7,6},{8,9},{9,8},{10,11... | collective-permute-start | bytes 393224 | tf_op jit(solution)/shard_map/ppermute | solution.py:19
  42.5 0.1 select_select_fusion.4
  42.5 0.2 fusion
  42.7 1.3 %copy.16 = bf16[64,16,128]{2,1,0:T(8,128)(2,1)} copy(bf16[64,16,128]{0,1,2:T(8,128)(2,1)S(1)} %fusion) | data formatting | bytes 524288
  44.0 0.0 collective-permute-done.12.edge_ref
  44.0 2.4 %backward.1 = bf16[2,16,128,128]{3,2,1,0:T(8,128)(2,1)} custom-call(bf16[256,256]{1,0:T(8,128)(2,1)S(1)} %collective-permute-done.12.edge_ref, bf16[256,256]{1,0:T(8,128)(2,1)S(1)} %get-tuple-element.88.col_adj_ref, bf16[256,768]{1,0:T(8,128)(2,1)S(1)} %get-tuple-element.89.row_adj_ref, bf16[512,256]{1,0:T(8,128)(2,1)S(1)} %get-tuple-element.90.refs_0_, ...), custom_call_target="tpu_custom_call" | custom-call | tf_op jit(solution)/shard_map/backward/pallas_call | solution.py:513
  (15 shorter events, 0.1 us)
Async XLA Ops:
  1.6 2.8 %collective-permute-start = (bf16[2,16,16,128]{3,2,1,0:T(8,128)(2,1)S(1)}, bf16[2,16,16,128]{3,2,1,0:T(8,128)(2,1)S(1)}, u32[]{:S(2)}, u32[]{:S(2)}) collective-permute-start(bf16[2,16,16,128]{3,2,1,0:T(8,128)(2,1)S(1)} %constant_dynamic-slice_fusion), channel_id=1, source_target_pairs={{0,1},{1,0},{2,3},{3,2},{4,5},{5,4},{6,7},{7,6},{8,9},{9,8},{10,11... | collective-permute-start | bytes 393224 | tf_op jit(solution)/shard_map/ppermute | solution.py:19
  4.4 1.3 %copy-start.3 = (f32[1,3,65]{2,0,1:T(1,128)S(1)}, f32[1,3,65]{2,0,1:T(1,128)}, u32[]{:S(2)}) copy-start(f32[1,3,65]{2,0,1:T(1,128)} %param.16) | copy-start | bytes 2344
  5.6 3.9 %copy-start.4 = (s32[1,3]{1,0:T(1,128)S(1)}, s32[1,3]{1,0:T(1,128)}, u32[]{:S(2)}) copy-start(s32[1,3]{1,0:T(1,128)} %param.17) | copy-start | bytes 40
  6.7 6.6 %collective-permute-start.2 = (bf16[512,128]{1,0:T(8,128)(2,1)S(1)}, bf16[512,128]{1,0:T(8,128)(2,1)S(1)}, u32[]{:S(2)}, u32[]{:S(2)}) collective-permute-start(bf16[512,128]{1,0:T(8,128)(2,1)S(1)} %get-tuple-element.63), channel_id=1, source_target_pairs={{0,2},{2,0},{1,3},{3,1},{4,6},{6,4},{5,7},{7,5},{8,10},{10,8},{9,1... | collective-permute-start | bytes 393224 | tf_op jit(solution)/shard_map/ppermute | solution.py:19
  9.5 7.4 %collective-permute-start.1 = (bf16[512,128]{1,0:T(8,128)(2,1)S(1)}, bf16[512,128]{1,0:T(8,128)(2,1)S(1)}, u32[]{:S(2)}, u32[]{:S(2)}) collective-permute-start(bf16[512,128]{1,0:T(8,128)(2,1)S(1)} %get-tuple-element.60), channel_id=1, source_target_pairs={{0,2},{2,0},{1,3},{3,1},{4,6},{6,4},{5,7},{7,5},{8,10},{10,8},{9,1... | collective-permute-start | bytes 393224 | tf_op jit(solution)/shard_map/ppermute | solution.py:19
  10.8 6.7 %copy-start = (f32[25]{0:T(128)S(1)}, f32[25]{0:T(128)}, u32[]{:S(2)}) copy-start(f32[25]{0:T(128)} %col_ref) | copy-start | bytes 304
  10.8 6.7 %copy-start.1 = (f32[25]{0:T(128)S(1)}, f32[25]{0:T(128)}, u32[]{:S(2)}) copy-start(f32[25]{0:T(128)} %row_ref) | copy-start | bytes 304
  10.8 11.7 %copy-start.2 = (s32[128,1]{0,1:T(1,128)S(1)}, s32[128,1]{0,1:T(1,128)}, u32[]{:S(2)}) copy-start(s32[128,1]{0,1:T(1,128)} %param.11) | copy-start | bytes 1540
  13.3 5.2 %collective-permute-start.5 = (bf16[272,128]{1,0:T(8,128)(2,1)S(1)}, bf16[272,128]{1,0:T(8,128)(2,1)S(1)}, u32[]{:S(2)}, u32[]{:S(2)}) collective-permute-start(bf16[272,128]{1,0:T(8,128)(2,1)S(1)} %sum.5), channel_id=1, source_target_pairs={{0,12},{4,8},{8,4},{12,0},{1,13},{5,9},{9,5},{13,1},{2,14},{6,10},... | collective-permute-start | bytes 208904 | tf_op jit(solution)/shard_map/ppermute | solution.py:19
  16.8 5.8 %collective-permute-start.4 = (bf16[272,128]{1,0:T(8,128)(2,1)S(1)}, bf16[272,128]{1,0:T(8,128)(2,1)S(1)}, u32[]{:S(2)}, u32[]{:S(2)}) collective-permute-start(bf16[272,128]{1,0:T(8,128)(2,1)S(1)} %sum.4), channel_id=1, source_target_pairs={{0,8},{4,12},{8,0},{12,4},{1,9},{5,13},{9,1},{13,5},{2,10},{6,14},... | collective-permute-start | bytes 208904 | tf_op jit(solution)/shard_map/ppermute | solution.py:19
  16.9 5.7 %collective-permute-start.3 = (bf16[272,128]{1,0:T(8,128)(2,1)S(1)}, bf16[272,128]{1,0:T(8,128)(2,1)S(1)}, u32[]{:S(2)}, u32[]{:S(2)}) collective-permute-start(bf16[272,128]{1,0:T(8,128)(2,1)S(1)} %sum.3), channel_id=1, source_target_pairs={{0,4},{4,0},{8,12},{12,8},{1,5},{5,1},{9,13},{13,9},{2,6},{6,2},{1... | collective-permute-start | bytes 208904 | tf_op jit(solution)/shard_map/ppermute | solution.py:19
  23.4 4.8 %collective-permute-start.10 = (bf16[16,16,128]{2,1,0:T(8,128)(2,1)S(1)}, bf16[16,16,128]{2,1,0:T(8,128)(2,1)S(1)}, u32[]{:S(2)}, u32[]{:S(2)}) collective-permute-start(bf16[16,16,128]{2,1,0:T(8,128)(2,1)S(1)} %get-tuple-element.72), channel_id=1, source_target_pairs={{0,4},{4,0},{8,12},{12,8},{1,5},{5,1},{9,13},{13,9},{2,6},{6,2},{1... | collective-permute-start | bytes 196616 | tf_op jit(solution)/shard_map/ppermute | solution.py:19
  23.5 6.2 %collective-permute-start.6 = (bf16[16,16,128]{2,1,0:T(8,128)(2,1)S(1)}, bf16[16,16,128]{2,1,0:T(8,128)(2,1)S(1)}, u32[]{:S(2)}, u32[]{:S(2)}) collective-permute-start(bf16[16,16,128]{2,1,0:T(8,128)(2,1)S(1)} %get-tuple-element.69), channel_id=1, source_target_pairs={{0,8},{4,12},{8,0},{12,4},{1,9},{5,13},{9,1},{13,5},{2,10},{6,14},... | collective-permute-start | bytes 196616 | tf_op jit(solution)/shard_map/ppermute | solution.py:19
  24.3 5.6 %collective-permute-start.7 = (bf16[16,16,128]{2,1,0:T(8,128)(2,1)S(1)}, bf16[16,16,128]{2,1,0:T(8,128)(2,1)S(1)}, u32[]{:S(2)}, u32[]{:S(2)}) collective-permute-start(bf16[16,16,128]{2,1,0:T(8,128)(2,1)S(1)} %get-tuple-element.70), channel_id=1, source_target_pairs={{0,12},{4,8},{8,4},{12,0},{1,13},{5,9},{9,5},{13,1},{2,14},{6,10},... | collective-permute-start | bytes 196616 | tf_op jit(solution)/shard_map/ppermute | solution.py:19
  27.0 3.4 %collective-permute-start.8 = (bf16[16,16,128]{2,1,0:T(8,128)(2,1)S(1)}, bf16[16,16,128]{2,1,0:T(8,128)(2,1)S(1)}, u32[]{:S(2)}, u32[]{:S(2)}) collective-permute-start(bf16[16,16,128]{2,1,0:T(8,128)(2,1)S(1)} %get-tuple-element.71.refs_0_), channel_id=1, source_target_pairs={{0,2},{2,0},{4,6},{6,4},{8,10},{10,8},{12,14},{14,12},{1,3},{3,1},... | collective-permute-start | bytes 196616 | tf_op jit(solution)/shard_map/ppermute | solution.py:29
  28.2 4.0 %collective-permute-start.9 = (bf16[16,16,128]{2,1,0:T(8,128)(2,1)S(1)}, bf16[16,16,128]{2,1,0:T(8,128)(2,1)S(1)}, u32[]{:S(2)}, u32[]{:S(2)}) collective-permute-start(bf16[16,16,128]{2,1,0:T(8,128)(2,1)S(1)} %get-tuple-element.72), channel_id=1, source_target_pairs={{0,6},{2,4},{4,2},{6,0},{8,14},{10,12},{12,10},{14,8},{1,7},{3,5},... | collective-permute-start | bytes 196616 | tf_op jit(solution)/shard_map/ppermute | solution.py:29
  32.3 4.3 %collective-permute-start.11 = (bf16[32,16,128]{2,1,0:T(8,128)(2,1)S(1)}, bf16[32,16,128]{2,1,0:T(8,128)(2,1)S(1)}, u32[]{:S(2)}, u32[]{:S(2)}) collective-permute-start(bf16[32,16,128]{2,1,0:T(8,128)(2,1)S(1)} %pad_maximum_fusion), channel_id=1, source_target_pairs={{0,2},{2,0},{1,3},{3,1},{4,6},{6,4},{5,7},{7,5},{8,10},{10,8},{9,1... | collective-permute-start | bytes 393224 | tf_op jit(solution)/shard_map/ppermute | solution.py:19
  38.0 6.0 %collective-permute-start.12 = (bf16[256,256]{1,0:T(8,128)(2,1)S(1)}, bf16[256,256]{1,0:T(8,128)(2,1)S(1)}, u32[]{:S(2)}, u32[]{:S(2)}) collective-permute-start(bf16[256,256]{1,0:T(8,128)(2,1)S(1)} %select_select_fusion), channel_id=1, source_target_pairs={{0,1},{1,0},{2,3},{3,2},{4,5},{5,4},{6,7},{7,6},{8,9},{9,8},{10,11... | collective-permute-start | bytes 393224 | tf_op jit(solution)/shard_map/ppermute | solution.py:19

commit v8 on v7

--- a/solution.py
+++ b/solution.py
@@ -17,16 +17,6 @@
 def exchange(cells, axis, flip):
     count = lax.axis_size(axis)
     return lax.ppermute(cells, axis, [(i, i ^ flip) for i in range(count)])
-
-
-def crossed(cells, plane_flip, wide_flip):
-    count, size = lax.axis_size("planes"), lax.axis_size("wide")
-    pairs = [
-        (w * count + p, (w ^ wide_flip) * count + (p ^ plane_flip))
-        for w in range(size)
-        for p in range(count)
-    ]
-    return lax.ppermute(cells, ("wide", "planes"), pairs)
 
 
 def iota(shape, dim):
@@ -119,9 +109,13 @@
     col_fwd = column_band(col_ref, rim, -1)
     col_fwd_ref[...] = col_fwd
     row_fwd_ref[...] = row_band_forward(row_ref, rim, frames)
-    for n, copy in enumerate(movie_copies):
+    for copy in (*movie_copies, packed_copy, *code_copies):
+        copy.wait()
+    loose_ref[...] = packed_ref[...].astype(F32)
+    code_ref[...] = support_ref[...] * 2 + mask_ref[...]
+    unit = (iota((LANES, LANES), 0) == iota((LANES, LANES), 1)).astype(BF16)
+    for n in range(planes * cuts):
         p, first = n // cuts, n % cuts * some
-        copy.wait()
         full = jnp.dot(
             movie_ref[p, first : first + some].reshape(some * rows, LANES), col_fwd,
             preferred_element_type=F32,
@@ -129,18 +123,12 @@
         smooth_ref[first : first + some, BLOCK : BLOCK + rows, p * LANES : (p + 1) * LANES] = (
             full.astype(BF16).reshape(some, rows, LANES)
         )
-    packed_copy.wait()
-    loose_ref[...] = packed_ref[...].astype(F32)
-    unit = (iota((LANES, LANES), 0) == iota((LANES, LANES), 1)).astype(BF16)
     for p in range(planes):
         shapes = loose_ref[pl.ds(p, templates_ref.shape[1], stride=planes), :].astype(BF16)
         flat_ref[:, p * LANES : (p + 1) * LANES] = shapes
         templates_ref[p * LANES : (p + 1) * LANES, :] = lax.dot_general(
             unit, shapes, (((1,), (1,)), ((), ())), preferred_element_type=F32
         ).astype(BF16)
-    for copy in code_copies:
-        copy.wait()
-    code_ref[...] = support_ref[...] * 2 + mask_ref[...]
 
 
 def forward_kernel(
@@ -472,7 +460,8 @@
     swapped = {k: exchange(traces[k], "wide", k) for k in far_ks + near_ks[1:]}
     swapped[0] = traces[0]
     late = range(1, plane_count)
-    direct = {flip: [crossed(traces[k], flip, k) for k in near_ks] for flip in late}
+    near = jnp.concatenate([swapped[k] for k in near_ks])
+    passed = {flip: exchange(near, "planes", flip) for flip in late}
 
     residual, edges, ordered = {}, {}, {}
     back_keys = [(flip, far) for flip in range(plane_count) for far in (0, 1)]
@@ -485,14 +474,12 @@
             0, 3 + len(got), scratch=[pltpu.VMEM((len(spots), share * frames, names), BF16)],
         )(filtered[flip, far], code, flat_templates, *got)
 
-    subtract(0, 0, [[k] for k in near_ks], [swapped[k] for k in near_ks])
-    distant, direct, _ = lax.optimization_barrier(
-        ([swapped[k] for k in far_ks], direct, edges[0, 0])
-    )
+    subtract(0, 0, [near_ks], [near])
+    distant, _ = lax.optimization_barrier(([swapped[k] for k in far_ks], edges[0, 0]))
     joined = jnp.concatenate(distant)
     subtract(0, 1, [[k] for k in far_ks], distant)
     for flip in late:
-        subtract(flip, 0, [[k] for k in near_ks], direct[flip])
+        subtract(flip, 0, [near_ks], [passed[flip]])
         subtract(flip, 1, [far_ks], [exchange(joined, "planes", flip)])
 
     def pick(table, part, half):

time: 46.6 us -> 43.8 us (0.940)
  waiting for transfers between devices: 9.22 us -> 6.62 us
  Pallas kernels: 16.9 us -> 16.1 us
  starting transfers between devices: 16.6 us -> 17.2 us
    ppermute x2 -> x0, waiting for transfers between devices: 2.37 us -> none  [crossed(): return lax.ppermute(cells, ('wide', 'planes'), pairs)]
    ppermute x11 -> x12, starting transfers between devices: 15.4 us -> 17.2 us  [exchange(): return lax.ppermute(cells, axis, [(i, i ^ flip) for i in range(count)])]
    ppermute x2 -> x0, starting transfers between devices: 1.22 us -> none  [crossed(): return lax.ppermute(cells, ('wide', 'planes'), pairs)]
    pallas_call x1, Pallas kernels: 2.66 us -> 1.9 us  [on_device(): pl.pallas_call(functools.partial(prepare_kernel, rim, cuts), out_shape=(s...]
    ppermute x11 -> x12, waiting for transfers between devices: 6.84 us -> 6.62 us  [exchange(): return lax.ppermute(cells, axis, [(i, i ^ flip) for i in range(count)])]
    unnamed x12 -> x13, local copies, waits for them, and re-layouts: 1.31 us -> 1.31 us
  transfers between devices with their start and end apart: 13 -> 12, of which waited for: 6 -> 4; matrix products, arithmetic and copies ran while one was open for 4% -> 4% of each run, Pallas kernels for 22% -> 21%
where the time goes in v8:
time: 43.8 us; the launch traced here: 43.6 us
  starting transfers between devices  17.2 us (39%)
  Pallas kernels  16.1 us (37%)
  waiting for transfers between devices  6.62 us (15%)
  local copies, waits for them, and re-layouts  2.26 us (5%)
  between operations  0.87 us (2%)
  other arithmetic  0.54 us (1%)
    ppermute x12, starting transfers between devices, exchange(): return lax.ppermute(cells, axis, [(i, i ^ flip) for i in range(count)])  17.2 us
    ppermute x12, waiting for transfers between devices, exchange(): return lax.ppermute(cells, axis, [(i, i ^ flip) for i in range(count)])  6.62 us
    pallas_call x4, Pallas kernels, subtract(): call(functools.partial(residual_kernel, flip, far, wide, spots), 'residua...  5.57 us
    pallas_call x4, Pallas kernels, on_device(): call(functools.partial(forward_kernel, flip, far, turn == 0, wide, halves...  4.42 us
    pallas_call x1, Pallas kernels, on_device(): pl.pallas_call(functools.partial(backward_kernel, back_keys, wide), out_s...  2.37 us
    pallas_call x1, Pallas kernels, on_device(): pl.pallas_call(functools.partial(prepare_kernel, rim, cuts), out_shape=(s...  1.9 us
    unnamed x13, local copies, waits for them, and re-layouts  1.31 us
    pallas_call x1, Pallas kernels, on_device(): call(functools.partial(bands_kernel, rim, frames), 'bands', [(width, widt...  1 us
  transfers between devices with their start and end apart: 12, of which 4 were waited for; matrix products, arithmetic and copies ran while one was open for 4% of the time, Pallas kernels for 21%

profile of v8, /device:TPU:1, one launch (start us, length us, event | category | flops | bytes accessed | tf_op | source)
XLA Modules:
  0.0 43.6 jit_solution(8247416314552057486)
XLA Ops:
  0.6 0.9 %constant_dynamic-slice_fusion = bf16[2,16,16,128]{3,2,1,0:T(8,128)(2,1)S(1)} fusion(bf16[2,16,128,128]{3,2,1,0:T(8,128)(2,1)} %movie_hbm.1, s32[]{:T(128)S(6)} %select_n.131), kind=kLoop, calls=%fused_computation.15 | loop fusion | bytes 262148 | tf_op jit(solution)/shard_map/dynamic_slice | solution.py:369
  1.6 0.1 collective-permute-start
  1.7 1.9 %prepare.1 = (bf16[16,160,256]{2,1,0:T(8,128)(2,1)S(1)}, bf16[128,128]{1,0:T(8,128)(2,1)S(1)}, bf16[256,768]{1,0:T(8,128)(2,1)S(1)}, s32[128,128]{1,0:T(8,128)S(...) custom-call(f32[25]{0:T(128)} %col_ref, f32[25]{0:T(128)} %row_ref, bf16[2,16,128,128]{3,2,1,0:T(8,128)(2,1)} %movie_hbm.1, ...), custom_call_target="tpu_custom_call" | custom-call | tf_op jit(solution)/shard_map/prepare/pallas_call | solution.py:372
  3.6 0.0 copy-start.3
  3.6 0.0 collective-permute-done.edge_ref
  3.6 1.2 %forward.4 = (bf16[16,160,256]{2,1,0:T(8,128)(2,1)S(1)}, bf16[512,256]{1,0:T(8,128)(2,1)S(1)}, bf16[512,128]{1,0:T(8,128)(2,1)S(1)}) custom-call(bf16[16,160,256]{2,1,0:T(8,128)(2,1)S(1)} %get-tuple-element.46.smooth_in_ref, bf16[2,16,16,128]{3,2,1,0:T(8,128)(2,1)S(1)} %collective-permute-done.edge_ref, ...), custom_call_target="tpu_custom_call", output_to_operand_aliasing={{0}: (0, {})} | custom-call | tf_op jit(solution)/shard_map/forward/pallas_call | solution.py:409
  4.9 0.0 copy-start.4
  4.9 0.0 copy-done.3
  4.9 1.1 %forward.5 = (bf16[16,160,256]{2,1,0:T(8,128)(2,1)S(1)}, bf16[512,256]{1,0:T(8,128)(2,1)S(1)}, bf16[512,128]{1,0:T(8,128)(2,1)S(1)}) custom-call(bf16[16,160,256]{2,1,0:T(8,128)(2,1)S(1)} %get-tuple-element.51.smooth_in_ref, bf16[2,16,16,128]{3,2,1,0:T(8,128)(2,1)S(1)} %collective-permute-done.edge_ref, ...), custom_call_target="tpu_custom_call", output_to_operand_aliasing={{0}: (0, {})} | custom-call | tf_op jit(solution)/shard_map/forward/pallas_call | solution.py:409
  6.0 2.8 %collective-permute-start.2 = (bf16[512,128]{1,0:T(8,128)(2,1)S(1)}, bf16[512,128]{1,0:T(8,128)(2,1)S(1)}, u32[]{:S(2)}, u32[]{:S(2)}) collective-permute-start(bf16[512,128]{1,0:T(8,128)(2,1)S(1)} %get-tuple-element.61), channel_id=1, source_target_pairs={{0,2},{2,0},{1,3},{3,1},{4,6},{6,4},{5,7},{7,5},{8,10},{10,8},{9,1... | collective-permute-start | bytes 393224 | tf_op jit(solution)/shard_map/ppermute | solution.py:19
  8.7 0.0 collective-permute-start.1
  8.8 0.1 broadcast_multiply_fusion
  8.8 0.1 select_reduce_fusion
  9.0 1.1 %forward.6 = (bf16[16,160,256]{2,1,0:T(8,128)(2,1)S(1)}, bf16[512,256]{1,0:T(8,128)(2,1)S(1)}, bf16[512,128]{1,0:T(8,128)(2,1)S(1)}) custom-call(bf16[16,160,256]{2,1,0:T(8,128)(2,1)S(1)} %get-tuple-element.56.smooth_in_ref, bf16[2,16,16,128]{3,2,1,0:T(8,128)(2,1)S(1)} %collective-permute-done.edge_ref, ...), custom_call_target="tpu_custom_call", output_to_operand_aliasing={{0}: (0, {})} | custom-call | tf_op jit(solution)/shard_map/forward/pallas_call | solution.py:409
  10.1 0.0 copy-start.1
  10.1 0.0 copy-start.2
  10.1 1.1 %forward.7 = (bf16[16,160,256]{2,1,0:T(8,128)(2,1)S(1)}, bf16[512,256]{1,0:T(8,128)(2,1)S(1)}, bf16[512,128]{1,0:T(8,128)(2,1)S(1)}) custom-call(bf16[16,160,256]{2,1,0:T(8,128)(2,1)S(1)} %get-tuple-element.59.smooth_in_ref, bf16[2,16,16,128]{3,2,1,0:T(8,128)(2,1)S(1)} %collective-permute-done.edge_ref, ...), custom_call_target="tpu_custom_call", output_to_operand_aliasing={{0}: (0, {})} | custom-call | tf_op jit(solution)/shard_map/forward/pallas_call | solution.py:409
  11.2 1.4 %collective-permute-done.2.refs_1_ = bf16[512,128]{1,0:T(8,128)(2,1)S(1)} collective-permute-done((bf16[512,128]{1,0:T(8,128)(2,1)S(1)}, bf16[512,128]{1,0:T(8,128)(2,1)S(1)}, u32[]{:S(2)}, u32[]{:S(2)}) %collective-permute-start.2) | collective-permute-done | bytes 131104 | tf_op jit(solution)/shard_map/ppermute | solution.py:19
  12.6 3.4 %collective-permute-start.5 = (bf16[272,128]{1,0:T(8,128)(2,1)S(1)}, bf16[272,128]{1,0:T(8,128)(2,1)S(1)}, u32[]{:S(2)}, u32[]{:S(2)}) collective-permute-start(bf16[272,128]{1,0:T(8,128)(2,1)S(1)} %sum.5), channel_id=1, source_target_pairs={{0,12},{4,8},{8,4},{12,0},{1,13},{5,9},{9,5},{13,1},{2,14},{6,10},... | collective-permute-start | bytes 208904 | tf_op jit(solution)/shard_map/ppermute | solution.py:19
  16.0 0.1 collective-permute-start.4
  16.1 0.0 collective-permute-done.1.refs_1_
  16.1 0.6 %collective-permute-start.3 = (bf16[272,128]{1,0:T(8,128)(2,1)S(1)}, bf16[272,128]{1,0:T(8,128)(2,1)S(1)}, u32[]{:S(2)}, u32[]{:S(2)}) collective-permute-start(bf16[272,128]{1,0:T(8,128)(2,1)S(1)} %sum.3), channel_id=1, source_target_pairs={{0,4},{4,0},{8,12},{12,8},{1,5},{5,1},{9,13},{13,9},{2,6},{6,2},{1... | collective-permute-start | bytes 208904 | tf_op jit(solution)/shard_map/ppermute | solution.py:19
  16.8 0.0 copy-done
  16.8 1.0 %bands.1 = (bf16[256,256]{1,0:T(8,128)(2,1)S(1)}, bf16[256,768]{1,0:T(8,128)(2,1)S(1)}) custom-call(f32[25]{0:T(128)S(1)} %copy-done, f32[25]{0:T(128)S(1)} %copy-done.1), custom_call_target="tpu_custom_call" | custom-call | tf_op jit(solution)/shard_map/bands/pallas_call | solution.py:442
  17.8 0.0 collective-permute-done.5.refs_4_
  17.8 4.0 %collective-permute-done.4.refs_3_ = bf16[272,128]{1,0:T(8,128)(2,1)S(1)} collective-permute-done((bf16[272,128]{1,0:T(8,128)(2,1)S(1)}, bf16[272,128]{1,0:T(8,128)(2,1)S(1)}, u32[]{:S(2)}, u32[]{:S(2)}) %collective-permute-start.4) | collective-permute-done | bytes 69664 | tf_op jit(solution)/shard_map/ppermute | solution.py:19
  21.8 0.0 collective-permute-done.3.refs_2_
  21.8 0.8 %mix.1 = (bf16[16,16,128]{2,1,0:T(8,128)(2,1)S(1)}, bf16[16,16,128]{2,1,0:T(8,128)(2,1)S(1)}, bf16[16,16,128]{2,1,0:T(8,128)(2,1)S(1)}, bf16[16,16,128]{2,1,0:T(8,128)(2,1)S(1)}) custom-call(s32[1,128]{1,0:T(1,128)S(1)} %bitcast.10, bf16[16,128]{1,0:T(8,128)(2,1)S(1)} %pad_bitcast_fusion.lag_ref, bf16[512,128]{1,0:T(8,128)(2,1)S(1)} %get-tuple-element.66.refs_0_, ...), custom_call_target="tpu_custom_call" | custom-call | tf_op jit(solution)/shard_map/mix/pallas_call | solution.py:450
  22.6 0.1 collective-permute-start.8
  22.7 0.8 %collective-permute-start.6 = (bf16[16,16,128]{2,1,0:T(8,128)(2,1)S(1)}, bf16[16,16,128]{2,1,0:T(8,128)(2,1)S(1)}, u32[]{:S(2)}, u32[]{:S(2)}) collective-permute-start(bf16[16,16,128]{2,1,0:T(8,128)(2,1)S(1)} %get-tuple-element.67), channel_id=1, source_target_pairs={{0,8},{4,12},{8,0},{12,4},{1,9},{5,13},{9,1},{13,5},{2,10},{6,14},... | collective-permute-start | bytes 196616 | tf_op jit(solution)/shard_map/ppermute | solution.py:19
  23.5 2.7 %collective-permute-start.7 = (bf16[16,16,128]{2,1,0:T(8,128)(2,1)S(1)}, bf16[16,16,128]{2,1,0:T(8,128)(2,1)S(1)}, u32[]{:S(2)}, u32[]{:S(2)}) collective-permute-start(bf16[16,16,128]{2,1,0:T(8,128)(2,1)S(1)} %get-tuple-element.68), channel_id=1, source_target_pairs={{0,12},{4,8},{8,4},{12,0},{1,13},{5,9},{9,5},{13,1},{2,14},{6,10},... | collective-permute-start | bytes 196616 | tf_op jit(solution)/shard_map/ppermute | solution.py:19
  26.2 0.0 collective-permute-done.8
  26.3 1.3 %collective-permute-start.10 = (bf16[32,16,128]{2,1,0:T(8,128)(2,1)S(1)}, bf16[32,16,128]{2,1,0:T(8,128)(2,1)S(1)}, u32[]{:S(2)}, u32[]{:S(2)}) collective-permute-start(bf16[32,16,128]{2,1,0:T(8,128)(2,1)S(1)} %constant_dynamic-update-slice_fusion.refs_0_), channel_id=1, source_target_pairs={{0,2},{2,0},{1,3},{3,1},{4,6},{6,4},{5,7},{7,5},{8,10},{10,8},{9,1... | collective-permute-start | bytes 393224 | tf_op jit(solution)/shard_map/ppermute | solution.py:19
  27.6 1.4 %residual.4 = (bf16[512,256]{1,0:T(8,128)(2,1)S(1)}, bf16[256,256]{1,0:T(8,128)(2,1)S(1)}, bf16[32,16,128]{2,1,0:T(8,128)(2,1)S(1)}) custom-call(bf16[512,256]{1,0:T(8,128)(2,1)S(1)} %get-tuple-element.69.filtered_ref, s32[128,128]{1,0:T(8,128)S(1)} %get-tuple-element.49.code_ref, bf16[512,256]{1,0:T(8,128)(2,1)S(1)} %get-tuple-element.53.templates_ref, ...), custom_call_target="tpu_custom_call" | custom-call | tf_op jit(solution)/shard_map/residual/pallas_call | solution.py:471
  28.9 0.0 collective-permute-done.6.refs_0_
  29.0 0.2 collective-permute-done.7.refs_1_
  29.1 1.3 %collective-permute-start.9 = (bf16[32,16,128]{2,1,0:T(8,128)(2,1)S(1)}, bf16[32,16,128]{2,1,0:T(8,128)(2,1)S(1)}, u32[]{:S(2)}, u32[]{:S(2)}) collective-permute-start(bf16[32,16,128]{2,1,0:T(8,128)(2,1)S(1)} %pad_maximum_fusion), channel_id=1, source_target_pairs={{0,2},{2,0},{1,3},{3,1},{4,6},{6,4},{5,7},{7,5},{8,10},{10,8},{9,1... | collective-permute-start | bytes 393224 | tf_op jit(solution)/shard_map/ppermute | solution.py:19
  30.4 1.4 %residual.7 = (bf16[512,256]{1,0:T(8,128)(2,1)S(1)}, bf16[256,256]{1,0:T(8,128)(2,1)S(1)}, bf16[32,16,128]{2,1,0:T(8,128)(2,1)S(1)}) custom-call(bf16[512,256]{1,0:T(8,128)(2,1)S(1)} %get-tuple-element.78.filtered_ref, s32[128,128]{1,0:T(8,128)S(1)} %get-tuple-element.49.code_ref, bf16[512,256]{1,0:T(8,128)(2,1)S(1)} %get-tuple-element.53.templates_ref, ...), custom_call_target="tpu_custom_call" | custom-call | tf_op jit(solution)/shard_map/residual/pallas_call | solution.py:471
  31.8 0.0 collective-permute-done.10.refs_0_
  31.8 1.4 %residual.6 = (bf16[512,256]{1,0:T(8,128)(2,1)S(1)}, bf16[256,256]{1,0:T(8,128)(2,1)S(1)}, bf16[32,16,128]{2,1,0:T(8,128)(2,1)S(1)}) custom-call(bf16[512,256]{1,0:T(8,128)(2,1)S(1)} %get-tuple-element.76.filtered_ref, s32[128,128]{1,0:T(8,128)S(1)} %get-tuple-element.49.code_ref, bf16[512,256]{1,0:T(8,128)(2,1)S(1)} %get-tuple-element.53.templates_ref, ...), custom_call_target="tpu_custom_call" | custom-call | tf_op jit(solution)/shard_map/residual/pallas_call | solution.py:471
  33.2 1.0 %collective-permute-done.9.refs_0_ = bf16[32,16,128]{2,1,0:T(8,128)(2,1)S(1)} collective-permute-done((bf16[32,16,128]{2,1,0:T(8,128)(2,1)S(1)}, bf16[32,16,128]{2,1,0:T(8,128)(2,1)S(1)}, u32[]{:S(2)}, u32[]{:S(2)}) %collective-permute-start.9) | collective-permute-done | bytes 131104 | tf_op jit(solution)/shard_map/ppermute | solution.py:19
  34.3 1.4 %residual.5 = (bf16[512,256]{1,0:T(8,128)(2,1)S(1)}, bf16[256,256]{1,0:T(8,128)(2,1)S(1)}, bf16[32,16,128]{2,1,0:T(8,128)(2,1)S(1)}) custom-call(bf16[512,256]{1,0:T(8,128)(2,1)S(1)} %get-tuple-element.52.filtered_ref, s32[128,128]{1,0:T(8,128)S(1)} %get-tuple-element.49.code_ref, bf16[512,256]{1,0:T(8,128)(2,1)S(1)} %get-tuple-element.53.templates_ref, ...), custom_call_target="tpu_custom_call" | custom-call | tf_op jit(solution)/shard_map/residual/pallas_call | solution.py:471
  35.7 4.0 %collective-permute-start.11 = (bf16[256,256]{1,0:T(8,128)(2,1)S(1)}, bf16[256,256]{1,0:T(8,128)(2,1)S(1)}, u32[]{:S(2)}, u32[]{:S(2)}) collective-permute-start(bf16[256,256]{1,0:T(8,128)(2,1)S(1)} %select_select_fusion), channel_id=1, source_target_pairs={{0,1},{1,0},{2,3},{3,2},{4,5},{5,4},{6,7},{7,6},{8,9},{9,8},{10,11... | collective-permute-start | bytes 393224 | tf_op jit(solution)/shard_map/ppermute | solution.py:19
  39.7 0.1 select_select_fusion.4
  39.7 0.2 fusion
  40.0 1.3 %copy.16 = bf16[64,16,128]{2,1,0:T(8,128)(2,1)} copy(bf16[64,16,128]{0,1,2:T(8,128)(2,1)S(1)} %fusion) | data formatting | bytes 524288
  41.2 0.0 collective-permute-done.11.edge_ref
  41.2 2.4 %backward.1 = bf16[2,16,128,128]{3,2,1,0:T(8,128)(2,1)} custom-call(bf16[256,256]{1,0:T(8,128)(2,1)S(1)} %collective-permute-done.11.edge_ref, bf16[256,256]{1,0:T(8,128)(2,1)S(1)} %get-tuple-element.84.col_adj_ref, bf16[256,768]{1,0:T(8,128)(2,1)S(1)} %get-tuple-element.85.row_adj_ref, bf16[512,256]{1,0:T(8,128)(2,1)S(1)} %get-tuple-element.86.refs_0_, ...), custom_call_target="tpu_custom_call" | custom-call | tf_op jit(solution)/shard_map/backward/pallas_call | solution.py:500
  (15 shorter events, 0.1 us)
Async XLA Ops:
  1.6 2.1 %collective-permute-start = (bf16[2,16,16,128]{3,2,1,0:T(8,128)(2,1)S(1)}, bf16[2,16,16,128]{3,2,1,0:T(8,128)(2,1)S(1)}, u32[]{:S(2)}, u32[]{:S(2)}) collective-permute-start(bf16[2,16,16,128]{3,2,1,0:T(8,128)(2,1)S(1)} %constant_dynamic-slice_fusion), channel_id=1, source_target_pairs={{0,1},{1,0},{2,3},{3,2},{4,5},{5,4},{6,7},{7,6},{8,9},{9,8},{10,11... | collective-permute-start | bytes 393224 | tf_op jit(solution)/shard_map/ppermute | solution.py:19
  3.6 1.3 %copy-start.3 = (f32[1,3,65]{2,0,1:T(1,128)S(1)}, f32[1,3,65]{2,0,1:T(1,128)}, u32[]{:S(2)}) copy-start(f32[1,3,65]{2,0,1:T(1,128)} %param.16) | copy-start | bytes 2344
  4.9 3.9 %copy-start.4 = (s32[1,3]{1,0:T(1,128)S(1)}, s32[1,3]{1,0:T(1,128)}, u32[]{:S(2)}) copy-start(s32[1,3]{1,0:T(1,128)} %param.17) | copy-start | bytes 40
  6.0 6.6 %collective-permute-start.2 = (bf16[512,128]{1,0:T(8,128)(2,1)S(1)}, bf16[512,128]{1,0:T(8,128)(2,1)S(1)}, u32[]{:S(2)}, u32[]{:S(2)}) collective-permute-start(bf16[512,128]{1,0:T(8,128)(2,1)S(1)} %get-tuple-element.61), channel_id=1, source_target_pairs={{0,2},{2,0},{1,3},{3,1},{4,6},{6,4},{5,7},{7,5},{8,10},{10,8},{9,1... | collective-permute-start | bytes 393224 | tf_op jit(solution)/shard_map/ppermute | solution.py:19
  8.7 7.4 %collective-permute-start.1 = (bf16[512,128]{1,0:T(8,128)(2,1)S(1)}, bf16[512,128]{1,0:T(8,128)(2,1)S(1)}, u32[]{:S(2)}, u32[]{:S(2)}) collective-permute-start(bf16[512,128]{1,0:T(8,128)(2,1)S(1)} %get-tuple-element.58), channel_id=1, source_target_pairs={{0,2},{2,0},{1,3},{3,1},{4,6},{6,4},{5,7},{7,5},{8,10},{10,8},{9,1... | collective-permute-start | bytes 393224 | tf_op jit(solution)/shard_map/ppermute | solution.py:19
  10.1 6.7 %copy-start = (f32[25]{0:T(128)S(1)}, f32[25]{0:T(128)}, u32[]{:S(2)}) copy-start(f32[25]{0:T(128)} %col_ref) | copy-start | bytes 304
  10.1 6.7 %copy-start.1 = (f32[25]{0:T(128)S(1)}, f32[25]{0:T(128)}, u32[]{:S(2)}) copy-start(f32[25]{0:T(128)} %row_ref) | copy-start | bytes 304
  10.1 11.8 %copy-start.2 = (s32[128,1]{0,1:T(1,128)S(1)}, s32[128,1]{0,1:T(1,128)}, u32[]{:S(2)}) copy-start(s32[128,1]{0,1:T(1,128)} %param.11) | copy-start | bytes 1540
  12.6 5.2 %collective-permute-start.5 = (bf16[272,128]{1,0:T(8,128)(2,1)S(1)}, bf16[272,128]{1,0:T(8,128)(2,1)S(1)}, u32[]{:S(2)}, u32[]{:S(2)}) collective-permute-start(bf16[272,128]{1,0:T(8,128)(2,1)S(1)} %sum.5), channel_id=1, source_target_pairs={{0,12},{4,8},{8,4},{12,0},{1,13},{5,9},{9,5},{13,1},{2,14},{6,10},... | collective-permute-start | bytes 208904 | tf_op jit(solution)/shard_map/ppermute | solution.py:19
  16.0 5.8 %collective-permute-start.4 = (bf16[272,128]{1,0:T(8,128)(2,1)S(1)}, bf16[272,128]{1,0:T(8,128)(2,1)S(1)}, u32[]{:S(2)}, u32[]{:S(2)}) collective-permute-start(bf16[272,128]{1,0:T(8,128)(2,1)S(1)} %sum.4), channel_id=1, source_target_pairs={{0,8},{4,12},{8,0},{12,4},{1,9},{5,13},{9,1},{13,5},{2,10},{6,14},... | collective-permute-start | bytes 208904 | tf_op jit(solution)/shard_map/ppermute | solution.py:19
  16.1 5.7 %collective-permute-start.3 = (bf16[272,128]{1,0:T(8,128)(2,1)S(1)}, bf16[272,128]{1,0:T(8,128)(2,1)S(1)}, u32[]{:S(2)}, u32[]{:S(2)}) collective-permute-start(bf16[272,128]{1,0:T(8,128)(2,1)S(1)} %sum.3), channel_id=1, source_target_pairs={{0,4},{4,0},{8,12},{12,8},{1,5},{5,1},{9,13},{13,9},{2,6},{6,2},{1... | collective-permute-start | bytes 208904 | tf_op jit(solution)/shard_map/ppermute | solution.py:19
  22.6 3.6 %collective-permute-start.8 = (bf16[16,16,128]{2,1,0:T(8,128)(2,1)S(1)}, bf16[16,16,128]{2,1,0:T(8,128)(2,1)S(1)}, u32[]{:S(2)}, u32[]{:S(2)}) collective-permute-start(bf16[16,16,128]{2,1,0:T(8,128)(2,1)S(1)} %get-tuple-element.71), channel_id=1, source_target_pairs={{0,4},{4,0},{8,12},{12,8},{1,5},{5,1},{9,13},{13,9},{2,6},{6,2},{1... | collective-permute-start | bytes 196616 | tf_op jit(solution)/shard_map/ppermute | solution.py:19
  22.7 6.2 %collective-permute-start.6 = (bf16[16,16,128]{2,1,0:T(8,128)(2,1)S(1)}, bf16[16,16,128]{2,1,0:T(8,128)(2,1)S(1)}, u32[]{:S(2)}, u32[]{:S(2)}) collective-permute-start(bf16[16,16,128]{2,1,0:T(8,128)(2,1)S(1)} %get-tuple-element.67), channel_id=1, source_target_pairs={{0,8},{4,12},{8,0},{12,4},{1,9},{5,13},{9,1},{13,5},{2,10},{6,14},... | collective-permute-start | bytes 196616 | tf_op jit(solution)/shard_map/ppermute | solution.py:19
  23.5 5.6 %collective-permute-start.7 = (bf16[16,16,128]{2,1,0:T(8,128)(2,1)S(1)}, bf16[16,16,128]{2,1,0:T(8,128)(2,1)S(1)}, u32[]{:S(2)}, u32[]{:S(2)}) collective-permute-start(bf16[16,16,128]{2,1,0:T(8,128)(2,1)S(1)} %get-tuple-element.68), channel_id=1, source_target_pairs={{0,12},{4,8},{8,4},{12,0},{1,13},{5,9},{9,5},{13,1},{2,14},{6,10},... | collective-permute-start | bytes 196616 | tf_op jit(solution)/shard_map/ppermute | solution.py:19
  26.3 5.5 %collective-permute-start.10 = (bf16[32,16,128]{2,1,0:T(8,128)(2,1)S(1)}, bf16[32,16,128]{2,1,0:T(8,128)(2,1)S(1)}, u32[]{:S(2)}, u32[]{:S(2)}) collective-permute-start(bf16[32,16,128]{2,1,0:T(8,128)(2,1)S(1)} %constant_dynamic-update-slice_fusion.refs_0_), channel_id=1, source_target_pairs={{0,2},{2,0},{1,3},{3,1},{4,6},{6,4},{5,7},{7,5},{8,10},{10,8},{9,1... | collective-permute-start | bytes 393224 | tf_op jit(solution)/shard_map/ppermute | solution.py:19
  29.1 5.1 %collective-permute-start.9 = (bf16[32,16,128]{2,1,0:T(8,128)(2,1)S(1)}, bf16[32,16,128]{2,1,0:T(8,128)(2,1)S(1)}, u32[]{:S(2)}, u32[]{:S(2)}) collective-permute-start(bf16[32,16,128]{2,1,0:T(8,128)(2,1)S(1)} %pad_maximum_fusion), channel_id=1, source_target_pairs={{0,2},{2,0},{1,3},{3,1},{4,6},{6,4},{5,7},{7,5},{8,10},{10,8},{9,1... | collective-permute-start | bytes 393224 | tf_op jit(solution)/shard_map/ppermute | solution.py:19
  35.7 5.5 %collective-permute-start.11 = (bf16[256,256]{1,0:T(8,128)(2,1)S(1)}, bf16[256,256]{1,0:T(8,128)(2,1)S(1)}, u32[]{:S(2)}, u32[]{:S(2)}) collective-permute-start(bf16[256,256]{1,0:T(8,128)(2,1)S(1)} %select_select_fusion), channel_id=1, source_target_pairs={{0,1},{1,0},{2,3},{3,2},{4,5},{5,4},{6,7},{7,6},{8,9},{9,8},{10,11... | collective-permute-start | bytes 393224 | tf_op jit(solution)/shard_map/ppermute | solution.py:19

commit v9 on v8

--- a/solution.py
+++ b/solution.py
@@ -404,7 +404,8 @@
     halves = {1: far_ks, 0: near_ks[::-1]}
     half_rows = here // 2
     filtered, projected = {}, {}
-    keys = [((turn + 1) % plane_count, far) for turn in range(plane_count) for far in (0, 1)]
+    flips = [(turn + 1) % plane_count for turn in range(plane_count)]
+    keys = [(flip, far) for far in (1, 0) for flip in flips]
     for turn, (flip, far) in enumerate(keys):
         smooth, filtered[flip, far], mine = call(
             functools.partial(forward_kernel, flip, far, turn == 0, wide, halves[far]), "forward",

time: 43.8 us -> 42.8 us (0.977)
  starting transfers between devices: 17.2 us -> 16.4 us
    ppermute x12, starting transfers between devices: 17.2 us -> 16.4 us  [exchange(): return lax.ppermute(cells, axis, [(i, i ^ flip) for i in range(count)])]
  transfers between devices with their start and end apart: 12 -> 12, of which waited for: 4 -> 4; matrix products, arithmetic and copies ran while one was open for 4% -> 4% of each run, Pallas kernels for 21% -> 24%
where the time goes in v9:
time: 42.8 us; the launch traced here: 42.6 us
  starting transfers between devices  16.4 us (38%)
  Pallas kernels  16.1 us (38%)
  waiting for transfers between devices  6.4 us (15%)
  local copies, waits for them, and re-layouts  2.26 us (5%)
  between operations  0.87 us (2%)
  other arithmetic  0.54 us (1%)
    ppermute x12, starting transfers between devices, exchange(): return lax.ppermute(cells, axis, [(i, i ^ flip) for i in range(count)])  16.4 us
    ppermute x12, waiting for transfers between devices, exchange(): return lax.ppermute(cells, axis, [(i, i ^ flip) for i in range(count)])  6.4 us
    pallas_call x4, Pallas kernels, subtract(): call(functools.partial(residual_kernel, flip, far, wide, spots), 'residua...  5.57 us
    pallas_call x4, Pallas kernels, on_device(): call(functools.partial(forward_kernel, flip, far, turn == 0, wide, halves...  4.41 us
    pallas_call x1, Pallas kernels, on_device(): pl.pallas_call(functools.partial(backward_kernel, back_keys, wide), out_s...  2.37 us
    pallas_call x1, Pallas kernels, on_device(): pl.pallas_call(functools.partial(prepare_kernel, rim, cuts), out_shape=(s...  1.9 us
    unnamed x13, local copies, waits for them, and re-layouts  1.32 us
    pallas_call x1, Pallas kernels, on_device(): call(functools.partial(bands_kernel, rim, frames), 'bands', [(width, widt...  1 us
  transfers between devices with their start and end apart: 12, of which 4 were waited for; matrix products, arithmetic and copies ran while one was open for 4% of the time, Pallas kernels for 24%

profile of v9, /device:TPU:1, one launch (start us, length us, event | category | flops | bytes accessed | tf_op | source)
XLA Modules:
  0.0 42.6 jit_solution(716084277798524970)
XLA Ops:
  0.6 0.9 %constant_dynamic-slice_fusion = bf16[2,16,16,128]{3,2,1,0:T(8,128)(2,1)S(1)} fusion(bf16[2,16,128,128]{3,2,1,0:T(8,128)(2,1)} %movie_hbm.1, s32[]{:T(128)S(6)} %select_n.131), kind=kLoop, calls=%fused_computation.15 | loop fusion | bytes 262148 | tf_op jit(solution)/shard_map/dynamic_slice | solution.py:369
  1.6 0.1 collective-permute-start
  1.7 1.9 %prepare.1 = (bf16[16,160,256]{2,1,0:T(8,128)(2,1)S(1)}, bf16[128,128]{1,0:T(8,128)(2,1)S(1)}, bf16[256,768]{1,0:T(8,128)(2,1)S(1)}, s32[128,128]{1,0:T(8,128)S(...) custom-call(f32[25]{0:T(128)} %col_ref, f32[25]{0:T(128)} %row_ref, bf16[2,16,128,128]{3,2,1,0:T(8,128)(2,1)} %movie_hbm.1, ...), custom_call_target="tpu_custom_call" | custom-call | tf_op jit(solution)/shard_map/prepare/pallas_call | solution.py:372
  3.6 0.0 copy-start.3
  3.6 0.0 collective-permute-done.edge_ref
  3.6 1.2 %forward.4 = (bf16[16,160,256]{2,1,0:T(8,128)(2,1)S(1)}, bf16[512,256]{1,0:T(8,128)(2,1)S(1)}, bf16[512,128]{1,0:T(8,128)(2,1)S(1)}) custom-call(bf16[16,160,256]{2,1,0:T(8,128)(2,1)S(1)} %get-tuple-element.46.smooth_in_ref, bf16[2,16,16,128]{3,2,1,0:T(8,128)(2,1)S(1)} %collective-permute-done.edge_ref, ...), custom_call_target="tpu_custom_call", output_to_operand_aliasing={{0}: (0, {})} | custom-call | tf_op jit(solution)/shard_map/forward/pallas_call | solution.py:410
  4.9 0.0 copy-done.3
  4.9 2.7 %collective-permute-start.2 = (bf16[512,128]{1,0:T(8,128)(2,1)S(1)}, bf16[512,128]{1,0:T(8,128)(2,1)S(1)}, u32[]{:S(2)}, u32[]{:S(2)}) collective-permute-start(bf16[512,128]{1,0:T(8,128)(2,1)S(1)} %get-tuple-element.61), channel_id=1, source_target_pairs={{0,2},{2,0},{1,3},{3,1},{4,6},{6,4},{5,7},{7,5},{8,10},{10,8},{9,1... | collective-permute-start | bytes 393224 | tf_op jit(solution)/shard_map/ppermute | solution.py:19
  7.6 1.0 %forward.5 = (bf16[16,160,256]{2,1,0:T(8,128)(2,1)S(1)}, bf16[512,256]{1,0:T(8,128)(2,1)S(1)}, bf16[512,128]{1,0:T(8,128)(2,1)S(1)}) custom-call(bf16[16,160,256]{2,1,0:T(8,128)(2,1)S(1)} %get-tuple-element.53.smooth_in_ref, bf16[2,16,16,128]{3,2,1,0:T(8,128)(2,1)S(1)} %collective-permute-done.edge_ref, ...), custom_call_target="tpu_custom_call", output_to_operand_aliasing={{0}: (0, {})} | custom-call | tf_op jit(solution)/shard_map/forward/pallas_call | solution.py:410
  8.7 0.0 copy-start.4
  8.7 1.1 %forward.6 = (bf16[16,160,256]{2,1,0:T(8,128)(2,1)S(1)}, bf16[512,256]{1,0:T(8,128)(2,1)S(1)}, bf16[512,128]{1,0:T(8,128)(2,1)S(1)}) custom-call(bf16[16,160,256]{2,1,0:T(8,128)(2,1)S(1)} %get-tuple-element.56.smooth_in_ref, bf16[2,16,16,128]{3,2,1,0:T(8,128)(2,1)S(1)} %collective-permute-done.edge_ref, ...), custom_call_target="tpu_custom_call", output_to_operand_aliasing={{0}: (0, {})} | custom-call | tf_op jit(solution)/shard_map/forward/pallas_call | solution.py:410
  9.7 0.1 collective-permute-start.1
  9.8 0.0 copy-done.4
  9.8 0.1 broadcast_multiply_fusion
  9.9 0.1 select_reduce_fusion
  10.1 0.0 copy-start.1
  10.1 0.0 copy-start.2
  10.1 1.1 %forward.7 = (bf16[16,160,256]{2,1,0:T(8,128)(2,1)S(1)}, bf16[512,256]{1,0:T(8,128)(2,1)S(1)}, bf16[512,128]{1,0:T(8,128)(2,1)S(1)}) custom-call(bf16[16,160,256]{2,1,0:T(8,128)(2,1)S(1)} %get-tuple-element.57.smooth_in_ref, bf16[2,16,16,128]{3,2,1,0:T(8,128)(2,1)S(1)} %collective-permute-done.edge_ref, ...), custom_call_target="tpu_custom_call", output_to_operand_aliasing={{0}: (0, {})} | custom-call | tf_op jit(solution)/shard_map/forward/pallas_call | solution.py:410
  11.2 0.3 collective-permute-done.2.refs_1_
  11.5 3.4 %collective-permute-start.5 = (bf16[272,128]{1,0:T(8,128)(2,1)S(1)}, bf16[272,128]{1,0:T(8,128)(2,1)S(1)}, u32[]{:S(2)}, u32[]{:S(2)}) collective-permute-start(bf16[272,128]{1,0:T(8,128)(2,1)S(1)} %sum.5), channel_id=1, source_target_pairs={{0,12},{4,8},{8,4},{12,0},{1,13},{5,9},{9,5},{13,1},{2,14},{6,10},... | collective-permute-start | bytes 208904 | tf_op jit(solution)/shard_map/ppermute | solution.py:19
  14.9 0.1 collective-permute-start.4
  15.0 0.0 collective-permute-done.1.refs_1_
  15.1 0.9 %collective-permute-start.3 = (bf16[272,128]{1,0:T(8,128)(2,1)S(1)}, bf16[272,128]{1,0:T(8,128)(2,1)S(1)}, u32[]{:S(2)}, u32[]{:S(2)}) collective-permute-start(bf16[272,128]{1,0:T(8,128)(2,1)S(1)} %sum.3), channel_id=1, source_target_pairs={{0,4},{4,0},{8,12},{12,8},{1,5},{5,1},{9,13},{13,9},{2,6},{6,2},{1... | collective-permute-start | bytes 208904 | tf_op jit(solution)/shard_map/ppermute | solution.py:19
  16.0 1.0 %bands.1 = (bf16[256,256]{1,0:T(8,128)(2,1)S(1)}, bf16[256,768]{1,0:T(8,128)(2,1)S(1)}) custom-call(f32[25]{0:T(128)S(1)} %copy-done, f32[25]{0:T(128)S(1)} %copy-done.1), custom_call_target="tpu_custom_call" | custom-call | tf_op jit(solution)/shard_map/bands/pallas_call | solution.py:443
  17.0 0.0 collective-permute-done.5.refs_4_
  17.0 3.9 %collective-permute-done.4.refs_3_ = bf16[272,128]{1,0:T(8,128)(2,1)S(1)} collective-permute-done((bf16[272,128]{1,0:T(8,128)(2,1)S(1)}, bf16[272,128]{1,0:T(8,128)(2,1)S(1)}, u32[]{:S(2)}, u32[]{:S(2)}) %collective-permute-start.4) | collective-permute-done | bytes 69664 | tf_op jit(solution)/shard_map/ppermute | solution.py:19
  20.9 0.0 collective-permute-done.3.refs_2_
  20.9 0.8 %mix.1 = (bf16[16,16,128]{2,1,0:T(8,128)(2,1)S(1)}, bf16[16,16,128]{2,1,0:T(8,128)(2,1)S(1)}, bf16[16,16,128]{2,1,0:T(8,128)(2,1)S(1)}, bf16[16,16,128]{2,1,0:T(8,128)(2,1)S(1)}) custom-call(s32[1,128]{1,0:T(1,128)S(1)} %bitcast.10, bf16[16,128]{1,0:T(8,128)(2,1)S(1)} %pad_bitcast_fusion.lag_ref, bf16[512,128]{1,0:T(8,128)(2,1)S(1)} %get-tuple-element.66.refs_0_, ...), custom_call_target="tpu_custom_call" | custom-call | tf_op jit(solution)/shard_map/mix/pallas_call | solution.py:451
  21.7 0.1 collective-permute-start.8
  21.8 1.8 %collective-permute-start.6 = (bf16[16,16,128]{2,1,0:T(8,128)(2,1)S(1)}, bf16[16,16,128]{2,1,0:T(8,128)(2,1)S(1)}, u32[]{:S(2)}, u32[]{:S(2)}) collective-permute-start(bf16[16,16,128]{2,1,0:T(8,128)(2,1)S(1)} %get-tuple-element.67), channel_id=1, source_target_pairs={{0,8},{4,12},{8,0},{12,4},{1,9},{5,13},{9,1},{13,5},{2,10},{6,14},... | collective-permute-start | bytes 196616 | tf_op jit(solution)/shard_map/ppermute | solution.py:19
  23.6 1.7 %collective-permute-start.7 = (bf16[16,16,128]{2,1,0:T(8,128)(2,1)S(1)}, bf16[16,16,128]{2,1,0:T(8,128)(2,1)S(1)}, u32[]{:S(2)}, u32[]{:S(2)}) collective-permute-start(bf16[16,16,128]{2,1,0:T(8,128)(2,1)S(1)} %get-tuple-element.68), channel_id=1, source_target_pairs={{0,12},{4,8},{8,4},{12,0},{1,13},{5,9},{9,5},{13,1},{2,14},{6,10},... | collective-permute-start | bytes 196616 | tf_op jit(solution)/shard_map/ppermute | solution.py:19
  25.4 0.0 collective-permute-done.8
  25.4 1.1 %collective-permute-start.10 = (bf16[32,16,128]{2,1,0:T(8,128)(2,1)S(1)}, bf16[32,16,128]{2,1,0:T(8,128)(2,1)S(1)}, u32[]{:S(2)}, u32[]{:S(2)}) collective-permute-start(bf16[32,16,128]{2,1,0:T(8,128)(2,1)S(1)} %constant_dynamic-update-slice_fusion.refs_0_), channel_id=1, source_target_pairs={{0,2},{2,0},{1,3},{3,1},{4,6},{6,4},{5,7},{7,5},{8,10},{10,8},{9,1... | collective-permute-start | bytes 393224 | tf_op jit(solution)/shard_map/ppermute | solution.py:19
  26.4 1.4 %residual.4 = (bf16[512,256]{1,0:T(8,128)(2,1)S(1)}, bf16[256,256]{1,0:T(8,128)(2,1)S(1)}, bf16[32,16,128]{2,1,0:T(8,128)(2,1)S(1)}) custom-call(bf16[512,256]{1,0:T(8,128)(2,1)S(1)} %get-tuple-element.69.filtered_ref, s32[128,128]{1,0:T(8,128)S(1)} %get-tuple-element.49.code_ref, bf16[512,256]{1,0:T(8,128)(2,1)S(1)} %get-tuple-element.52.templates_ref, ...), custom_call_target="tpu_custom_call" | custom-call | tf_op jit(solution)/shard_map/residual/pallas_call | solution.py:472
  27.8 0.0 collective-permute-done.6.refs_0_
  27.8 1.5 %collective-permute-done.7.refs_1_ = bf16[16,16,128]{2,1,0:T(8,128)(2,1)S(1)} collective-permute-done((bf16[16,16,128]{2,1,0:T(8,128)(2,1)S(1)}, bf16[16,16,128]{2,1,0:T(8,128)(2,1)S(1)}, u32[]{:S(2)}, u32[]{:S(2)}) %collective-permute-start.7) | collective-permute-done | bytes 65568 | tf_op jit(solution)/shard_map/ppermute | solution.py:19
  29.3 0.4 collective-permute-start.9
  29.7 1.4 %residual.7 = (bf16[512,256]{1,0:T(8,128)(2,1)S(1)}, bf16[256,256]{1,0:T(8,128)(2,1)S(1)}, bf16[32,16,128]{2,1,0:T(8,128)(2,1)S(1)}) custom-call(bf16[512,256]{1,0:T(8,128)(2,1)S(1)} %get-tuple-element.78.filtered_ref, s32[128,128]{1,0:T(8,128)S(1)} %get-tuple-element.49.code_ref, bf16[512,256]{1,0:T(8,128)(2,1)S(1)} %get-tuple-element.52.templates_ref, ...), custom_call_target="tpu_custom_call" | custom-call | tf_op jit(solution)/shard_map/residual/pallas_call | solution.py:472
  31.1 0.0 collective-permute-done.10.refs_0_
  31.1 1.4 %residual.6 = (bf16[512,256]{1,0:T(8,128)(2,1)S(1)}, bf16[256,256]{1,0:T(8,128)(2,1)S(1)}, bf16[32,16,128]{2,1,0:T(8,128)(2,1)S(1)}) custom-call(bf16[512,256]{1,0:T(8,128)(2,1)S(1)} %get-tuple-element.76.filtered_ref, s32[128,128]{1,0:T(8,128)S(1)} %get-tuple-element.49.code_ref, bf16[512,256]{1,0:T(8,128)(2,1)S(1)} %get-tuple-element.52.templates_ref, ...), custom_call_target="tpu_custom_call" | custom-call | tf_op jit(solution)/shard_map/residual/pallas_call | solution.py:472
  32.5 0.7 %collective-permute-done.9.refs_0_ = bf16[32,16,128]{2,1,0:T(8,128)(2,1)S(1)} collective-permute-done((bf16[32,16,128]{2,1,0:T(8,128)(2,1)S(1)}, bf16[32,16,128]{2,1,0:T(8,128)(2,1)S(1)}, u32[]{:S(2)}, u32[]{:S(2)}) %collective-permute-start.9) | collective-permute-done | bytes 131104 | tf_op jit(solution)/shard_map/ppermute | solution.py:19
  33.2 1.4 %residual.5 = (bf16[512,256]{1,0:T(8,128)(2,1)S(1)}, bf16[256,256]{1,0:T(8,128)(2,1)S(1)}, bf16[32,16,128]{2,1,0:T(8,128)(2,1)S(1)}) custom-call(bf16[512,256]{1,0:T(8,128)(2,1)S(1)} %get-tuple-element.51.filtered_ref, s32[128,128]{1,0:T(8,128)S(1)} %get-tuple-element.49.code_ref, bf16[512,256]{1,0:T(8,128)(2,1)S(1)} %get-tuple-element.52.templates_ref, ...), custom_call_target="tpu_custom_call" | custom-call | tf_op jit(solution)/shard_map/residual/pallas_call | solution.py:472
  34.6 4.0 %collective-permute-start.11 = (bf16[256,256]{1,0:T(8,128)(2,1)S(1)}, bf16[256,256]{1,0:T(8,128)(2,1)S(1)}, u32[]{:S(2)}, u32[]{:S(2)}) collective-permute-start(bf16[256,256]{1,0:T(8,128)(2,1)S(1)} %select_select_fusion), channel_id=1, source_target_pairs={{0,1},{1,0},{2,3},{3,2},{4,5},{5,4},{6,7},{7,6},{8,9},{9,8},{10,11... | collective-permute-start | bytes 393224 | tf_op jit(solution)/shard_map/ppermute | solution.py:19
  38.7 0.1 select_select_fusion.4
  38.7 0.2 fusion
  38.9 1.3 %copy.16 = bf16[64,16,128]{2,1,0:T(8,128)(2,1)} copy(bf16[64,16,128]{0,1,2:T(8,128)(2,1)S(1)} %fusion) | data formatting | bytes 524288
  40.2 0.0 collective-permute-done.11.edge_ref
  40.2 2.4 %backward.1 = bf16[2,16,128,128]{3,2,1,0:T(8,128)(2,1)} custom-call(bf16[256,256]{1,0:T(8,128)(2,1)S(1)} %collective-permute-done.11.edge_ref, bf16[256,256]{1,0:T(8,128)(2,1)S(1)} %get-tuple-element.84.col_adj_ref, bf16[256,768]{1,0:T(8,128)(2,1)S(1)} %get-tuple-element.85.row_adj_ref, bf16[512,256]{1,0:T(8,128)(2,1)S(1)} %get-tuple-element.86.refs_0_, ...), custom_call_target="tpu_custom_call" | custom-call | tf_op jit(solution)/shard_map/backward/pallas_call | solution.py:501
  (15 shorter events, 0.1 us)
Async XLA Ops:
  1.6 2.1 %collective-permute-start = (bf16[2,16,16,128]{3,2,1,0:T(8,128)(2,1)S(1)}, bf16[2,16,16,128]{3,2,1,0:T(8,128)(2,1)S(1)}, u32[]{:S(2)}, u32[]{:S(2)}) collective-permute-start(bf16[2,16,16,128]{3,2,1,0:T(8,128)(2,1)S(1)} %constant_dynamic-slice_fusion), channel_id=1, source_target_pairs={{0,1},{1,0},{2,3},{3,2},{4,5},{5,4},{6,7},{7,6},{8,9},{9,8},{10,11... | collective-permute-start | bytes 393224 | tf_op jit(solution)/shard_map/ppermute | solution.py:19
  3.6 1.3 %copy-start.3 = (f32[1,3,65]{2,0,1:T(1,128)S(1)}, f32[1,3,65]{2,0,1:T(1,128)}, u32[]{:S(2)}) copy-start(f32[1,3,65]{2,0,1:T(1,128)} %param.16) | copy-start | bytes 2344
  4.9 6.6 %collective-permute-start.2 = (bf16[512,128]{1,0:T(8,128)(2,1)S(1)}, bf16[512,128]{1,0:T(8,128)(2,1)S(1)}, u32[]{:S(2)}, u32[]{:S(2)}) collective-permute-start(bf16[512,128]{1,0:T(8,128)(2,1)S(1)} %get-tuple-element.61), channel_id=1, source_target_pairs={{0,2},{2,0},{1,3},{3,1},{4,6},{6,4},{5,7},{7,5},{8,10},{10,8},{9,1... | collective-permute-start | bytes 393224 | tf_op jit(solution)/shard_map/ppermute | solution.py:19
  8.7 1.2 %copy-start.4 = (s32[1,3]{1,0:T(1,128)S(1)}, s32[1,3]{1,0:T(1,128)}, u32[]{:S(2)}) copy-start(s32[1,3]{1,0:T(1,128)} %param.17) | copy-start | bytes 40
  9.7 5.3 %collective-permute-start.1 = (bf16[512,128]{1,0:T(8,128)(2,1)S(1)}, bf16[512,128]{1,0:T(8,128)(2,1)S(1)}, u32[]{:S(2)}, u32[]{:S(2)}) collective-permute-start(bf16[512,128]{1,0:T(8,128)(2,1)S(1)} %get-tuple-element.59), channel_id=1, source_target_pairs={{0,2},{2,0},{1,3},{3,1},{4,6},{6,4},{5,7},{7,5},{8,10},{10,8},{9,1... | collective-permute-start | bytes 393224 | tf_op jit(solution)/shard_map/ppermute | solution.py:19
  10.0 5.9 %copy-start = (f32[25]{0:T(128)S(1)}, f32[25]{0:T(128)}, u32[]{:S(2)}) copy-start(f32[25]{0:T(128)} %col_ref) | copy-start | bytes 304
  10.1 5.9 %copy-start.1 = (f32[25]{0:T(128)S(1)}, f32[25]{0:T(128)}, u32[]{:S(2)}) copy-start(f32[25]{0:T(128)} %row_ref) | copy-start | bytes 304
  10.1 10.9 %copy-start.2 = (s32[128,1]{0,1:T(1,128)S(1)}, s32[128,1]{0,1:T(1,128)}, u32[]{:S(2)}) copy-start(s32[128,1]{0,1:T(1,128)} %param.11) | copy-start | bytes 1540
  11.5 5.5 %collective-permute-start.5 = (bf16[272,128]{1,0:T(8,128)(2,1)S(1)}, bf16[272,128]{1,0:T(8,128)(2,1)S(1)}, u32[]{:S(2)}, u32[]{:S(2)}) collective-permute-start(bf16[272,128]{1,0:T(8,128)(2,1)S(1)} %sum.5), channel_id=1, source_target_pairs={{0,12},{4,8},{8,4},{12,0},{1,13},{5,9},{9,5},{13,1},{2,14},{6,10},... | collective-permute-start | bytes 208904 | tf_op jit(solution)/shard_map/ppermute | solution.py:19
  14.9 6.0 %collective-permute-start.4 = (bf16[272,128]{1,0:T(8,128)(2,1)S(1)}, bf16[272,128]{1,0:T(8,128)(2,1)S(1)}, u32[]{:S(2)}, u32[]{:S(2)}) collective-permute-start(bf16[272,128]{1,0:T(8,128)(2,1)S(1)} %sum.4), channel_id=1, source_target_pairs={{0,8},{4,12},{8,0},{12,4},{1,9},{5,13},{9,1},{13,5},{2,10},{6,14},... | collective-permute-start | bytes 208904 | tf_op jit(solution)/shard_map/ppermute | solution.py:19
  15.1 5.9 %collective-permute-start.3 = (bf16[272,128]{1,0:T(8,128)(2,1)S(1)}, bf16[272,128]{1,0:T(8,128)(2,1)S(1)}, u32[]{:S(2)}, u32[]{:S(2)}) collective-permute-start(bf16[272,128]{1,0:T(8,128)(2,1)S(1)} %sum.3), channel_id=1, source_target_pairs={{0,4},{4,0},{8,12},{12,8},{1,5},{5,1},{9,13},{13,9},{2,6},{6,2},{1... | collective-permute-start | bytes 208904 | tf_op jit(solution)/shard_map/ppermute | solution.py:19
  21.7 3.6 %collective-permute-start.8 = (bf16[16,16,128]{2,1,0:T(8,128)(2,1)S(1)}, bf16[16,16,128]{2,1,0:T(8,128)(2,1)S(1)}, u32[]{:S(2)}, u32[]{:S(2)}) collective-permute-start(bf16[16,16,128]{2,1,0:T(8,128)(2,1)S(1)} %get-tuple-element.71), channel_id=1, source_target_pairs={{0,4},{4,0},{8,12},{12,8},{1,5},{5,1},{9,13},{13,9},{2,6},{6,2},{1... | collective-permute-start | bytes 196616 | tf_op jit(solution)/shard_map/ppermute | solution.py:19
  21.8 6.0 %collective-permute-start.6 = (bf16[16,16,128]{2,1,0:T(8,128)(2,1)S(1)}, bf16[16,16,128]{2,1,0:T(8,128)(2,1)S(1)}, u32[]{:S(2)}, u32[]{:S(2)}) collective-permute-start(bf16[16,16,128]{2,1,0:T(8,128)(2,1)S(1)} %get-tuple-element.67), channel_id=1, source_target_pairs={{0,8},{4,12},{8,0},{12,4},{1,9},{5,13},{9,1},{13,5},{2,10},{6,14},... | collective-permute-start | bytes 196616 | tf_op jit(solution)/shard_map/ppermute | solution.py:19
  23.6 5.7 %collective-permute-start.7 = (bf16[16,16,128]{2,1,0:T(8,128)(2,1)S(1)}, bf16[16,16,128]{2,1,0:T(8,128)(2,1)S(1)}, u32[]{:S(2)}, u32[]{:S(2)}) collective-permute-start(bf16[16,16,128]{2,1,0:T(8,128)(2,1)S(1)} %get-tuple-element.68), channel_id=1, source_target_pairs={{0,12},{4,8},{8,4},{12,0},{1,13},{5,9},{9,5},{13,1},{2,14},{6,10},... | collective-permute-start | bytes 196616 | tf_op jit(solution)/shard_map/ppermute | solution.py:19
  25.4 5.7 %collective-permute-start.10 = (bf16[32,16,128]{2,1,0:T(8,128)(2,1)S(1)}, bf16[32,16,128]{2,1,0:T(8,128)(2,1)S(1)}, u32[]{:S(2)}, u32[]{:S(2)}) collective-permute-start(bf16[32,16,128]{2,1,0:T(8,128)(2,1)S(1)} %constant_dynamic-update-slice_fusion.refs_0_), channel_id=1, source_target_pairs={{0,2},{2,0},{1,3},{3,1},{4,6},{6,4},{5,7},{7,5},{8,10},{10,8},{9,1... | collective-permute-start | bytes 393224 | tf_op jit(solution)/shard_map/ppermute | solution.py:19
  29.3 3.9 %collective-permute-start.9 = (bf16[32,16,128]{2,1,0:T(8,128)(2,1)S(1)}, bf16[32,16,128]{2,1,0:T(8,128)(2,1)S(1)}, u32[]{:S(2)}, u32[]{:S(2)}) collective-permute-start(bf16[32,16,128]{2,1,0:T(8,128)(2,1)S(1)} %pad_maximum_fusion), channel_id=1, source_target_pairs={{0,2},{2,0},{1,3},{3,1},{4,6},{6,4},{5,7},{7,5},{8,10},{10,8},{9,1... | collective-permute-start | bytes 393224 | tf_op jit(solution)/shard_map/ppermute | solution.py:19
  34.6 5.6 %collective-permute-start.11 = (bf16[256,256]{1,0:T(8,128)(2,1)S(1)}, bf16[256,256]{1,0:T(8,128)(2,1)S(1)}, u32[]{:S(2)}, u32[]{:S(2)}) collective-permute-start(bf16[256,256]{1,0:T(8,128)(2,1)S(1)} %select_select_fusion), channel_id=1, source_target_pairs={{0,1},{1,0},{2,3},{3,2},{4,5},{5,4},{6,7},{7,6},{8,9},{9,8},{10,11... | collective-permute-start | bytes 393224 | tf_op jit(solution)/shard_map/ppermute | solution.py:19

commit v10 on v9

--- a/solution.py
+++ b/solution.py
@@ -73,6 +73,10 @@
     spread = jnp.dot(tall, right, preferred_element_type=F32)
     same = remainder(iota((out_rows, depth), 1), frames) == quotient(iota((out_rows, depth), 0), BLOCK)
     return jnp.where(same, spread, 0.0).astype(BF16)
+
+
+def aligned(start, size):
+    return pl.ds(start if size % 8 else pl.multiple_of(start, size), size)
 
 
 def half_of(flip, far, wide):
@@ -250,32 +254,27 @@
         source, offset = traces[source], offset * share
         top = base + block * share
         for g in range(share // group):
-            support = code_ref[pl.ds(top + g * group, group), :] >> 1
+            support = code_ref[aligned(top + g * group, group), :] >> 1
             support = jnp.concatenate([support] * (8 // group), axis=0)
-            columns = [
-                jnp.transpose(
-                    jnp.where(quotient(support, tile) == t, support & (tile - 1), -1).astype(F32)
-                )
-                for t in range(names // tile)
-            ]
+            columns = jnp.transpose(support.astype(F32))
             for i in range(group):
                 h = g * group + i
-                hits = jnp.concatenate(
-                    [
+                named = jnp.broadcast_to(columns[:, i : i + 1], (lanes, lanes))
+                hits = []
+                for t in range(names // tile):
+                    offset_name = (named - float(t * tile)).astype(BF16)
+                    hits.append(
                         jnp.where(
-                            marks
-                            == jnp.broadcast_to(column[:, i : i + 1], (lanes, tile)).astype(BF16),
+                            marks == jnp.concatenate([offset_name] * 2, axis=1),
                             jnp.ones((), BF16), jnp.zeros((), BF16),
                         )
-                        for column in columns
-                    ],
-                    axis=1,
-                )
+                    )
+                hits = jnp.concatenate(hits, axis=1)
                 slots_ref[n, h * frames : (h + 1) * frames, :] = jnp.dot(
                     source[offset + h], hits, preferred_element_type=F32
                 ).astype(BF16)
         model = jnp.dot(slots_ref[n], templates_ref[...], preferred_element_type=F32)
-        mask = (code_ref[pl.ds(top, share), :] & 1).astype(F32)
+        mask = (code_ref[aligned(top, share), :] & 1).astype(F32)
         mask = jnp.broadcast_to(mask[:, None, :], (share, frames, lanes)).reshape(-1, lanes)
         size = share * frames
         spot = pl.ds(pl.multiple_of(block * size, size), size)

time: 42.8 us -> 42.6 us (level)
  Pallas kernels: 16.1 us -> 15.6 us
    pallas_call x4, Pallas kernels: 5.57 us -> 5.04 us  [subtract(): call(functools.partial(residual_kernel, flip, far, wide, spots), 'residua...]
  transfers between devices with their start and end apart: 12 -> 12, of which waited for: 4 -> 4; matrix products, arithmetic and copies ran while one was open for 4% -> 4% of each run, Pallas kernels for 24% -> 23%
where the time goes in v10:
time: 42.6 us; the launch traced here: 42.5 us
  starting transfers between devices  16.4 us (38%)
  Pallas kernels  15.6 us (37%)
  waiting for transfers between devices  6.8 us (16%)
  local copies, waits for them, and re-layouts  2.26 us (5%)
  between operations  0.87 us (2%)
  other arithmetic  0.54 us (1%)
    ppermute x12, starting transfers between devices, exchange(): return lax.ppermute(cells, axis, [(i, i ^ flip) for i in range(count)])  16.4 us
    ppermute x12, waiting for transfers between devices, exchange(): return lax.ppermute(cells, axis, [(i, i ^ flip) for i in range(count)])  6.8 us
    pallas_call x4, Pallas kernels, subtract(): call(functools.partial(residual_kernel, flip, far, wide, spots), 'residua...  5.04 us
    pallas_call x4, Pallas kernels, on_device(): call(functools.partial(forward_kernel, flip, far, turn == 0, wide, halves...  4.41 us
    pallas_call x1, Pallas kernels, on_device(): pl.pallas_call(functools.partial(backward_kernel, back_keys, wide), out_s...  2.38 us
    pallas_call x1, Pallas kernels, on_device(): pl.pallas_call(functools.partial(prepare_kernel, rim, cuts), out_shape=(s...  1.9 us
    unnamed x13, local copies, waits for them, and re-layouts  1.32 us
    pallas_call x1, Pallas kernels, on_device(): call(functools.partial(bands_kernel, rim, frames), 'bands', [(width, widt...  1 us
  transfers between devices with their start and end apart: 12, of which 4 were waited for; matrix products, arithmetic and copies ran while one was open for 4% of the time, Pallas kernels for 23%

profile of v10, /device:TPU:1, one launch (start us, length us, event | category | flops | bytes accessed | tf_op | source)
XLA Modules:
  0.0 42.5 jit_solution(9568152239096240718)
XLA Ops:
  0.6 0.9 %constant_dynamic-slice_fusion = bf16[2,16,16,128]{3,2,1,0:T(8,128)(2,1)S(1)} fusion(bf16[2,16,128,128]{3,2,1,0:T(8,128)(2,1)} %movie_hbm.1, s32[]{:T(128)S(6)} %select_n.131), kind=kLoop, calls=%fused_computation.15 | loop fusion | bytes 262148 | tf_op jit(solution)/shard_map/dynamic_slice | solution.py:368
  1.6 0.1 collective-permute-start
  1.7 1.9 %prepare.1 = (bf16[16,160,256]{2,1,0:T(8,128)(2,1)S(1)}, bf16[128,128]{1,0:T(8,128)(2,1)S(1)}, bf16[256,768]{1,0:T(8,128)(2,1)S(1)}, s32[128,128]{1,0:T(8,128)S(...) custom-call(f32[25]{0:T(128)} %col_ref, f32[25]{0:T(128)} %row_ref, bf16[2,16,128,128]{3,2,1,0:T(8,128)(2,1)} %movie_hbm.1, ...), custom_call_target="tpu_custom_call" | custom-call | tf_op jit(solution)/shard_map/prepare/pallas_call | solution.py:371
  3.6 0.0 copy-start.3
  3.6 0.0 collective-permute-done.edge_ref
  3.6 1.2 %forward.4 = (bf16[16,160,256]{2,1,0:T(8,128)(2,1)S(1)}, bf16[512,256]{1,0:T(8,128)(2,1)S(1)}, bf16[512,128]{1,0:T(8,128)(2,1)S(1)}) custom-call(bf16[16,160,256]{2,1,0:T(8,128)(2,1)S(1)} %get-tuple-element.46.smooth_in_ref, bf16[2,16,16,128]{3,2,1,0:T(8,128)(2,1)S(1)} %collective-permute-done.edge_ref, ...), custom_call_target="tpu_custom_call", output_to_operand_aliasing={{0}: (0, {})} | custom-call | tf_op jit(solution)/shard_map/forward/pallas_call | solution.py:409
  4.9 0.0 copy-done.3
  4.9 2.7 %collective-permute-start.2 = (bf16[512,128]{1,0:T(8,128)(2,1)S(1)}, bf16[512,128]{1,0:T(8,128)(2,1)S(1)}, u32[]{:S(2)}, u32[]{:S(2)}) collective-permute-start(bf16[512,128]{1,0:T(8,128)(2,1)S(1)} %get-tuple-element.61), channel_id=1, source_target_pairs={{0,2},{2,0},{1,3},{3,1},{4,6},{6,4},{5,7},{7,5},{8,10},{10,8},{9,1... | collective-permute-start | bytes 393224 | tf_op jit(solution)/shard_map/ppermute | solution.py:19
  7.6 1.0 %forward.5 = (bf16[16,160,256]{2,1,0:T(8,128)(2,1)S(1)}, bf16[512,256]{1,0:T(8,128)(2,1)S(1)}, bf16[512,128]{1,0:T(8,128)(2,1)S(1)}) custom-call(bf16[16,160,256]{2,1,0:T(8,128)(2,1)S(1)} %get-tuple-element.53.smooth_in_ref, bf16[2,16,16,128]{3,2,1,0:T(8,128)(2,1)S(1)} %collective-permute-done.edge_ref, ...), custom_call_target="tpu_custom_call", output_to_operand_aliasing={{0}: (0, {})} | custom-call | tf_op jit(solution)/shard_map/forward/pallas_call | solution.py:409
  8.7 0.0 copy-start.4
  8.7 1.1 %forward.6 = (bf16[16,160,256]{2,1,0:T(8,128)(2,1)S(1)}, bf16[512,256]{1,0:T(8,128)(2,1)S(1)}, bf16[512,128]{1,0:T(8,128)(2,1)S(1)}) custom-call(bf16[16,160,256]{2,1,0:T(8,128)(2,1)S(1)} %get-tuple-element.56.smooth_in_ref, bf16[2,16,16,128]{3,2,1,0:T(8,128)(2,1)S(1)} %collective-permute-done.edge_ref, ...), custom_call_target="tpu_custom_call", output_to_operand_aliasing={{0}: (0, {})} | custom-call | tf_op jit(solution)/shard_map/forward/pallas_call | solution.py:409
  9.7 0.1 collective-permute-start.1
  9.8 0.0 copy-done.4
  9.8 0.1 broadcast_multiply_fusion
  9.9 0.1 select_reduce_fusion
  10.1 0.0 copy-start.1
  10.1 0.0 copy-start.2
  10.1 1.1 %forward.7 = (bf16[16,160,256]{2,1,0:T(8,128)(2,1)S(1)}, bf16[512,256]{1,0:T(8,128)(2,1)S(1)}, bf16[512,128]{1,0:T(8,128)(2,1)S(1)}) custom-call(bf16[16,160,256]{2,1,0:T(8,128)(2,1)S(1)} %get-tuple-element.57.smooth_in_ref, bf16[2,16,16,128]{3,2,1,0:T(8,128)(2,1)S(1)} %collective-permute-done.edge_ref, ...), custom_call_target="tpu_custom_call", output_to_operand_aliasing={{0}: (0, {})} | custom-call | tf_op jit(solution)/shard_map/forward/pallas_call | solution.py:409
  11.2 0.3 collective-permute-done.2.refs_1_
  11.5 3.4 %collective-permute-start.5 = (bf16[272,128]{1,0:T(8,128)(2,1)S(1)}, bf16[272,128]{1,0:T(8,128)(2,1)S(1)}, u32[]{:S(2)}, u32[]{:S(2)}) collective-permute-start(bf16[272,128]{1,0:T(8,128)(2,1)S(1)} %sum.5), channel_id=1, source_target_pairs={{0,12},{4,8},{8,4},{12,0},{1,13},{5,9},{9,5},{13,1},{2,14},{6,10},... | collective-permute-start | bytes 208904 | tf_op jit(solution)/shard_map/ppermute | solution.py:19
  14.9 0.1 collective-permute-start.4
  15.0 0.0 collective-permute-done.1.refs_1_
  15.1 0.9 %collective-permute-start.3 = (bf16[272,128]{1,0:T(8,128)(2,1)S(1)}, bf16[272,128]{1,0:T(8,128)(2,1)S(1)}, u32[]{:S(2)}, u32[]{:S(2)}) collective-permute-start(bf16[272,128]{1,0:T(8,128)(2,1)S(1)} %sum.3), channel_id=1, source_target_pairs={{0,4},{4,0},{8,12},{12,8},{1,5},{5,1},{9,13},{13,9},{2,6},{6,2},{1... | collective-permute-start | bytes 208904 | tf_op jit(solution)/shard_map/ppermute | solution.py:19
  16.0 1.0 %bands.1 = (bf16[256,256]{1,0:T(8,128)(2,1)S(1)}, bf16[256,768]{1,0:T(8,128)(2,1)S(1)}) custom-call(f32[25]{0:T(128)S(1)} %copy-done, f32[25]{0:T(128)S(1)} %copy-done.1), custom_call_target="tpu_custom_call" | custom-call | tf_op jit(solution)/shard_map/bands/pallas_call | solution.py:442
  17.0 0.0 collective-permute-done.5.refs_4_
  17.0 3.9 %collective-permute-done.4.refs_3_ = bf16[272,128]{1,0:T(8,128)(2,1)S(1)} collective-permute-done((bf16[272,128]{1,0:T(8,128)(2,1)S(1)}, bf16[272,128]{1,0:T(8,128)(2,1)S(1)}, u32[]{:S(2)}, u32[]{:S(2)}) %collective-permute-start.4) | collective-permute-done | bytes 69664 | tf_op jit(solution)/shard_map/ppermute | solution.py:19
  20.9 0.0 collective-permute-done.3.refs_2_
  20.9 0.8 %mix.1 = (bf16[16,16,128]{2,1,0:T(8,128)(2,1)S(1)}, bf16[16,16,128]{2,1,0:T(8,128)(2,1)S(1)}, bf16[16,16,128]{2,1,0:T(8,128)(2,1)S(1)}, bf16[16,16,128]{2,1,0:T(8,128)(2,1)S(1)}) custom-call(s32[1,128]{1,0:T(1,128)S(1)} %bitcast.10, bf16[16,128]{1,0:T(8,128)(2,1)S(1)} %pad_bitcast_fusion.lag_ref, bf16[512,128]{1,0:T(8,128)(2,1)S(1)} %get-tuple-element.66.refs_0_, ...), custom_call_target="tpu_custom_call" | custom-call | tf_op jit(solution)/shard_map/mix/pallas_call | solution.py:450
  21.7 0.1 collective-permute-start.8
  21.8 1.8 %collective-permute-start.6 = (bf16[16,16,128]{2,1,0:T(8,128)(2,1)S(1)}, bf16[16,16,128]{2,1,0:T(8,128)(2,1)S(1)}, u32[]{:S(2)}, u32[]{:S(2)}) collective-permute-start(bf16[16,16,128]{2,1,0:T(8,128)(2,1)S(1)} %get-tuple-element.67), channel_id=1, source_target_pairs={{0,8},{4,12},{8,0},{12,4},{1,9},{5,13},{9,1},{13,5},{2,10},{6,14},... | collective-permute-start | bytes 196616 | tf_op jit(solution)/shard_map/ppermute | solution.py:19
  23.6 1.7 %collective-permute-start.7 = (bf16[16,16,128]{2,1,0:T(8,128)(2,1)S(1)}, bf16[16,16,128]{2,1,0:T(8,128)(2,1)S(1)}, u32[]{:S(2)}, u32[]{:S(2)}) collective-permute-start(bf16[16,16,128]{2,1,0:T(8,128)(2,1)S(1)} %get-tuple-element.68), channel_id=1, source_target_pairs={{0,12},{4,8},{8,4},{12,0},{1,13},{5,9},{9,5},{13,1},{2,14},{6,10},... | collective-permute-start | bytes 196616 | tf_op jit(solution)/shard_map/ppermute | solution.py:19
  25.4 0.0 collective-permute-done.8
  25.4 1.1 %collective-permute-start.10 = (bf16[32,16,128]{2,1,0:T(8,128)(2,1)S(1)}, bf16[32,16,128]{2,1,0:T(8,128)(2,1)S(1)}, u32[]{:S(2)}, u32[]{:S(2)}) collective-permute-start(bf16[32,16,128]{2,1,0:T(8,128)(2,1)S(1)} %constant_dynamic-update-slice_fusion.refs_0_), channel_id=1, source_target_pairs={{0,2},{2,0},{1,3},{3,1},{4,6},{6,4},{5,7},{7,5},{8,10},{10,8},{9,1... | collective-permute-start | bytes 393224 | tf_op jit(solution)/shard_map/ppermute | solution.py:19
  26.4 1.3 %residual.4 = (bf16[512,256]{1,0:T(8,128)(2,1)S(1)}, bf16[256,256]{1,0:T(8,128)(2,1)S(1)}, bf16[32,16,128]{2,1,0:T(8,128)(2,1)S(1)}) custom-call(bf16[512,256]{1,0:T(8,128)(2,1)S(1)} %get-tuple-element.69.filtered_ref, s32[128,128]{1,0:T(8,128)S(1)} %get-tuple-element.49.code_ref, bf16[512,256]{1,0:T(8,128)(2,1)S(1)} %get-tuple-element.52.templates_ref, ...), custom_call_target="tpu_custom_call" | custom-call | tf_op jit(solution)/shard_map/residual/pallas_call | solution.py:471
  27.7 0.0 collective-permute-done.6.refs_0_
  27.7 1.6 %collective-permute-done.7.refs_1_ = bf16[16,16,128]{2,1,0:T(8,128)(2,1)S(1)} collective-permute-done((bf16[16,16,128]{2,1,0:T(8,128)(2,1)S(1)}, bf16[16,16,128]{2,1,0:T(8,128)(2,1)S(1)}, u32[]{:S(2)}, u32[]{:S(2)}) %collective-permute-start.7) | collective-permute-done | bytes 65568 | tf_op jit(solution)/shard_map/ppermute | solution.py:19
  29.3 0.4 collective-permute-start.9
  29.7 1.3 %residual.7 = (bf16[512,256]{1,0:T(8,128)(2,1)S(1)}, bf16[256,256]{1,0:T(8,128)(2,1)S(1)}, bf16[32,16,128]{2,1,0:T(8,128)(2,1)S(1)}) custom-call(bf16[512,256]{1,0:T(8,128)(2,1)S(1)} %get-tuple-element.78.filtered_ref, s32[128,128]{1,0:T(8,128)S(1)} %get-tuple-element.49.code_ref, bf16[512,256]{1,0:T(8,128)(2,1)S(1)} %get-tuple-element.52.templates_ref, ...), custom_call_target="tpu_custom_call" | custom-call | tf_op jit(solution)/shard_map/residual/pallas_call | solution.py:471
  30.9 0.0 collective-permute-done.10.refs_0_
  31.0 1.3 %residual.6 = (bf16[512,256]{1,0:T(8,128)(2,1)S(1)}, bf16[256,256]{1,0:T(8,128)(2,1)S(1)}, bf16[32,16,128]{2,1,0:T(8,128)(2,1)S(1)}) custom-call(bf16[512,256]{1,0:T(8,128)(2,1)S(1)} %get-tuple-element.76.filtered_ref, s32[128,128]{1,0:T(8,128)S(1)} %get-tuple-element.49.code_ref, bf16[512,256]{1,0:T(8,128)(2,1)S(1)} %get-tuple-element.52.templates_ref, ...), custom_call_target="tpu_custom_call" | custom-call | tf_op jit(solution)/shard_map/residual/pallas_call | solution.py:471
  32.2 1.0 %collective-permute-done.9.refs_0_ = bf16[32,16,128]{2,1,0:T(8,128)(2,1)S(1)} collective-permute-done((bf16[32,16,128]{2,1,0:T(8,128)(2,1)S(1)}, bf16[32,16,128]{2,1,0:T(8,128)(2,1)S(1)}, u32[]{:S(2)}, u32[]{:S(2)}) %collective-permute-start.9) | collective-permute-done | bytes 131104 | tf_op jit(solution)/shard_map/ppermute | solution.py:19
  33.2 1.3 %residual.5 = (bf16[512,256]{1,0:T(8,128)(2,1)S(1)}, bf16[256,256]{1,0:T(8,128)(2,1)S(1)}, bf16[32,16,128]{2,1,0:T(8,128)(2,1)S(1)}) custom-call(bf16[512,256]{1,0:T(8,128)(2,1)S(1)} %get-tuple-element.51.filtered_ref, s32[128,128]{1,0:T(8,128)S(1)} %get-tuple-element.49.code_ref, bf16[512,256]{1,0:T(8,128)(2,1)S(1)} %get-tuple-element.52.templates_ref, ...), custom_call_target="tpu_custom_call" | custom-call | tf_op jit(solution)/shard_map/residual/pallas_call | solution.py:471
  34.5 4.0 %collective-permute-start.11 = (bf16[256,256]{1,0:T(8,128)(2,1)S(1)}, bf16[256,256]{1,0:T(8,128)(2,1)S(1)}, u32[]{:S(2)}, u32[]{:S(2)}) collective-permute-start(bf16[256,256]{1,0:T(8,128)(2,1)S(1)} %select_select_fusion), channel_id=1, source_target_pairs={{0,1},{1,0},{2,3},{3,2},{4,5},{5,4},{6,7},{7,6},{8,9},{9,8},{10,11... | collective-permute-start | bytes 393224 | tf_op jit(solution)/shard_map/ppermute | solution.py:19
  38.5 0.1 select_select_fusion.4
  38.6 0.2 fusion
  38.8 1.3 %copy.16 = bf16[64,16,128]{2,1,0:T(8,128)(2,1)} copy(bf16[64,16,128]{0,1,2:T(8,128)(2,1)S(1)} %fusion) | data formatting | bytes 524288
  40.1 0.0 collective-permute-done.11.edge_ref
  40.1 2.4 %backward.1 = bf16[2,16,128,128]{3,2,1,0:T(8,128)(2,1)} custom-call(bf16[256,256]{1,0:T(8,128)(2,1)S(1)} %collective-permute-done.11.edge_ref, bf16[256,256]{1,0:T(8,128)(2,1)S(1)} %get-tuple-element.84.col_adj_ref, bf16[256,768]{1,0:T(8,128)(2,1)S(1)} %get-tuple-element.85.row_adj_ref, bf16[512,256]{1,0:T(8,128)(2,1)S(1)} %get-tuple-element.86.refs_0_, ...), custom_call_target="tpu_custom_call" | custom-call | tf_op jit(solution)/shard_map/backward/pallas_call | solution.py:500
  (15 shorter events, 0.1 us)
Async XLA Ops:
  1.6 2.1 %collective-permute-start = (bf16[2,16,16,128]{3,2,1,0:T(8,128)(2,1)S(1)}, bf16[2,16,16,128]{3,2,1,0:T(8,128)(2,1)S(1)}, u32[]{:S(2)}, u32[]{:S(2)}) collective-permute-start(bf16[2,16,16,128]{3,2,1,0:T(8,128)(2,1)S(1)} %constant_dynamic-slice_fusion), channel_id=1, source_target_pairs={{0,1},{1,0},{2,3},{3,2},{4,5},{5,4},{6,7},{7,6},{8,9},{9,8},{10,11... | collective-permute-start | bytes 393224 | tf_op jit(solution)/shard_map/ppermute | solution.py:19
  3.6 1.3 %copy-start.3 = (f32[1,3,65]{2,0,1:T(1,128)S(1)}, f32[1,3,65]{2,0,1:T(1,128)}, u32[]{:S(2)}) copy-start(f32[1,3,65]{2,0,1:T(1,128)} %param.16) | copy-start | bytes 2344
  4.9 6.6 %collective-permute-start.2 = (bf16[512,128]{1,0:T(8,128)(2,1)S(1)}, bf16[512,128]{1,0:T(8,128)(2,1)S(1)}, u32[]{:S(2)}, u32[]{:S(2)}) collective-permute-start(bf16[512,128]{1,0:T(8,128)(2,1)S(1)} %get-tuple-element.61), channel_id=1, source_target_pairs={{0,2},{2,0},{1,3},{3,1},{4,6},{6,4},{5,7},{7,5},{8,10},{10,8},{9,1... | collective-permute-start | bytes 393224 | tf_op jit(solution)/shard_map/ppermute | solution.py:19
  8.7 1.2 %copy-start.4 = (s32[1,3]{1,0:T(1,128)S(1)}, s32[1,3]{1,0:T(1,128)}, u32[]{:S(2)}) copy-start(s32[1,3]{1,0:T(1,128)} %param.17) | copy-start | bytes 40
  9.7 5.3 %collective-permute-start.1 = (bf16[512,128]{1,0:T(8,128)(2,1)S(1)}, bf16[512,128]{1,0:T(8,128)(2,1)S(1)}, u32[]{:S(2)}, u32[]{:S(2)}) collective-permute-start(bf16[512,128]{1,0:T(8,128)(2,1)S(1)} %get-tuple-element.59), channel_id=1, source_target_pairs={{0,2},{2,0},{1,3},{3,1},{4,6},{6,4},{5,7},{7,5},{8,10},{10,8},{9,1... | collective-permute-start | bytes 393224 | tf_op jit(solution)/shard_map/ppermute | solution.py:19
  10.0 5.9 %copy-start = (f32[25]{0:T(128)S(1)}, f32[25]{0:T(128)}, u32[]{:S(2)}) copy-start(f32[25]{0:T(128)} %col_ref) | copy-start | bytes 304
  10.1 5.9 %copy-start.1 = (f32[25]{0:T(128)S(1)}, f32[25]{0:T(128)}, u32[]{:S(2)}) copy-start(f32[25]{0:T(128)} %row_ref) | copy-start | bytes 304
  10.1 10.9 %copy-start.2 = (s32[128,1]{0,1:T(1,128)S(1)}, s32[128,1]{0,1:T(1,128)}, u32[]{:S(2)}) copy-start(s32[128,1]{0,1:T(1,128)} %param.11) | copy-start | bytes 1540
  11.5 5.5 %collective-permute-start.5 = (bf16[272,128]{1,0:T(8,128)(2,1)S(1)}, bf16[272,128]{1,0:T(8,128)(2,1)S(1)}, u32[]{:S(2)}, u32[]{:S(2)}) collective-permute-start(bf16[272,128]{1,0:T(8,128)(2,1)S(1)} %sum.5), channel_id=1, source_target_pairs={{0,12},{4,8},{8,4},{12,0},{1,13},{5,9},{9,5},{13,1},{2,14},{6,10},... | collective-permute-start | bytes 208904 | tf_op jit(solution)/shard_map/ppermute | solution.py:19
  14.9 6.0 %collective-permute-start.4 = (bf16[272,128]{1,0:T(8,128)(2,1)S(1)}, bf16[272,128]{1,0:T(8,128)(2,1)S(1)}, u32[]{:S(2)}, u32[]{:S(2)}) collective-permute-start(bf16[272,128]{1,0:T(8,128)(2,1)S(1)} %sum.4), channel_id=1, source_target_pairs={{0,8},{4,12},{8,0},{12,4},{1,9},{5,13},{9,1},{13,5},{2,10},{6,14},... | collective-permute-start | bytes 208904 | tf_op jit(solution)/shard_map/ppermute | solution.py:19
  15.1 5.9 %collective-permute-start.3 = (bf16[272,128]{1,0:T(8,128)(2,1)S(1)}, bf16[272,128]{1,0:T(8,128)(2,1)S(1)}, u32[]{:S(2)}, u32[]{:S(2)}) collective-permute-start(bf16[272,128]{1,0:T(8,128)(2,1)S(1)} %sum.3), channel_id=1, source_target_pairs={{0,4},{4,0},{8,12},{12,8},{1,5},{5,1},{9,13},{13,9},{2,6},{6,2},{1... | collective-permute-start | bytes 208904 | tf_op jit(solution)/shard_map/ppermute | solution.py:19
  21.7 3.6 %collective-permute-start.8 = (bf16[16,16,128]{2,1,0:T(8,128)(2,1)S(1)}, bf16[16,16,128]{2,1,0:T(8,128)(2,1)S(1)}, u32[]{:S(2)}, u32[]{:S(2)}) collective-permute-start(bf16[16,16,128]{2,1,0:T(8,128)(2,1)S(1)} %get-tuple-element.71), channel_id=1, source_target_pairs={{0,4},{4,0},{8,12},{12,8},{1,5},{5,1},{9,13},{13,9},{2,6},{6,2},{1... | collective-permute-start | bytes 196616 | tf_op jit(solution)/shard_map/ppermute | solution.py:19
  21.8 5.9 %collective-permute-start.6 = (bf16[16,16,128]{2,1,0:T(8,128)(2,1)S(1)}, bf16[16,16,128]{2,1,0:T(8,128)(2,1)S(1)}, u32[]{:S(2)}, u32[]{:S(2)}) collective-permute-start(bf16[16,16,128]{2,1,0:T(8,128)(2,1)S(1)} %get-tuple-element.67), channel_id=1, source_target_pairs={{0,8},{4,12},{8,0},{12,4},{1,9},{5,13},{9,1},{13,5},{2,10},{6,14},... | collective-permute-start | bytes 196616 | tf_op jit(solution)/shard_map/ppermute | solution.py:19
  23.6 5.7 %collective-permute-start.7 = (bf16[16,16,128]{2,1,0:T(8,128)(2,1)S(1)}, bf16[16,16,128]{2,1,0:T(8,128)(2,1)S(1)}, u32[]{:S(2)}, u32[]{:S(2)}) collective-permute-start(bf16[16,16,128]{2,1,0:T(8,128)(2,1)S(1)} %get-tuple-element.68), channel_id=1, source_target_pairs={{0,12},{4,8},{8,4},{12,0},{1,13},{5,9},{9,5},{13,1},{2,14},{6,10},... | collective-permute-start | bytes 196616 | tf_op jit(solution)/shard_map/ppermute | solution.py:19
  25.4 5.6 %collective-permute-start.10 = (bf16[32,16,128]{2,1,0:T(8,128)(2,1)S(1)}, bf16[32,16,128]{2,1,0:T(8,128)(2,1)S(1)}, u32[]{:S(2)}, u32[]{:S(2)}) collective-permute-start(bf16[32,16,128]{2,1,0:T(8,128)(2,1)S(1)} %constant_dynamic-update-slice_fusion.refs_0_), channel_id=1, source_target_pairs={{0,2},{2,0},{1,3},{3,1},{4,6},{6,4},{5,7},{7,5},{8,10},{10,8},{9,1... | collective-permute-start | bytes 393224 | tf_op jit(solution)/shard_map/ppermute | solution.py:19
  29.3 3.9 %collective-permute-start.9 = (bf16[32,16,128]{2,1,0:T(8,128)(2,1)S(1)}, bf16[32,16,128]{2,1,0:T(8,128)(2,1)S(1)}, u32[]{:S(2)}, u32[]{:S(2)}) collective-permute-start(bf16[32,16,128]{2,1,0:T(8,128)(2,1)S(1)} %pad_maximum_fusion), channel_id=1, source_target_pairs={{0,2},{2,0},{1,3},{3,1},{4,6},{6,4},{5,7},{7,5},{8,10},{10,8},{9,1... | collective-permute-start | bytes 393224 | tf_op jit(solution)/shard_map/ppermute | solution.py:19
  34.5 5.6 %collective-permute-start.11 = (bf16[256,256]{1,0:T(8,128)(2,1)S(1)}, bf16[256,256]{1,0:T(8,128)(2,1)S(1)}, u32[]{:S(2)}, u32[]{:S(2)}) collective-permute-start(bf16[256,256]{1,0:T(8,128)(2,1)S(1)} %select_select_fusion), channel_id=1, source_target_pairs={{0,1},{1,0},{2,3},{3,2},{4,5},{5,4},{6,7},{7,6},{8,9},{9,8},{10,11... | collective-permute-start | bytes 393224 | tf_op jit(solution)/shard_map/ppermute | solution.py:19

commit v11 on v10

--- a/solution.py
+++ b/solution.py
@@ -474,10 +474,11 @@
             0, 3 + len(got), scratch=[pltpu.VMEM((len(spots), share * frames, names), BF16)],
         )(filtered[flip, far], code, flat_templates, *got)
 
-    subtract(0, 0, [near_ks], [near])
-    distant, _ = lax.optimization_barrier(([swapped[k] for k in far_ks], edges[0, 0]))
+    distant = [swapped[k] for k in far_ks]
     joined = jnp.concatenate(distant)
     subtract(0, 1, [[k] for k in far_ks], distant)
+    late_near, _ = lax.optimization_barrier((near, edges[0, 1]))
+    subtract(0, 0, [near_ks], [late_near])
     for flip in late:
         subtract(flip, 0, [near_ks], [passed[flip]])
         subtract(flip, 1, [far_ks], [exchange(joined, "planes", flip)])

time: 42.6 us -> 43.1 us (1.012)
  waiting for transfers between devices: 6.8 us -> 7.62 us
    ppermute x12, waiting for transfers between devices: 6.8 us -> 7.62 us  [exchange(): return lax.ppermute(cells, axis, [(i, i ^ flip) for i in range(count)])]
  transfers between devices with their start and end apart: 12 -> 12, of which waited for: 4 -> 3; matrix products, arithmetic and copies ran while one was open for 4% -> 4% of each run, Pallas kernels for 23% -> 23%
where the time goes in v11:
time: 43.1 us; the launch traced here: 43 us
  starting transfers between devices  16.1 us (37%)
  Pallas kernels  15.6 us (36%)
  waiting for transfers between devices  7.62 us (18%)
  local copies, waits for them, and re-layouts  2.26 us (5%)
  between operations  0.87 us (2%)
  other arithmetic  0.54 us (1%)
    ppermute x12, starting transfers between devices, exchange(): return lax.ppermute(cells, axis, [(i, i ^ flip) for i in range(count)])  16.1 us
    ppermute x12, waiting for transfers between devices, exchange(): return lax.ppermute(cells, axis, [(i, i ^ flip) for i in range(count)])  7.62 us
    pallas_call x4, Pallas kernels, subtract(): call(functools.partial(residual_kernel, flip, far, wide, spots), 'residua...  5.06 us
    pallas_call x4, Pallas kernels, on_device(): call(functools.partial(forward_kernel, flip, far, turn == 0, wide, halves...  4.41 us
    pallas_call x1, Pallas kernels, on_device(): pl.pallas_call(functools.partial(backward_kernel, back_keys, wide), out_s...  2.37 us
    pallas_call x1, Pallas kernels, on_device(): pl.pallas_call(functools.partial(prepare_kernel, rim, cuts), out_shape=(s...  1.9 us
    unnamed x13, local copies, waits for them, and re-layouts  1.32 us
    pallas_call x1, Pallas kernels, on_device(): call(functools.partial(bands_kernel, rim, frames), 'bands', [(width, widt...  1 us
  transfers between devices with their start and end apart: 12, of which 3 were waited for; matrix products, arithmetic and copies ran while one was open for 4% of the time, Pallas kernels for 23%

profile of v11, /device:TPU:1, one launch (start us, length us, event | category | flops | bytes accessed | tf_op | source)
XLA Modules:
  0.0 43.0 jit_solution(15944271822763559095)
XLA Ops:
  0.6 0.9 %constant_dynamic-slice_fusion = bf16[2,16,16,128]{3,2,1,0:T(8,128)(2,1)S(1)} fusion(bf16[2,16,128,128]{3,2,1,0:T(8,128)(2,1)} %movie_hbm.1, s32[]{:T(128)S(6)} %select_n.131), kind=kLoop, calls=%fused_computation.15 | loop fusion | bytes 262148 | tf_op jit(solution)/shard_map/dynamic_slice | solution.py:368
  1.6 0.1 collective-permute-start
  1.7 1.9 %prepare.1 = (bf16[16,160,256]{2,1,0:T(8,128)(2,1)S(1)}, bf16[128,128]{1,0:T(8,128)(2,1)S(1)}, bf16[256,768]{1,0:T(8,128)(2,1)S(1)}, s32[128,128]{1,0:T(8,128)S(...) custom-call(f32[25]{0:T(128)} %col_ref, f32[25]{0:T(128)} %row_ref, bf16[2,16,128,128]{3,2,1,0:T(8,128)(2,1)} %movie_hbm.1, ...), custom_call_target="tpu_custom_call" | custom-call | tf_op jit(solution)/shard_map/prepare/pallas_call | solution.py:371
  3.6 0.0 copy-start.3
  3.6 0.0 collective-permute-done.edge_ref
  3.6 1.2 %forward.4 = (bf16[16,160,256]{2,1,0:T(8,128)(2,1)S(1)}, bf16[512,256]{1,0:T(8,128)(2,1)S(1)}, bf16[512,128]{1,0:T(8,128)(2,1)S(1)}) custom-call(bf16[16,160,256]{2,1,0:T(8,128)(2,1)S(1)} %get-tuple-element.45.smooth_in_ref, bf16[2,16,16,128]{3,2,1,0:T(8,128)(2,1)S(1)} %collective-permute-done.edge_ref, ...), custom_call_target="tpu_custom_call", output_to_operand_aliasing={{0}: (0, {})} | custom-call | tf_op jit(solution)/shard_map/forward/pallas_call | solution.py:409
  4.9 0.0 copy-done.3
  4.9 2.7 %collective-permute-start.2 = (bf16[512,128]{1,0:T(8,128)(2,1)S(1)}, bf16[512,128]{1,0:T(8,128)(2,1)S(1)}, u32[]{:S(2)}, u32[]{:S(2)}) collective-permute-start(bf16[512,128]{1,0:T(8,128)(2,1)S(1)} %get-tuple-element.60), channel_id=1, source_target_pairs={{0,2},{2,0},{1,3},{3,1},{4,6},{6,4},{5,7},{7,5},{8,10},{10,8},{9,1... | collective-permute-start | bytes 393224 | tf_op jit(solution)/shard_map/ppermute | solution.py:19
  7.6 1.0 %forward.5 = (bf16[16,160,256]{2,1,0:T(8,128)(2,1)S(1)}, bf16[512,256]{1,0:T(8,128)(2,1)S(1)}, bf16[512,128]{1,0:T(8,128)(2,1)S(1)}) custom-call(bf16[16,160,256]{2,1,0:T(8,128)(2,1)S(1)} %get-tuple-element.52.smooth_in_ref, bf16[2,16,16,128]{3,2,1,0:T(8,128)(2,1)S(1)} %collective-permute-done.edge_ref, ...), custom_call_target="tpu_custom_call", output_to_operand_aliasing={{0}: (0, {})} | custom-call | tf_op jit(solution)/shard_map/forward/pallas_call | solution.py:409
  8.7 0.0 copy-start.4
  8.7 1.1 %forward.6 = (bf16[16,160,256]{2,1,0:T(8,128)(2,1)S(1)}, bf16[512,256]{1,0:T(8,128)(2,1)S(1)}, bf16[512,128]{1,0:T(8,128)(2,1)S(1)}) custom-call(bf16[16,160,256]{2,1,0:T(8,128)(2,1)S(1)} %get-tuple-element.55.smooth_in_ref, bf16[2,16,16,128]{3,2,1,0:T(8,128)(2,1)S(1)} %collective-permute-done.edge_ref, ...), custom_call_target="tpu_custom_call", output_to_operand_aliasing={{0}: (0, {})} | custom-call | tf_op jit(solution)/shard_map/forward/pallas_call | solution.py:409
  9.7 0.1 collective-permute-start.1
  9.8 0.1 broadcast_multiply_fusion
  9.9 0.1 select_reduce_fusion
  10.1 0.0 copy-start.1
  10.1 0.0 copy-start.2
  10.1 1.1 %forward.7 = (bf16[16,160,256]{2,1,0:T(8,128)(2,1)S(1)}, bf16[512,256]{1,0:T(8,128)(2,1)S(1)}, bf16[512,128]{1,0:T(8,128)(2,1)S(1)}) custom-call(bf16[16,160,256]{2,1,0:T(8,128)(2,1)S(1)} %get-tuple-element.56.smooth_in_ref, bf16[2,16,16,128]{3,2,1,0:T(8,128)(2,1)S(1)} %collective-permute-done.edge_ref, ...), custom_call_target="tpu_custom_call", output_to_operand_aliasing={{0}: (0, {})} | custom-call | tf_op jit(solution)/shard_map/forward/pallas_call | solution.py:409
  11.2 0.3 collective-permute-done.2.refs_1_
  11.5 3.4 %collective-permute-start.5 = (bf16[272,128]{1,0:T(8,128)(2,1)S(1)}, bf16[272,128]{1,0:T(8,128)(2,1)S(1)}, u32[]{:S(2)}, u32[]{:S(2)}) collective-permute-start(bf16[272,128]{1,0:T(8,128)(2,1)S(1)} %sum.5), channel_id=1, source_target_pairs={{0,12},{4,8},{8,4},{12,0},{1,13},{5,9},{9,5},{13,1},{2,14},{6,10},... | collective-permute-start | bytes 208904 | tf_op jit(solution)/shard_map/ppermute | solution.py:19
  14.9 0.1 collective-permute-start.4
  15.0 0.0 collective-permute-done.1.refs_1_
  15.1 0.9 %collective-permute-start.3 = (bf16[272,128]{1,0:T(8,128)(2,1)S(1)}, bf16[272,128]{1,0:T(8,128)(2,1)S(1)}, u32[]{:S(2)}, u32[]{:S(2)}) collective-permute-start(bf16[272,128]{1,0:T(8,128)(2,1)S(1)} %sum.3), channel_id=1, source_target_pairs={{0,4},{4,0},{8,12},{12,8},{1,5},{5,1},{9,13},{13,9},{2,6},{6,2},{1... | collective-permute-start | bytes 208904 | tf_op jit(solution)/shard_map/ppermute | solution.py:19
  16.0 0.0 copy-done.1
  16.0 1.0 %bands.1 = (bf16[256,256]{1,0:T(8,128)(2,1)S(1)}, bf16[256,768]{1,0:T(8,128)(2,1)S(1)}) custom-call(f32[25]{0:T(128)S(1)} %copy-done, f32[25]{0:T(128)S(1)} %copy-done.1), custom_call_target="tpu_custom_call" | custom-call | tf_op jit(solution)/shard_map/bands/pallas_call | solution.py:442
  17.0 0.0 collective-permute-done.5.refs_4_
  17.0 3.9 %collective-permute-done.4.refs_3_ = bf16[272,128]{1,0:T(8,128)(2,1)S(1)} collective-permute-done((bf16[272,128]{1,0:T(8,128)(2,1)S(1)}, bf16[272,128]{1,0:T(8,128)(2,1)S(1)}, u32[]{:S(2)}, u32[]{:S(2)}) %collective-permute-start.4) | collective-permute-done | bytes 69664 | tf_op jit(solution)/shard_map/ppermute | solution.py:19
  20.9 0.0 collective-permute-done.3.refs_2_
  20.9 0.8 %mix.1 = (bf16[16,16,128]{2,1,0:T(8,128)(2,1)S(1)}, bf16[16,16,128]{2,1,0:T(8,128)(2,1)S(1)}, bf16[16,16,128]{2,1,0:T(8,128)(2,1)S(1)}, bf16[16,16,128]{2,1,0:T(8,128)(2,1)S(1)}) custom-call(s32[1,128]{1,0:T(1,128)S(1)} %bitcast.10, bf16[16,128]{1,0:T(8,128)(2,1)S(1)} %pad_bitcast_fusion.lag_ref, bf16[512,128]{1,0:T(8,128)(2,1)S(1)} %get-tuple-element.65.refs_0_, ...), custom_call_target="tpu_custom_call" | custom-call | tf_op jit(solution)/shard_map/mix/pallas_call | solution.py:450
  21.7 0.1 collective-permute-start.6
  21.8 1.8 %collective-permute-start.7 = (bf16[16,16,128]{2,1,0:T(8,128)(2,1)S(1)}, bf16[16,16,128]{2,1,0:T(8,128)(2,1)S(1)}, u32[]{:S(2)}, u32[]{:S(2)}) collective-permute-start(bf16[16,16,128]{2,1,0:T(8,128)(2,1)S(1)} %get-tuple-element.67), channel_id=1, source_target_pairs={{0,12},{4,8},{8,4},{12,0},{1,13},{5,9},{9,5},{13,1},{2,14},{6,10},... | collective-permute-start | bytes 196616 | tf_op jit(solution)/shard_map/ppermute | solution.py:19
  23.6 0.9 %collective-permute-start.9 = (bf16[16,16,128]{2,1,0:T(8,128)(2,1)S(1)}, bf16[16,16,128]{2,1,0:T(8,128)(2,1)S(1)}, u32[]{:S(2)}, u32[]{:S(2)}) collective-permute-start(bf16[16,16,128]{2,1,0:T(8,128)(2,1)S(1)} %get-tuple-element.71), channel_id=1, source_target_pairs={{0,4},{4,0},{8,12},{12,8},{1,5},{5,1},{9,13},{13,9},{2,6},{6,2},{1... | collective-permute-start | bytes 196616 | tf_op jit(solution)/shard_map/ppermute | solution.py:19
  24.5 3.4 %collective-permute-done.9 = bf16[16,16,128]{2,1,0:T(8,128)(2,1)S(1)} collective-permute-done((bf16[16,16,128]{2,1,0:T(8,128)(2,1)S(1)}, bf16[16,16,128]{2,1,0:T(8,128)(2,1)S(1)}, u32[]{:S(2)}, u32[]{:S(2)}) %collective-permute-start.9) | collective-permute-done | bytes 65568 | tf_op jit(solution)/shard_map/ppermute | solution.py:19
  27.8 0.8 %collective-permute-start.10 = (bf16[32,16,128]{2,1,0:T(8,128)(2,1)S(1)}, bf16[32,16,128]{2,1,0:T(8,128)(2,1)S(1)}, u32[]{:S(2)}, u32[]{:S(2)}) collective-permute-start(bf16[32,16,128]{2,1,0:T(8,128)(2,1)S(1)} %constant_dynamic-update-slice_fusion.refs_0_), channel_id=1, source_target_pairs={{0,2},{2,0},{1,3},{3,1},{4,6},{6,4},{5,7},{7,5},{8,10},{10,8},{9,1... | collective-permute-start | bytes 393224 | tf_op jit(solution)/shard_map/ppermute | solution.py:19
  28.6 0.0 collective-permute-done.6.refs_0_
  28.6 0.0 collective-permute-done.7.refs_1_
  28.6 0.8 %collective-permute-start.8 = (bf16[32,16,128]{2,1,0:T(8,128)(2,1)S(1)}, bf16[32,16,128]{2,1,0:T(8,128)(2,1)S(1)}, u32[]{:S(2)}, u32[]{:S(2)}) collective-permute-start(bf16[32,16,128]{2,1,0:T(8,128)(2,1)S(1)} %pad_maximum_fusion), channel_id=1, source_target_pairs={{0,2},{2,0},{1,3},{3,1},{4,6},{6,4},{5,7},{7,5},{8,10},{10,8},{9,1... | collective-permute-start | bytes 393224 | tf_op jit(solution)/shard_map/ppermute | solution.py:19
  29.5 1.3 %residual.6 = (bf16[512,256]{1,0:T(8,128)(2,1)S(1)}, bf16[256,256]{1,0:T(8,128)(2,1)S(1)}, bf16[32,16,128]{2,1,0:T(8,128)(2,1)S(1)}) custom-call(bf16[512,256]{1,0:T(8,128)(2,1)S(1)} %get-tuple-element.73.filtered_ref, s32[128,128]{1,0:T(8,128)S(1)} %get-tuple-element.48.code_ref, bf16[512,256]{1,0:T(8,128)(2,1)S(1)} %get-tuple-element.51.templates_ref, ...), custom_call_target="tpu_custom_call" | custom-call | tf_op jit(solution)/shard_map/residual/pallas_call | solution.py:471
  30.7 1.3 %residual.7 = (bf16[512,256]{1,0:T(8,128)(2,1)S(1)}, bf16[256,256]{1,0:T(8,128)(2,1)S(1)}, bf16[32,16,128]{2,1,0:T(8,128)(2,1)S(1)}) custom-call(bf16[512,256]{1,0:T(8,128)(2,1)S(1)} %get-tuple-element.75.filtered_ref, s32[128,128]{1,0:T(8,128)S(1)} %get-tuple-element.48.code_ref, bf16[512,256]{1,0:T(8,128)(2,1)S(1)} %get-tuple-element.51.templates_ref, ...), custom_call_target="tpu_custom_call" | custom-call | tf_op jit(solution)/shard_map/residual/pallas_call | solution.py:471
  32.0 0.0 collective-permute-done.10.refs_0_
  32.0 1.3 %residual.5 = (bf16[512,256]{1,0:T(8,128)(2,1)S(1)}, bf16[256,256]{1,0:T(8,128)(2,1)S(1)}, bf16[32,16,128]{2,1,0:T(8,128)(2,1)S(1)}) custom-call(bf16[512,256]{1,0:T(8,128)(2,1)S(1)} %get-tuple-element.69.filtered_ref, s32[128,128]{1,0:T(8,128)S(1)} %get-tuple-element.48.code_ref, bf16[512,256]{1,0:T(8,128)(2,1)S(1)} %get-tuple-element.51.templates_ref, ...), custom_call_target="tpu_custom_call" | custom-call | tf_op jit(solution)/shard_map/residual/pallas_call | solution.py:471
  33.3 0.0 collective-permute-done.8.refs_0_
  33.3 1.3 %residual.4 = (bf16[512,256]{1,0:T(8,128)(2,1)S(1)}, bf16[256,256]{1,0:T(8,128)(2,1)S(1)}, bf16[32,16,128]{2,1,0:T(8,128)(2,1)S(1)}) custom-call(bf16[512,256]{1,0:T(8,128)(2,1)S(1)} %get-tuple-element.50.filtered_ref, s32[128,128]{1,0:T(8,128)S(1)} %get-tuple-element.48.code_ref, bf16[512,256]{1,0:T(8,128)(2,1)S(1)} %get-tuple-element.51.templates_ref, ...), custom_call_target="tpu_custom_call" | custom-call | tf_op jit(solution)/shard_map/residual/pallas_call | solution.py:471
  34.6 4.4 %collective-permute-start.11 = (bf16[256,256]{1,0:T(8,128)(2,1)S(1)}, bf16[256,256]{1,0:T(8,128)(2,1)S(1)}, u32[]{:S(2)}, u32[]{:S(2)}) collective-permute-start(bf16[256,256]{1,0:T(8,128)(2,1)S(1)} %select_select_fusion), channel_id=1, source_target_pairs={{0,1},{1,0},{2,3},{3,2},{4,5},{5,4},{6,7},{7,6},{8,9},{9,8},{10,11... | collective-permute-start | bytes 393224 | tf_op jit(solution)/shard_map/ppermute | solution.py:19
  39.0 0.1 select_select_fusion.4
  39.1 0.2 fusion
  39.3 1.3 %copy.16 = bf16[64,16,128]{2,1,0:T(8,128)(2,1)} copy(bf16[64,16,128]{0,1,2:T(8,128)(2,1)S(1)} %fusion) | data formatting | bytes 524288
  40.6 0.0 collective-permute-done.11.edge_ref
  40.6 2.4 %backward.1 = bf16[2,16,128,128]{3,2,1,0:T(8,128)(2,1)} custom-call(bf16[256,256]{1,0:T(8,128)(2,1)S(1)} %collective-permute-done.11.edge_ref, bf16[256,256]{1,0:T(8,128)(2,1)S(1)} %get-tuple-element.82.col_adj_ref, bf16[256,768]{1,0:T(8,128)(2,1)S(1)} %get-tuple-element.83.row_adj_ref, bf16[512,256]{1,0:T(8,128)(2,1)S(1)} %get-tuple-element.84.refs_0_, ...), custom_call_target="tpu_custom_call" | custom-call | tf_op jit(solution)/shard_map/backward/pallas_call | solution.py:501
  (15 shorter events, 0.1 us)
Async XLA Ops:
  1.6 2.1 %collective-permute-start = (bf16[2,16,16,128]{3,2,1,0:T(8,128)(2,1)S(1)}, bf16[2,16,16,128]{3,2,1,0:T(8,128)(2,1)S(1)}, u32[]{:S(2)}, u32[]{:S(2)}) collective-permute-start(bf16[2,16,16,128]{3,2,1,0:T(8,128)(2,1)S(1)} %constant_dynamic-slice_fusion), channel_id=1, source_target_pairs={{0,1},{1,0},{2,3},{3,2},{4,5},{5,4},{6,7},{7,6},{8,9},{9,8},{10,11... | collective-permute-start | bytes 393224 | tf_op jit(solution)/shard_map/ppermute | solution.py:19
  3.6 1.3 %copy-start.3 = (f32[1,3,65]{2,0,1:T(1,128)S(1)}, f32[1,3,65]{2,0,1:T(1,128)}, u32[]{:S(2)}) copy-start(f32[1,3,65]{2,0,1:T(1,128)} %param.16) | copy-start | bytes 2344
  4.9 6.6 %collective-permute-start.2 = (bf16[512,128]{1,0:T(8,128)(2,1)S(1)}, bf16[512,128]{1,0:T(8,128)(2,1)S(1)}, u32[]{:S(2)}, u32[]{:S(2)}) collective-permute-start(bf16[512,128]{1,0:T(8,128)(2,1)S(1)} %get-tuple-element.60), channel_id=1, source_target_pairs={{0,2},{2,0},{1,3},{3,1},{4,6},{6,4},{5,7},{7,5},{8,10},{10,8},{9,1... | collective-permute-start | bytes 393224 | tf_op jit(solution)/shard_map/ppermute | solution.py:19
  8.7 1.2 %copy-start.4 = (s32[1,3]{1,0:T(1,128)S(1)}, s32[1,3]{1,0:T(1,128)}, u32[]{:S(2)}) copy-start(s32[1,3]{1,0:T(1,128)} %param.17) | copy-start | bytes 40
  9.7 5.3 %collective-permute-start.1 = (bf16[512,128]{1,0:T(8,128)(2,1)S(1)}, bf16[512,128]{1,0:T(8,128)(2,1)S(1)}, u32[]{:S(2)}, u32[]{:S(2)}) collective-permute-start(bf16[512,128]{1,0:T(8,128)(2,1)S(1)} %get-tuple-element.58), channel_id=1, source_target_pairs={{0,2},{2,0},{1,3},{3,1},{4,6},{6,4},{5,7},{7,5},{8,10},{10,8},{9,1... | collective-permute-start | bytes 393224 | tf_op jit(solution)/shard_map/ppermute | solution.py:19
  10.0 5.9 %copy-start = (f32[25]{0:T(128)S(1)}, f32[25]{0:T(128)}, u32[]{:S(2)}) copy-start(f32[25]{0:T(128)} %col_ref) | copy-start | bytes 304
  10.1 5.9 %copy-start.1 = (f32[25]{0:T(128)S(1)}, f32[25]{0:T(128)}, u32[]{:S(2)}) copy-start(f32[25]{0:T(128)} %row_ref) | copy-start | bytes 304
  10.1 10.9 %copy-start.2 = (s32[128,1]{0,1:T(1,128)S(1)}, s32[128,1]{0,1:T(1,128)}, u32[]{:S(2)}) copy-start(s32[128,1]{0,1:T(1,128)} %param.11) | copy-start | bytes 1540
  11.5 5.5 %collective-permute-start.5 = (bf16[272,128]{1,0:T(8,128)(2,1)S(1)}, bf16[272,128]{1,0:T(8,128)(2,1)S(1)}, u32[]{:S(2)}, u32[]{:S(2)}) collective-permute-start(bf16[272,128]{1,0:T(8,128)(2,1)S(1)} %sum.5), channel_id=1, source_target_pairs={{0,12},{4,8},{8,4},{12,0},{1,13},{5,9},{9,5},{13,1},{2,14},{6,10},... | collective-permute-start | bytes 208904 | tf_op jit(solution)/shard_map/ppermute | solution.py:19
  14.9 6.0 %collective-permute-start.4 = (bf16[272,128]{1,0:T(8,128)(2,1)S(1)}, bf16[272,128]{1,0:T(8,128)(2,1)S(1)}, u32[]{:S(2)}, u32[]{:S(2)}) collective-permute-start(bf16[272,128]{1,0:T(8,128)(2,1)S(1)} %sum.4), channel_id=1, source_target_pairs={{0,8},{4,12},{8,0},{12,4},{1,9},{5,13},{9,1},{13,5},{2,10},{6,14},... | collective-permute-start | bytes 208904 | tf_op jit(solution)/shard_map/ppermute | solution.py:19
  15.1 5.9 %collective-permute-start.3 = (bf16[272,128]{1,0:T(8,128)(2,1)S(1)}, bf16[272,128]{1,0:T(8,128)(2,1)S(1)}, u32[]{:S(2)}, u32[]{:S(2)}) collective-permute-start(bf16[272,128]{1,0:T(8,128)(2,1)S(1)} %sum.3), channel_id=1, source_target_pairs={{0,4},{4,0},{8,12},{12,8},{1,5},{5,1},{9,13},{13,9},{2,6},{6,2},{1... | collective-permute-start | bytes 208904 | tf_op jit(solution)/shard_map/ppermute | solution.py:19
  21.7 6.9 %collective-permute-start.6 = (bf16[16,16,128]{2,1,0:T(8,128)(2,1)S(1)}, bf16[16,16,128]{2,1,0:T(8,128)(2,1)S(1)}, u32[]{:S(2)}, u32[]{:S(2)}) collective-permute-start(bf16[16,16,128]{2,1,0:T(8,128)(2,1)S(1)} %get-tuple-element.66), channel_id=1, source_target_pairs={{0,8},{4,12},{8,0},{12,4},{1,9},{5,13},{9,1},{13,5},{2,10},{6,14},... | collective-permute-start | bytes 196616 | tf_op jit(solution)/shard_map/ppermute | solution.py:19
  21.8 6.8 %collective-permute-start.7 = (bf16[16,16,128]{2,1,0:T(8,128)(2,1)S(1)}, bf16[16,16,128]{2,1,0:T(8,128)(2,1)S(1)}, u32[]{:S(2)}, u32[]{:S(2)}) collective-permute-start(bf16[16,16,128]{2,1,0:T(8,128)(2,1)S(1)} %get-tuple-element.67), channel_id=1, source_target_pairs={{0,12},{4,8},{8,4},{12,0},{1,13},{5,9},{9,5},{13,1},{2,14},{6,10},... | collective-permute-start | bytes 196616 | tf_op jit(solution)/shard_map/ppermute | solution.py:19
  23.6 4.2 %collective-permute-start.9 = (bf16[16,16,128]{2,1,0:T(8,128)(2,1)S(1)}, bf16[16,16,128]{2,1,0:T(8,128)(2,1)S(1)}, u32[]{:S(2)}, u32[]{:S(2)}) collective-permute-start(bf16[16,16,128]{2,1,0:T(8,128)(2,1)S(1)} %get-tuple-element.71), channel_id=1, source_target_pairs={{0,4},{4,0},{8,12},{12,8},{1,5},{5,1},{9,13},{13,9},{2,6},{6,2},{1... | collective-permute-start | bytes 196616 | tf_op jit(solution)/shard_map/ppermute | solution.py:19
  27.8 4.2 %collective-permute-start.10 = (bf16[32,16,128]{2,1,0:T(8,128)(2,1)S(1)}, bf16[32,16,128]{2,1,0:T(8,128)(2,1)S(1)}, u32[]{:S(2)}, u32[]{:S(2)}) collective-permute-start(bf16[32,16,128]{2,1,0:T(8,128)(2,1)S(1)} %constant_dynamic-update-slice_fusion.refs_0_), channel_id=1, source_target_pairs={{0,2},{2,0},{1,3},{3,1},{4,6},{6,4},{5,7},{7,5},{8,10},{10,8},{9,1... | collective-permute-start | bytes 393224 | tf_op jit(solution)/shard_map/ppermute | solution.py:19
  28.6 4.6 %collective-permute-start.8 = (bf16[32,16,128]{2,1,0:T(8,128)(2,1)S(1)}, bf16[32,16,128]{2,1,0:T(8,128)(2,1)S(1)}, u32[]{:S(2)}, u32[]{:S(2)}) collective-permute-start(bf16[32,16,128]{2,1,0:T(8,128)(2,1)S(1)} %pad_maximum_fusion), channel_id=1, source_target_pairs={{0,2},{2,0},{1,3},{3,1},{4,6},{6,4},{5,7},{7,5},{8,10},{10,8},{9,1... | collective-permute-start | bytes 393224 | tf_op jit(solution)/shard_map/ppermute | solution.py:19
  34.6 6.0 %collective-permute-start.11 = (bf16[256,256]{1,0:T(8,128)(2,1)S(1)}, bf16[256,256]{1,0:T(8,128)(2,1)S(1)}, u32[]{:S(2)}, u32[]{:S(2)}) collective-permute-start(bf16[256,256]{1,0:T(8,128)(2,1)S(1)} %select_select_fusion), channel_id=1, source_target_pairs={{0,1},{1,0},{2,3},{3,2},{4,5},{5,4},{6,7},{7,6},{8,9},{9,8},{10,11... | collective-permute-start | bytes 393224 | tf_op jit(solution)/shard_map/ppermute | solution.py:19

commit v12 on v10

--- a/solution.py
+++ b/solution.py
@@ -320,6 +320,26 @@
         copy.wait()
 
 
+def emit_kernel(keys, wide, *refs):
+    parts, (out_hbm, rows_ref, turned_ref, out_ref, sem) = refs[: len(keys)], refs[len(keys) :]
+    share, frames, rows = out_ref.shape
+    size = rows_ref.shape[0] // len(keys)
+    for (flip, far), part in zip(keys, parts):
+        spot = pl.multiple_of(half_of(flip, far, wide) * size, size)
+        rows_ref[pl.ds(spot, size), :] = part[...].reshape(size, LANES).astype(F32)
+    first = lax.axis_index(PLANE) * share
+    select = (iota((share, LANES), 1) == iota((share, LANES), 0) + first).astype(BF16)
+    for f in range(frames):
+        cells = rows_ref[pl.ds(f, rows, stride=frames), :].astype(BF16)
+        turned_ref[pl.ds(f, share, stride=frames), :] = lax.dot_general(
+            select, cells, (((1,), (1,)), ((), ())), preferred_element_type=F32
+        )
+    out_ref[...] = turned_ref[...].astype(BF16).reshape(share, frames, rows)
+    copy = pltpu.make_async_copy(out_ref, out_hbm, sem)
+    copy.start()
+    copy.wait()
+
+
 VMEM = pl.BlockSpec(memory_space=pltpu.VMEM)
 SMEM = pl.BlockSpec(memory_space=pltpu.SMEM)
 HBM = pl.BlockSpec(memory_space=pltpu.HBM)
@@ -493,9 +513,20 @@
     tip = exchange(tip, "rep", 1)
 
     foot_share = support.shape[1] // plane_count
-    in_order = [pick(ordered, q, half) for q in range(plane_count) for half in (0, 1)]
-    mine = lax.dynamic_slice_in_dim(jnp.concatenate(in_order), plane * foot_share, foot_share, 2)
-    trace_out = jnp.transpose(mine, (2, 1, 0))
+    trace_out = pl.pallas_call(
+        functools.partial(emit_kernel, back_keys, wide),
+        out_shape=shaped((foot_share, frames, rows)),
+        in_specs=[VMEM] * len(back_keys),
+        out_specs=HBM,
+        scratch_shapes=[
+            pltpu.VMEM((rows * frames, LANES), F32),
+            pltpu.VMEM((foot_share * frames, rows), F32),
+            pltpu.VMEM((foot_share, frames, rows), BF16),
+            pltpu.SemaphoreType.DMA(()),
+        ],
+        compiler_params=pltpu.CompilerParams(vmem_limit_bytes=32 * mib),
+        name="emit",
+    )(*[ordered[key] for key in back_keys])
 
     back_projected = pl.pallas_call(
         functools.partial(backward_kernel, back_keys, wide),

time: 42.6 us -> 43.9 us (1.031)
  Pallas kernels: 15.6 us -> 17 us
  waiting for transfers between devices: 6.8 us -> 8.1 us
  local copies, waits for them, and re-layouts: 2.26 us -> 0.98 us
    pallas_call x0 -> x1, Pallas kernels: none -> 1.39 us  [on_device(): pl.pallas_call(functools.partial(emit_kernel, back_keys, wide), out_shape...]
    ppermute x12, waiting for transfers between devices: 6.8 us -> 8.1 us  [exchange(): return lax.ppermute(cells, axis, [(i, i ^ flip) for i in range(count)])]
    unnamed x13 -> x12, local copies, waits for them, and re-layouts: 1.32 us -> 0.04 us
  transfers between devices with their start and end apart: 12 -> 12, of which waited for: 4 -> 5; matrix products, arithmetic and copies ran while one was open for 4% -> 1% of each run, Pallas kernels for 23% -> 26%
where the time goes in v12:
time: 43.9 us; the launch traced here: 43.7 us
  Pallas kernels  17 us (39%)
  starting transfers between devices  16.5 us (38%)
  waiting for transfers between devices  8.1 us (18%)
  local copies, waits for them, and re-layouts  0.98 us (2%)
  between operations  0.88 us (2%)
    ppermute x12, starting transfers between devices, exchange(): return lax.ppermute(cells, axis, [(i, i ^ flip) for i in range(count)])  16.5 us
    ppermute x12, waiting for transfers between devices, exchange(): return lax.ppermute(cells, axis, [(i, i ^ flip) for i in range(count)])  8.1 us
    pallas_call x4, Pallas kernels, subtract(): call(functools.partial(residual_kernel, flip, far, wide, spots), 'residua...  5.04 us
    pallas_call x4, Pallas kernels, on_device(): call(functools.partial(forward_kernel, flip, far, turn == 0, wide, halves...  4.41 us
    pallas_call x1, Pallas kernels, on_device(): pl.pallas_call(functools.partial(backward_kernel, back_keys, wide), out_s...  2.38 us
    pallas_call x1, Pallas kernels, on_device(): pl.pallas_call(functools.partial(prepare_kernel, rim, cuts), out_shape=(s...  1.9 us
    pallas_call x1, Pallas kernels, on_device(): pl.pallas_call(functools.partial(emit_kernel, back_keys, wide), out_shape...  1.39 us
    pallas_call x1, Pallas kernels, on_device(): call(functools.partial(bands_kernel, rim, frames), 'bands', [(width, widt...  1 us
  transfers between devices with their start and end apart: 12, of which 5 were waited for; matrix products, arithmetic and copies ran while one was open for 1% of the time, Pallas kernels for 26%

profile of v12, /device:TPU:1, one launch (start us, length us, event | category | flops | bytes accessed | tf_op | source)
XLA Modules:
  0.0 43.7 jit_solution(1607542013043536153)
XLA Ops:
  0.6 0.9 %constant_dynamic-slice_fusion = bf16[2,16,16,128]{3,2,1,0:T(8,128)(2,1)S(1)} fusion(bf16[2,16,128,128]{3,2,1,0:T(8,128)(2,1)} %movie_hbm.1, s32[]{:T(128)S(6)} %select_n.40), kind=kLoop, calls=%fused_computation.10 | loop fusion | bytes 262148 | tf_op jit(solution)/shard_map/dynamic_slice | solution.py:388
  1.6 0.1 collective-permute-start
  1.7 1.9 %prepare.1 = (bf16[16,160,256]{2,1,0:T(8,128)(2,1)S(1)}, bf16[128,128]{1,0:T(8,128)(2,1)S(1)}, bf16[256,768]{1,0:T(8,128)(2,1)S(1)}, s32[128,128]{1,0:T(8,128)S(...) custom-call(f32[25]{0:T(128)} %col_ref, f32[25]{0:T(128)} %row_ref, bf16[2,16,128,128]{3,2,1,0:T(8,128)(2,1)} %movie_hbm.1, ...), custom_call_target="tpu_custom_call" | custom-call | tf_op jit(solution)/shard_map/prepare/pallas_call | solution.py:391
  3.6 0.0 copy-start.3
  3.6 0.0 collective-permute-done.edge_ref
  3.6 1.2 %forward.4 = (bf16[16,160,256]{2,1,0:T(8,128)(2,1)S(1)}, bf16[512,256]{1,0:T(8,128)(2,1)S(1)}, bf16[512,128]{1,0:T(8,128)(2,1)S(1)}) custom-call(bf16[16,160,256]{2,1,0:T(8,128)(2,1)S(1)} %get-tuple-element.46.smooth_in_ref, bf16[2,16,16,128]{3,2,1,0:T(8,128)(2,1)S(1)} %collective-permute-done.edge_ref, ...), custom_call_target="tpu_custom_call", output_to_operand_aliasing={{0}: (0, {})} | custom-call | tf_op jit(solution)/shard_map/forward/pallas_call | solution.py:429
  4.9 0.0 copy-done.3
  4.9 2.7 %collective-permute-start.2 = (bf16[512,128]{1,0:T(8,128)(2,1)S(1)}, bf16[512,128]{1,0:T(8,128)(2,1)S(1)}, u32[]{:S(2)}, u32[]{:S(2)}) collective-permute-start(bf16[512,128]{1,0:T(8,128)(2,1)S(1)} %get-tuple-element.61), channel_id=1, source_target_pairs={{0,2},{2,0},{1,3},{3,1},{4,6},{6,4},{5,7},{7,5},{8,10},{10,8},{9,1... | collective-permute-start | bytes 393224 | tf_op jit(solution)/shard_map/ppermute | solution.py:19
  7.6 1.0 %forward.5 = (bf16[16,160,256]{2,1,0:T(8,128)(2,1)S(1)}, bf16[512,256]{1,0:T(8,128)(2,1)S(1)}, bf16[512,128]{1,0:T(8,128)(2,1)S(1)}) custom-call(bf16[16,160,256]{2,1,0:T(8,128)(2,1)S(1)} %get-tuple-element.51.smooth_in_ref, bf16[2,16,16,128]{3,2,1,0:T(8,128)(2,1)S(1)} %collective-permute-done.edge_ref, ...), custom_call_target="tpu_custom_call", output_to_operand_aliasing={{0}: (0, {})} | custom-call | tf_op jit(solution)/shard_map/forward/pallas_call | solution.py:429
  8.7 0.0 copy-start.4
  8.7 1.1 %forward.6 = (bf16[16,160,256]{2,1,0:T(8,128)(2,1)S(1)}, bf16[512,256]{1,0:T(8,128)(2,1)S(1)}, bf16[512,128]{1,0:T(8,128)(2,1)S(1)}) custom-call(bf16[16,160,256]{2,1,0:T(8,128)(2,1)S(1)} %get-tuple-element.52.smooth_in_ref, bf16[2,16,16,128]{3,2,1,0:T(8,128)(2,1)S(1)} %collective-permute-done.edge_ref, ...), custom_call_target="tpu_custom_call", output_to_operand_aliasing={{0}: (0, {})} | custom-call | tf_op jit(solution)/shard_map/forward/pallas_call | solution.py:429
  9.7 0.1 collective-permute-start.1
  9.8 0.0 copy-done.4
  9.8 0.1 broadcast_multiply_fusion
  9.9 0.1 select_reduce_fusion
  10.0 0.0 copy-start
  10.1 0.0 copy-start.1
  10.1 0.0 copy-start.2
  10.1 1.1 %forward.7 = (bf16[16,160,256]{2,1,0:T(8,128)(2,1)S(1)}, bf16[512,256]{1,0:T(8,128)(2,1)S(1)}, bf16[512,128]{1,0:T(8,128)(2,1)S(1)}) custom-call(bf16[16,160,256]{2,1,0:T(8,128)(2,1)S(1)} %get-tuple-element.53.smooth_in_ref, bf16[2,16,16,128]{3,2,1,0:T(8,128)(2,1)S(1)} %collective-permute-done.edge_ref, ...), custom_call_target="tpu_custom_call", output_to_operand_aliasing={{0}: (0, {})} | custom-call | tf_op jit(solution)/shard_map/forward/pallas_call | solution.py:429
  11.2 0.3 collective-permute-done.2.refs_1_
  11.5 3.4 %collective-permute-start.5 = (bf16[272,128]{1,0:T(8,128)(2,1)S(1)}, bf16[272,128]{1,0:T(8,128)(2,1)S(1)}, u32[]{:S(2)}, u32[]{:S(2)}) collective-permute-start(bf16[272,128]{1,0:T(8,128)(2,1)S(1)} %sum.5), channel_id=1, source_target_pairs={{0,12},{4,8},{8,4},{12,0},{1,13},{5,9},{9,5},{13,1},{2,14},{6,10},... | collective-permute-start | bytes 208904 | tf_op jit(solution)/shard_map/ppermute | solution.py:19
  14.9 0.1 collective-permute-start.4
  15.0 0.0 collective-permute-done.1.refs_1_
  15.1 0.9 %collective-permute-start.3 = (bf16[272,128]{1,0:T(8,128)(2,1)S(1)}, bf16[272,128]{1,0:T(8,128)(2,1)S(1)}, u32[]{:S(2)}, u32[]{:S(2)}) collective-permute-start(bf16[272,128]{1,0:T(8,128)(2,1)S(1)} %sum.3), channel_id=1, source_target_pairs={{0,4},{4,0},{8,12},{12,8},{1,5},{5,1},{9,13},{13,9},{2,6},{6,2},{1... | collective-permute-start | bytes 208904 | tf_op jit(solution)/shard_map/ppermute | solution.py:19
  16.0 0.0 copy-done
  16.0 1.0 %bands.1 = (bf16[256,256]{1,0:T(8,128)(2,1)S(1)}, bf16[256,768]{1,0:T(8,128)(2,1)S(1)}) custom-call(f32[25]{0:T(128)S(1)} %copy-done, f32[25]{0:T(128)S(1)} %copy-done.1), custom_call_target="tpu_custom_call" | custom-call | tf_op jit(solution)/shard_map/bands/pallas_call | solution.py:462
  17.0 0.0 collective-permute-done.5.refs_4_
  17.0 3.9 %collective-permute-done.4.refs_3_ = bf16[272,128]{1,0:T(8,128)(2,1)S(1)} collective-permute-done((bf16[272,128]{1,0:T(8,128)(2,1)S(1)}, bf16[272,128]{1,0:T(8,128)(2,1)S(1)}, u32[]{:S(2)}, u32[]{:S(2)}) %collective-permute-start.4) | collective-permute-done | bytes 69664 | tf_op jit(solution)/shard_map/ppermute | solution.py:19
  20.9 0.0 collective-permute-done.3.refs_2_
  20.9 0.8 %mix.1 = (bf16[16,16,128]{2,1,0:T(8,128)(2,1)S(1)}, bf16[16,16,128]{2,1,0:T(8,128)(2,1)S(1)}, bf16[16,16,128]{2,1,0:T(8,128)(2,1)S(1)}, bf16[16,16,128]{2,1,0:T(8,128)(2,1)S(1)}) custom-call(s32[1,128]{1,0:T(1,128)S(1)} %bitcast.8, bf16[16,128]{1,0:T(8,128)(2,1)S(1)} %pad_bitcast_fusion.lag_ref, bf16[512,128]{1,0:T(8,128)(2,1)S(1)} %get-tuple-element.66.refs_0_, ...), custom_call_target="tpu_custom_call" | custom-call | tf_op jit(solution)/shard_map/mix/pallas_call | solution.py:470
  21.7 0.1 collective-permute-start.6
  21.8 1.8 %collective-permute-start.7 = (bf16[16,16,128]{2,1,0:T(8,128)(2,1)S(1)}, bf16[16,16,128]{2,1,0:T(8,128)(2,1)S(1)}, u32[]{:S(2)}, u32[]{:S(2)}) collective-permute-start(bf16[16,16,128]{2,1,0:T(8,128)(2,1)S(1)} %get-tuple-element.71), channel_id=1, source_target_pairs={{0,8},{4,12},{8,0},{12,4},{1,9},{5,13},{9,1},{13,5},{2,10},{6,14},... | collective-permute-start | bytes 196616 | tf_op jit(solution)/shard_map/ppermute | solution.py:19
  23.6 1.7 %collective-permute-start.8 = (bf16[16,16,128]{2,1,0:T(8,128)(2,1)S(1)}, bf16[16,16,128]{2,1,0:T(8,128)(2,1)S(1)}, u32[]{:S(2)}, u32[]{:S(2)}) collective-permute-start(bf16[16,16,128]{2,1,0:T(8,128)(2,1)S(1)} %get-tuple-element.72), channel_id=1, source_target_pairs={{0,12},{4,8},{8,4},{12,0},{1,13},{5,9},{9,5},{13,1},{2,14},{6,10},... | collective-permute-start | bytes 196616 | tf_op jit(solution)/shard_map/ppermute | solution.py:19
  25.4 0.0 collective-permute-done.6
  25.4 1.3 %residual.4 = (bf16[512,256]{1,0:T(8,128)(2,1)S(1)}, bf16[256,256]{1,0:T(8,128)(2,1)S(1)}, bf16[32,16,128]{2,1,0:T(8,128)(2,1)S(1)}) custom-call(bf16[512,256]{1,0:T(8,128)(2,1)S(1)} %get-tuple-element.54.filtered_ref, s32[128,128]{1,0:T(8,128)S(1)} %get-tuple-element.49.code_ref, bf16[512,256]{1,0:T(8,128)(2,1)S(1)} %get-tuple-element.55.templates_ref, ...), custom_call_target="tpu_custom_call" | custom-call | tf_op jit(solution)/shard_map/residual/pallas_call | solution.py:491
  26.7 0.0 collective-permute-done.7.refs_0_
  26.7 2.6 %collective-permute-done.8.refs_1_ = bf16[16,16,128]{2,1,0:T(8,128)(2,1)S(1)} collective-permute-done((bf16[16,16,128]{2,1,0:T(8,128)(2,1)S(1)}, bf16[16,16,128]{2,1,0:T(8,128)(2,1)S(1)}, u32[]{:S(2)}, u32[]{:S(2)}) %collective-permute-start.8) | collective-permute-done | bytes 65568 | tf_op jit(solution)/shard_map/ppermute | solution.py:19
  29.3 0.4 collective-permute-start.10
  29.7 1.2 %collective-permute-start.9 = (bf16[32,16,128]{2,1,0:T(8,128)(2,1)S(1)}, bf16[32,16,128]{2,1,0:T(8,128)(2,1)S(1)}, u32[]{:S(2)}, u32[]{:S(2)}) collective-permute-start(bf16[32,16,128]{2,1,0:T(8,128)(2,1)S(1)} %constant_dynamic-update-slice_fusion.refs_0_), channel_id=1, source_target_pairs={{0,2},{2,0},{1,3},{3,1},{4,6},{6,4},{5,7},{7,5},{8,10},{10,8},{9,1... | collective-permute-start | bytes 393224 | tf_op jit(solution)/shard_map/ppermute | solution.py:19
  30.8 1.3 %residual.5 = (bf16[512,256]{1,0:T(8,128)(2,1)S(1)}, bf16[256,256]{1,0:T(8,128)(2,1)S(1)}, bf16[32,16,128]{2,1,0:T(8,128)(2,1)S(1)}) custom-call(bf16[512,256]{1,0:T(8,128)(2,1)S(1)} %get-tuple-element.70.filtered_ref, s32[128,128]{1,0:T(8,128)S(1)} %get-tuple-element.49.code_ref, bf16[512,256]{1,0:T(8,128)(2,1)S(1)} %get-tuple-element.55.templates_ref, ...), custom_call_target="tpu_custom_call" | custom-call | tf_op jit(solution)/shard_map/residual/pallas_call | solution.py:491
  32.1 1.1 %collective-permute-done.10.refs_0_ = bf16[32,16,128]{2,1,0:T(8,128)(2,1)S(1)} collective-permute-done((bf16[32,16,128]{2,1,0:T(8,128)(2,1)S(1)}, bf16[32,16,128]{2,1,0:T(8,128)(2,1)S(1)}, u32[]{:S(2)}, u32[]{:S(2)}) %collective-permute-start.10) | collective-permute-done | bytes 131104 | tf_op jit(solution)/shard_map/ppermute | solution.py:19
  33.2 1.3 %residual.7 = (bf16[512,256]{1,0:T(8,128)(2,1)S(1)}, bf16[256,256]{1,0:T(8,128)(2,1)S(1)}, bf16[32,16,128]{2,1,0:T(8,128)(2,1)S(1)}) custom-call(bf16[512,256]{1,0:T(8,128)(2,1)S(1)} %get-tuple-element.79.filtered_ref, s32[128,128]{1,0:T(8,128)S(1)} %get-tuple-element.49.code_ref, bf16[512,256]{1,0:T(8,128)(2,1)S(1)} %get-tuple-element.55.templates_ref, ...), custom_call_target="tpu_custom_call" | custom-call | tf_op jit(solution)/shard_map/residual/pallas_call | solution.py:491
  34.5 0.1 collective-permute-done.9.refs_0_
  34.6 1.3 %residual.6 = (bf16[512,256]{1,0:T(8,128)(2,1)S(1)}, bf16[256,256]{1,0:T(8,128)(2,1)S(1)}, bf16[32,16,128]{2,1,0:T(8,128)(2,1)S(1)}) custom-call(bf16[512,256]{1,0:T(8,128)(2,1)S(1)} %get-tuple-element.77.filtered_ref, s32[128,128]{1,0:T(8,128)S(1)} %get-tuple-element.49.code_ref, bf16[512,256]{1,0:T(8,128)(2,1)S(1)} %get-tuple-element.55.templates_ref, ...), custom_call_target="tpu_custom_call" | custom-call | tf_op jit(solution)/shard_map/residual/pallas_call | solution.py:491
  35.9 4.0 %collective-permute-start.11 = (bf16[256,256]{1,0:T(8,128)(2,1)S(1)}, bf16[256,256]{1,0:T(8,128)(2,1)S(1)}, u32[]{:S(2)}, u32[]{:S(2)}) collective-permute-start(bf16[256,256]{1,0:T(8,128)(2,1)S(1)} %select_select_fusion), channel_id=1, source_target_pairs={{0,1},{1,0},{2,3},{3,2},{4,5},{5,4},{6,7},{7,6},{8,9},{9,8},{10,11... | collective-permute-start | bytes 393224 | tf_op jit(solution)/shard_map/ppermute | solution.py:19
  39.9 1.4 %emit.1 = bf16[64,16,128]{2,1,0:T(8,128)(2,1)} custom-call(bf16[32,16,128]{2,1,0:T(8,128)(2,1)S(1)} %get-tuple-element.69.refs_0_, bf16[32,16,128]{2,1,0:T(8,128)(2,1)S(1)} %get-tuple-element.76.refs_1_, bf16[32,16,128]{2,1,0:T(8,128)(2,1)S(1)} %get-tuple-element.78.refs_2_, bf16[32,16,128]{2,1,0:T(8,128)(2,1)S(1)} %get-tuple-element.80.refs_3_), custom_call_target="tpu_custom_call" | custom-call | tf_op jit(solution)/shard_map/emit/pallas_call | solution.py:516
  41.3 0.0 collective-permute-done.11.edge_ref
  41.4 2.4 %backward.1 = bf16[2,16,128,128]{3,2,1,0:T(8,128)(2,1)} custom-call(bf16[256,256]{1,0:T(8,128)(2,1)S(1)} %collective-permute-done.11.edge_ref, bf16[256,256]{1,0:T(8,128)(2,1)S(1)} %get-tuple-element.84.col_adj_ref, bf16[256,768]{1,0:T(8,128)(2,1)S(1)} %get-tuple-element.85.row_adj_ref, bf16[512,256]{1,0:T(8,128)(2,1)S(1)} %get-tuple-element.86.refs_0_, ...), custom_call_target="tpu_custom_call" | custom-call | tf_op jit(solution)/shard_map/backward/pallas_call | solution.py:531
  (13 shorter events, 0.1 us)
Async XLA Ops:
  1.6 2.1 %collective-permute-start = (bf16[2,16,16,128]{3,2,1,0:T(8,128)(2,1)S(1)}, bf16[2,16,16,128]{3,2,1,0:T(8,128)(2,1)S(1)}, u32[]{:S(2)}, u32[]{:S(2)}) collective-permute-start(bf16[2,16,16,128]{3,2,1,0:T(8,128)(2,1)S(1)} %constant_dynamic-slice_fusion), channel_id=1, source_target_pairs={{0,1},{1,0},{2,3},{3,2},{4,5},{5,4},{6,7},{7,6},{8,9},{9,8},{10,11... | collective-permute-start | bytes 393224 | tf_op jit(solution)/shard_map/ppermute | solution.py:19
  3.6 1.3 %copy-start.3 = (f32[1,3,65]{2,0,1:T(1,128)S(1)}, f32[1,3,65]{2,0,1:T(1,128)}, u32[]{:S(2)}) copy-start(f32[1,3,65]{2,0,1:T(1,128)} %param.16) | copy-start | bytes 2344
  4.9 6.6 %collective-permute-start.2 = (bf16[512,128]{1,0:T(8,128)(2,1)S(1)}, bf16[512,128]{1,0:T(8,128)(2,1)S(1)}, u32[]{:S(2)}, u32[]{:S(2)}) collective-permute-start(bf16[512,128]{1,0:T(8,128)(2,1)S(1)} %get-tuple-element.61), channel_id=1, source_target_pairs={{0,2},{2,0},{1,3},{3,1},{4,6},{6,4},{5,7},{7,5},{8,10},{10,8},{9,1... | collective-permute-start | bytes 393224 | tf_op jit(solution)/shard_map/ppermute | solution.py:19
  8.7 1.2 %copy-start.4 = (s32[1,3]{1,0:T(1,128)S(1)}, s32[1,3]{1,0:T(1,128)}, u32[]{:S(2)}) copy-start(s32[1,3]{1,0:T(1,128)} %param.17) | copy-start | bytes 40
  9.7 5.3 %collective-permute-start.1 = (bf16[512,128]{1,0:T(8,128)(2,1)S(1)}, bf16[512,128]{1,0:T(8,128)(2,1)S(1)}, u32[]{:S(2)}, u32[]{:S(2)}) collective-permute-start(bf16[512,128]{1,0:T(8,128)(2,1)S(1)} %get-tuple-element.59), channel_id=1, source_target_pairs={{0,2},{2,0},{1,3},{3,1},{4,6},{6,4},{5,7},{7,5},{8,10},{10,8},{9,1... | collective-permute-start | bytes 393224 | tf_op jit(solution)/shard_map/ppermute | solution.py:19
  10.0 5.9 %copy-start = (f32[25]{0:T(128)S(1)}, f32[25]{0:T(128)}, u32[]{:S(2)}) copy-start(f32[25]{0:T(128)} %col_ref) | copy-start | bytes 304
  10.1 5.9 %copy-start.1 = (f32[25]{0:T(128)S(1)}, f32[25]{0:T(128)}, u32[]{:S(2)}) copy-start(f32[25]{0:T(128)} %row_ref) | copy-start | bytes 304
  10.1 10.9 %copy-start.2 = (s32[128,1]{0,1:T(1,128)S(1)}, s32[128,1]{0,1:T(1,128)}, u32[]{:S(2)}) copy-start(s32[128,1]{0,1:T(1,128)} %param.11) | copy-start | bytes 1540
  11.5 5.5 %collective-permute-start.5 = (bf16[272,128]{1,0:T(8,128)(2,1)S(1)}, bf16[272,128]{1,0:T(8,128)(2,1)S(1)}, u32[]{:S(2)}, u32[]{:S(2)}) collective-permute-start(bf16[272,128]{1,0:T(8,128)(2,1)S(1)} %sum.5), channel_id=1, source_target_pairs={{0,12},{4,8},{8,4},{12,0},{1,13},{5,9},{9,5},{13,1},{2,14},{6,10},... | collective-permute-start | bytes 208904 | tf_op jit(solution)/shard_map/ppermute | solution.py:19
  14.9 6.0 %collective-permute-start.4 = (bf16[272,128]{1,0:T(8,128)(2,1)S(1)}, bf16[272,128]{1,0:T(8,128)(2,1)S(1)}, u32[]{:S(2)}, u32[]{:S(2)}) collective-permute-start(bf16[272,128]{1,0:T(8,128)(2,1)S(1)} %sum.4), channel_id=1, source_target_pairs={{0,8},{4,12},{8,0},{12,4},{1,9},{5,13},{9,1},{13,5},{2,10},{6,14},... | collective-permute-start | bytes 208904 | tf_op jit(solution)/shard_map/ppermute | solution.py:19
  15.1 5.9 %collective-permute-start.3 = (bf16[272,128]{1,0:T(8,128)(2,1)S(1)}, bf16[272,128]{1,0:T(8,128)(2,1)S(1)}, u32[]{:S(2)}, u32[]{:S(2)}) collective-permute-start(bf16[272,128]{1,0:T(8,128)(2,1)S(1)} %sum.3), channel_id=1, source_target_pairs={{0,4},{4,0},{8,12},{12,8},{1,5},{5,1},{9,13},{13,9},{2,6},{6,2},{1... | collective-permute-start | bytes 208904 | tf_op jit(solution)/shard_map/ppermute | solution.py:19
  21.7 3.6 %collective-permute-start.6 = (bf16[16,16,128]{2,1,0:T(8,128)(2,1)S(1)}, bf16[16,16,128]{2,1,0:T(8,128)(2,1)S(1)}, u32[]{:S(2)}, u32[]{:S(2)}) collective-permute-start(bf16[16,16,128]{2,1,0:T(8,128)(2,1)S(1)} %get-tuple-element.68), channel_id=1, source_target_pairs={{0,4},{4,0},{8,12},{12,8},{1,5},{5,1},{9,13},{13,9},{2,6},{6,2},{1... | collective-permute-start | bytes 196616 | tf_op jit(solution)/shard_map/ppermute | solution.py:19
  21.8 4.8 %collective-permute-start.7 = (bf16[16,16,128]{2,1,0:T(8,128)(2,1)S(1)}, bf16[16,16,128]{2,1,0:T(8,128)(2,1)S(1)}, u32[]{:S(2)}, u32[]{:S(2)}) collective-permute-start(bf16[16,16,128]{2,1,0:T(8,128)(2,1)S(1)} %get-tuple-element.71), channel_id=1, source_target_pairs={{0,8},{4,12},{8,0},{12,4},{1,9},{5,13},{9,1},{13,5},{2,10},{6,14},... | collective-permute-start | bytes 196616 | tf_op jit(solution)/shard_map/ppermute | solution.py:19
  23.6 5.7 %collective-permute-start.8 = (bf16[16,16,128]{2,1,0:T(8,128)(2,1)S(1)}, bf16[16,16,128]{2,1,0:T(8,128)(2,1)S(1)}, u32[]{:S(2)}, u32[]{:S(2)}) collective-permute-start(bf16[16,16,128]{2,1,0:T(8,128)(2,1)S(1)} %get-tuple-element.72), channel_id=1, source_target_pairs={{0,12},{4,8},{8,4},{12,0},{1,13},{5,9},{9,5},{13,1},{2,14},{6,10},... | collective-permute-start | bytes 196616 | tf_op jit(solution)/shard_map/ppermute | solution.py:19
  29.3 3.9 %collective-permute-start.10 = (bf16[32,16,128]{2,1,0:T(8,128)(2,1)S(1)}, bf16[32,16,128]{2,1,0:T(8,128)(2,1)S(1)}, u32[]{:S(2)}, u32[]{:S(2)}) collective-permute-start(bf16[32,16,128]{2,1,0:T(8,128)(2,1)S(1)} %pad_maximum_fusion), channel_id=1, source_target_pairs={{0,2},{2,0},{1,3},{3,1},{4,6},{6,4},{5,7},{7,5},{8,10},{10,8},{9,1... | collective-permute-start | bytes 393224 | tf_op jit(solution)/shard_map/ppermute | solution.py:19
  29.7 4.9 %collective-permute-start.9 = (bf16[32,16,128]{2,1,0:T(8,128)(2,1)S(1)}, bf16[32,16,128]{2,1,0:T(8,128)(2,1)S(1)}, u32[]{:S(2)}, u32[]{:S(2)}) collective-permute-start(bf16[32,16,128]{2,1,0:T(8,128)(2,1)S(1)} %constant_dynamic-update-slice_fusion.refs_0_), channel_id=1, source_target_pairs={{0,2},{2,0},{1,3},{3,1},{4,6},{6,4},{5,7},{7,5},{8,10},{10,8},{9,1... | collective-permute-start | bytes 393224 | tf_op jit(solution)/shard_map/ppermute | solution.py:19
  35.9 5.4 %collective-permute-start.11 = (bf16[256,256]{1,0:T(8,128)(2,1)S(1)}, bf16[256,256]{1,0:T(8,128)(2,1)S(1)}, u32[]{:S(2)}, u32[]{:S(2)}) collective-permute-start(bf16[256,256]{1,0:T(8,128)(2,1)S(1)} %select_select_fusion), channel_id=1, source_target_pairs={{0,1},{1,0},{2,3},{3,2},{4,5},{5,4},{6,7},{7,6},{8,9},{9,8},{10,11... | collective-permute-start | bytes 393224 | tf_op jit(solution)/shard_map/ppermute | solution.py:19

commit v13 on v12

--- a/solution.py
+++ b/solution.py
@@ -288,8 +288,8 @@
     edge_ref[...] = out_ref[pl.ds(pl.multiple_of(start, edge), edge), :]
 
 
-def backward_kernel(keys, wide, edge_ref, col_adj_ref, row_adj_ref, *refs):
-    parts, (out_hbm, padded_ref, out_ref, sems) = refs[: len(keys)], refs[len(keys) :]
+def backward_kernel(keys, wide, turned_ref, edge_ref, col_adj_ref, row_adj_ref, *refs):
+    parts, (out_hbm, trace_hbm, padded_ref, out_ref, sems) = refs[: len(keys)], refs[len(keys) :]
     planes, frames, rows, _ = out_ref.shape
     edge, size = BLOCK * frames, parts[0].shape[0]
     zero = jnp.zeros_like(edge_ref)
@@ -302,7 +302,8 @@
         near = padded_ref[b * edge : (b + 3) * edge, :]
         return jnp.dot(row_adj_ref[...], near, preferred_element_type=F32).astype(BF16)
 
-    copies = []
+    copies = [pltpu.make_async_copy(turned_ref, trace_hbm, sems.at[rows // BLOCK])]
+    copies[0].start()
     back = along(0)
     for b in range(rows // BLOCK):
         ahead = along(b + 1) if b + 1 < rows // BLOCK else None
@@ -321,7 +322,7 @@
 
 
 def emit_kernel(keys, wide, *refs):
-    parts, (out_hbm, rows_ref, turned_ref, out_ref, sem) = refs[: len(keys)], refs[len(keys) :]
+    parts, (out_ref, rows_ref, turned_ref) = refs[: len(keys)], refs[len(keys) :]
     share, frames, rows = out_ref.shape
     size = rows_ref.shape[0] // len(keys)
     for (flip, far), part in zip(keys, parts):
@@ -335,9 +336,6 @@
             select, cells, (((1,), (1,)), ((), ())), preferred_element_type=F32
         )
     out_ref[...] = turned_ref[...].astype(BF16).reshape(share, frames, rows)
-    copy = pltpu.make_async_copy(out_ref, out_hbm, sem)
-    copy.start()
-    copy.wait()
 
 
 VMEM = pl.BlockSpec(memory_space=pltpu.VMEM)
@@ -500,7 +498,8 @@
     subtract(0, 1, [[k] for k in far_ks], distant)
     for flip in late:
         subtract(flip, 0, [near_ks], [passed[flip]])
-        subtract(flip, 1, [far_ks], [exchange(joined, "planes", flip)])
+        got, _ = lax.optimization_barrier((exchange(joined, "planes", flip), edges[flip, 0]))
+        subtract(flip, 1, [far_ks], [got])
 
     def pick(table, part, half):
         found = table[0, 0]
@@ -513,34 +512,32 @@
     tip = exchange(tip, "rep", 1)
 
     foot_share = support.shape[1] // plane_count
-    trace_out = pl.pallas_call(
+    turned = pl.pallas_call(
         functools.partial(emit_kernel, back_keys, wide),
         out_shape=shaped((foot_share, frames, rows)),
         in_specs=[VMEM] * len(back_keys),
-        out_specs=HBM,
+        out_specs=VMEM,
         scratch_shapes=[
             pltpu.VMEM((rows * frames, LANES), F32),
             pltpu.VMEM((foot_share * frames, rows), F32),
-            pltpu.VMEM((foot_share, frames, rows), BF16),
-            pltpu.SemaphoreType.DMA(()),
         ],
         compiler_params=pltpu.CompilerParams(vmem_limit_bytes=32 * mib),
         name="emit",
     )(*[ordered[key] for key in back_keys])
 
-    back_projected = pl.pallas_call(
+    back_projected, trace_out = pl.pallas_call(
         functools.partial(backward_kernel, back_keys, wide),
-        out_shape=shaped(movie_frames.shape),
-        in_specs=[VMEM] * (3 + len(back_keys)),
-        out_specs=HBM,
+        out_shape=(shaped(movie_frames.shape), shaped(turned.shape)),
+        in_specs=[VMEM] * (4 + len(back_keys)),
+        out_specs=(HBM, HBM),
         scratch_shapes=[
             pltpu.VMEM(((rows + 2 * BLOCK) * frames, width), BF16),
             pltpu.VMEM(movie_frames.shape, BF16),
-            pltpu.SemaphoreType.DMA((rows // BLOCK,)),
+            pltpu.SemaphoreType.DMA((rows // BLOCK + 1,)),
         ],
         compiler_params=pltpu.CompilerParams(vmem_limit_bytes=32 * mib),
         name="backward",
-    )(tip, col_adj, row_adj, *[residual[key] for key in back_keys])
+    )(turned, tip, col_adj, row_adj, *[residual[key] for key in back_keys])
     return trace_out, back_projected
 
 

time: 43.9 us -> 42.4 us (0.966)
  waiting for transfers between devices: 8.1 us -> 6.91 us
  Pallas kernels: 17 us -> 16.3 us
    ppermute x12, waiting for transfers between devices: 8.1 us -> 6.91 us  [exchange(): return lax.ppermute(cells, axis, [(i, i ^ flip) for i in range(count)])]
    pallas_call x1, Pallas kernels: 1.39 us -> 0.67 us  [on_device(): pl.pallas_call(functools.partial(emit_kernel, back_keys, wide), out_shape...]
  transfers between devices with their start and end apart: 12 -> 12, of which waited for: 5 -> 5; matrix products, arithmetic and copies ran while one was open for 1% -> 1% of each run, Pallas kernels for 26% -> 25%
where the time goes in v13:
time: 42.4 us; the launch traced here: 41.9 us
  starting transfers between devices  16.6 us (39%)
  Pallas kernels  16.3 us (38%)
  waiting for transfers between devices  6.91 us (16%)
  local copies, waits for them, and re-layouts  0.98 us (2%)
  between operations  0.87 us (2%)
    ppermute x12, starting transfers between devices, exchange(): return lax.ppermute(cells, axis, [(i, i ^ flip) for i in range(count)])  16.6 us
    ppermute x12, waiting for transfers between devices, exchange(): return lax.ppermute(cells, axis, [(i, i ^ flip) for i in range(count)])  6.91 us
    pallas_call x4, Pallas kernels, subtract(): call(functools.partial(residual_kernel, flip, far, wide, spots), 'residua...  5.03 us
    pallas_call x4, Pallas kernels, on_device(): call(functools.partial(forward_kernel, flip, far, turn == 0, wide, halves...  4.41 us
    pallas_call x1, Pallas kernels, on_device(): pl.pallas_call(functools.partial(backward_kernel, back_keys, wide), out_s...  2.38 us
    pallas_call x1, Pallas kernels, on_device(): pl.pallas_call(functools.partial(prepare_kernel, rim, cuts), out_shape=(s...  1.9 us
    pallas_call x1, Pallas kernels, on_device(): call(functools.partial(bands_kernel, rim, frames), 'bands', [(width, widt...  1 us
    dynamic_slice x1, local copies, waits for them, and re-layouts, on_device(): lax.dynamic_slice_in_dim(movie_frames, start, BLOCK, axis=2)  0.93 us
  transfers between devices with their start and end apart: 12, of which 5 were waited for; matrix products, arithmetic and copies ran while one was open for 1% of the time, Pallas kernels for 25%

profile of v13, /device:TPU:1, one launch (start us, length us, event | category | flops | bytes accessed | tf_op | source)
XLA Modules:
  0.0 41.9 jit_solution(6071230876432959923)
XLA Ops:
  0.6 0.9 %constant_dynamic-slice_fusion = bf16[2,16,16,128]{3,2,1,0:T(8,128)(2,1)S(1)} fusion(bf16[2,16,128,128]{3,2,1,0:T(8,128)(2,1)} %movie_hbm.1, s32[]{:T(128)S(6)} %select_n.40), kind=kLoop, calls=%fused_computation.10 | loop fusion | bytes 262148 | tf_op jit(solution)/shard_map/dynamic_slice | solution.py:386
  1.6 0.1 collective-permute-start
  1.7 1.9 %prepare.1 = (bf16[16,160,256]{2,1,0:T(8,128)(2,1)S(1)}, bf16[128,128]{1,0:T(8,128)(2,1)S(1)}, bf16[256,768]{1,0:T(8,128)(2,1)S(1)}, s32[128,128]{1,0:T(8,128)S(...) custom-call(f32[25]{0:T(128)} %col_ref, f32[25]{0:T(128)} %row_ref, bf16[2,16,128,128]{3,2,1,0:T(8,128)(2,1)} %movie_hbm.1, ...), custom_call_target="tpu_custom_call" | custom-call | tf_op jit(solution)/shard_map/prepare/pallas_call | solution.py:389
  3.6 0.0 copy-start.3
  3.6 0.0 collective-permute-done.edge_ref
  3.6 1.2 %forward.4 = (bf16[16,160,256]{2,1,0:T(8,128)(2,1)S(1)}, bf16[512,256]{1,0:T(8,128)(2,1)S(1)}, bf16[512,128]{1,0:T(8,128)(2,1)S(1)}) custom-call(bf16[16,160,256]{2,1,0:T(8,128)(2,1)S(1)} %get-tuple-element.49.smooth_in_ref, bf16[2,16,16,128]{3,2,1,0:T(8,128)(2,1)S(1)} %collective-permute-done.edge_ref, ...), custom_call_target="tpu_custom_call", output_to_operand_aliasing={{0}: (0, {})} | custom-call | tf_op jit(solution)/shard_map/forward/pallas_call | solution.py:427
  4.9 0.0 copy-done.3
  4.9 2.7 %collective-permute-start.2 = (bf16[512,128]{1,0:T(8,128)(2,1)S(1)}, bf16[512,128]{1,0:T(8,128)(2,1)S(1)}, u32[]{:S(2)}, u32[]{:S(2)}) collective-permute-start(bf16[512,128]{1,0:T(8,128)(2,1)S(1)} %get-tuple-element.64), channel_id=1, source_target_pairs={{0,2},{2,0},{1,3},{3,1},{4,6},{6,4},{5,7},{7,5},{8,10},{10,8},{9,1... | collective-permute-start | bytes 393224 | tf_op jit(solution)/shard_map/ppermute | solution.py:19
  7.6 1.0 %forward.5 = (bf16[16,160,256]{2,1,0:T(8,128)(2,1)S(1)}, bf16[512,256]{1,0:T(8,128)(2,1)S(1)}, bf16[512,128]{1,0:T(8,128)(2,1)S(1)}) custom-call(bf16[16,160,256]{2,1,0:T(8,128)(2,1)S(1)} %get-tuple-element.54.smooth_in_ref, bf16[2,16,16,128]{3,2,1,0:T(8,128)(2,1)S(1)} %collective-permute-done.edge_ref, ...), custom_call_target="tpu_custom_call", output_to_operand_aliasing={{0}: (0, {})} | custom-call | tf_op jit(solution)/shard_map/forward/pallas_call | solution.py:427
  8.7 0.0 copy-start.4
  8.7 1.1 %forward.6 = (bf16[16,160,256]{2,1,0:T(8,128)(2,1)S(1)}, bf16[512,256]{1,0:T(8,128)(2,1)S(1)}, bf16[512,128]{1,0:T(8,128)(2,1)S(1)}) custom-call(bf16[16,160,256]{2,1,0:T(8,128)(2,1)S(1)} %get-tuple-element.55.smooth_in_ref, bf16[2,16,16,128]{3,2,1,0:T(8,128)(2,1)S(1)} %collective-permute-done.edge_ref, ...), custom_call_target="tpu_custom_call", output_to_operand_aliasing={{0}: (0, {})} | custom-call | tf_op jit(solution)/shard_map/forward/pallas_call | solution.py:427
  9.7 0.1 collective-permute-start.1
  9.8 0.0 copy-done.4
  9.8 0.1 broadcast_multiply_fusion
  9.9 0.1 select_reduce_fusion
  10.0 0.0 copy-start
  10.1 0.0 copy-start.1
  10.1 0.0 copy-start.2
  10.1 1.1 %forward.7 = (bf16[16,160,256]{2,1,0:T(8,128)(2,1)S(1)}, bf16[512,256]{1,0:T(8,128)(2,1)S(1)}, bf16[512,128]{1,0:T(8,128)(2,1)S(1)}) custom-call(bf16[16,160,256]{2,1,0:T(8,128)(2,1)S(1)} %get-tuple-element.56.smooth_in_ref, bf16[2,16,16,128]{3,2,1,0:T(8,128)(2,1)S(1)} %collective-permute-done.edge_ref, ...), custom_call_target="tpu_custom_call", output_to_operand_aliasing={{0}: (0, {})} | custom-call | tf_op jit(solution)/shard_map/forward/pallas_call | solution.py:427
  11.2 0.3 collective-permute-done.2.refs_1_
  11.5 3.4 %collective-permute-start.5 = (bf16[272,128]{1,0:T(8,128)(2,1)S(1)}, bf16[272,128]{1,0:T(8,128)(2,1)S(1)}, u32[]{:S(2)}, u32[]{:S(2)}) collective-permute-start(bf16[272,128]{1,0:T(8,128)(2,1)S(1)} %sum.5), channel_id=1, source_target_pairs={{0,12},{4,8},{8,4},{12,0},{1,13},{5,9},{9,5},{13,1},{2,14},{6,10},... | collective-permute-start | bytes 208904 | tf_op jit(solution)/shard_map/ppermute | solution.py:19
  14.9 0.1 collective-permute-start.4
  15.0 0.0 collective-permute-done.1.refs_1_
  15.1 0.9 %collective-permute-start.3 = (bf16[272,128]{1,0:T(8,128)(2,1)S(1)}, bf16[272,128]{1,0:T(8,128)(2,1)S(1)}, u32[]{:S(2)}, u32[]{:S(2)}) collective-permute-start(bf16[272,128]{1,0:T(8,128)(2,1)S(1)} %sum.3), channel_id=1, source_target_pairs={{0,4},{4,0},{8,12},{12,8},{1,5},{5,1},{9,13},{13,9},{2,6},{6,2},{1... | collective-permute-start | bytes 208904 | tf_op jit(solution)/shard_map/ppermute | solution.py:19
  16.0 1.0 %bands.1 = (bf16[256,256]{1,0:T(8,128)(2,1)S(1)}, bf16[256,768]{1,0:T(8,128)(2,1)S(1)}) custom-call(f32[25]{0:T(128)S(1)} %copy-done, f32[25]{0:T(128)S(1)} %copy-done.1), custom_call_target="tpu_custom_call" | custom-call | tf_op jit(solution)/shard_map/bands/pallas_call | solution.py:460
  17.0 0.0 collective-permute-done.5.refs_4_
  17.0 3.9 %collective-permute-done.4.refs_3_ = bf16[272,128]{1,0:T(8,128)(2,1)S(1)} collective-permute-done((bf16[272,128]{1,0:T(8,128)(2,1)S(1)}, bf16[272,128]{1,0:T(8,128)(2,1)S(1)}, u32[]{:S(2)}, u32[]{:S(2)}) %collective-permute-start.4) | collective-permute-done | bytes 69664 | tf_op jit(solution)/shard_map/ppermute | solution.py:19
  20.9 0.0 collective-permute-done.3.refs_2_
  20.9 0.0 copy-done.2
  20.9 0.8 %mix.1 = (bf16[16,16,128]{2,1,0:T(8,128)(2,1)S(1)}, bf16[16,16,128]{2,1,0:T(8,128)(2,1)S(1)}, bf16[16,16,128]{2,1,0:T(8,128)(2,1)S(1)}, bf16[16,16,128]{2,1,0:T(8,128)(2,1)S(1)}) custom-call(s32[1,128]{1,0:T(1,128)S(1)} %bitcast.8, bf16[16,128]{1,0:T(8,128)(2,1)S(1)} %pad_bitcast_fusion.lag_ref, bf16[512,128]{1,0:T(8,128)(2,1)S(1)} %get-tuple-element.69.refs_0_, ...), custom_call_target="tpu_custom_call" | custom-call | tf_op jit(solution)/shard_map/mix/pallas_call | solution.py:468
  21.7 0.1 collective-permute-start.6
  21.8 1.8 %collective-permute-start.7 = (bf16[16,16,128]{2,1,0:T(8,128)(2,1)S(1)}, bf16[16,16,128]{2,1,0:T(8,128)(2,1)S(1)}, u32[]{:S(2)}, u32[]{:S(2)}) collective-permute-start(bf16[16,16,128]{2,1,0:T(8,128)(2,1)S(1)} %get-tuple-element.74), channel_id=1, source_target_pairs={{0,8},{4,12},{8,0},{12,4},{1,9},{5,13},{9,1},{13,5},{2,10},{6,14},... | collective-permute-start | bytes 196616 | tf_op jit(solution)/shard_map/ppermute | solution.py:19
  23.6 1.7 %collective-permute-start.8 = (bf16[16,16,128]{2,1,0:T(8,128)(2,1)S(1)}, bf16[16,16,128]{2,1,0:T(8,128)(2,1)S(1)}, u32[]{:S(2)}, u32[]{:S(2)}) collective-permute-start(bf16[16,16,128]{2,1,0:T(8,128)(2,1)S(1)} %get-tuple-element.75), channel_id=1, source_target_pairs={{0,12},{4,8},{8,4},{12,0},{1,13},{5,9},{9,5},{13,1},{2,14},{6,10},... | collective-permute-start | bytes 196616 | tf_op jit(solution)/shard_map/ppermute | solution.py:19
  25.4 0.0 collective-permute-done.6
  25.4 1.0 %collective-permute-start.9 = (bf16[32,16,128]{2,1,0:T(8,128)(2,1)S(1)}, bf16[32,16,128]{2,1,0:T(8,128)(2,1)S(1)}, u32[]{:S(2)}, u32[]{:S(2)}) collective-permute-start(bf16[32,16,128]{2,1,0:T(8,128)(2,1)S(1)} %constant_dynamic-update-slice_fusion.refs_0_), channel_id=1, source_target_pairs={{0,2},{2,0},{1,3},{3,1},{4,6},{6,4},{5,7},{7,5},{8,10},{10,8},{9,1... | collective-permute-start | bytes 393224 | tf_op jit(solution)/shard_map/ppermute | solution.py:19
  26.4 1.3 %residual.4 = (bf16[512,256]{1,0:T(8,128)(2,1)S(1)}, bf16[256,256]{1,0:T(8,128)(2,1)S(1)}, bf16[32,16,128]{2,1,0:T(8,128)(2,1)S(1)}) custom-call(bf16[512,256]{1,0:T(8,128)(2,1)S(1)} %get-tuple-element.57.filtered_ref, s32[128,128]{1,0:T(8,128)S(1)} %get-tuple-element.52.code_ref, bf16[512,256]{1,0:T(8,128)(2,1)S(1)} %get-tuple-element.58.templates_ref, ...), custom_call_target="tpu_custom_call" | custom-call | tf_op jit(solution)/shard_map/residual/pallas_call | solution.py:489
  27.7 0.0 collective-permute-done.7.refs_0_
  27.7 1.5 %collective-permute-done.8.refs_1_ = bf16[16,16,128]{2,1,0:T(8,128)(2,1)S(1)} collective-permute-done((bf16[16,16,128]{2,1,0:T(8,128)(2,1)S(1)}, bf16[16,16,128]{2,1,0:T(8,128)(2,1)S(1)}, u32[]{:S(2)}, u32[]{:S(2)}) %collective-permute-start.8) | collective-permute-done | bytes 65568 | tf_op jit(solution)/shard_map/ppermute | solution.py:19
  29.2 0.5 %collective-permute-start.10 = (bf16[32,16,128]{2,1,0:T(8,128)(2,1)S(1)}, bf16[32,16,128]{2,1,0:T(8,128)(2,1)S(1)}, u32[]{:S(2)}, u32[]{:S(2)}) collective-permute-start(bf16[32,16,128]{2,1,0:T(8,128)(2,1)S(1)} %pad_maximum_fusion), channel_id=1, source_target_pairs={{0,2},{2,0},{1,3},{3,1},{4,6},{6,4},{5,7},{7,5},{8,10},{10,8},{9,1... | collective-permute-start | bytes 393224 | tf_op jit(solution)/shard_map/ppermute | solution.py:19
  29.7 1.3 %residual.5 = (bf16[512,256]{1,0:T(8,128)(2,1)S(1)}, bf16[256,256]{1,0:T(8,128)(2,1)S(1)}, bf16[32,16,128]{2,1,0:T(8,128)(2,1)S(1)}) custom-call(bf16[512,256]{1,0:T(8,128)(2,1)S(1)} %get-tuple-element.73.filtered_ref, s32[128,128]{1,0:T(8,128)S(1)} %get-tuple-element.52.code_ref, bf16[512,256]{1,0:T(8,128)(2,1)S(1)} %get-tuple-element.58.templates_ref, ...), custom_call_target="tpu_custom_call" | custom-call | tf_op jit(solution)/shard_map/residual/pallas_call | solution.py:489
  30.9 0.0 collective-permute-done.9.refs_0_
  31.0 1.3 %residual.6 = (bf16[512,256]{1,0:T(8,128)(2,1)S(1)}, bf16[256,256]{1,0:T(8,128)(2,1)S(1)}, bf16[32,16,128]{2,1,0:T(8,128)(2,1)S(1)}) custom-call(bf16[512,256]{1,0:T(8,128)(2,1)S(1)} %get-tuple-element.80.filtered_ref, s32[128,128]{1,0:T(8,128)S(1)} %get-tuple-element.52.code_ref, bf16[512,256]{1,0:T(8,128)(2,1)S(1)} %get-tuple-element.58.templates_ref, ...), custom_call_target="tpu_custom_call" | custom-call | tf_op jit(solution)/shard_map/residual/pallas_call | solution.py:489
  32.2 0.9 %collective-permute-done.10.refs_0_ = bf16[32,16,128]{2,1,0:T(8,128)(2,1)S(1)} collective-permute-done((bf16[32,16,128]{2,1,0:T(8,128)(2,1)S(1)}, bf16[32,16,128]{2,1,0:T(8,128)(2,1)S(1)}, u32[]{:S(2)}, u32[]{:S(2)}) %collective-permute-start.10) | collective-permute-done | bytes 131104 | tf_op jit(solution)/shard_map/ppermute | solution.py:19
  33.1 1.3 %residual.7 = (bf16[512,256]{1,0:T(8,128)(2,1)S(1)}, bf16[256,256]{1,0:T(8,128)(2,1)S(1)}, bf16[32,16,128]{2,1,0:T(8,128)(2,1)S(1)}) custom-call(bf16[512,256]{1,0:T(8,128)(2,1)S(1)} %get-tuple-element.82.filtered_ref, s32[128,128]{1,0:T(8,128)S(1)} %get-tuple-element.52.code_ref, bf16[512,256]{1,0:T(8,128)(2,1)S(1)} %get-tuple-element.58.templates_ref, ...), custom_call_target="tpu_custom_call" | custom-call | tf_op jit(solution)/shard_map/residual/pallas_call | solution.py:489
  34.4 4.1 %collective-permute-start.11 = (bf16[256,256]{1,0:T(8,128)(2,1)S(1)}, bf16[256,256]{1,0:T(8,128)(2,1)S(1)}, u32[]{:S(2)}, u32[]{:S(2)}) collective-permute-start(bf16[256,256]{1,0:T(8,128)(2,1)S(1)} %select_select_fusion), channel_id=1, source_target_pairs={{0,1},{1,0},{2,3},{3,2},{4,5},{5,4},{6,7},{7,6},{8,9},{9,8},{10,11... | collective-permute-start | bytes 393224 | tf_op jit(solution)/shard_map/ppermute | solution.py:19
  38.5 0.7 %emit.1.turned_ref = bf16[64,16,128]{2,1,0:T(8,128)(2,1)S(1)} custom-call(bf16[32,16,128]{2,1,0:T(8,128)(2,1)S(1)} %get-tuple-element.72.refs_0_, bf16[32,16,128]{2,1,0:T(8,128)(2,1)S(1)} %get-tuple-element.79.refs_1_, bf16[32,16,128]{2,1,0:T(8,128)(2,1)S(1)} %get-tuple-element.81.refs_2_, bf16[32,16,128]{2,1,0:T(8,128)(2,1)S(1)} %get-tuple-element.85.refs_3_), custom_call_target="tpu_custom_call" | custom-call | tf_op jit(solution)/shard_map/emit/pallas_call | solution.py:515
  39.2 0.3 collective-permute-done.11.edge_ref
  39.5 2.4 %backward.1 = (bf16[2,16,128,128]{3,2,1,0:T(8,128)(2,1)}, bf16[64,16,128]{2,1,0:T(8,128)(2,1)}) custom-call(bf16[64,16,128]{2,1,0:T(8,128)(2,1)S(1)} %emit.1.turned_ref, bf16[256,256]{1,0:T(8,128)(2,1)S(1)} %collective-permute-done.11.edge_ref, bf16[256,256]{1,0:T(8,128)(2,1)S(1)} %get-tuple-element.88.col_adj_ref, ...), custom_call_target="tpu_custom_call" | custom-call | tf_op jit(solution)/shard_map/backward/pallas_call | solution.py:528
  (13 shorter events, 0.1 us)
Async XLA Ops:
  1.6 2.1 %collective-permute-start = (bf16[2,16,16,128]{3,2,1,0:T(8,128)(2,1)S(1)}, bf16[2,16,16,128]{3,2,1,0:T(8,128)(2,1)S(1)}, u32[]{:S(2)}, u32[]{:S(2)}) collective-permute-start(bf16[2,16,16,128]{3,2,1,0:T(8,128)(2,1)S(1)} %constant_dynamic-slice_fusion), channel_id=1, source_target_pairs={{0,1},{1,0},{2,3},{3,2},{4,5},{5,4},{6,7},{7,6},{8,9},{9,8},{10,11... | collective-permute-start | bytes 393224 | tf_op jit(solution)/shard_map/ppermute | solution.py:19
  3.6 1.3 %copy-start.3 = (f32[1,3,65]{2,0,1:T(1,128)S(1)}, f32[1,3,65]{2,0,1:T(1,128)}, u32[]{:S(2)}) copy-start(f32[1,3,65]{2,0,1:T(1,128)} %param.16) | copy-start | bytes 2344
  4.9 6.6 %collective-permute-start.2 = (bf16[512,128]{1,0:T(8,128)(2,1)S(1)}, bf16[512,128]{1,0:T(8,128)(2,1)S(1)}, u32[]{:S(2)}, u32[]{:S(2)}) collective-permute-start(bf16[512,128]{1,0:T(8,128)(2,1)S(1)} %get-tuple-element.64), channel_id=1, source_target_pairs={{0,2},{2,0},{1,3},{3,1},{4,6},{6,4},{5,7},{7,5},{8,10},{10,8},{9,1... | collective-permute-start | bytes 393224 | tf_op jit(solution)/shard_map/ppermute | solution.py:19
  8.7 1.2 %copy-start.4 = (s32[1,3]{1,0:T(1,128)S(1)}, s32[1,3]{1,0:T(1,128)}, u32[]{:S(2)}) copy-start(s32[1,3]{1,0:T(1,128)} %param.17) | copy-start | bytes 40
  9.7 5.3 %collective-permute-start.1 = (bf16[512,128]{1,0:T(8,128)(2,1)S(1)}, bf16[512,128]{1,0:T(8,128)(2,1)S(1)}, u32[]{:S(2)}, u32[]{:S(2)}) collective-permute-start(bf16[512,128]{1,0:T(8,128)(2,1)S(1)} %get-tuple-element.62), channel_id=1, source_target_pairs={{0,2},{2,0},{1,3},{3,1},{4,6},{6,4},{5,7},{7,5},{8,10},{10,8},{9,1... | collective-permute-start | bytes 393224 | tf_op jit(solution)/shard_map/ppermute | solution.py:19
  10.0 5.9 %copy-start = (f32[25]{0:T(128)S(1)}, f32[25]{0:T(128)}, u32[]{:S(2)}) copy-start(f32[25]{0:T(128)} %col_ref) | copy-start | bytes 304
  10.1 5.9 %copy-start.1 = (f32[25]{0:T(128)S(1)}, f32[25]{0:T(128)}, u32[]{:S(2)}) copy-start(f32[25]{0:T(128)} %row_ref) | copy-start | bytes 304
  10.1 10.9 %copy-start.2 = (s32[128,1]{0,1:T(1,128)S(1)}, s32[128,1]{0,1:T(1,128)}, u32[]{:S(2)}) copy-start(s32[128,1]{0,1:T(1,128)} %param.11) | copy-start | bytes 1540
  11.5 5.5 %collective-permute-start.5 = (bf16[272,128]{1,0:T(8,128)(2,1)S(1)}, bf16[272,128]{1,0:T(8,128)(2,1)S(1)}, u32[]{:S(2)}, u32[]{:S(2)}) collective-permute-start(bf16[272,128]{1,0:T(8,128)(2,1)S(1)} %sum.5), channel_id=1, source_target_pairs={{0,12},{4,8},{8,4},{12,0},{1,13},{5,9},{9,5},{13,1},{2,14},{6,10},... | collective-permute-start | bytes 208904 | tf_op jit(solution)/shard_map/ppermute | solution.py:19
  14.9 6.0 %collective-permute-start.4 = (bf16[272,128]{1,0:T(8,128)(2,1)S(1)}, bf16[272,128]{1,0:T(8,128)(2,1)S(1)}, u32[]{:S(2)}, u32[]{:S(2)}) collective-permute-start(bf16[272,128]{1,0:T(8,128)(2,1)S(1)} %sum.4), channel_id=1, source_target_pairs={{0,8},{4,12},{8,0},{12,4},{1,9},{5,13},{9,1},{13,5},{2,10},{6,14},... | collective-permute-start | bytes 208904 | tf_op jit(solution)/shard_map/ppermute | solution.py:19
  15.1 5.9 %collective-permute-start.3 = (bf16[272,128]{1,0:T(8,128)(2,1)S(1)}, bf16[272,128]{1,0:T(8,128)(2,1)S(1)}, u32[]{:S(2)}, u32[]{:S(2)}) collective-permute-start(bf16[272,128]{1,0:T(8,128)(2,1)S(1)} %sum.3), channel_id=1, source_target_pairs={{0,4},{4,0},{8,12},{12,8},{1,5},{5,1},{9,13},{13,9},{2,6},{6,2},{1... | collective-permute-start | bytes 208904 | tf_op jit(solution)/shard_map/ppermute | solution.py:19
  21.7 3.6 %collective-permute-start.6 = (bf16[16,16,128]{2,1,0:T(8,128)(2,1)S(1)}, bf16[16,16,128]{2,1,0:T(8,128)(2,1)S(1)}, u32[]{:S(2)}, u32[]{:S(2)}) collective-permute-start(bf16[16,16,128]{2,1,0:T(8,128)(2,1)S(1)} %get-tuple-element.71), channel_id=1, source_target_pairs={{0,4},{4,0},{8,12},{12,8},{1,5},{5,1},{9,13},{13,9},{2,6},{6,2},{1... | collective-permute-start | bytes 196616 | tf_op jit(solution)/shard_map/ppermute | solution.py:19
  21.8 5.9 %collective-permute-start.7 = (bf16[16,16,128]{2,1,0:T(8,128)(2,1)S(1)}, bf16[16,16,128]{2,1,0:T(8,128)(2,1)S(1)}, u32[]{:S(2)}, u32[]{:S(2)}) collective-permute-start(bf16[16,16,128]{2,1,0:T(8,128)(2,1)S(1)} %get-tuple-element.74), channel_id=1, source_target_pairs={{0,8},{4,12},{8,0},{12,4},{1,9},{5,13},{9,1},{13,5},{2,10},{6,14},... | collective-permute-start | bytes 196616 | tf_op jit(solution)/shard_map/ppermute | solution.py:19
  23.6 5.6 %collective-permute-start.8 = (bf16[16,16,128]{2,1,0:T(8,128)(2,1)S(1)}, bf16[16,16,128]{2,1,0:T(8,128)(2,1)S(1)}, u32[]{:S(2)}, u32[]{:S(2)}) collective-permute-start(bf16[16,16,128]{2,1,0:T(8,128)(2,1)S(1)} %get-tuple-element.75), channel_id=1, source_target_pairs={{0,12},{4,8},{8,4},{12,0},{1,13},{5,9},{9,5},{13,1},{2,14},{6,10},... | collective-permute-start | bytes 196616 | tf_op jit(solution)/shard_map/ppermute | solution.py:19
  25.4 5.6 %collective-permute-start.9 = (bf16[32,16,128]{2,1,0:T(8,128)(2,1)S(1)}, bf16[32,16,128]{2,1,0:T(8,128)(2,1)S(1)}, u32[]{:S(2)}, u32[]{:S(2)}) collective-permute-start(bf16[32,16,128]{2,1,0:T(8,128)(2,1)S(1)} %constant_dynamic-update-slice_fusion.refs_0_), channel_id=1, source_target_pairs={{0,2},{2,0},{1,3},{3,1},{4,6},{6,4},{5,7},{7,5},{8,10},{10,8},{9,1... | collective-permute-start | bytes 393224 | tf_op jit(solution)/shard_map/ppermute | solution.py:19
  29.2 3.9 %collective-permute-start.10 = (bf16[32,16,128]{2,1,0:T(8,128)(2,1)S(1)}, bf16[32,16,128]{2,1,0:T(8,128)(2,1)S(1)}, u32[]{:S(2)}, u32[]{:S(2)}) collective-permute-start(bf16[32,16,128]{2,1,0:T(8,128)(2,1)S(1)} %pad_maximum_fusion), channel_id=1, source_target_pairs={{0,2},{2,0},{1,3},{3,1},{4,6},{6,4},{5,7},{7,5},{8,10},{10,8},{9,1... | collective-permute-start | bytes 393224 | tf_op jit(solution)/shard_map/ppermute | solution.py:19
  34.4 5.1 %collective-permute-start.11 = (bf16[256,256]{1,0:T(8,128)(2,1)S(1)}, bf16[256,256]{1,0:T(8,128)(2,1)S(1)}, u32[]{:S(2)}, u32[]{:S(2)}) collective-permute-start(bf16[256,256]{1,0:T(8,128)(2,1)S(1)} %select_select_fusion), channel_id=1, source_target_pairs={{0,1},{1,0},{2,3},{3,2},{4,5},{5,4},{6,7},{7,6},{8,9},{9,8},{10,11... | collective-permute-start | bytes 393224 | tf_op jit(solution)/shard_map/ppermute | solution.py:19

commit v14 on v13

--- a/solution.py
+++ b/solution.py
@@ -288,18 +288,18 @@
     edge_ref[...] = out_ref[pl.ds(pl.multiple_of(start, edge), edge), :]
 
 
-def backward_kernel(keys, wide, turned_ref, edge_ref, col_adj_ref, row_adj_ref, *refs):
-    parts, (out_hbm, trace_hbm, padded_ref, out_ref, sems) = refs[: len(keys)], refs[len(keys) :]
+def backward_kernel(
+    turned_ref, edge_ref, col_adj_ref, row_adj_ref, body_ref, out_hbm, trace_hbm, out_ref, sems
+):
     planes, frames, rows, _ = out_ref.shape
-    edge, size = BLOCK * frames, parts[0].shape[0]
-    zero = jnp.zeros_like(edge_ref)
-    padded_ref[:edge, :] = jnp.where(lax.axis_index(REP) > 0, edge_ref[...], zero)
-    padded_ref[edge + rows * frames :, :] = jnp.where(lax.axis_index(REP) > 0, zero, edge_ref[...])
-    for (flip, far), part in zip(keys, parts):
-        spot = pl.multiple_of(edge + half_of(flip, far, wide) * size, edge)
-        padded_ref[pl.ds(spot, size), :] = part[...]
+    edge, last = BLOCK * frames, rows // BLOCK - 1
+
     def along(b):
-        near = padded_ref[b * edge : (b + 3) * edge, :]
+        near = body_ref[max(b - 1, 0) * edge : min(b + 2, last + 1) * edge, :]
+        if b == 0:
+            near = jnp.concatenate([jnp.where(lax.axis_index(REP) > 0, edge_ref[...], 0), near])
+        if b == last:
+            near = jnp.concatenate([near, jnp.where(lax.axis_index(REP) > 0, 0, edge_ref[...])])
         return jnp.dot(row_adj_ref[...], near, preferred_element_type=F32).astype(BF16)
 
     copies = [pltpu.make_async_copy(turned_ref, trace_hbm, sems.at[rows // BLOCK])]
@@ -322,7 +322,12 @@
 
 
 def emit_kernel(keys, wide, *refs):
-    parts, (out_ref, rows_ref, turned_ref) = refs[: len(keys)], refs[len(keys) :]
+    count = len(keys)
+    parts, pieces = refs[:count], refs[count : 2 * count]
+    out_ref, body_ref, rows_ref, turned_ref = refs[2 * count :]
+    for (flip, far), piece in zip(keys, pieces):
+        tall = piece.shape[0]
+        body_ref[pl.ds(pl.multiple_of(half_of(flip, far, wide) * tall, tall), tall), :] = piece[...]
     share, frames, rows = out_ref.shape
     size = rows_ref.shape[0] // len(keys)
     for (flip, far), part in zip(keys, parts):
@@ -512,32 +517,31 @@
     tip = exchange(tip, "rep", 1)
 
     foot_share = support.shape[1] // plane_count
-    turned = pl.pallas_call(
+    turned, body = pl.pallas_call(
         functools.partial(emit_kernel, back_keys, wide),
-        out_shape=shaped((foot_share, frames, rows)),
-        in_specs=[VMEM] * len(back_keys),
-        out_specs=VMEM,
+        out_shape=(shaped((foot_share, frames, rows)), shaped((rows * frames, width))),
+        in_specs=[VMEM] * (2 * len(back_keys)),
+        out_specs=(VMEM, VMEM),
         scratch_shapes=[
             pltpu.VMEM((rows * frames, LANES), F32),
             pltpu.VMEM((foot_share * frames, rows), F32),
         ],
         compiler_params=pltpu.CompilerParams(vmem_limit_bytes=32 * mib),
         name="emit",
-    )(*[ordered[key] for key in back_keys])
+    )(*[ordered[key] for key in back_keys], *[residual[key] for key in back_keys])
 
     back_projected, trace_out = pl.pallas_call(
-        functools.partial(backward_kernel, back_keys, wide),
+        backward_kernel,
         out_shape=(shaped(movie_frames.shape), shaped(turned.shape)),
-        in_specs=[VMEM] * (4 + len(back_keys)),
+        in_specs=[VMEM] * 5,
         out_specs=(HBM, HBM),
         scratch_shapes=[
-            pltpu.VMEM(((rows + 2 * BLOCK) * frames, width), BF16),
             pltpu.VMEM(movie_frames.shape, BF16),
             pltpu.SemaphoreType.DMA((rows // BLOCK + 1,)),
         ],
         compiler_params=pltpu.CompilerParams(vmem_limit_bytes=32 * mib),
         name="backward",
-    )(turned, tip, col_adj, row_adj, *[residual[key] for key in back_keys])
+    )(turned, tip, col_adj, row_adj, body)
     return trace_out, back_projected
 
 

time: 42.4 us -> 42.3 us (level)
  transfers between devices with their start and end apart: 12 -> 12, of which waited for: 5 -> 5; matrix products, arithmetic and copies ran while one was open for 1% -> 1% of each run, Pallas kernels for 25% -> 26%
where the time goes in v14:
time: 42.3 us; the launch traced here: 41.8 us
  starting transfers between devices  16.4 us (39%)
  Pallas kernels  16.3 us (39%)
  waiting for transfers between devices  7.03 us (17%)
  local copies, waits for them, and re-layouts  0.98 us (2%)
  between operations  0.87 us (2%)
    ppermute x12, starting transfers between devices, exchange(): return lax.ppermute(cells, axis, [(i, i ^ flip) for i in range(count)])  16.4 us
    ppermute x12, waiting for transfers between devices, exchange(): return lax.ppermute(cells, axis, [(i, i ^ flip) for i in range(count)])  7.03 us
    pallas_call x4, Pallas kernels, subtract(): call(functools.partial(residual_kernel, flip, far, wide, spots), 'residua...  5.04 us
    pallas_call x4, Pallas kernels, on_device(): call(functools.partial(forward_kernel, flip, far, turn == 0, wide, halves...  4.41 us
    pallas_call x1, Pallas kernels, on_device(): pl.pallas_call(backward_kernel, out_shape=(shaped(movie_frames.shape), sh...  2.3 us
    pallas_call x1, Pallas kernels, on_device(): pl.pallas_call(functools.partial(prepare_kernel, rim, cuts), out_shape=(s...  1.9 us
    pallas_call x1, Pallas kernels, on_device(): call(functools.partial(bands_kernel, rim, frames), 'bands', [(width, widt...  1 us
    dynamic_slice x1, local copies, waits for them, and re-layouts, on_device(): lax.dynamic_slice_in_dim(movie_frames, start, BLOCK, axis=2)  0.93 us
  transfers between devices with their start and end apart: 12, of which 5 were waited for; matrix products, arithmetic and copies ran while one was open for 1% of the time, Pallas kernels for 26%

profile of v14, /device:TPU:1, one launch (start us, length us, event | category | flops | bytes accessed | tf_op | source)
XLA Modules:
  0.0 41.8 jit_solution(7632133746135636501)
XLA Ops:
  0.6 0.9 %constant_dynamic-slice_fusion = bf16[2,16,16,128]{3,2,1,0:T(8,128)(2,1)S(1)} fusion(bf16[2,16,128,128]{3,2,1,0:T(8,128)(2,1)} %movie_hbm.1, s32[]{:T(128)S(6)} %select_n.40), kind=kLoop, calls=%fused_computation.10 | loop fusion | bytes 262148 | tf_op jit(solution)/shard_map/dynamic_slice | solution.py:391
  1.6 0.1 collective-permute-start
  1.7 1.9 %prepare.1 = (bf16[16,160,256]{2,1,0:T(8,128)(2,1)S(1)}, bf16[128,128]{1,0:T(8,128)(2,1)S(1)}, bf16[256,768]{1,0:T(8,128)(2,1)S(1)}, s32[128,128]{1,0:T(8,128)S(...) custom-call(f32[25]{0:T(128)} %col_ref, f32[25]{0:T(128)} %row_ref, bf16[2,16,128,128]{3,2,1,0:T(8,128)(2,1)} %movie_hbm.1, ...), custom_call_target="tpu_custom_call" | custom-call | tf_op jit(solution)/shard_map/prepare/pallas_call | solution.py:394
  3.6 0.0 copy-start.3
  3.6 0.0 collective-permute-done.edge_ref
  3.6 1.2 %forward.4 = (bf16[16,160,256]{2,1,0:T(8,128)(2,1)S(1)}, bf16[512,256]{1,0:T(8,128)(2,1)S(1)}, bf16[512,128]{1,0:T(8,128)(2,1)S(1)}) custom-call(bf16[16,160,256]{2,1,0:T(8,128)(2,1)S(1)} %get-tuple-element.51.smooth_in_ref, bf16[2,16,16,128]{3,2,1,0:T(8,128)(2,1)S(1)} %collective-permute-done.edge_ref, ...), custom_call_target="tpu_custom_call", output_to_operand_aliasing={{0}: (0, {})} | custom-call | tf_op jit(solution)/shard_map/forward/pallas_call | solution.py:432
  4.9 0.0 copy-done.3
  4.9 2.7 %collective-permute-start.2 = (bf16[512,128]{1,0:T(8,128)(2,1)S(1)}, bf16[512,128]{1,0:T(8,128)(2,1)S(1)}, u32[]{:S(2)}, u32[]{:S(2)}) collective-permute-start(bf16[512,128]{1,0:T(8,128)(2,1)S(1)} %get-tuple-element.66), channel_id=1, source_target_pairs={{0,2},{2,0},{1,3},{3,1},{4,6},{6,4},{5,7},{7,5},{8,10},{10,8},{9,1... | collective-permute-start | bytes 393224 | tf_op jit(solution)/shard_map/ppermute | solution.py:19
  7.6 1.0 %forward.5 = (bf16[16,160,256]{2,1,0:T(8,128)(2,1)S(1)}, bf16[512,256]{1,0:T(8,128)(2,1)S(1)}, bf16[512,128]{1,0:T(8,128)(2,1)S(1)}) custom-call(bf16[16,160,256]{2,1,0:T(8,128)(2,1)S(1)} %get-tuple-element.56.smooth_in_ref, bf16[2,16,16,128]{3,2,1,0:T(8,128)(2,1)S(1)} %collective-permute-done.edge_ref, ...), custom_call_target="tpu_custom_call", output_to_operand_aliasing={{0}: (0, {})} | custom-call | tf_op jit(solution)/shard_map/forward/pallas_call | solution.py:432
  8.7 0.0 copy-start.4
  8.7 1.1 %forward.6 = (bf16[16,160,256]{2,1,0:T(8,128)(2,1)S(1)}, bf16[512,256]{1,0:T(8,128)(2,1)S(1)}, bf16[512,128]{1,0:T(8,128)(2,1)S(1)}) custom-call(bf16[16,160,256]{2,1,0:T(8,128)(2,1)S(1)} %get-tuple-element.57.smooth_in_ref, bf16[2,16,16,128]{3,2,1,0:T(8,128)(2,1)S(1)} %collective-permute-done.edge_ref, ...), custom_call_target="tpu_custom_call", output_to_operand_aliasing={{0}: (0, {})} | custom-call | tf_op jit(solution)/shard_map/forward/pallas_call | solution.py:432
  9.7 0.1 collective-permute-start.1
  9.8 0.0 copy-done.4
  9.8 0.1 broadcast_multiply_fusion
  9.9 0.1 select_reduce_fusion
  10.0 0.0 copy-start
  10.1 0.0 copy-start.1
  10.1 0.0 copy-start.2
  10.1 1.1 %forward.7 = (bf16[16,160,256]{2,1,0:T(8,128)(2,1)S(1)}, bf16[512,256]{1,0:T(8,128)(2,1)S(1)}, bf16[512,128]{1,0:T(8,128)(2,1)S(1)}) custom-call(bf16[16,160,256]{2,1,0:T(8,128)(2,1)S(1)} %get-tuple-element.58.smooth_in_ref, bf16[2,16,16,128]{3,2,1,0:T(8,128)(2,1)S(1)} %collective-permute-done.edge_ref, ...), custom_call_target="tpu_custom_call", output_to_operand_aliasing={{0}: (0, {})} | custom-call | tf_op jit(solution)/shard_map/forward/pallas_call | solution.py:432
  11.2 0.3 collective-permute-done.2.refs_1_
  11.5 3.4 %collective-permute-start.5 = (bf16[272,128]{1,0:T(8,128)(2,1)S(1)}, bf16[272,128]{1,0:T(8,128)(2,1)S(1)}, u32[]{:S(2)}, u32[]{:S(2)}) collective-permute-start(bf16[272,128]{1,0:T(8,128)(2,1)S(1)} %sum.5), channel_id=1, source_target_pairs={{0,12},{4,8},{8,4},{12,0},{1,13},{5,9},{9,5},{13,1},{2,14},{6,10},... | collective-permute-start | bytes 208904 | tf_op jit(solution)/shard_map/ppermute | solution.py:19
  14.9 0.1 collective-permute-start.4
  15.0 0.0 collective-permute-done.1.refs_1_
  15.1 0.9 %collective-permute-start.3 = (bf16[272,128]{1,0:T(8,128)(2,1)S(1)}, bf16[272,128]{1,0:T(8,128)(2,1)S(1)}, u32[]{:S(2)}, u32[]{:S(2)}) collective-permute-start(bf16[272,128]{1,0:T(8,128)(2,1)S(1)} %sum.3), channel_id=1, source_target_pairs={{0,4},{4,0},{8,12},{12,8},{1,5},{5,1},{9,13},{13,9},{2,6},{6,2},{1... | collective-permute-start | bytes 208904 | tf_op jit(solution)/shard_map/ppermute | solution.py:19
  16.0 0.0 copy-done
  16.0 1.0 %bands.1 = (bf16[256,256]{1,0:T(8,128)(2,1)S(1)}, bf16[256,768]{1,0:T(8,128)(2,1)S(1)}) custom-call(f32[25]{0:T(128)S(1)} %copy-done, f32[25]{0:T(128)S(1)} %copy-done.1), custom_call_target="tpu_custom_call" | custom-call | tf_op jit(solution)/shard_map/bands/pallas_call | solution.py:465
  17.0 0.0 collective-permute-done.5.refs_4_
  17.0 3.9 %collective-permute-done.4.refs_3_ = bf16[272,128]{1,0:T(8,128)(2,1)S(1)} collective-permute-done((bf16[272,128]{1,0:T(8,128)(2,1)S(1)}, bf16[272,128]{1,0:T(8,128)(2,1)S(1)}, u32[]{:S(2)}, u32[]{:S(2)}) %collective-permute-start.4) | collective-permute-done | bytes 69664 | tf_op jit(solution)/shard_map/ppermute | solution.py:19
  20.9 0.0 collective-permute-done.3.refs_2_
  20.9 0.8 %mix.1 = (bf16[16,16,128]{2,1,0:T(8,128)(2,1)S(1)}, bf16[16,16,128]{2,1,0:T(8,128)(2,1)S(1)}, bf16[16,16,128]{2,1,0:T(8,128)(2,1)S(1)}, bf16[16,16,128]{2,1,0:T(8,128)(2,1)S(1)}) custom-call(s32[1,128]{1,0:T(1,128)S(1)} %bitcast.8, bf16[16,128]{1,0:T(8,128)(2,1)S(1)} %pad_bitcast_fusion.lag_ref, bf16[512,128]{1,0:T(8,128)(2,1)S(1)} %get-tuple-element.71.refs_0_, ...), custom_call_target="tpu_custom_call" | custom-call | tf_op jit(solution)/shard_map/mix/pallas_call | solution.py:473
  21.7 0.1 collective-permute-start.6
  21.8 1.8 %collective-permute-start.7 = (bf16[16,16,128]{2,1,0:T(8,128)(2,1)S(1)}, bf16[16,16,128]{2,1,0:T(8,128)(2,1)S(1)}, u32[]{:S(2)}, u32[]{:S(2)}) collective-permute-start(bf16[16,16,128]{2,1,0:T(8,128)(2,1)S(1)} %get-tuple-element.76), channel_id=1, source_target_pairs={{0,8},{4,12},{8,0},{12,4},{1,9},{5,13},{9,1},{13,5},{2,10},{6,14},... | collective-permute-start | bytes 196616 | tf_op jit(solution)/shard_map/ppermute | solution.py:19
  23.6 1.7 %collective-permute-start.8 = (bf16[16,16,128]{2,1,0:T(8,128)(2,1)S(1)}, bf16[16,16,128]{2,1,0:T(8,128)(2,1)S(1)}, u32[]{:S(2)}, u32[]{:S(2)}) collective-permute-start(bf16[16,16,128]{2,1,0:T(8,128)(2,1)S(1)} %get-tuple-element.77), channel_id=1, source_target_pairs={{0,12},{4,8},{8,4},{12,0},{1,13},{5,9},{9,5},{13,1},{2,14},{6,10},... | collective-permute-start | bytes 196616 | tf_op jit(solution)/shard_map/ppermute | solution.py:19
  25.4 0.0 collective-permute-done.6
  25.4 1.1 %collective-permute-start.9 = (bf16[32,16,128]{2,1,0:T(8,128)(2,1)S(1)}, bf16[32,16,128]{2,1,0:T(8,128)(2,1)S(1)}, u32[]{:S(2)}, u32[]{:S(2)}) collective-permute-start(bf16[32,16,128]{2,1,0:T(8,128)(2,1)S(1)} %constant_dynamic-update-slice_fusion.refs_0_), channel_id=1, source_target_pairs={{0,2},{2,0},{1,3},{3,1},{4,6},{6,4},{5,7},{7,5},{8,10},{10,8},{9,1... | collective-permute-start | bytes 393224 | tf_op jit(solution)/shard_map/ppermute | solution.py:19
  26.4 1.3 %residual.4 = (bf16[512,256]{1,0:T(8,128)(2,1)S(1)}, bf16[256,256]{1,0:T(8,128)(2,1)S(1)}, bf16[32,16,128]{2,1,0:T(8,128)(2,1)S(1)}) custom-call(bf16[512,256]{1,0:T(8,128)(2,1)S(1)} %get-tuple-element.59.filtered_ref, s32[128,128]{1,0:T(8,128)S(1)} %get-tuple-element.54.code_ref, bf16[512,256]{1,0:T(8,128)(2,1)S(1)} %get-tuple-element.60.templates_ref, ...), custom_call_target="tpu_custom_call" | custom-call | tf_op jit(solution)/shard_map/residual/pallas_call | solution.py:494
  27.7 0.0 collective-permute-done.7.refs_0_
  27.7 1.6 %collective-permute-done.8.refs_1_ = bf16[16,16,128]{2,1,0:T(8,128)(2,1)S(1)} collective-permute-done((bf16[16,16,128]{2,1,0:T(8,128)(2,1)S(1)}, bf16[16,16,128]{2,1,0:T(8,128)(2,1)S(1)}, u32[]{:S(2)}, u32[]{:S(2)}) %collective-permute-start.8) | collective-permute-done | bytes 65568 | tf_op jit(solution)/shard_map/ppermute | solution.py:19
  29.3 0.4 collective-permute-start.10
  29.7 1.3 %residual.5 = (bf16[512,256]{1,0:T(8,128)(2,1)S(1)}, bf16[256,256]{1,0:T(8,128)(2,1)S(1)}, bf16[32,16,128]{2,1,0:T(8,128)(2,1)S(1)}) custom-call(bf16[512,256]{1,0:T(8,128)(2,1)S(1)} %get-tuple-element.75.filtered_ref, s32[128,128]{1,0:T(8,128)S(1)} %get-tuple-element.54.code_ref, bf16[512,256]{1,0:T(8,128)(2,1)S(1)} %get-tuple-element.60.templates_ref, ...), custom_call_target="tpu_custom_call" | custom-call | tf_op jit(solution)/shard_map/residual/pallas_call | solution.py:494
  30.9 0.0 collective-permute-done.9.refs_0_
  31.0 1.3 %residual.6 = (bf16[512,256]{1,0:T(8,128)(2,1)S(1)}, bf16[256,256]{1,0:T(8,128)(2,1)S(1)}, bf16[32,16,128]{2,1,0:T(8,128)(2,1)S(1)}) custom-call(bf16[512,256]{1,0:T(8,128)(2,1)S(1)} %get-tuple-element.82.filtered_ref, s32[128,128]{1,0:T(8,128)S(1)} %get-tuple-element.54.code_ref, bf16[512,256]{1,0:T(8,128)(2,1)S(1)} %get-tuple-element.60.templates_ref, ...), custom_call_target="tpu_custom_call" | custom-call | tf_op jit(solution)/shard_map/residual/pallas_call | solution.py:494
  32.2 1.0 %collective-permute-done.10.refs_0_ = bf16[32,16,128]{2,1,0:T(8,128)(2,1)S(1)} collective-permute-done((bf16[32,16,128]{2,1,0:T(8,128)(2,1)S(1)}, bf16[32,16,128]{2,1,0:T(8,128)(2,1)S(1)}, u32[]{:S(2)}, u32[]{:S(2)}) %collective-permute-start.10) | collective-permute-done | bytes 131104 | tf_op jit(solution)/shard_map/ppermute | solution.py:19
  33.2 1.3 %residual.7 = (bf16[512,256]{1,0:T(8,128)(2,1)S(1)}, bf16[256,256]{1,0:T(8,128)(2,1)S(1)}, bf16[32,16,128]{2,1,0:T(8,128)(2,1)S(1)}) custom-call(bf16[512,256]{1,0:T(8,128)(2,1)S(1)} %get-tuple-element.84.filtered_ref, s32[128,128]{1,0:T(8,128)S(1)} %get-tuple-element.54.code_ref, bf16[512,256]{1,0:T(8,128)(2,1)S(1)} %get-tuple-element.60.templates_ref, ...), custom_call_target="tpu_custom_call" | custom-call | tf_op jit(solution)/shard_map/residual/pallas_call | solution.py:494
  34.5 4.0 %collective-permute-start.11 = (bf16[256,256]{1,0:T(8,128)(2,1)S(1)}, bf16[256,256]{1,0:T(8,128)(2,1)S(1)}, u32[]{:S(2)}, u32[]{:S(2)}) collective-permute-start(bf16[256,256]{1,0:T(8,128)(2,1)S(1)} %select_select_fusion), channel_id=1, source_target_pairs={{0,1},{1,0},{2,3},{3,2},{4,5},{5,4},{6,7},{7,6},{8,9},{9,8},{10,11... | collective-permute-start | bytes 393224 | tf_op jit(solution)/shard_map/ppermute | solution.py:19
  38.5 0.7 %emit.1 = (bf16[64,16,128]{2,1,0:T(8,128)(2,1)S(1)}, bf16[2048,256]{1,0:T(8,128)(2,1)S(1)}) custom-call(bf16[32,16,128]{2,1,0:T(8,128)(2,1)S(1)} %get-tuple-element.74.refs_0_, bf16[32,16,128]{2,1,0:T(8,128)(2,1)S(1)} %get-tuple-element.81.refs_1_, bf16[32,16,128]{2,1,0:T(8,128)(2,1)S(1)} %get-tuple-element.83.refs_2_, ...), custom_call_target="tpu_custom_call" | custom-call | tf_op jit(solution)/shard_map/emit/pallas_call | solution.py:520
  39.3 0.2 collective-permute-done.11.edge_ref
  39.5 2.3 %backward.1 = (bf16[2,16,128,128]{3,2,1,0:T(8,128)(2,1)}, bf16[64,16,128]{2,1,0:T(8,128)(2,1)}) custom-call(bf16[64,16,128]{2,1,0:T(8,128)(2,1)S(1)} %get-tuple-element.92.turned_ref, bf16[256,256]{1,0:T(8,128)(2,1)S(1)} %collective-permute-done.11.edge_ref, bf16[256,256]{1,0:T(8,128)(2,1)S(1)} %get-tuple-element.95.col_adj_ref, ...), custom_call_target="tpu_custom_call" | custom-call | tf_op jit(solution)/shard_map/backward/pallas_call | solution.py:533
  (13 shorter events, 0.1 us)
Async XLA Ops:
  1.6 2.1 %collective-permute-start = (bf16[2,16,16,128]{3,2,1,0:T(8,128)(2,1)S(1)}, bf16[2,16,16,128]{3,2,1,0:T(8,128)(2,1)S(1)}, u32[]{:S(2)}, u32[]{:S(2)}) collective-permute-start(bf16[2,16,16,128]{3,2,1,0:T(8,128)(2,1)S(1)} %constant_dynamic-slice_fusion), channel_id=1, source_target_pairs={{0,1},{1,0},{2,3},{3,2},{4,5},{5,4},{6,7},{7,6},{8,9},{9,8},{10,11... | collective-permute-start | bytes 393224 | tf_op jit(solution)/shard_map/ppermute | solution.py:19
  3.6 1.3 %copy-start.3 = (f32[1,3,65]{2,0,1:T(1,128)S(1)}, f32[1,3,65]{2,0,1:T(1,128)}, u32[]{:S(2)}) copy-start(f32[1,3,65]{2,0,1:T(1,128)} %param.16) | copy-start | bytes 2344
  4.9 6.6 %collective-permute-start.2 = (bf16[512,128]{1,0:T(8,128)(2,1)S(1)}, bf16[512,128]{1,0:T(8,128)(2,1)S(1)}, u32[]{:S(2)}, u32[]{:S(2)}) collective-permute-start(bf16[512,128]{1,0:T(8,128)(2,1)S(1)} %get-tuple-element.66), channel_id=1, source_target_pairs={{0,2},{2,0},{1,3},{3,1},{4,6},{6,4},{5,7},{7,5},{8,10},{10,8},{9,1... | collective-permute-start | bytes 393224 | tf_op jit(solution)/shard_map/ppermute | solution.py:19
  8.7 1.2 %copy-start.4 = (s32[1,3]{1,0:T(1,128)S(1)}, s32[1,3]{1,0:T(1,128)}, u32[]{:S(2)}) copy-start(s32[1,3]{1,0:T(1,128)} %param.17) | copy-start | bytes 40
  9.7 5.3 %collective-permute-start.1 = (bf16[512,128]{1,0:T(8,128)(2,1)S(1)}, bf16[512,128]{1,0:T(8,128)(2,1)S(1)}, u32[]{:S(2)}, u32[]{:S(2)}) collective-permute-start(bf16[512,128]{1,0:T(8,128)(2,1)S(1)} %get-tuple-element.64), channel_id=1, source_target_pairs={{0,2},{2,0},{1,3},{3,1},{4,6},{6,4},{5,7},{7,5},{8,10},{10,8},{9,1... | collective-permute-start | bytes 393224 | tf_op jit(solution)/shard_map/ppermute | solution.py:19
  10.0 5.9 %copy-start = (f32[25]{0:T(128)S(1)}, f32[25]{0:T(128)}, u32[]{:S(2)}) copy-start(f32[25]{0:T(128)} %col_ref) | copy-start | bytes 304
  10.1 5.9 %copy-start.1 = (f32[25]{0:T(128)S(1)}, f32[25]{0:T(128)}, u32[]{:S(2)}) copy-start(f32[25]{0:T(128)} %row_ref) | copy-start | bytes 304
  10.1 10.9 %copy-start.2 = (s32[128,1]{0,1:T(1,128)S(1)}, s32[128,1]{0,1:T(1,128)}, u32[]{:S(2)}) copy-start(s32[128,1]{0,1:T(1,128)} %param.11) | copy-start | bytes 1540
  11.5 5.5 %collective-permute-start.5 = (bf16[272,128]{1,0:T(8,128)(2,1)S(1)}, bf16[272,128]{1,0:T(8,128)(2,1)S(1)}, u32[]{:S(2)}, u32[]{:S(2)}) collective-permute-start(bf16[272,128]{1,0:T(8,128)(2,1)S(1)} %sum.5), channel_id=1, source_target_pairs={{0,12},{4,8},{8,4},{12,0},{1,13},{5,9},{9,5},{13,1},{2,14},{6,10},... | collective-permute-start | bytes 208904 | tf_op jit(solution)/shard_map/ppermute | solution.py:19
  14.9 6.0 %collective-permute-start.4 = (bf16[272,128]{1,0:T(8,128)(2,1)S(1)}, bf16[272,128]{1,0:T(8,128)(2,1)S(1)}, u32[]{:S(2)}, u32[]{:S(2)}) collective-permute-start(bf16[272,128]{1,0:T(8,128)(2,1)S(1)} %sum.4), channel_id=1, source_target_pairs={{0,8},{4,12},{8,0},{12,4},{1,9},{5,13},{9,1},{13,5},{2,10},{6,14},... | collective-permute-start | bytes 208904 | tf_op jit(solution)/shard_map/ppermute | solution.py:19
  15.1 5.9 %collective-permute-start.3 = (bf16[272,128]{1,0:T(8,128)(2,1)S(1)}, bf16[272,128]{1,0:T(8,128)(2,1)S(1)}, u32[]{:S(2)}, u32[]{:S(2)}) collective-permute-start(bf16[272,128]{1,0:T(8,128)(2,1)S(1)} %sum.3), channel_id=1, source_target_pairs={{0,4},{4,0},{8,12},{12,8},{1,5},{5,1},{9,13},{13,9},{2,6},{6,2},{1... | collective-permute-start | bytes 208904 | tf_op jit(solution)/shard_map/ppermute | solution.py:19
  21.7 3.6 %collective-permute-start.6 = (bf16[16,16,128]{2,1,0:T(8,128)(2,1)S(1)}, bf16[16,16,128]{2,1,0:T(8,128)(2,1)S(1)}, u32[]{:S(2)}, u32[]{:S(2)}) collective-permute-start(bf16[16,16,128]{2,1,0:T(8,128)(2,1)S(1)} %get-tuple-element.73), channel_id=1, source_target_pairs={{0,4},{4,0},{8,12},{12,8},{1,5},{5,1},{9,13},{13,9},{2,6},{6,2},{1... | collective-permute-start | bytes 196616 | tf_op jit(solution)/shard_map/ppermute | solution.py:19
  21.8 5.9 %collective-permute-start.7 = (bf16[16,16,128]{2,1,0:T(8,128)(2,1)S(1)}, bf16[16,16,128]{2,1,0:T(8,128)(2,1)S(1)}, u32[]{:S(2)}, u32[]{:S(2)}) collective-permute-start(bf16[16,16,128]{2,1,0:T(8,128)(2,1)S(1)} %get-tuple-element.76), channel_id=1, source_target_pairs={{0,8},{4,12},{8,0},{12,4},{1,9},{5,13},{9,1},{13,5},{2,10},{6,14},... | collective-permute-start | bytes 196616 | tf_op jit(solution)/shard_map/ppermute | solution.py:19
  23.6 5.7 %collective-permute-start.8 = (bf16[16,16,128]{2,1,0:T(8,128)(2,1)S(1)}, bf16[16,16,128]{2,1,0:T(8,128)(2,1)S(1)}, u32[]{:S(2)}, u32[]{:S(2)}) collective-permute-start(bf16[16,16,128]{2,1,0:T(8,128)(2,1)S(1)} %get-tuple-element.77), channel_id=1, source_target_pairs={{0,12},{4,8},{8,4},{12,0},{1,13},{5,9},{9,5},{13,1},{2,14},{6,10},... | collective-permute-start | bytes 196616 | tf_op jit(solution)/shard_map/ppermute | solution.py:19
  25.4 5.6 %collective-permute-start.9 = (bf16[32,16,128]{2,1,0:T(8,128)(2,1)S(1)}, bf16[32,16,128]{2,1,0:T(8,128)(2,1)S(1)}, u32[]{:S(2)}, u32[]{:S(2)}) collective-permute-start(bf16[32,16,128]{2,1,0:T(8,128)(2,1)S(1)} %constant_dynamic-update-slice_fusion.refs_0_), channel_id=1, source_target_pairs={{0,2},{2,0},{1,3},{3,1},{4,6},{6,4},{5,7},{7,5},{8,10},{10,8},{9,1... | collective-permute-start | bytes 393224 | tf_op jit(solution)/shard_map/ppermute | solution.py:19
  29.3 3.9 %collective-permute-start.10 = (bf16[32,16,128]{2,1,0:T(8,128)(2,1)S(1)}, bf16[32,16,128]{2,1,0:T(8,128)(2,1)S(1)}, u32[]{:S(2)}, u32[]{:S(2)}) collective-permute-start(bf16[32,16,128]{2,1,0:T(8,128)(2,1)S(1)} %pad_maximum_fusion), channel_id=1, source_target_pairs={{0,2},{2,0},{1,3},{3,1},{4,6},{6,4},{5,7},{7,5},{8,10},{10,8},{9,1... | collective-permute-start | bytes 393224 | tf_op jit(solution)/shard_map/ppermute | solution.py:19
  34.5 5.0 %collective-permute-start.11 = (bf16[256,256]{1,0:T(8,128)(2,1)S(1)}, bf16[256,256]{1,0:T(8,128)(2,1)S(1)}, u32[]{:S(2)}, u32[]{:S(2)}) collective-permute-start(bf16[256,256]{1,0:T(8,128)(2,1)S(1)} %select_select_fusion), channel_id=1, source_target_pairs={{0,1},{1,0},{2,3},{3,2},{4,5},{5,4},{6,7},{7,6},{8,9},{9,8},{10,11... | collective-permute-start | bytes 393224 | tf_op jit(solution)/shard_map/ppermute | solution.py:19
